TPU v7x, 512 devices: a whole 4x8x8 slice. The times are simulated.
512 devices in a mesh: ctx: 32 (over x_hi, z, core), tp: 16 (over x_lo, y).
Axes of the slice: x: 4 (x_hi: 2, x_lo: 2; x = x_hi * 2 + x_lo), y: 8, z: 8, core: 2. Of those that a mesh axis runs over, the one named last changes fastest.
Arguments:
- queries: bfloat16 [5120, 4096], P('ctx', 'tp'), may hold values from -2.109375 to 2.109375
- keys: bfloat16 [5120, 4096], P('ctx', 'tp'), may hold values from -2.109375 to 2.109375
- values: bfloat16 [5120, 4096], P('ctx', 'tp'), may hold values from -6 to 6
- rates: float32 [32, 5120], P('tp', 'ctx'), may hold values from 2.5e-05 to 0.06, as said below
- init_weight: float32 [32, 128, 128], P('tp'), may hold values from -1.5 to 1.5
- out_weight: bfloat16 [4096, 6144], P('tp'), may hold values from -0.09375 to 0.09375
Outputs:
- mixed: bfloat16 [5120, 6144], P('ctx', 'tp')
Inputs may be any that keep to these rules, and one draw needn't show every extreme that they name: `rates`: positive.
All inputs are finite; a program needn't handle non-finite values.
Results may differ from a plain program's by a relative error of at most 0.0049.
Values sent between devices are 32-bit elements; how exact they have to be, the bound alone decides.
No kernel may reach another device: no remote copies, remote signals or barrier semaphores. Data moves between devices by JAX's collectives and lax.ppermute only.
A program may use at most 64 MiB of HBM per device.

v0:
```python
import functools

import jax
import jax.numpy as jnp
from jax import lax
from jax.experimental import pallas as pl
from jax.experimental.pallas import tpu as pltpu
from jax.sharding import Mesh, PartitionSpec as P

MB = 16
HW = 128
XH, Z, CORE, XL, Y = "xh", "z", "core", "xl", "y"
SIZES = (2, 8, 2, 2, 8)
f32 = jnp.float32
bf16 = jnp.bfloat16
VM = pl.BlockSpec(memory_space=pltpu.VMEM)
SM = pl.BlockSpec(memory_space=pltpu.SMEM)


def exact(a, b, contract=((1,), (0,))):
    return lax.dot_general(
        a, b, (contract, ((), ())), precision=lax.Precision.HIGHEST, preferred_element_type=f32
    )


def single(a, b, contract=((1,), (0,))):
    return lax.dot_general(a, b, (contract, ((), ())), preferred_element_type=f32)


def call(kernel, out_shapes, *args, scalars=0, scratch=(), cost=1e6):
    outs = [jax.ShapeDtypeStruct(s, d) for s, d in out_shapes]
    return pl.pallas_call(
        kernel,
        out_shape=outs,
        in_specs=[SM] * scalars + [VM] * (len(args) - scalars),
        out_specs=[VM] * len(outs),
        scratch_shapes=list(scratch),
        compiler_params=pltpu.CompilerParams(vmem_limit_bytes=40 * 2**20),
        cost_estimate=pl.CostEstimate(flops=int(cost), bytes_accessed=int(cost / 100), transcendentals=0),
    )(*args)


def shard_maps(core_ref, q_ref, k_ref, v_ref, r_ref, keep_ref, send_ref, lead_ref, rest_ref, x_ref):
    rows = q_ref.shape[0]
    core = core_ref[0]
    s_at = lax.broadcasted_iota(jnp.int32, (rows, rows), 0)
    t_at = lax.broadcasted_iota(jnp.int32, (rows, rows), 1)
    earlier_block = (t_at // MB) < (s_at // MB)
    causal = t_at <= s_at
    diagonal = t_at == s_at
    eye = (
        lax.broadcasted_iota(jnp.int32, (HW, 2 * HW), 0)
        == lax.broadcasted_iota(jnp.int32, (HW, 2 * HW), 1)
    ).astype(f32)
    mix, key_gram, columns = [], [], []
    for h in range(2):
        at = slice(h * HW, (h + 1) * HW)
        q, k, v = q_ref[:, at], k_ref[:, at], v_ref[:, at]
        r = r_ref[h : h + 1, :]
        columns.append(jnp.sum(jnp.where(diagonal, r, 0.0), axis=1, keepdims=True))
        key_gram.append(jnp.where(earlier_block, single(k, k, ((1,), (1,))) * r, 0.0))
        mix.append(jnp.where(causal, single(q, k, ((1,), (1,))) * r, 0.0))
        x_ref[h, :, :HW] = k.astype(f32)
        x_ref[h, :, HW:] = v.astype(f32)
    for i in range(1, rows // MB):
        at = slice(i * MB, (i + 1) * MB)
        for h in range(2):
            x_ref[h, at, :] = x_ref[h, at, :] - exact(key_gram[h][at, :], x_ref[h])
    maps = []
    for h in range(2):
        at = slice(h * HW, (h + 1) * HW)
        x = x_ref[h]
        y = exact(mix[h], x)
        lead_ref[:, at] = q_ref[:, at].astype(f32) - y[:, :HW]
        rest_ref[:, at] = y[:, HW:]
        ab = exact(k_ref[:, at].astype(f32) * columns[h], x, ((0,), (0,)))
        sign = jnp.where(lax.broadcasted_iota(jnp.int32, (HW, 2 * HW), 1) < HW, -1.0, 1.0)
        maps.append(eye + sign * ab)
    first = core == 0
    keep_ref[...] = jnp.where(first, maps[0], maps[1])
    send_ref[...] = jnp.where(first, maps[1], maps[0])


def after(second, first):
    moved = exact(second[:, :HW], first)
    return moved + jnp.where(lax.broadcasted_iota(jnp.int32, second.shape, 1) < HW, 0.0, second)


def chip_map(core_ref, keep_ref, got_ref, out_ref):
    first = core_ref[0] == 0
    early = jnp.where(first, keep_ref[...], got_ref[...])
    late = jnp.where(first, got_ref[...], keep_ref[...])
    out_ref[...] = after(late, early)


def ring_prefix(at_ref, w0_ref, own, l1, l2, l3, r1, r2, r3, far, pre_ref, end_ref, maps, state):
    z = at_ref[0]
    x_hi = at_ref[1]
    n = SIZES[1]
    for offset, ref in ((0, own), (-1, l1), (-2, l2), (-3, l3), (1, r1), (2, r2), (3, r3), (4, far)):
        maps[lax.rem(z + (offset + n), n)] = ref[...]
    eye = (
        lax.broadcasted_iota(jnp.int32, (HW, HW), 0) == lax.broadcasted_iota(jnp.int32, (HW, HW), 1)
    ).astype(f32)
    now = jnp.concatenate([eye, jnp.where(x_hi == 0, w0_ref[...], 0.0)], axis=1)
    state[0] = now
    for i in range(n):
        now = after(maps[i], now)
        state[i + 1] = now
    pre_ref[...] = state[z]
    end_ref[...] = now[:, HW:]


def shard_states(at_ref, pre_ref, got_ref, keep_map_ref, got_map_ref, keep_ref, send_ref):
    x_hi, core = at_ref[1], at_ref[2]
    first = core == 0
    pre = pre_ref[...]
    start = jnp.where(x_hi == 0, pre[:, HW:], exact(pre[:, :HW], got_ref[...]) + pre[:, HW:])
    early = jnp.where(first, keep_map_ref[...], got_map_ref[...])
    middle = exact(early[:, :HW], start) + early[:, HW:]
    keep_ref[...] = jnp.where(first, start, middle)
    send_ref[...] = jnp.where(first, middle, start)


def outputs(at_ref, keep_ref, got_ref, lead_ref, rest_ref, z_ref):
    first = at_ref[2] == 0
    states = (
        jnp.where(first, keep_ref[...], got_ref[...]),
        jnp.where(first, got_ref[...], keep_ref[...]),
    )
    for h in range(2):
        at = slice(h * HW, (h + 1) * HW)
        z = exact(lead_ref[:, at], states[h]) + rest_ref[:, at]
        z_ref[:, at] = z.astype(bf16).astype(f32)


def narrow(at_ref, mine_ref, other_ref, out_ref):
    first = at_ref[2] == 0
    out_ref[:HW, :] = jnp.where(first, mine_ref[...], other_ref[...]).astype(bf16)
    out_ref[HW:, :] = jnp.where(first, other_ref[...], mine_ref[...]).astype(bf16)


def project(z_ref, zx_ref, w_ref, wx_ref, out_ref):
    out_ref[0] = single(z_ref[...].astype(bf16), w_ref[...]) + single(
        zx_ref[...].astype(bf16), wx_ref[...]
    )


def rotated(x, axis, by):
    n = lax.axis_size(axis)
    return lax.ppermute(x, axis, [(i, (i + by) % n) for i in range(n)])


def gather_ring(x, axis):
    half = x.shape[0] // 2
    before, beyond = [x], [x]
    for _ in range(3):
        before.append(rotated(before[-1], axis, 1))
        beyond.append(rotated(beyond[-1], axis, -1))
    low = rotated(before[-1][:half], axis, 1)
    high = rotated(beyond[-1][half:], axis, -1)
    return before[1:], beyond[1:], jnp.concatenate([low, high], axis=0)


def scatter_ring(pieces, axis):
    n = lax.axis_size(axis)
    me = lax.axis_index(axis)
    half = pieces.shape[1] // 2

    def piece(offset):
        return lax.dynamic_index_in_dim(pieces, lax.rem(me + (offset + n), n), 0, keepdims=False)

    far = piece(4)
    down = jnp.concatenate([rotated(far[:half], axis, -1), jnp.zeros_like(far[half:])], axis=0) + piece(-3)
    up = jnp.concatenate([jnp.zeros_like(far[:half]), rotated(far[half:], axis, 1)], axis=0) + piece(3)
    for step in (2, 1):
        down = rotated(down, axis, -1) + piece(-step)
        up = rotated(up, axis, 1) + piece(step)
    return rotated(down, axis, -1) + rotated(up, axis, 1) + piece(0)


def local(queries, keys, values, rates, init_weight, out_weight):
    rows = queries.shape[0]
    x_hi, z, core, x_lo = (lax.axis_index(a) for a in (XH, Z, CORE, XL))
    at = jnp.stack([z, x_hi, core]).astype(jnp.int32)
    core_at = core.reshape(1).astype(jnp.int32)
    features = out_weight.shape[1] // 2
    chunk = features // SIZES[4]

    mine_columns = lax.dynamic_slice_in_dim(out_weight, x_lo * features, features, 1)
    to_send = lax.dynamic_slice(out_weight, (core * HW, (1 - x_lo) * features), (HW, features))
    from_pair = rotated(to_send.astype(f32), XL, 1)
    from_core = rotated(from_pair, CORE, 1)

    keep, send, lead, rest = call(
        shard_maps,
        [((HW, 2 * HW), f32)] * 2 + [((rows, 2 * HW), f32)] * 2,
        core_at, queries, keys, values, rates,
        scalars=1, scratch=[pltpu.VMEM((2, rows, 2 * HW), f32)], cost=2e9,
    )
    got = rotated(send, CORE, 1)
    (own,) = call(chip_map, [((HW, 2 * HW), f32)], core_at, keep, got, scalars=1)
    before, beyond, far = gather_ring(own, Z)
    w0 = lax.dynamic_index_in_dim(init_weight, core, 0, keepdims=False)
    pre, end = call(
        ring_prefix,
        [((HW, 2 * HW), f32), ((HW, HW), f32)],
        at, w0, own, *before, *beyond, far,
        scalars=1,
        scratch=[pltpu.VMEM((8, HW, 2 * HW), f32), pltpu.VMEM((9, HW, 2 * HW), f32)],
    )
    arrived = lax.ppermute(end, XH, [(0, 1)])
    kept, leaving = call(
        shard_states, [((HW, HW), f32)] * 2, at, pre, arrived, keep, got, scalars=1
    )
    came = rotated(leaving, CORE, 1)
    (z_rows,) = call(outputs, [((rows, 2 * HW), f32)], at, kept, came, lead, rest, scalars=1)
    z_pair = rotated(z_rows, XL, 1)

    (pair_columns,) = call(narrow, [((2 * HW, features), bf16)], at, from_pair, from_core, scalars=1)
    pieces = pl.pallas_call(
        project,
        grid=(SIZES[4],),
        out_shape=jax.ShapeDtypeStruct((SIZES[4], rows, chunk), f32),
        in_specs=[
            pl.BlockSpec((rows, 2 * HW), lambda i: (0, 0)),
            pl.BlockSpec((rows, 2 * HW), lambda i: (0, 0)),
            pl.BlockSpec((2 * HW, chunk), lambda i: (0, i)),
            pl.BlockSpec((2 * HW, chunk), lambda i: (0, i)),
        ],
        out_specs=pl.BlockSpec((1, rows, chunk), lambda i: (i, 0, 0)),
        compiler_params=pltpu.CompilerParams(vmem_limit_bytes=40 * 2**20),
    )(z_rows, z_pair, mine_columns, pair_columns)
    return scatter_ring(pieces, Y).astype(bf16)


def solution(mesh):
    fine = Mesh(mesh.devices.reshape(SIZES), (XH, Z, CORE, XL, Y))
    ctx, tp = (XH, Z, CORE), (XL, Y)
    in_specs = (P(ctx, tp), P(ctx, tp), P(ctx, tp), P(tp, ctx), P(tp, None, None), P(tp, None))
    return jax.shard_map(local, mesh=fine, in_specs=in_specs, out_specs=P(ctx, tp), check_vma=False)
```

profile of v0, /device:TPU:4, one launch (start us, length us, event | category | flops | bytes accessed | tf_op | source)
XLA Modules:
  0.0 172.8 jit_solution(824060912840388085)
XLA Ops:
  0.0 1.4 dynamic-slice_convert_fusion
  1.4 3.1 %collective-permute-start.12 = (f32[128,3072]{1,0:T(8,128)S(1)}, f32[128,3072]{1,0:T(8,128)S(1)}, u32[]{:S(2)}, u32[]{:S(2)}) collective-permute-start(f32[128,3072]{1,0:T(8,128)S(1)} %dynamic-slice_convert_fusion), channel_id=1, source_target_pairs={{0,8},{8,0},{1,9},{9,1},{2,10},{10,2},{3,11},{11,3},{4,12},{12,4},... | collective-permute-start | bytes 4718600 | tf_op jit(solution)/shard_map/ppermute | solution.py:151
  4.5 34.9 %collective-permute-done.12.mine_ref = f32[128,3072]{1,0:T(8,128)S(1)} collective-permute-done((f32[128,3072]{1,0:T(8,128)S(1)}, f32[128,3072]{1,0:T(8,128)S(1)}, u32[]{:S(2)}, u32[]{:S(2)}) %collective-permute-start.12) | collective-permute-done | bytes 1572896 | tf_op jit(solution)/shard_map/ppermute | solution.py:151
  39.4 1.9 %collective-permute-start.13 = (f32[128,3072]{1,0:T(8,128)S(1)}, f32[128,3072]{1,0:T(8,128)S(1)}, u32[]{:S(2)}, u32[]{:S(2)}) collective-permute-start(f32[128,3072]{1,0:T(8,128)S(1)} %collective-permute-done.12.mine_ref), channel_id=1, source_target_pairs={{0,16},{16,0},{1,17},{17,1},{2,18},{18,2},{3,19},{19,3},{4,20},{20... | collective-permute-start | bytes 4718600 | tf_op jit(solution)/shard_map/ppermute | solution.py:151
  41.4 2.9 %shard_map.64 = (f32[128,256]{1,0:T(8,128)S(1)}, f32[128,256]{1,0:T(8,128)S(1)}, f32[160,256]{1,0:T(8,128)S(1)}, f32[160,256]{1,0:T(8,128)S(1)}) custom-call(s32[1]{0:T(128)} %bitcast.2.core_ref, bf16[160,256]{1,0:T(8,128)(2,1)S(1)} %copy-done.14, bf16[160,256]{1,0:T(8,128)(2,1)S(1)} %copy-done.15, bf16[160,256]{1,0:T(8,128)(2,1)S(1)} %copy-done.16, ...), custom_call_target="tpu_custom_call" | custom-call | flops 2000000000 | bytes 20000000 | tf_op jit(solution)/shard_map/pallas_call | solution.py:32
  44.3 2.4 %collective-permute-start = (f32[128,256]{1,0:T(8,128)S(1)}, f32[128,256]{1,0:T(8,128)S(1)}, u32[]{:S(2)}, u32[]{:S(2)}) collective-permute-start(f32[128,256]{1,0:T(8,128)S(1)} %get-tuple-element.14), channel_id=1, source_target_pairs={{0,16},{16,0},{1,17},{17,1},{2,18},{18,2},{3,19},{19,3},{4,20},{20... | collective-permute-start | bytes 393224 | tf_op jit(solution)/shard_map/ppermute | solution.py:151
  46.7 1.0 collective-permute-done.got_ref.got_map_ref
  47.7 0.3 shard_map.65.own
  48.0 4.3 %collective-permute-start.1 = (f32[128,256]{1,0:T(8,128)S(1)}, f32[128,256]{1,0:T(8,128)S(1)}, u32[]{:S(2)}, u32[]{:S(2)}) collective-permute-start(f32[128,256]{1,0:T(8,128)S(1)} %shard_map.65.own), channel_id=1, source_target_pairs={{0,32},{32,64},{64,96},{96,128},{128,160},{160,192},{192,224},{224... | collective-permute-start | bytes 393224 | tf_op jit(solution)/shard_map/ppermute | solution.py:151
  52.3 8.6 %collective-permute-start.4 = (f32[128,256]{1,0:T(8,128)S(1)}, f32[128,256]{1,0:T(8,128)S(1)}, u32[]{:S(2)}, u32[]{:S(2)}) collective-permute-start(f32[128,256]{1,0:T(8,128)S(1)} %shard_map.65.own), channel_id=1, source_target_pairs={{0,224},{32,0},{64,32},{96,64},{128,96},{160,128},{192,160},{224,1... | collective-permute-start | bytes 393224 | tf_op jit(solution)/shard_map/ppermute | solution.py:151
  60.9 0.7 copy-done.2
  61.5 1.4 collective-permute-done.1.l1
  62.9 1.9 %collective-permute-start.2 = (f32[128,256]{1,0:T(8,128)S(1)}, f32[128,256]{1,0:T(8,128)}, u32[]{:S(2)}, u32[]{:S(2)}) collective-permute-start(f32[128,256]{1,0:T(8,128)S(1)} %collective-permute-done.1.l1), channel_id=1, source_target_pairs={{0,32},{32,64},{64,96},{96,128},{128,160},{160,192},{192,224},{224... | collective-permute-start | bytes 393224 | tf_op jit(solution)/shard_map/ppermute | solution.py:151
  64.9 0.6 copy-done.8
  65.5 5.1 %collective-permute-start.5 = (f32[128,256]{1,0:T(8,128)S(1)}, f32[128,256]{1,0:T(8,128)}, u32[]{:S(2)}, u32[]{:S(2)}) collective-permute-start(f32[128,256]{1,0:T(8,128)S(1)} %collective-permute-done.4.r1), channel_id=1, source_target_pairs={{0,224},{32,0},{64,32},{96,64},{128,96},{160,128},{192,160},{224,1... | collective-permute-start | bytes 393224 | tf_op jit(solution)/shard_map/ppermute | solution.py:151
  70.7 0.6 copy-done.10
  71.3 0.0 collective-permute-done.2.l2
  71.3 1.9 %collective-permute-start.3 = (f32[128,256]{1,0:T(8,128)}, f32[128,256]{1,0:T(8,128)}, u32[]{:S(2)}, u32[]{:S(2)}) collective-permute-start(f32[128,256]{1,0:T(8,128)} %collective-permute-done.2.l2), channel_id=1, source_target_pairs={{0,32},{32,64},{64,96},{96,128},{128,160},{160,192},{192,224},{224... | collective-permute-start | bytes 393224 | tf_op jit(solution)/shard_map/ppermute | solution.py:151
  73.2 5.6 %collective-permute-start.6 = (f32[128,256]{1,0:T(8,128)}, f32[128,256]{1,0:T(8,128)}, u32[]{:S(2)}, u32[]{:S(2)}) collective-permute-start(f32[128,256]{1,0:T(8,128)} %collective-permute-done.5.r2), channel_id=1, source_target_pairs={{0,224},{32,0},{64,32},{96,64},{128,96},{160,128},{192,160},{224,1... | collective-permute-start | bytes 393224 | tf_op jit(solution)/shard_map/ppermute | solution.py:151
  78.8 0.8 collective-permute-done.3.l3
  79.7 0.8 slice.24
  80.5 1.9 %collective-permute-start.7 = (f32[64,256]{1,0:T(8,128)S(1)}, f32[64,256]{1,0:T(8,128)S(1)}, u32[]{:S(2)}, u32[]{:S(2)}) collective-permute-start(f32[64,256]{1,0:T(8,128)S(1)} %slice.24), channel_id=1, source_target_pairs={{0,32},{32,64},{64,96},{96,128},{128,160},{160,192},{192,224},{224... | collective-permute-start | bytes 196616 | tf_op jit(solution)/shard_map/ppermute | solution.py:151
  82.5 0.8 slice.25
  83.3 5.1 %collective-permute-start.8 = (f32[64,256]{1,0:T(8,128)S(1)}, f32[64,256]{1,0:T(8,128)S(1)}, u32[]{:S(2)}, u32[]{:S(2)}) collective-permute-start(f32[64,256]{1,0:T(8,128)S(1)} %slice.25), channel_id=1, source_target_pairs={{0,224},{32,0},{64,32},{96,64},{128,96},{160,128},{192,160},{224,1... | collective-permute-start | bytes 196616 | tf_op jit(solution)/shard_map/ppermute | solution.py:151
  88.4 0.1 pad_add_fusion.at_ref
  88.5 1.8 %collective-permute-done.8 = f32[64,256]{1,0:T(8,128)S(1)} collective-permute-done((f32[64,256]{1,0:T(8,128)S(1)}, f32[64,256]{1,0:T(8,128)S(1)}, u32[]{:S(2)}, u32[]{:S(2)}) %collective-permute-start.8) | collective-permute-done | bytes 65568 | tf_op jit(solution)/shard_map/ppermute | solution.py:151
  90.3 0.9 copy-done.3
  91.2 0.9 copy-done.9
  92.1 0.9 copy-done.11
  93.0 3.2 %shard_map.66 = (f32[128,256]{1,0:T(8,128)S(1)}, f32[128,128]{1,0:T(8,128)S(1)}) custom-call(s32[3]{0:T(128)S(1)} %pad_add_fusion.at_ref, f32[128,128]{1,0:T(8,128)S(1)} %dynamic-slice_bitcast_fusion.2.w0_ref, f32[128,256]{1,0:T(8,128)S(1)} %copy-done.3, f32[128,256]{1,0:T(8,128)S(1)} %copy-done.9, f32[128,256]{1,0:T(8,128)} %collective-permute-done.2.l2, ...), custom_call_target="tpu_custom_call" | custom-call | flops 1000000 | bytes 10000 | tf_op jit(solution)/shard_map/pallas_call | solution.py:32
  96.2 1.3 collective-permute-start.9
  97.5 6.4 %collective-permute-done.9.got_ref = f32[128,128]{1,0:T(8,128)S(1)} collective-permute-done((f32[128,128]{1,0:T(8,128)S(1)}, f32[128,128]{1,0:T(8,128)S(1)}, u32[]{:S(2)}, u32[]{:S(2)}) %collective-permute-start.9) | collective-permute-done | bytes 65568 | tf_op jit(solution)/shard_map/ppermute | solution.py:212
  103.9 1.6 shard_map.67
  105.5 0.6 copy-done.12
  106.1 1.9 %collective-permute-start.10 = (f32[128,128]{1,0:T(8,128)}, f32[128,128]{1,0:T(8,128)S(1)}, u32[]{:S(2)}, u32[]{:S(2)}) collective-permute-start(f32[128,128]{1,0:T(8,128)} %get-tuple-element.18), channel_id=1, source_target_pairs={{0,16},{16,0},{1,17},{17,1},{2,18},{18,2},{3,19},{19,3},{4,20},{20... | collective-permute-start | bytes 196616 | tf_op jit(solution)/shard_map/ppermute | solution.py:151
  108.1 1.4 collective-permute-done.10.got_ref
  109.5 0.9 copy-done.5
  110.4 0.9 copy-done.7
  111.3 0.8 copy-done.13
  112.2 0.8 shard_map.68.z_ref
  113.0 3.1 %collective-permute-start.11 = (f32[160,256]{1,0:T(8,128)S(1)}, f32[160,256]{1,0:T(8,128)}, u32[]{:S(2)}, u32[]{:S(2)}) collective-permute-start(f32[160,256]{1,0:T(8,128)S(1)} %shard_map.68.z_ref), channel_id=1, source_target_pairs={{0,8},{8,0},{1,9},{9,1},{2,10},{10,2},{3,11},{11,3},{4,12},{12,4},... | collective-permute-start | bytes 491528 | tf_op jit(solution)/shard_map/ppermute | solution.py:151
  116.1 2.7 %constant_dynamic-slice_fusion.w_ref = bf16[256,3072]{1,0:T(8,128)(2,1)} fusion(bf16[256,6144]{1,0:T(8,128)(2,1)} %param.11, s32[]{:T(128)S(6)} %select_n.39), kind=kLoop, calls=%fused_computation.13 | loop fusion | bytes 3145732 | tf_op jit(solution)/shard_map/dynamic_slice | solution.py:190
  118.8 0.8 shard_map.69.wx_ref
  119.7 1.6 collective-permute-done.11.zx_ref
  121.3 3.2 %shard_map.70 = f32[8,160,384]{2,1,0:T(8,128)S(1)} custom-call(f32[160,256]{1,0:T(8,128)S(1)} %shard_map.68.z_ref, f32[160,256]{1,0:T(8,128)} %collective-permute-done.11.zx_ref, bf16[256,3072]{1,0:T(8,128)(2,1)S(1)} %copy-done.1, bf16[256,3072]{1,0:T(8,128)(2,1)S(1)} %shard_map.69.wx_ref), custom_call_target="tpu_custom_call" | custom-call | tf_op jit(solution)/shard_map/pallas_call | solution.py:221
  124.6 5.4 %collective-permute-start.14 = (f32[80,384]{1,0:T(8,128)S(1)}, f32[80,384]{1,0:T(8,128)S(1)}, u32[]{:S(2)}, u32[]{:S(2)}) collective-permute-start(f32[80,384]{1,0:T(8,128)S(1)} %get-tuple-element.28), channel_id=1, source_target_pairs={{0,7},{1,0},{2,1},{3,2},{4,3},{5,4},{6,5},{7,6},{8,15},{9,8},{10,9... | collective-permute-start | bytes 368648 | tf_op jit(solution)/shard_map/ppermute | solution.py:151
  129.9 1.9 %collective-permute-start.18 = (f32[80,384]{1,0:T(8,128)S(1)}, f32[80,384]{1,0:T(8,128)S(1)}, u32[]{:S(2)}, u32[]{:S(2)}) collective-permute-start(f32[80,384]{1,0:T(8,128)S(1)} %get-tuple-element.27), channel_id=1, source_target_pairs={{0,1},{1,2},{2,3},{3,4},{4,5},{5,6},{6,7},{7,0},{8,9},{9,10},{10,1... | collective-permute-start | bytes 368648 | tf_op jit(solution)/shard_map/ppermute | solution.py:151
  131.9 0.5 collective-permute-done.14
  132.4 5.6 %collective-permute-done.18 = f32[80,384]{1,0:T(8,128)S(1)} collective-permute-done((f32[80,384]{1,0:T(8,128)S(1)}, f32[80,384]{1,0:T(8,128)S(1)}, u32[]{:S(2)}, u32[]{:S(2)}) %collective-permute-start.18) | collective-permute-done | bytes 122912 | tf_op jit(solution)/shard_map/ppermute | solution.py:151
  138.0 2.0 %collective-permute-start.15 = (f32[160,384]{1,0:T(8,128)S(1)}, f32[160,384]{1,0:T(8,128)S(1)}, u32[]{:S(2)}, u32[]{:S(2)}) collective-permute-start(f32[160,384]{1,0:T(8,128)S(1)} %get-tuple-element.26), channel_id=1, source_target_pairs={{0,7},{1,0},{2,1},{3,2},{4,3},{5,4},{6,5},{7,6},{8,15},{9,8},{10,9... | collective-permute-start | bytes 737288 | tf_op jit(solution)/shard_map/ppermute | solution.py:151
  140.0 3.8 %collective-permute-start.19 = (f32[160,384]{1,0:T(8,128)S(1)}, f32[160,384]{1,0:T(8,128)S(1)}, u32[]{:S(2)}, u32[]{:S(2)}) collective-permute-start(f32[160,384]{1,0:T(8,128)S(1)} %get-tuple-element.25), channel_id=1, source_target_pairs={{0,1},{1,2},{2,3},{3,4},{4,5},{5,6},{6,7},{7,0},{8,9},{9,10},{10,1... | collective-permute-start | bytes 737288 | tf_op jit(solution)/shard_map/ppermute | solution.py:151
  143.8 2.2 %collective-permute-done.15 = f32[160,384]{1,0:T(8,128)S(1)} collective-permute-done((f32[160,384]{1,0:T(8,128)S(1)}, f32[160,384]{1,0:T(8,128)S(1)}, u32[]{:S(2)}, u32[]{:S(2)}) %collective-permute-start.15) | collective-permute-done | bytes 245792 | tf_op jit(solution)/shard_map/ppermute | solution.py:151
  146.1 3.3 %collective-permute-done.19 = f32[160,384]{1,0:T(8,128)S(1)} collective-permute-done((f32[160,384]{1,0:T(8,128)S(1)}, f32[160,384]{1,0:T(8,128)S(1)}, u32[]{:S(2)}, u32[]{:S(2)}) %collective-permute-start.19) | collective-permute-done | bytes 245792 | tf_op jit(solution)/shard_map/ppermute | solution.py:151
  149.3 0.1 bitcast_add_fusion.2
  149.4 2.0 %collective-permute-start.16 = (f32[160,384]{1,0:T(8,128)S(1)}, f32[160,384]{1,0:T(8,128)S(1)}, u32[]{:S(2)}, u32[]{:S(2)}) collective-permute-start(f32[160,384]{1,0:T(8,128)S(1)} %get-tuple-element.24), channel_id=1, source_target_pairs={{0,7},{1,0},{2,1},{3,2},{4,3},{5,4},{6,5},{7,6},{8,15},{9,8},{10,9... | collective-permute-start | bytes 737288 | tf_op jit(solution)/shard_map/ppermute | solution.py:151
  151.4 3.8 %collective-permute-start.20 = (f32[160,384]{1,0:T(8,128)S(1)}, f32[160,384]{1,0:T(8,128)S(1)}, u32[]{:S(2)}, u32[]{:S(2)}) collective-permute-start(f32[160,384]{1,0:T(8,128)S(1)} %get-tuple-element.23), channel_id=1, source_target_pairs={{0,1},{1,2},{2,3},{3,4},{4,5},{5,6},{6,7},{7,0},{8,9},{9,10},{10,1... | collective-permute-start | bytes 737288 | tf_op jit(solution)/shard_map/ppermute | solution.py:151
  155.2 2.2 %collective-permute-done.16 = f32[160,384]{1,0:T(8,128)S(1)} collective-permute-done((f32[160,384]{1,0:T(8,128)S(1)}, f32[160,384]{1,0:T(8,128)S(1)}, u32[]{:S(2)}, u32[]{:S(2)}) %collective-permute-start.16) | collective-permute-done | bytes 245792 | tf_op jit(solution)/shard_map/ppermute | solution.py:151
  157.5 3.3 %collective-permute-done.20 = f32[160,384]{1,0:T(8,128)S(1)} collective-permute-done((f32[160,384]{1,0:T(8,128)S(1)}, f32[160,384]{1,0:T(8,128)S(1)}, u32[]{:S(2)}, u32[]{:S(2)}) %collective-permute-start.20) | collective-permute-done | bytes 245792 | tf_op jit(solution)/shard_map/ppermute | solution.py:151
  160.7 0.1 bitcast_add_fusion.1
  160.8 2.0 %collective-permute-start.17 = (f32[160,384]{1,0:T(8,128)S(1)}, f32[160,384]{1,0:T(8,128)S(1)}, u32[]{:S(2)}, u32[]{:S(2)}) collective-permute-start(f32[160,384]{1,0:T(8,128)S(1)} %get-tuple-element.22), channel_id=1, source_target_pairs={{0,7},{1,0},{2,1},{3,2},{4,3},{5,4},{6,5},{7,6},{8,15},{9,8},{10,9... | collective-permute-start | bytes 737288 | tf_op jit(solution)/shard_map/ppermute | solution.py:151
  162.8 3.8 %collective-permute-start.21 = (f32[160,384]{1,0:T(8,128)S(1)}, f32[160,384]{1,0:T(8,128)S(1)}, u32[]{:S(2)}, u32[]{:S(2)}) collective-permute-start(f32[160,384]{1,0:T(8,128)S(1)} %get-tuple-element.21), channel_id=1, source_target_pairs={{0,1},{1,2},{2,3},{3,4},{4,5},{5,6},{6,7},{7,0},{8,9},{9,10},{10,1... | collective-permute-start | bytes 737288 | tf_op jit(solution)/shard_map/ppermute | solution.py:151
  166.7 2.2 %collective-permute-done.17 = f32[160,384]{1,0:T(8,128)S(1)} collective-permute-done((f32[160,384]{1,0:T(8,128)S(1)}, f32[160,384]{1,0:T(8,128)S(1)}, u32[]{:S(2)}, u32[]{:S(2)}) %collective-permute-start.17) | collective-permute-done | bytes 245792 | tf_op jit(solution)/shard_map/ppermute | solution.py:151
  168.9 3.3 %collective-permute-done.21 = f32[160,384]{1,0:T(8,128)S(1)} collective-permute-done((f32[160,384]{1,0:T(8,128)S(1)}, f32[160,384]{1,0:T(8,128)S(1)}, u32[]{:S(2)}, u32[]{:S(2)}) %collective-permute-start.21) | collective-permute-done | bytes 245792 | tf_op jit(solution)/shard_map/ppermute | solution.py:151
  172.1 0.7 fusion
  (35 shorter events, 0.2 us)
Async XLA Ops:
  0.0 78.8 %copy-start = (f32[2,128,128]{2,1,0:T(8,128)S(1)}, f32[2,128,128]{2,1,0:T(8,128)}, u32[]{:S(2)}) copy-start(f32[2,128,128]{2,1,0:T(8,128)} %param.10) | copy-start | bytes 393220
  0.0 41.4 %copy-start.14 = (bf16[160,256]{1,0:T(8,128)(2,1)S(1)}, bf16[160,256]{1,0:T(8,128)(2,1)}, u32[]{:S(2)}) copy-start(bf16[160,256]{1,0:T(8,128)(2,1)} %q_ref.1) | copy-start | bytes 245764
  0.0 41.4 %copy-start.17 = (f32[2,160]{1,0:T(2,128)S(1)}, f32[2,160]{1,0:T(2,128)}, u32[]{:S(2)}) copy-start(f32[2,160]{1,0:T(2,128)} %r_ref.1) | copy-start | bytes 3844
  0.0 41.4 %copy-start.15 = (bf16[160,256]{1,0:T(8,128)(2,1)S(1)}, bf16[160,256]{1,0:T(8,128)(2,1)}, u32[]{:S(2)}) copy-start(bf16[160,256]{1,0:T(8,128)(2,1)} %k_ref.1) | copy-start | bytes 245764
  0.0 41.4 %copy-start.16 = (bf16[160,256]{1,0:T(8,128)(2,1)S(1)}, bf16[160,256]{1,0:T(8,128)(2,1)}, u32[]{:S(2)}) copy-start(bf16[160,256]{1,0:T(8,128)(2,1)} %v_ref.1) | copy-start | bytes 245764
  1.4 38.0 %collective-permute-start.12 = (f32[128,3072]{1,0:T(8,128)S(1)}, f32[128,3072]{1,0:T(8,128)S(1)}, u32[]{:S(2)}, u32[]{:S(2)}) collective-permute-start(f32[128,3072]{1,0:T(8,128)S(1)} %dynamic-slice_convert_fusion), channel_id=1, source_target_pairs={{0,8},{8,0},{1,9},{9,1},{2,10},{10,2},{3,11},{11,3},{4,12},{12,4},... | collective-permute-start | bytes 4718600 | tf_op jit(solution)/shard_map/ppermute | solution.py:151
  39.4 79.4 %collective-permute-start.13 = (f32[128,3072]{1,0:T(8,128)S(1)}, f32[128,3072]{1,0:T(8,128)S(1)}, u32[]{:S(2)}, u32[]{:S(2)}) collective-permute-start(f32[128,3072]{1,0:T(8,128)S(1)} %collective-permute-done.12.mine_ref), channel_id=1, source_target_pairs={{0,16},{16,0},{1,17},{17,1},{2,18},{18,2},{3,19},{19,3},{4,20},{20... | collective-permute-start | bytes 4718600 | tf_op jit(solution)/shard_map/ppermute | solution.py:151
  44.3 21.2 %copy-start.4 = (f32[160,256]{1,0:T(8,128)}, f32[160,256]{1,0:T(8,128)S(1)}, u32[]{:S(2)}) copy-start(f32[160,256]{1,0:T(8,128)S(1)} %get-tuple-element.19.lead_ref) | copy-start | bytes 491524
  44.3 26.3 %copy-start.6 = (f32[160,256]{1,0:T(8,128)}, f32[160,256]{1,0:T(8,128)S(1)}, u32[]{:S(2)}) copy-start(f32[160,256]{1,0:T(8,128)S(1)} %get-tuple-element.20.rest_ref) | copy-start | bytes 491524
  44.3 3.4 %collective-permute-start = (f32[128,256]{1,0:T(8,128)S(1)}, f32[128,256]{1,0:T(8,128)S(1)}, u32[]{:S(2)}, u32[]{:S(2)}) collective-permute-start(f32[128,256]{1,0:T(8,128)S(1)} %get-tuple-element.14), channel_id=1, source_target_pairs={{0,16},{16,0},{1,17},{17,1},{2,18},{18,2},{3,19},{19,3},{4,20},{20... | collective-permute-start | bytes 393224 | tf_op jit(solution)/shard_map/ppermute | solution.py:151
  48.0 15.0 %collective-permute-start.1 = (f32[128,256]{1,0:T(8,128)S(1)}, f32[128,256]{1,0:T(8,128)S(1)}, u32[]{:S(2)}, u32[]{:S(2)}) collective-permute-start(f32[128,256]{1,0:T(8,128)S(1)} %shard_map.65.own), channel_id=1, source_target_pairs={{0,32},{32,64},{64,96},{96,128},{128,160},{160,192},{192,224},{224... | collective-permute-start | bytes 393224 | tf_op jit(solution)/shard_map/ppermute | solution.py:151
  52.3 13.2 %collective-permute-start.4 = (f32[128,256]{1,0:T(8,128)S(1)}, f32[128,256]{1,0:T(8,128)S(1)}, u32[]{:S(2)}, u32[]{:S(2)}) collective-permute-start(f32[128,256]{1,0:T(8,128)S(1)} %shard_map.65.own), channel_id=1, source_target_pairs={{0,224},{32,0},{64,32},{96,64},{128,96},{160,128},{192,160},{224,1... | collective-permute-start | bytes 393224 | tf_op jit(solution)/shard_map/ppermute | solution.py:151
  60.9 0.7 copy-start.2
  62.9 8.4 %collective-permute-start.2 = (f32[128,256]{1,0:T(8,128)S(1)}, f32[128,256]{1,0:T(8,128)}, u32[]{:S(2)}, u32[]{:S(2)}) collective-permute-start(f32[128,256]{1,0:T(8,128)S(1)} %collective-permute-done.1.l1), channel_id=1, source_target_pairs={{0,32},{32,64},{64,96},{96,128},{128,160},{160,192},{192,224},{224... | collective-permute-start | bytes 393224 | tf_op jit(solution)/shard_map/ppermute | solution.py:151
  64.8 0.7 copy-start.8
  65.5 7.7 %collective-permute-start.5 = (f32[128,256]{1,0:T(8,128)S(1)}, f32[128,256]{1,0:T(8,128)}, u32[]{:S(2)}, u32[]{:S(2)}) collective-permute-start(f32[128,256]{1,0:T(8,128)S(1)} %collective-permute-done.4.r1), channel_id=1, source_target_pairs={{0,224},{32,0},{64,32},{96,64},{128,96},{160,128},{192,160},{224,1... | collective-permute-start | bytes 393224 | tf_op jit(solution)/shard_map/ppermute | solution.py:151
  70.6 0.7 copy-start.10
  71.3 8.4 %collective-permute-start.3 = (f32[128,256]{1,0:T(8,128)}, f32[128,256]{1,0:T(8,128)}, u32[]{:S(2)}, u32[]{:S(2)}) collective-permute-start(f32[128,256]{1,0:T(8,128)} %collective-permute-done.2.l2), channel_id=1, source_target_pairs={{0,32},{32,64},{64,96},{96,128},{128,160},{160,192},{192,224},{224... | collective-permute-start | bytes 393224 | tf_op jit(solution)/shard_map/ppermute | solution.py:151
  73.2 9.2 %collective-permute-start.6 = (f32[128,256]{1,0:T(8,128)}, f32[128,256]{1,0:T(8,128)}, u32[]{:S(2)}, u32[]{:S(2)}) collective-permute-start(f32[128,256]{1,0:T(8,128)} %collective-permute-done.5.r2), channel_id=1, source_target_pairs={{0,224},{32,0},{64,32},{96,64},{128,96},{160,128},{192,160},{224,1... | collective-permute-start | bytes 393224 | tf_op jit(solution)/shard_map/ppermute | solution.py:151
  80.5 8.0 %collective-permute-start.7 = (f32[64,256]{1,0:T(8,128)S(1)}, f32[64,256]{1,0:T(8,128)S(1)}, u32[]{:S(2)}, u32[]{:S(2)}) collective-permute-start(f32[64,256]{1,0:T(8,128)S(1)} %slice.24), channel_id=1, source_target_pairs={{0,32},{32,64},{64,96},{96,128},{128,160},{160,192},{192,224},{224... | collective-permute-start | bytes 196616 | tf_op jit(solution)/shard_map/ppermute | solution.py:151
  83.3 7.0 %collective-permute-start.8 = (f32[64,256]{1,0:T(8,128)S(1)}, f32[64,256]{1,0:T(8,128)S(1)}, u32[]{:S(2)}, u32[]{:S(2)}) collective-permute-start(f32[64,256]{1,0:T(8,128)S(1)} %slice.25), channel_id=1, source_target_pairs={{0,224},{32,0},{64,32},{96,64},{128,96},{160,128},{192,160},{224,1... | collective-permute-start | bytes 196616 | tf_op jit(solution)/shard_map/ppermute | solution.py:151
  90.3 0.9 copy-start.3
  91.2 0.9 copy-start.9
  92.1 0.9 copy-start.11
  96.2 7.7 %collective-permute-start.9 = (f32[128,128]{1,0:T(8,128)S(1)}, f32[128,128]{1,0:T(8,128)S(1)}, u32[]{:S(2)}, u32[]{:S(2)}) collective-permute-start(f32[128,128]{1,0:T(8,128)S(1)} %get-tuple-element.16), channel_id=1, source_target_pairs={{0,256},{1,257},{2,258},{3,259},{4,260},{5,261},{6,262},{7,263},{8... | collective-permute-start | bytes 196616 | tf_op jit(solution)/shard_map/ppermute | solution.py:212
  105.5 0.6 copy-start.12
  106.1 3.3 %collective-permute-start.10 = (f32[128,128]{1,0:T(8,128)}, f32[128,128]{1,0:T(8,128)S(1)}, u32[]{:S(2)}, u32[]{:S(2)}) collective-permute-start(f32[128,128]{1,0:T(8,128)} %get-tuple-element.18), channel_id=1, source_target_pairs={{0,16},{16,0},{1,17},{17,1},{2,18},{18,2},{3,19},{19,3},{4,20},{20... | collective-permute-start | bytes 196616 | tf_op jit(solution)/shard_map/ppermute | solution.py:151
  109.5 0.9 copy-start.5
  110.4 0.9 copy-start.7
  111.3 0.8 copy-start.13
  113.0 8.3 %collective-permute-start.11 = (f32[160,256]{1,0:T(8,128)S(1)}, f32[160,256]{1,0:T(8,128)}, u32[]{:S(2)}, u32[]{:S(2)}) collective-permute-start(f32[160,256]{1,0:T(8,128)S(1)} %shard_map.68.z_ref), channel_id=1, source_target_pairs={{0,8},{8,0},{1,9},{9,1},{2,10},{10,2},{3,11},{11,3},{4,12},{12,4},... | collective-permute-start | bytes 491528 | tf_op jit(solution)/shard_map/ppermute | solution.py:151
  118.8 2.4 %copy-start.1 = (bf16[256,3072]{1,0:T(8,128)(2,1)S(1)}, bf16[256,3072]{1,0:T(8,128)(2,1)}, u32[]{:S(2)}) copy-start(bf16[256,3072]{1,0:T(8,128)(2,1)} %constant_dynamic-slice_fusion.w_ref) | copy-start | bytes 4718596
  124.6 7.8 %collective-permute-start.14 = (f32[80,384]{1,0:T(8,128)S(1)}, f32[80,384]{1,0:T(8,128)S(1)}, u32[]{:S(2)}, u32[]{:S(2)}) collective-permute-start(f32[80,384]{1,0:T(8,128)S(1)} %get-tuple-element.28), channel_id=1, source_target_pairs={{0,7},{1,0},{2,1},{3,2},{4,3},{5,4},{6,5},{7,6},{8,15},{9,8},{10,9... | collective-permute-start | bytes 368648 | tf_op jit(solution)/shard_map/ppermute | solution.py:151
  129.9 8.0 %collective-permute-start.18 = (f32[80,384]{1,0:T(8,128)S(1)}, f32[80,384]{1,0:T(8,128)S(1)}, u32[]{:S(2)}, u32[]{:S(2)}) collective-permute-start(f32[80,384]{1,0:T(8,128)S(1)} %get-tuple-element.27), channel_id=1, source_target_pairs={{0,1},{1,2},{2,3},{3,4},{4,5},{5,6},{6,7},{7,0},{8,9},{9,10},{10,1... | collective-permute-start | bytes 368648 | tf_op jit(solution)/shard_map/ppermute | solution.py:151
  138.0 8.1 %collective-permute-start.15 = (f32[160,384]{1,0:T(8,128)S(1)}, f32[160,384]{1,0:T(8,128)S(1)}, u32[]{:S(2)}, u32[]{:S(2)}) collective-permute-start(f32[160,384]{1,0:T(8,128)S(1)} %get-tuple-element.26), channel_id=1, source_target_pairs={{0,7},{1,0},{2,1},{3,2},{4,3},{5,4},{6,5},{7,6},{8,15},{9,8},{10,9... | collective-permute-start | bytes 737288 | tf_op jit(solution)/shard_map/ppermute | solution.py:151
  140.0 9.3 %collective-permute-start.19 = (f32[160,384]{1,0:T(8,128)S(1)}, f32[160,384]{1,0:T(8,128)S(1)}, u32[]{:S(2)}, u32[]{:S(2)}) collective-permute-start(f32[160,384]{1,0:T(8,128)S(1)} %get-tuple-element.25), channel_id=1, source_target_pairs={{0,1},{1,2},{2,3},{3,4},{4,5},{5,6},{6,7},{7,0},{8,9},{9,10},{10,1... | collective-permute-start | bytes 737288 | tf_op jit(solution)/shard_map/ppermute | solution.py:151
  149.4 8.1 %collective-permute-start.16 = (f32[160,384]{1,0:T(8,128)S(1)}, f32[160,384]{1,0:T(8,128)S(1)}, u32[]{:S(2)}, u32[]{:S(2)}) collective-permute-start(f32[160,384]{1,0:T(8,128)S(1)} %get-tuple-element.24), channel_id=1, source_target_pairs={{0,7},{1,0},{2,1},{3,2},{4,3},{5,4},{6,5},{7,6},{8,15},{9,8},{10,9... | collective-permute-start | bytes 737288 | tf_op jit(solution)/shard_map/ppermute | solution.py:151
  151.4 9.3 %collective-permute-start.20 = (f32[160,384]{1,0:T(8,128)S(1)}, f32[160,384]{1,0:T(8,128)S(1)}, u32[]{:S(2)}, u32[]{:S(2)}) collective-permute-start(f32[160,384]{1,0:T(8,128)S(1)} %get-tuple-element.23), channel_id=1, source_target_pairs={{0,1},{1,2},{2,3},{3,4},{4,5},{5,6},{6,7},{7,0},{8,9},{9,10},{10,1... | collective-permute-start | bytes 737288 | tf_op jit(solution)/shard_map/ppermute | solution.py:151
  160.8 8.1 %collective-permute-start.17 = (f32[160,384]{1,0:T(8,128)S(1)}, f32[160,384]{1,0:T(8,128)S(1)}, u32[]{:S(2)}, u32[]{:S(2)}) collective-permute-start(f32[160,384]{1,0:T(8,128)S(1)} %get-tuple-element.22), channel_id=1, source_target_pairs={{0,7},{1,0},{2,1},{3,2},{4,3},{5,4},{6,5},{7,6},{8,15},{9,8},{10,9... | collective-permute-start | bytes 737288 | tf_op jit(solution)/shard_map/ppermute | solution.py:151
  162.8 9.3 %collective-permute-start.21 = (f32[160,384]{1,0:T(8,128)S(1)}, f32[160,384]{1,0:T(8,128)S(1)}, u32[]{:S(2)}, u32[]{:S(2)}) collective-permute-start(f32[160,384]{1,0:T(8,128)S(1)} %get-tuple-element.21), channel_id=1, source_target_pairs={{0,1},{1,2},{2,3},{3,4},{4,5},{5,6},{6,7},{7,0},{8,9},{9,10},{10,1... | collective-permute-start | bytes 737288 | tf_op jit(solution)/shard_map/ppermute | solution.py:151
where the time goes:
time: 174 us; the launch traced here: 173 us
  starting transfers between devices  73 us (42%)
  waiting for transfers between devices  71.9 us (41%)
  Pallas kernels  12.9 us (7%)
  local copies, waits for them, and re-layouts  12.4 us (7%)
  other arithmetic  2.29 us (1%)
    ppermute x21, starting transfers between devices, rotated(): return lax.ppermute(x, axis, [(i, (i + by) % n) for i in range(n)])  71.7 us
    ppermute x21, waiting for transfers between devices, rotated(): return lax.ppermute(x, axis, [(i, (i + by) % n) for i in range(n)])  65.5 us
    pallas_call x6, Pallas kernels, call(): pl.pallas_call(kernel, out_shape=outs, in_specs=[SM] * scalars + [VM] * (...  9.62 us
    unnamed x36, local copies, waits for them, and re-layouts  7.97 us
    ppermute x1, waiting for transfers between devices, local(): arrived = lax.ppermute(end, XH, [(0, 1)])  6.36 us
  transfers between devices with their start and end apart: 22, of which 16 were waited for; matrix products, arithmetic and copies ran while one was open for 3% of the time, Pallas kernels for 6%

commit v1 on v0

v1 whole, which is shorter than its diff:
```python
import jax
import jax.numpy as jnp
from jax import lax
from jax.experimental import pallas as pl
from jax.experimental.pallas import tpu as pltpu
from jax.sharding import Mesh, PartitionSpec as P

MB = 16
HW = 128
XH, Z, CORE, XL, Y = "xh", "z", "core", "xl", "y"
SIZES = (2, 8, 2, 2, 8)
f32 = jnp.float32
bf16 = jnp.bfloat16
VM = pl.BlockSpec(memory_space=pltpu.VMEM)
SM = pl.BlockSpec(memory_space=pltpu.SMEM)
MIB = 2**20


def exact(a, b, contract=((1,), (0,))):
    return lax.dot_general(
        a, b, (contract, ((), ())), precision=lax.Precision.HIGHEST, preferred_element_type=f32
    )


def single(a, b, contract=((1,), (0,))):
    return lax.dot_general(a, b, (contract, ((), ())), preferred_element_type=f32)


def call(kernel, out_shapes, at, *args, later=(), scratch=(), limit=4, us=1.0):
    outs = [jax.ShapeDtypeStruct(s, d) for s, d in out_shapes]
    n = 1 + len(args)

    def body(*refs):
        kernel(*refs[:n], *refs[n + len(later) :])

    return pl.pallas_call(
        body,
        out_shape=outs,
        in_specs=[SM] + [VM] * len(args) + [pl.BlockSpec(memory_space=pl.ANY)] * len(later),
        out_specs=[VM] * len(outs),
        scratch_shapes=list(scratch),
        compiler_params=pltpu.CompilerParams(vmem_limit_bytes=limit * MIB),
        cost_estimate=pl.CostEstimate(flops=int(us * 1e9), bytes_accessed=1 << 17, transcendentals=0),
    )(at, *args, *later)


def place(at_ref):
    return at_ref[0], at_ref[1], at_ref[2]


def left_half(shape):
    return lax.broadcasted_iota(jnp.int32, shape, 1) < HW


def identity(columns):
    rows_at = lax.broadcasted_iota(jnp.int32, (HW, columns), 0)
    return (rows_at == lax.broadcasted_iota(jnp.int32, (HW, columns), 1)).astype(f32)


def after(second, first):
    return exact(second[:, :HW], first) + jnp.where(left_half(second.shape), 0.0, second)


def applied(pair, state):
    return exact(pair[:, :HW], state) + pair[:, HW:]


def shard_maps(at_ref, q_ref, k_ref, v_ref, r_ref, keep_ref, send_ref, rows_ref, x_ref):
    rows = q_ref.shape[0]
    _, _, core = place(at_ref)
    s_at = lax.broadcasted_iota(jnp.int32, (rows, rows), 0)
    t_at = lax.broadcasted_iota(jnp.int32, (rows, rows), 1)
    earlier_block = (t_at // MB) < (s_at // MB)
    causal = t_at <= s_at
    diagonal = t_at == s_at
    mix, key_gram, columns = [], [], []
    for h in range(2):
        at = slice(h * HW, (h + 1) * HW)
        q, k, v = q_ref[:, at], k_ref[:, at], v_ref[:, at]
        r = r_ref[h : h + 1, :]
        columns.append(jnp.sum(jnp.where(diagonal, r, 0.0), axis=1, keepdims=True))
        key_gram.append(jnp.where(earlier_block, single(k, k, ((1,), (1,))) * r, 0.0))
        mix.append(jnp.where(causal, single(q, k, ((1,), (1,))) * r, 0.0))
        x_ref[h, :, :HW] = k.astype(f32)
        x_ref[h, :, HW:] = v.astype(f32)
    for i in range(1, rows // MB):
        at = slice(i * MB, (i + 1) * MB)
        for h in range(2):
            x_ref[h, at, :] = x_ref[h, at, :] - exact(key_gram[h][at, :], x_ref[h])
    maps = []
    for h in range(2):
        at = slice(h * HW, (h + 1) * HW)
        x = x_ref[h]
        y = exact(mix[h], x)
        rows_ref[:, at] = q_ref[:, at].astype(f32) - y[:, :HW]
        rows_ref[:, (2 + h) * HW : (3 + h) * HW] = y[:, HW:]
        ab = exact(k_ref[:, at].astype(f32) * columns[h], x, ((0,), (0,)))
        maps.append(identity(2 * HW) + jnp.where(left_half(ab.shape), -ab, ab))
    first = core == 0
    keep_ref[...] = jnp.where(first, maps[0], maps[1])
    send_ref[...] = jnp.where(first, maps[1], maps[0])


def chip_map(at_ref, keep_ref, got_ref, out_ref):
    first = place(at_ref)[2] == 0
    early = jnp.where(first, keep_ref[...], got_ref[...])
    late = jnp.where(first, got_ref[...], keep_ref[...])
    out_ref[...] = after(late, early)


def join_chips(at_ref, own_ref, got_ref, both_ref, pre_ref):
    upper = lax.rem(place(at_ref)[0], 2) == 1
    low = jnp.where(upper, got_ref[...], own_ref[...])
    high = jnp.where(upper, own_ref[...], got_ref[...])
    both_ref[...] = after(high, low)
    pre_ref[...] = jnp.where(upper, low, identity(2 * HW))


def join_pairs(at_ref, own_ref, got_ref, pre_in_ref, both_ref, pre_ref):
    upper = lax.rem(place(at_ref)[0], 4) >= 2
    low = jnp.where(upper, got_ref[...], own_ref[...])
    high = jnp.where(upper, own_ref[...], got_ref[...])
    both_ref[...] = after(high, low)
    pre = pre_in_ref[...]
    pre_ref[...] = jnp.where(upper, after(pre, low), pre)


def join_ring(at_ref, own_ref, got_ref, pre_in_ref, first_ref, end_ref, pre_ref):
    z, _, core = place(at_ref)
    upper = z >= 4
    low = jnp.where(upper, got_ref[...], own_ref[...])
    high = jnp.where(upper, own_ref[...], got_ref[...])
    end_ref[...] = applied(high, applied(low, first_ref[core]))
    pre = pre_in_ref[...]
    pre_ref[...] = jnp.where(upper, after(pre, low), pre)


def shard_states(at_ref, pre_ref, arrived_ref, first_ref, keep_ref, got_ref, out_ref):
    _, x_hi, core = place(at_ref)
    start = applied(pre_ref[...], jnp.where(x_hi == 0, first_ref[core], arrived_ref[...]))
    out_ref[:, :HW] = start
    out_ref[:, HW:] = applied(jnp.where(core == 0, keep_ref[...], got_ref[...]), start)


def piece_weights(to_ref, own_ref, pair_ref, out_ref):
    del to_ref
    out_ref[0, : 2 * HW, :] = own_ref[...]
    out_ref[0, 2 * HW :, :] = pair_ref[0].astype(bf16)


def pair_weights(to_ref, w_ref, later_ref, out_ref):
    del to_ref, later_ref
    out_ref[0] = w_ref[...].astype(f32)


def outputs(at_ref, s00, s01, s10, s11, r00, r01, r10, r11, w_ref, z_ref, piece_ref):
    core = place(at_ref)[2]
    first = core == 0
    rows = r00.shape[0]
    for g, (mine, others, own_rows, far_rows) in enumerate(((s00, s01, r00, r01), (s10, s11, r10, r11))):
        for h in range(2):
            states = jnp.where(core == h, mine[...], others[...])
            near = jnp.where(first, states[:, :HW], states[:, HW:])
            far = jnp.where(first, states[:, HW:], states[:, :HW])
            at = slice((2 * g + h) * HW, (2 * g + h + 1) * HW)
            lead, rest = slice(h * HW, (h + 1) * HW), slice((2 + h) * HW, (3 + h) * HW)
            z_ref[:rows, at] = (exact(own_rows[:, lead], near) + own_rows[:, rest]).astype(bf16)
            z_ref[rows:, at] = (exact(far_rows[:, lead], far) + far_rows[:, rest]).astype(bf16)
    piece_ref[...] = single(z_ref[:rows, :], w_ref[0])


def project(z_ref, w_ref, out_ref):
    for i in range(4):
        out_ref[i] = single(z_ref[...], w_ref[i + 1])


def swapped(x, axes):
    n = 2 ** len(axes)
    return lax.ppermute(x, axes, [(i, n - 1 - i) for i in range(n)])


def ring_step(x):
    n = SIZES[4]
    pairs = [(i, (i - 1) % n) for i in range(n)] + [(n + i, n + (i + 1) % n) for i in range(n)]
    return lax.ppermute(x, (CORE, Y), pairs)


def local(queries, keys, values, rates, init_weight, out_weight):
    rows = queries.shape[0]
    x_hi, z, core, x_lo, y = (lax.axis_index(a) for a in (XH, Z, CORE, XL, Y))
    at = jnp.stack([z, x_hi, core]).astype(jnp.int32)
    chunk = out_weight.shape[1] // (SIZES[3] * SIZES[4])
    square, wide = ((HW, HW), f32), ((HW, 2 * HW), f32)

    keep, send, own_rows = call(
        shard_maps, [wide, wide, ((rows, 4 * HW), f32)], at, queries, keys, values, rates,
        scratch=[pltpu.VMEM((2, rows, 2 * HW), f32)], limit=8, us=3,
    )
    away = jnp.array([4, 3, 2, 1, 0], jnp.int32) * (2 * core - 1)
    dest = lax.rem(y + away + SIZES[4], SIZES[4]).astype(jnp.int32)
    to_pair = pl.pallas_call(
        pair_weights,
        grid_spec=pltpu.PrefetchScalarGridSpec(
            num_scalar_prefetch=1,
            grid=(5,),
            in_specs=[
                pl.BlockSpec((2 * HW, chunk), lambda i, to: (0, to[i])),
                pl.BlockSpec(memory_space=pl.ANY),
            ],
            out_specs=pl.BlockSpec((1, 2 * HW, chunk), lambda i, to: (i, 0, 0)),
        ),
        out_shape=jax.ShapeDtypeStruct((5, 2 * HW, chunk), f32),
        compiler_params=pltpu.CompilerParams(vmem_limit_bytes=4 * MIB),
    )(dest + (1 - x_lo) * SIZES[4], out_weight, send)
    from_pair = swapped(to_pair, (XL,))

    rows_core, rows_pair, rows_both = (
        swapped(own_rows, (CORE,)), swapped(own_rows, (XL,)), swapped(own_rows, (CORE, XL))
    )
    got = swapped(send, (CORE,))
    (chip,) = call(chip_map, [wide], at, keep, got)

    def across_z(x, to):
        return lax.ppermute(x, Z, [(i, to(i)) for i in range(SIZES[1])])

    both, pre = call(join_chips, [wide, wide], at, chip, across_z(chip, lambda i: i ^ 1), later=[rows_core])
    four, pre = call(join_pairs, [wide, wide], at, both, across_z(both, lambda i: i ^ 2), pre, later=[rows_pair])
    end, pre = call(join_ring, [square, wide], at, four, across_z(four, lambda i: 7 - i), pre, init_weight, later=[rows_both])
    arrived = lax.ppermute(end, XH, [(0, 1)])
    weights = pl.pallas_call(
        piece_weights,
        grid_spec=pltpu.PrefetchScalarGridSpec(
            num_scalar_prefetch=1,
            grid=(5,),
            in_specs=[
                pl.BlockSpec((2 * HW, chunk), lambda i, to: (0, to[i])),
                pl.BlockSpec((1, 2 * HW, chunk), lambda i, to: (i, 0, 0)),
            ],
            out_specs=pl.BlockSpec((1, 4 * HW, chunk), lambda i, to: (i, 0, 0)),
        ),
        out_shape=jax.ShapeDtypeStruct((5, 4 * HW, chunk), bf16),
        compiler_params=pltpu.CompilerParams(vmem_limit_bytes=4 * MIB),
    )(dest + x_lo * SIZES[4], out_weight, from_pair)

    (states,) = call(shard_states, [wide], at, pre, arrived, init_weight, keep, got, later=[weights])

    states_pair = swapped(states, (XL,))
    states_core = swapped(states, (CORE,))
    states_both = swapped(states_pair, (CORE,))

    z_rows, leaving = call(
        outputs, [((2 * rows, 4 * HW), bf16), ((rows, chunk), f32)], at,
        states, states_core, states_pair, states_both, own_rows, rows_core, rows_pair, rows_both, weights,
        limit=16,
    )
    arriving = ring_step(leaving)
    pieces = pl.pallas_call(
        project,
        out_shape=jax.ShapeDtypeStruct((4, 2 * rows, chunk), f32),
        in_specs=[VM, VM],
        out_specs=VM,
        compiler_params=pltpu.CompilerParams(vmem_limit_bytes=16 * MIB),
        cost_estimate=pl.CostEstimate(flops=int(1e9), bytes_accessed=1 << 21, transcendentals=0),
    )(z_rows, weights)
    total = pieces[0].at[:rows].add(arriving)
    for i in (1, 2):
        total = ring_step(total) + pieces[i]
    total = ring_step(total)
    others = swapped(total[rows:], (CORE,))
    return (total[:rows] + others + pieces[3, :rows]).astype(bf16)


def solution(mesh):
    fine = Mesh(mesh.devices.reshape(SIZES), (XH, Z, CORE, XL, Y))
    ctx, tp = (XH, Z, CORE), (XL, Y)
    in_specs = (P(ctx, tp), P(ctx, tp), P(ctx, tp), P(tp, ctx), P(tp, None, None), P(tp, None))
    return jax.shard_map(local, mesh=fine, in_specs=in_specs, out_specs=P(ctx, tp), check_vma=False)
```

time: 174 us -> 161 us (0.925)
  the two profiles are of different devices: /device:TPU:4 before, /device:TPU:1 now
where the time goes in v1:
time: 161 us; the launch traced here: 160 us
  starting transfers between devices  72.8 us (45%)
  waiting for transfers between devices  60.2 us (37%)
  Pallas kernels  18.6 us (12%)
  local copies, waits for them, and re-layouts  6.62 us (4%)
    ppermute x9, starting transfers between devices, swapped(): return lax.ppermute(x, axes, [(i, n - 1 - i) for i in range(n)])  38.8 us
    ppermute x4, waiting for transfers between devices, ring_step(): return lax.ppermute(x, (CORE, Y), pairs)  32 us
    ppermute x9, waiting for transfers between devices, swapped(): return lax.ppermute(x, axes, [(i, n - 1 - i) for i in range(n)])  23.2 us
    ppermute x3, starting transfers between devices, across_z(): return lax.ppermute(x, Z, [(i, to(i)) for i in range(SIZES[1])])  20.4 us
    pallas_call x7, Pallas kernels, call(): pl.pallas_call(body, out_shape=outs, in_specs=[SM] + [VM] * len(args) + [...  11 us
    ppermute x4, starting transfers between devices, ring_step(): return lax.ppermute(x, (CORE, Y), pairs)  8.97 us
    unnamed x34, local copies, waits for them, and re-layouts  6.57 us
    ppermute x3, waiting for transfers between devices, across_z(): return lax.ppermute(x, Z, [(i, to(i)) for i in range(SIZES[1])])  5.01 us
  transfers between devices with their start and end apart: 17, of which 9 were waited for; matrix products, arithmetic and copies ran while one was open for 0% of the time, Pallas kernels for 5%

profile of v1, /device:TPU:1, one launch (start us, length us, event | category | flops | bytes accessed | tf_op | source)
XLA Modules:
  0.0 160.2 jit_solution(6569176850522739284)
XLA Ops:
  0.0 0.1 pad_add_fusion.refs_0_
  0.1 0.7 broadcast_add_fusion
  0.7 0.9 copy-done.9
  1.6 0.9 copy-done.10
  2.5 0.9 copy-done.11
  3.4 0.7 copy-done.12
  4.1 3.4 %shard_map.73 = (f32[128,256]{1,0:T(8,128)S(1)}, f32[128,256]{1,0:T(8,128)S(1)}, f32[160,512]{1,0:T(8,128)S(1)}) custom-call(s32[3]{0:T(128)S(1)} %pad_add_fusion.refs_0_, bf16[160,256]{1,0:T(8,128)(2,1)S(1)} %copy-done.9, bf16[160,256]{1,0:T(8,128)(2,1)S(1)} %copy-done.10, bf16[160,256]{1,0:T(8,128)(2,1)S(1)} %copy-done.11, f32[2,160]{1,0:T(2,128)S(1)} %copy-done.12), custom_call_target="tpu_custom_call" | custom-call | flops 3000000000 | bytes 131072 | tf_op jit(solution)/shard_map/pallas_call | solution.py:36
  7.5 0.0 copy-start.13
  7.5 0.0 copy-done
  7.5 3.0 %shard_map.78 = f32[5,256,384]{2,1,0:T(8,128)} custom-call(s32[5]{0:T(128)S(1)} %get-tuple-element.39.to_ref, bf16[256,6144]{1,0:T(8,128)(2,1)S(1)} %copy-done, f32[128,256]{1,0:T(8,128)S(1)} %get-tuple-element.29.later_ref), custom_call_target="tpu_custom_call" | custom-call | tf_op jit(solution)/shard_map/pallas_call | solution.py:201
  10.5 3.9 %collective-permute-start.8 = (f32[5,256,384]{2,1,0:T(8,128)}, f32[5,256,384]{2,1,0:T(8,128)}, u32[]{:S(2)}, u32[]{:S(2)}) collective-permute-start(f32[5,256,384]{2,1,0:T(8,128)} %shard_map.78), channel_id=1, source_target_pairs={{0,8},{8,0},{1,9},{9,1},{2,10},{10,2},{3,11},{11,3},{4,12},{12,4},... | collective-permute-start | bytes 5898248 | tf_op jit(solution)/shard_map/ppermute | solution.py:179
  14.5 6.8 %collective-permute-start = (f32[128,256]{1,0:T(8,128)S(1)}, f32[128,256]{1,0:T(8,128)S(1)}, u32[]{:S(2)}, u32[]{:S(2)}) collective-permute-start(f32[128,256]{1,0:T(8,128)S(1)} %get-tuple-element.29.later_ref), channel_id=1, source_target_pairs={{0,16},{16,0},{1,17},{17,1},{2,18},{18,2},{3,19},{19,3},{4,20},{20... | collective-permute-start | bytes 393224 | tf_op jit(solution)/shard_map/ppermute | solution.py:179
  21.2 1.9 %collective-permute-start.2 = (f32[160,512]{1,0:T(8,128)S(1)}, f32[160,512]{1,0:T(8,128)S(1)}, u32[]{:S(2)}, u32[]{:S(2)}) collective-permute-start(f32[160,512]{1,0:T(8,128)S(1)} %get-tuple-element.30.refs_5_), channel_id=1, source_target_pairs={{0,16},{16,0},{1,17},{17,1},{2,18},{18,2},{3,19},{19,3},{4,20},{20... | collective-permute-start | bytes 983048 | tf_op jit(solution)/shard_map/ppermute | solution.py:179
  23.2 0.0 collective-permute-done.refs_2_.refs_5_
  23.2 0.0 copy-start.7
  23.2 0.0 copy-done.13
  23.2 0.8 shard_map.74.refs_1_
  24.0 1.9 %collective-permute-start.1 = (f32[128,256]{1,0:T(8,128)S(1)}, f32[128,256]{1,0:T(8,128)S(1)}, u32[]{:S(2)}, u32[]{:S(2)}) collective-permute-start(f32[128,256]{1,0:T(8,128)S(1)} %shard_map.74.refs_1_), channel_id=1, source_target_pairs={{0,32},{32,0},{64,96},{96,64},{128,160},{160,128},{192,224},{224,1... | collective-permute-start | bytes 393224 | tf_op jit(solution)/shard_map/ppermute | solution.py:224
  25.9 3.6 %collective-permute-start.4 = (f32[160,512]{1,0:T(8,128)S(1)}, f32[160,512]{1,0:T(8,128)S(1)}, u32[]{:S(2)}, u32[]{:S(2)}) collective-permute-start(f32[160,512]{1,0:T(8,128)S(1)} %get-tuple-element.30.refs_5_), channel_id=1, source_target_pairs={{0,8},{8,0},{1,9},{9,1},{2,10},{10,2},{3,11},{11,3},{4,12},{12,4},... | collective-permute-start | bytes 983048 | tf_op jit(solution)/shard_map/ppermute | solution.py:179
  29.6 1.0 collective-permute-done.1.refs_2_
  30.6 0.0 collective-permute-done.2.refs_3_.refs_6_
  30.6 0.8 shard_map.75
  31.4 2.9 %collective-permute-start.3 = (f32[128,256]{1,0:T(8,128)S(1)}, f32[128,256]{1,0:T(8,128)S(1)}, u32[]{:S(2)}, u32[]{:S(2)}) collective-permute-start(f32[128,256]{1,0:T(8,128)S(1)} %get-tuple-element.31.refs_1_), channel_id=1, source_target_pairs={{0,64},{32,96},{64,0},{96,32},{128,192},{160,224},{192,128},{224,1... | collective-permute-start | bytes 393224 | tf_op jit(solution)/shard_map/ppermute | solution.py:224
  34.3 3.8 %collective-permute-start.6 = (f32[160,512]{1,0:T(8,128)S(1)}, f32[160,512]{1,0:T(8,128)}, u32[]{:S(2)}, u32[]{:S(2)}) collective-permute-start(f32[160,512]{1,0:T(8,128)S(1)} %get-tuple-element.30.refs_5_), channel_id=1, source_target_pairs={{0,24},{8,16},{16,8},{24,0},{1,25},{9,17},{17,9},{25,1},{2,26},{10... | collective-permute-start | bytes 983048 | tf_op jit(solution)/shard_map/ppermute | solution.py:179
  38.1 21.1 %collective-permute-done.4.refs_4_.refs_7_ = f32[160,512]{1,0:T(8,128)S(1)} collective-permute-done((f32[160,512]{1,0:T(8,128)S(1)}, f32[160,512]{1,0:T(8,128)S(1)}, u32[]{:S(2)}, u32[]{:S(2)}) %collective-permute-start.4) | collective-permute-done | bytes 327712 | tf_op jit(solution)/shard_map/ppermute | solution.py:179
  59.2 0.0 collective-permute-done.3.refs_2_
  59.2 1.5 shard_map.76
  60.7 0.7 copy-done.3
  61.4 0.7 copy-done.15
  62.1 15.6 %collective-permute-start.5 = (f32[128,256]{1,0:T(8,128)}, f32[128,256]{1,0:T(8,128)}, u32[]{:S(2)}, u32[]{:S(2)}) collective-permute-start(f32[128,256]{1,0:T(8,128)} %get-tuple-element.33.refs_1_), channel_id=1, source_target_pairs={{0,224},{32,192},{64,160},{96,128},{128,96},{160,64},{192,32},{224... | collective-permute-start | bytes 393224 | tf_op jit(solution)/shard_map/ppermute | solution.py:224
  77.7 0.0 collective-permute-done.6.refs_5_.refs_8_
  77.7 4.0 %collective-permute-done.5.refs_2_ = f32[128,256]{1,0:T(8,128)} collective-permute-done((f32[128,256]{1,0:T(8,128)}, f32[128,256]{1,0:T(8,128)}, u32[]{:S(2)}, u32[]{:S(2)}) %collective-permute-start.5) | collective-permute-done | bytes 131104 | tf_op jit(solution)/shard_map/ppermute | solution.py:224
  81.7 0.9 copy-done.5
  82.6 0.9 copy-done.16
  83.5 1.5 shard_map.77
  85.1 4.6 %collective-permute-start.7 = (f32[128,128]{1,0:T(8,128)S(1)}, f32[128,128]{1,0:T(8,128)S(1)}, u32[]{:S(2)}, u32[]{:S(2)}) collective-permute-start(f32[128,128]{1,0:T(8,128)S(1)} %get-tuple-element.36), channel_id=1, source_target_pairs={{0,256},{1,257},{2,258},{3,259},{4,260},{5,261},{6,262},{7,263},{8... | collective-permute-start | bytes 196616 | tf_op jit(solution)/shard_map/ppermute | solution.py:229
  89.8 0.0 copy-start.6
  89.8 0.0 copy-start.8
  89.8 0.0 copy-start.14
  89.8 0.0 collective-permute-done.8.pair_ref
  89.8 3.8 %shard_map.79.refs_6_.refs_9_.w_ref = bf16[5,512,384]{2,1,0:T(8,128)(2,1)S(1)} custom-call(s32[5]{0:T(128)S(1)} %broadcast_add_fusion.1.to_ref, bf16[256,6144]{1,0:T(8,128)(2,1)S(1)} %copy-done, f32[5,256,384]{2,1,0:T(8,128)} %collective-permute-done.8.pair_ref), custom_call_target="tpu_custom_call" | custom-call | tf_op jit(solution)/shard_map/pallas_call | solution.py:230
  93.6 0.0 collective-permute-done.7.refs_2_
  93.7 1.0 shard_map.80.refs_1_
  94.7 2.2 %collective-permute-start.10 = (f32[128,256]{1,0:T(8,128)S(1)}, f32[128,256]{1,0:T(8,128)S(1)}, u32[]{:S(2)}, u32[]{:S(2)}) collective-permute-start(f32[128,256]{1,0:T(8,128)S(1)} %shard_map.80.refs_1_), channel_id=1, source_target_pairs={{0,8},{8,0},{1,9},{9,1},{2,10},{10,2},{3,11},{11,3},{4,12},{12,4},... | collective-permute-start | bytes 393224 | tf_op jit(solution)/shard_map/ppermute | solution.py:179
  96.9 6.0 %collective-permute-start.9 = (f32[128,256]{1,0:T(8,128)S(1)}, f32[128,256]{1,0:T(8,128)S(1)}, u32[]{:S(2)}, u32[]{:S(2)}) collective-permute-start(f32[128,256]{1,0:T(8,128)S(1)} %shard_map.80.refs_1_), channel_id=1, source_target_pairs={{0,16},{16,0},{1,17},{17,1},{2,18},{18,2},{3,19},{19,3},{4,20},{20... | collective-permute-start | bytes 393224 | tf_op jit(solution)/shard_map/ppermute | solution.py:179
  103.0 0.0 collective-permute-done.10.refs_3_
  103.0 4.3 %collective-permute-start.11 = (f32[128,256]{1,0:T(8,128)S(1)}, f32[128,256]{1,0:T(8,128)S(1)}, u32[]{:S(2)}, u32[]{:S(2)}) collective-permute-start(f32[128,256]{1,0:T(8,128)S(1)} %collective-permute-done.10.refs_3_), channel_id=1, source_target_pairs={{0,16},{16,0},{1,17},{17,1},{2,18},{18,2},{3,19},{19,3},{4,20},{20... | collective-permute-start | bytes 393224 | tf_op jit(solution)/shard_map/ppermute | solution.py:179
  107.3 0.0 collective-permute-done.9.refs_2_
  107.3 1.0 collective-permute-done.11.refs_4_
  108.3 1.9 %shard_map.81 = (bf16[320,512]{1,0:T(8,128)(2,1)S(1)}, f32[160,384]{1,0:T(8,128)S(1)}) custom-call(s32[3]{0:T(128)S(1)} %pad_add_fusion.refs_0_, f32[128,256]{1,0:T(8,128)S(1)} %shard_map.80.refs_1_, f32[128,256]{1,0:T(8,128)S(1)} %collective-permute-done.9.refs_2_, f32[128,256]{1,0:T(8,128)S(1)} %collective-permute-done.10.refs_3_, ...), custom_call_target="tpu_custom_call" | custom-call | flops 1000000000 | bytes 131072 | tf_op jit(solution)/shard_map/pallas_call | solution.py:36
  110.2 0.8 shard_map.82
  111.0 3.2 %collective-permute-start.12 = (f32[160,384]{1,0:T(8,128)S(1)}, f32[160,384]{1,0:T(8,128)S(1)}, u32[]{:S(2)}, u32[]{:S(2)}) collective-permute-start(f32[160,384]{1,0:T(8,128)S(1)} %get-tuple-element.38), channel_id=1, source_target_pairs={{0,7},{1,0},{2,1},{3,2},{4,3},{5,4},{6,5},{7,6},{16,17},{17,18},{1... | collective-permute-start | bytes 737288 | tf_op jit(solution)/shard_map/ppermute | solution.py:185
  114.3 5.4 %collective-permute-done.12 = f32[160,384]{1,0:T(8,128)S(1)} collective-permute-done((f32[160,384]{1,0:T(8,128)S(1)}, f32[160,384]{1,0:T(8,128)S(1)}, u32[]{:S(2)}, u32[]{:S(2)}) %collective-permute-start.12) | collective-permute-done | bytes 245792 | tf_op jit(solution)/shard_map/ppermute | solution.py:185
  119.7 1.9 %collective-permute-start.13 = (f32[320,384]{1,0:T(8,128)S(1)}, f32[320,384]{1,0:T(8,128)S(1)}, u32[]{:S(2)}, u32[]{:S(2)}) collective-permute-start(f32[320,384]{1,0:T(8,128)S(1)} %fusion.5), channel_id=1, source_target_pairs={{0,7},{1,0},{2,1},{3,2},{4,3},{5,4},{6,5},{7,6},{16,17},{17,18},{1... | collective-permute-start | bytes 1474568 | tf_op jit(solution)/shard_map/ppermute | solution.py:185
  121.7 8.9 %collective-permute-done.13 = f32[320,384]{1,0:T(8,128)S(1)} collective-permute-done((f32[320,384]{1,0:T(8,128)S(1)}, f32[320,384]{1,0:T(8,128)S(1)}, u32[]{:S(2)}, u32[]{:S(2)}) %collective-permute-start.13) | collective-permute-done | bytes 491552 | tf_op jit(solution)/shard_map/ppermute | solution.py:185
  130.5 0.1 fusion.1
  130.6 1.9 %collective-permute-start.14 = (f32[320,384]{1,0:T(8,128)S(1)}, f32[320,384]{1,0:T(8,128)S(1)}, u32[]{:S(2)}, u32[]{:S(2)}) collective-permute-start(f32[320,384]{1,0:T(8,128)S(1)} %fusion.1), channel_id=1, source_target_pairs={{0,7},{1,0},{2,1},{3,2},{4,3},{5,4},{6,5},{7,6},{16,17},{17,18},{1... | collective-permute-start | bytes 1474568 | tf_op jit(solution)/shard_map/ppermute | solution.py:185
  132.5 8.9 %collective-permute-done.14 = f32[320,384]{1,0:T(8,128)S(1)} collective-permute-done((f32[320,384]{1,0:T(8,128)S(1)}, f32[320,384]{1,0:T(8,128)S(1)}, u32[]{:S(2)}, u32[]{:S(2)}) %collective-permute-start.14) | collective-permute-done | bytes 491552 | tf_op jit(solution)/shard_map/ppermute | solution.py:185
  141.4 0.1 fusion
  141.4 1.9 %collective-permute-start.15 = (f32[320,384]{1,0:T(8,128)S(1)}, f32[320,384]{1,0:T(8,128)S(1)}, u32[]{:S(2)}, u32[]{:S(2)}) collective-permute-start(f32[320,384]{1,0:T(8,128)S(1)} %fusion), channel_id=1, source_target_pairs={{0,7},{1,0},{2,1},{3,2},{4,3},{5,4},{6,5},{7,6},{16,17},{17,18},{1... | collective-permute-start | bytes 1474568 | tf_op jit(solution)/shard_map/ppermute | solution.py:185
  143.3 8.9 %collective-permute-done.15 = f32[320,384]{1,0:T(8,128)S(1)} collective-permute-done((f32[320,384]{1,0:T(8,128)S(1)}, f32[320,384]{1,0:T(8,128)S(1)}, u32[]{:S(2)}, u32[]{:S(2)}) %collective-permute-start.15) | collective-permute-done | bytes 491552 | tf_op jit(solution)/shard_map/ppermute | solution.py:185
  152.2 6.1 %collective-permute-start.16 = (f32[160,384]{1,0:T(8,128)S(1)}, f32[160,384]{1,0:T(8,128)S(1)}, u32[]{:S(2)}, u32[]{:S(2)}) collective-permute-start(f32[160,384]{1,0:T(8,128)S(1)} %slice.50), channel_id=1, source_target_pairs={{0,16},{16,0},{1,17},{17,1},{2,18},{18,2},{3,19},{19,3},{4,20},{20... | collective-permute-start | bytes 737288 | tf_op jit(solution)/shard_map/ppermute | solution.py:179
  158.3 1.1 collective-permute-done.16
  159.5 0.7 fusion.3
  (23 shorter events, 0.1 us)
Async XLA Ops:
  0.7 0.9 copy-start.9
  1.6 0.9 copy-start.10
  2.5 0.9 copy-start.11
  3.4 0.7 copy-start.12
  4.1 3.4 %copy-start = (bf16[256,6144]{1,0:T(8,128)(2,1)S(1)}, bf16[256,6144]{1,0:T(8,128)(2,1)}, u32[]{:S(2)}) copy-start(bf16[256,6144]{1,0:T(8,128)(2,1)} %own_ref.1) | copy-start | bytes 9437188
  7.5 15.7 %copy-start.13 = (f32[128,256]{1,0:T(8,128)}, f32[128,256]{1,0:T(8,128)S(1)}, u32[]{:S(2)}) copy-start(f32[128,256]{1,0:T(8,128)S(1)} %get-tuple-element.28.refs_1_.refs_4_) | copy-start | bytes 393220
  10.5 79.3 %collective-permute-start.8 = (f32[5,256,384]{2,1,0:T(8,128)}, f32[5,256,384]{2,1,0:T(8,128)}, u32[]{:S(2)}, u32[]{:S(2)}) collective-permute-start(f32[5,256,384]{2,1,0:T(8,128)} %shard_map.78), channel_id=1, source_target_pairs={{0,8},{8,0},{1,9},{9,1},{2,10},{10,2},{3,11},{11,3},{4,12},{12,4},... | collective-permute-start | bytes 5898248 | tf_op jit(solution)/shard_map/ppermute | solution.py:179
  14.5 8.7 %collective-permute-start = (f32[128,256]{1,0:T(8,128)S(1)}, f32[128,256]{1,0:T(8,128)S(1)}, u32[]{:S(2)}, u32[]{:S(2)}) collective-permute-start(f32[128,256]{1,0:T(8,128)S(1)} %get-tuple-element.29.later_ref), channel_id=1, source_target_pairs={{0,16},{16,0},{1,17},{17,1},{2,18},{18,2},{3,19},{19,3},{4,20},{20... | collective-permute-start | bytes 393224 | tf_op jit(solution)/shard_map/ppermute | solution.py:179
  21.2 9.3 %collective-permute-start.2 = (f32[160,512]{1,0:T(8,128)S(1)}, f32[160,512]{1,0:T(8,128)S(1)}, u32[]{:S(2)}, u32[]{:S(2)}) collective-permute-start(f32[160,512]{1,0:T(8,128)S(1)} %get-tuple-element.30.refs_5_), channel_id=1, source_target_pairs={{0,16},{16,0},{1,17},{17,1},{2,18},{18,2},{3,19},{19,3},{4,20},{20... | collective-permute-start | bytes 983048 | tf_op jit(solution)/shard_map/ppermute | solution.py:179
  23.2 8.2 %copy-start.7 = (f32[128,256]{1,0:T(8,128)}, f32[128,256]{1,0:T(8,128)S(1)}, u32[]{:S(2)}) copy-start(f32[128,256]{1,0:T(8,128)S(1)} %collective-permute-done.refs_2_.refs_5_) | copy-start | bytes 393220
  24.0 6.6 %collective-permute-start.1 = (f32[128,256]{1,0:T(8,128)S(1)}, f32[128,256]{1,0:T(8,128)S(1)}, u32[]{:S(2)}, u32[]{:S(2)}) collective-permute-start(f32[128,256]{1,0:T(8,128)S(1)} %shard_map.74.refs_1_), channel_id=1, source_target_pairs={{0,32},{32,0},{64,96},{96,64},{128,160},{160,128},{192,224},{224,1... | collective-permute-start | bytes 393224 | tf_op jit(solution)/shard_map/ppermute | solution.py:224
  25.9 33.3 %collective-permute-start.4 = (f32[160,512]{1,0:T(8,128)S(1)}, f32[160,512]{1,0:T(8,128)S(1)}, u32[]{:S(2)}, u32[]{:S(2)}) collective-permute-start(f32[160,512]{1,0:T(8,128)S(1)} %get-tuple-element.30.refs_5_), channel_id=1, source_target_pairs={{0,8},{8,0},{1,9},{9,1},{2,10},{10,2},{3,11},{11,3},{4,12},{12,4},... | collective-permute-start | bytes 983048 | tf_op jit(solution)/shard_map/ppermute | solution.py:179
  30.6 28.6 %copy-start.1 = (f32[160,512]{1,0:T(8,128)}, f32[160,512]{1,0:T(8,128)S(1)}, u32[]{:S(2)}) copy-start(f32[160,512]{1,0:T(8,128)S(1)} %collective-permute-done.2.refs_3_.refs_6_) | copy-start | bytes 983044
  31.4 27.8 %collective-permute-start.3 = (f32[128,256]{1,0:T(8,128)S(1)}, f32[128,256]{1,0:T(8,128)S(1)}, u32[]{:S(2)}, u32[]{:S(2)}) collective-permute-start(f32[128,256]{1,0:T(8,128)S(1)} %get-tuple-element.31.refs_1_), channel_id=1, source_target_pairs={{0,64},{32,96},{64,0},{96,32},{128,192},{160,224},{192,128},{224,1... | collective-permute-start | bytes 393224 | tf_op jit(solution)/shard_map/ppermute | solution.py:224
  34.3 43.4 %collective-permute-start.6 = (f32[160,512]{1,0:T(8,128)S(1)}, f32[160,512]{1,0:T(8,128)}, u32[]{:S(2)}, u32[]{:S(2)}) collective-permute-start(f32[160,512]{1,0:T(8,128)S(1)} %get-tuple-element.30.refs_5_), channel_id=1, source_target_pairs={{0,24},{8,16},{16,8},{24,0},{1,25},{9,17},{17,9},{25,1},{2,26},{10... | collective-permute-start | bytes 983048 | tf_op jit(solution)/shard_map/ppermute | solution.py:179
  60.7 0.7 copy-start.3
  61.4 0.7 copy-start.15
  62.1 19.6 %collective-permute-start.5 = (f32[128,256]{1,0:T(8,128)}, f32[128,256]{1,0:T(8,128)}, u32[]{:S(2)}, u32[]{:S(2)}) collective-permute-start(f32[128,256]{1,0:T(8,128)} %get-tuple-element.33.refs_1_), channel_id=1, source_target_pairs={{0,224},{32,192},{64,160},{96,128},{128,96},{160,64},{192,32},{224... | collective-permute-start | bytes 393224 | tf_op jit(solution)/shard_map/ppermute | solution.py:224
  81.7 0.9 copy-start.5
  82.6 0.9 copy-start.16
  85.1 8.5 %collective-permute-start.7 = (f32[128,128]{1,0:T(8,128)S(1)}, f32[128,128]{1,0:T(8,128)S(1)}, u32[]{:S(2)}, u32[]{:S(2)}) collective-permute-start(f32[128,128]{1,0:T(8,128)S(1)} %get-tuple-element.36), channel_id=1, source_target_pairs={{0,256},{1,257},{2,258},{3,259},{4,260},{5,261},{6,262},{7,263},{8... | collective-permute-start | bytes 196616 | tf_op jit(solution)/shard_map/ppermute | solution.py:229
  89.8 3.9 %copy-start.6 = (f32[2,128,128]{2,1,0:T(8,128)S(1)}, f32[2,128,128]{2,1,0:T(8,128)}, u32[]{:S(2)}) copy-start(f32[2,128,128]{2,1,0:T(8,128)} %refs_3_.3) | copy-start | bytes 393220
  89.8 3.9 %copy-start.8 = (f32[128,256]{1,0:T(8,128)S(1)}, f32[128,256]{1,0:T(8,128)}, u32[]{:S(2)}) copy-start(f32[128,256]{1,0:T(8,128)} %copy-done.7) | copy-start | bytes 393220
  89.8 3.9 %copy-start.14 = (f32[128,256]{1,0:T(8,128)S(1)}, f32[128,256]{1,0:T(8,128)}, u32[]{:S(2)}) copy-start(f32[128,256]{1,0:T(8,128)} %copy-done.13) | copy-start | bytes 393220
  93.6 14.7 %copy-start.2 = (f32[160,512]{1,0:T(8,128)S(1)}, f32[160,512]{1,0:T(8,128)}, u32[]{:S(2)}) copy-start(f32[160,512]{1,0:T(8,128)} %copy-done.1) | copy-start | bytes 983044
  93.6 14.6 %copy-start.4 = (f32[160,512]{1,0:T(8,128)S(1)}, f32[160,512]{1,0:T(8,128)}, u32[]{:S(2)}) copy-start(f32[160,512]{1,0:T(8,128)} %copy-done.3) | copy-start | bytes 983044
  94.7 8.3 %collective-permute-start.10 = (f32[128,256]{1,0:T(8,128)S(1)}, f32[128,256]{1,0:T(8,128)S(1)}, u32[]{:S(2)}, u32[]{:S(2)}) collective-permute-start(f32[128,256]{1,0:T(8,128)S(1)} %shard_map.80.refs_1_), channel_id=1, source_target_pairs={{0,8},{8,0},{1,9},{9,1},{2,10},{10,2},{3,11},{11,3},{4,12},{12,4},... | collective-permute-start | bytes 393224 | tf_op jit(solution)/shard_map/ppermute | solution.py:179
  96.9 10.4 %collective-permute-start.9 = (f32[128,256]{1,0:T(8,128)S(1)}, f32[128,256]{1,0:T(8,128)S(1)}, u32[]{:S(2)}, u32[]{:S(2)}) collective-permute-start(f32[128,256]{1,0:T(8,128)S(1)} %shard_map.80.refs_1_), channel_id=1, source_target_pairs={{0,16},{16,0},{1,17},{17,1},{2,18},{18,2},{3,19},{19,3},{4,20},{20... | collective-permute-start | bytes 393224 | tf_op jit(solution)/shard_map/ppermute | solution.py:179
  103.0 5.3 %collective-permute-start.11 = (f32[128,256]{1,0:T(8,128)S(1)}, f32[128,256]{1,0:T(8,128)S(1)}, u32[]{:S(2)}, u32[]{:S(2)}) collective-permute-start(f32[128,256]{1,0:T(8,128)S(1)} %collective-permute-done.10.refs_3_), channel_id=1, source_target_pairs={{0,16},{16,0},{1,17},{17,1},{2,18},{18,2},{3,19},{19,3},{4,20},{20... | collective-permute-start | bytes 393224 | tf_op jit(solution)/shard_map/ppermute | solution.py:179
  111.0 8.7 %collective-permute-start.12 = (f32[160,384]{1,0:T(8,128)S(1)}, f32[160,384]{1,0:T(8,128)S(1)}, u32[]{:S(2)}, u32[]{:S(2)}) collective-permute-start(f32[160,384]{1,0:T(8,128)S(1)} %get-tuple-element.38), channel_id=1, source_target_pairs={{0,7},{1,0},{2,1},{3,2},{4,3},{5,4},{6,5},{7,6},{16,17},{17,18},{1... | collective-permute-start | bytes 737288 | tf_op jit(solution)/shard_map/ppermute | solution.py:185
  119.7 10.8 %collective-permute-start.13 = (f32[320,384]{1,0:T(8,128)S(1)}, f32[320,384]{1,0:T(8,128)S(1)}, u32[]{:S(2)}, u32[]{:S(2)}) collective-permute-start(f32[320,384]{1,0:T(8,128)S(1)} %fusion.5), channel_id=1, source_target_pairs={{0,7},{1,0},{2,1},{3,2},{4,3},{5,4},{6,5},{7,6},{16,17},{17,18},{1... | collective-permute-start | bytes 1474568 | tf_op jit(solution)/shard_map/ppermute | solution.py:185
  130.6 10.8 %collective-permute-start.14 = (f32[320,384]{1,0:T(8,128)S(1)}, f32[320,384]{1,0:T(8,128)S(1)}, u32[]{:S(2)}, u32[]{:S(2)}) collective-permute-start(f32[320,384]{1,0:T(8,128)S(1)} %fusion.1), channel_id=1, source_target_pairs={{0,7},{1,0},{2,1},{3,2},{4,3},{5,4},{6,5},{7,6},{16,17},{17,18},{1... | collective-permute-start | bytes 1474568 | tf_op jit(solution)/shard_map/ppermute | solution.py:185
  141.4 10.8 %collective-permute-start.15 = (f32[320,384]{1,0:T(8,128)S(1)}, f32[320,384]{1,0:T(8,128)S(1)}, u32[]{:S(2)}, u32[]{:S(2)}) collective-permute-start(f32[320,384]{1,0:T(8,128)S(1)} %fusion), channel_id=1, source_target_pairs={{0,7},{1,0},{2,1},{3,2},{4,3},{5,4},{6,5},{7,6},{16,17},{17,18},{1... | collective-permute-start | bytes 1474568 | tf_op jit(solution)/shard_map/ppermute | solution.py:185
  152.2 7.2 %collective-permute-start.16 = (f32[160,384]{1,0:T(8,128)S(1)}, f32[160,384]{1,0:T(8,128)S(1)}, u32[]{:S(2)}, u32[]{:S(2)}) collective-permute-start(f32[160,384]{1,0:T(8,128)S(1)} %slice.50), channel_id=1, source_target_pairs={{0,16},{16,0},{1,17},{17,1},{2,18},{18,2},{3,19},{19,3},{4,20},{20... | collective-permute-start | bytes 737288 | tf_op jit(solution)/shard_map/ppermute | solution.py:179

commit v2 on v1

v2 whole, which is shorter than its diff:
```python
import jax
import jax.numpy as jnp
from jax import lax
from jax.experimental import pallas as pl
from jax.experimental.pallas import tpu as pltpu
from jax.sharding import Mesh, PartitionSpec as P

MB = 16
HW = 128
XH, Z, CORE, XL, Y = "xh", "z", "core", "xl", "y"
SIZES = (2, 8, 2, 2, 8)
f32 = jnp.float32
bf16 = jnp.bfloat16
VM = pl.BlockSpec(memory_space=pltpu.VMEM)
SM = pl.BlockSpec(memory_space=pltpu.SMEM)
MIB = 2**20


def exact(a, b, contract=((1,), (0,))):
    return lax.dot_general(
        a, b, (contract, ((), ())), precision=lax.Precision.HIGHEST, preferred_element_type=f32
    )


def single(a, b, contract=((1,), (0,))):
    return lax.dot_general(a, b, (contract, ((), ())), preferred_element_type=f32)


def call(kernel, out_shapes, at, *args, later=(), scratch=(), limit=4, us=1.0):
    outs = [jax.ShapeDtypeStruct(s, d) for s, d in out_shapes]
    n = 1 + len(args)

    def body(*refs):
        kernel(*refs[:n], *refs[n + len(later) :])

    return pl.pallas_call(
        body,
        out_shape=outs,
        in_specs=[SM] + [VM] * len(args) + [pl.BlockSpec(memory_space=pl.ANY)] * len(later),
        out_specs=[VM] * len(outs),
        scratch_shapes=list(scratch),
        compiler_params=pltpu.CompilerParams(vmem_limit_bytes=limit * MIB),
        cost_estimate=pl.CostEstimate(flops=int(us * 1e9), bytes_accessed=1 << 17, transcendentals=0),
    )(at, *args, *later)


def place(at_ref):
    return at_ref[0], at_ref[1], at_ref[2]


def left_half(shape):
    return lax.broadcasted_iota(jnp.int32, shape, 1) < HW


def identity(columns):
    rows_at = lax.broadcasted_iota(jnp.int32, (HW, columns), 0)
    return (rows_at == lax.broadcasted_iota(jnp.int32, (HW, columns), 1)).astype(f32)


def after(second, first):
    return exact(second[:, :HW], first) + jnp.where(left_half(second.shape), 0.0, second)


def applied(pair, state):
    return exact(pair[:, :HW], state) + pair[:, HW:]


def shard_maps(at_ref, q_ref, k_ref, v_ref, r_ref, keep_ref, send_ref, rows_ref, x_ref):
    rows = q_ref.shape[0]
    _, _, core = place(at_ref)
    s_at = lax.broadcasted_iota(jnp.int32, (rows, rows), 0)
    t_at = lax.broadcasted_iota(jnp.int32, (rows, rows), 1)
    earlier_block = (t_at // MB) < (s_at // MB)
    causal = t_at <= s_at
    diagonal = t_at == s_at
    mix, key_gram, columns = [], [], []
    for h in range(2):
        at = slice(h * HW, (h + 1) * HW)
        q, k, v = q_ref[:, at], k_ref[:, at], v_ref[:, at]
        r = r_ref[h : h + 1, :]
        columns.append(jnp.sum(jnp.where(diagonal, r, 0.0), axis=1, keepdims=True))
        key_gram.append(jnp.where(earlier_block, single(k, k, ((1,), (1,))) * r, 0.0))
        mix.append(jnp.where(causal, single(q, k, ((1,), (1,))) * r, 0.0))
        x_ref[h, :, :HW] = k.astype(f32)
        x_ref[h, :, HW:] = v.astype(f32)
    for i in range(1, rows // MB):
        at = slice(i * MB, (i + 1) * MB)
        for h in range(2):
            x_ref[h, at, :] = x_ref[h, at, :] - exact(key_gram[h][at, :], x_ref[h])
    maps = []
    for h in range(2):
        at = slice(h * HW, (h + 1) * HW)
        x = x_ref[h]
        y = exact(mix[h], x)
        rows_ref[:, at] = q_ref[:, at].astype(f32) - y[:, :HW]
        rows_ref[:, (2 + h) * HW : (3 + h) * HW] = y[:, HW:]
        ab = exact(k_ref[:, at].astype(f32) * columns[h], x, ((0,), (0,)))
        maps.append(identity(2 * HW) + jnp.where(left_half(ab.shape), -ab, ab))
    first = core == 0
    keep_ref[...] = jnp.where(first, maps[0], maps[1])
    send_ref[...] = jnp.where(first, maps[1], maps[0])


def chip_map(at_ref, keep_ref, got_ref, out_ref):
    first = place(at_ref)[2] == 0
    early = jnp.where(first, keep_ref[...], got_ref[...])
    late = jnp.where(first, got_ref[...], keep_ref[...])
    out_ref[...] = after(late, early)


def join_chips(at_ref, own_ref, got_ref, both_ref, pre_ref):
    upper = lax.rem(place(at_ref)[0], 2) == 1
    low = jnp.where(upper, got_ref[...], own_ref[...])
    high = jnp.where(upper, own_ref[...], got_ref[...])
    both_ref[...] = after(high, low)
    pre_ref[...] = jnp.where(upper, low, identity(2 * HW))


def join_pairs(at_ref, own_ref, got_ref, pre_in_ref, both_ref, pre_ref):
    upper = lax.rem(place(at_ref)[0], 4) >= 2
    low = jnp.where(upper, got_ref[...], own_ref[...])
    high = jnp.where(upper, own_ref[...], got_ref[...])
    both_ref[...] = after(high, low)
    pre = pre_in_ref[...]
    pre_ref[...] = jnp.where(upper, after(pre, low), pre)


def join_ring(at_ref, own_ref, got_ref, pre_in_ref, first_ref, end_ref, pre_ref):
    z, _, core = place(at_ref)
    upper = z >= 4
    low = jnp.where(upper, got_ref[...], own_ref[...])
    high = jnp.where(upper, own_ref[...], got_ref[...])
    end_ref[...] = applied(high, applied(low, first_ref[core]))
    pre = pre_in_ref[...]
    pre_ref[...] = jnp.where(upper, after(pre, low), pre)


def shard_prefixes(at_ref, pre_ref, keep_ref, got_ref, mine_ref, other_ref):
    first = place(at_ref)[2] == 0
    pre = pre_ref[...]
    middle = after(jnp.where(first, keep_ref[...], got_ref[...]), pre)
    mine_ref[...] = jnp.where(first, pre, middle)
    other_ref[...] = jnp.where(first, middle, pre)


def shard_states(at_ref, mine_ref, other_ref, arrived_ref, first_ref, keep_ref, send_ref):
    _, x_hi, core = place(at_ref)
    state = jnp.where(x_hi == 0, first_ref[core], arrived_ref[...])
    send_ref[...] = applied(other_ref[...], state)
    keep_ref[...] = applied(mine_ref[...], state)


def outputs(at_ref, keep_ref, got_ref, rows_ref, z_ref):
    core = place(at_ref)[2]
    for h in range(2):
        state = jnp.where(core == h, keep_ref[...], got_ref[...])
        at = slice(h * HW, (h + 1) * HW)
        z = exact(rows_ref[:, at], state) + rows_ref[:, (2 + h) * HW : (3 + h) * HW]
        z_ref[:, at] = z.astype(bf16).astype(f32)


def pair_weights(to_ref, w_ref, later_ref, near_ref, far_ref):
    del to_ref, later_ref
    near_ref[...] = w_ref[:HW, :].astype(f32)
    far_ref[...] = w_ref[HW:, :].astype(f32)


def piece(z, z_pair, to, w_ref, near_ref, far_ref):
    chunk = w_ref.shape[1] // (SIZES[3] * SIZES[4])
    x_lo, y = to
    at = pl.ds(pl.multiple_of(y * chunk, HW), chunk)
    own_at = pl.ds(pl.multiple_of((x_lo * SIZES[4] + y) * chunk, HW), chunk)
    return (
        single(z, w_ref[:, own_at])
        + single(z_pair[:, :HW], near_ref[:, at].astype(bf16))
        + single(z_pair[:, HW:], far_ref[:, at].astype(bf16))
    )


def farthest(at_ref, z_ref, zx_ref, w_ref, near_ref, far_ref, low_ref, high_ref):
    half = low_ref.shape[0]
    to = (at_ref[3], lax.rem(at_ref[4] + 4, SIZES[4]))
    out = piece(z_ref[...].astype(bf16), zx_ref[...].astype(bf16), to, w_ref, near_ref, far_ref)
    low_ref[...] = out[:half]
    high_ref[...] = out[half:]


OFFSETS = (-3, 3, -2, 2, -1, 1, 0)


def nearer(at_ref, z_ref, zx_ref, w_ref, near_ref, far_ref, *out_refs):
    z, zx = z_ref[...].astype(bf16), zx_ref[...].astype(bf16)
    for offset, out_ref in zip(OFFSETS, out_refs):
        to = (at_ref[3], lax.rem(at_ref[4] + (offset + SIZES[4]), SIZES[4]))
        out_ref[...] = piece(z, zx, to, w_ref, near_ref, far_ref)


def swapped(x, axes):
    n = 2 ** len(axes)
    return lax.ppermute(x, axes, [(i, n - 1 - i) for i in range(n)])


def passed(x, axis, by):
    n = lax.axis_size(axis)
    return lax.ppermute(x, axis, [(i, (i + by) % n) for i in range(n)])


def local(queries, keys, values, rates, init_weight, out_weight):
    rows = queries.shape[0]
    x_hi, z, core, x_lo, y = (lax.axis_index(a) for a in (XH, Z, CORE, XL, Y))
    at = jnp.stack([z, x_hi, core, x_lo, y]).astype(jnp.int32)
    columns = out_weight.shape[1] // SIZES[3]
    chunk = columns // SIZES[4]
    square, wide, out_piece = ((HW, HW), f32), ((HW, 2 * HW), f32), ((rows, chunk), f32)

    keep, send, own_rows = call(
        shard_maps, [wide, wide, ((rows, 4 * HW), f32)], at, queries, keys, values, rates,
        scratch=[pltpu.VMEM((2, rows, 2 * HW), f32)], limit=56, us=3,
    )
    got = swapped(send, (CORE,))

    def across_z(x, to):
        return lax.ppermute(x, Z, [(i, to(i)) for i in range(SIZES[1])])

    (chip,) = call(chip_map, [wide], at, keep, got)
    parts = 4
    near_out, far_out = pl.pallas_call(
        pair_weights,
        grid_spec=pltpu.PrefetchScalarGridSpec(
            num_scalar_prefetch=1,
            grid=(parts,),
            in_specs=[
                pl.BlockSpec((2 * HW, columns // parts), lambda i, to: (0, to[0] * parts + i)),
                pl.BlockSpec(memory_space=pl.ANY),
            ],
            out_specs=[pl.BlockSpec((HW, columns // parts), lambda i, to: (0, i))] * 2,
        ),
        out_shape=[jax.ShapeDtypeStruct((HW, columns), f32)] * 2,
        compiler_params=pltpu.CompilerParams(vmem_limit_bytes=6 * MIB),
    )((1 - x_lo).reshape(1).astype(jnp.int32), out_weight, chip)
    near = swapped(near_out, (XL,))
    far = swapped(far_out, (XH, XL))

    both, pre = call(join_chips, [wide, wide], at, chip, across_z(chip, lambda i: i ^ 1), later=[near_out], us=3)
    four, pre = call(join_pairs, [wide, wide], at, both, across_z(both, lambda i: i ^ 2), pre, us=3)
    end, pre = call(join_ring, [square, wide], at, four, across_z(four, lambda i: 7 - i), pre, init_weight, us=3)
    arrived = lax.ppermute(end, XH, [(0, 1)])
    mine, other = call(shard_prefixes, [wide, wide], at, pre, keep, got, us=3)
    kept, leaving = call(shard_states, [square, square], at, mine, other, arrived, init_weight, us=3)
    (z_rows,) = call(outputs, [((rows, 2 * HW), f32)], at, kept, swapped(leaving, (CORE,)), own_rows)
    z_pair = swapped(z_rows, (XL,))

    factors = (z_rows, z_pair, out_weight, near, far)
    low, high = call(farthest, [((rows // 2, chunk), f32)] * 2, at, *factors, limit=16)
    down, up = passed(low, Y, -1), passed(high, Y, 1)
    pieces = call(nearer, [out_piece] * len(OFFSETS), at, *factors, later=[low], limit=16)
    down = pieces[0] + jnp.concatenate([down, jnp.zeros_like(down)], axis=0)
    up = pieces[1] + jnp.concatenate([jnp.zeros_like(up), up], axis=0)
    for i in (2, 4):
        down = passed(down, Y, -1) + pieces[i]
        up = passed(up, Y, 1) + pieces[i + 1]
    return (passed(down, Y, -1) + passed(up, Y, 1) + pieces[6]).astype(bf16)


def solution(mesh):
    fine = Mesh(mesh.devices.reshape(SIZES), (XH, Z, CORE, XL, Y))
    ctx, tp = (XH, Z, CORE), (XL, Y)
    in_specs = (P(ctx, tp), P(ctx, tp), P(ctx, tp), P(tp, ctx), P(tp, None, None), P(tp, None))
    return jax.shard_map(local, mesh=fine, in_specs=in_specs, out_specs=P(ctx, tp), check_vma=False)
```

time: 161 us -> 122 us (0.76)
  the two profiles are of different devices: /device:TPU:1 before, /device:TPU:4 now
where the time goes in v2:
time: 122 us
  starting transfers between devices  62.5 us (51%)
  waiting for transfers between devices  42.7 us (35%)
  Pallas kernels  13.8 us (11%)
  local copies, waits for them, and re-layouts  1.59 us (1%)
    ppermute x8, starting transfers between devices, passed(): return lax.ppermute(x, axis, [(i, (i + by) % n) for i in range(n)])  29.4 us
    ppermute x3, starting transfers between devices, across_z(): return lax.ppermute(x, Z, [(i, to(i)) for i in range(SIZES[1])])  18.9 us
    ppermute x1, waiting for transfers between devices, local(): arrived = lax.ppermute(end, XH, [(0, 1)])  16.5 us
    pallas_call x10, Pallas kernels, call(): pl.pallas_call(body, out_shape=outs, in_specs=[SM] + [VM] * len(args) + [...  13.1 us
    ppermute x5, starting transfers between devices, swapped(): return lax.ppermute(x, axes, [(i, n - 1 - i) for i in range(n)])  12.8 us
    ppermute x8, waiting for transfers between devices, passed(): return lax.ppermute(x, axis, [(i, (i + by) % n) for i in range(n)])  11.3 us
    ppermute x3, waiting for transfers between devices, across_z(): return lax.ppermute(x, Z, [(i, to(i)) for i in range(SIZES[1])])  7.58 us
    ppermute x5, waiting for transfers between devices, swapped(): return lax.ppermute(x, axes, [(i, n - 1 - i) for i in range(n)])  7.32 us
  transfers between devices with their start and end apart: 17, of which 11 were waited for; matrix products, arithmetic and copies ran while one was open for 0% of the time, Pallas kernels for 5%

profile of v2, /device:TPU:4, one launch (start us, length us, event | category | flops | bytes accessed | tf_op | source)
XLA Modules:
  0.0 121.6 jit_solution(12094598877668346632)
XLA Ops:
  0.0 0.7 stack.23.refs_0_
  0.7 0.0 copy-start.1
  0.7 4.7 %shard_map.64 = (f32[128,256]{1,0:T(8,128)}, f32[128,256]{1,0:T(8,128)}, f32[160,512]{1,0:T(8,128)}) custom-call(s32[5]{0:T(128)} %stack.23.refs_0_, bf16[160,256]{1,0:T(8,128)(2,1)} %refs_1_.1, bf16[160,256]{1,0:T(8,128)(2,1)} %refs_2_.1, bf16[160,256]{1,0:T(8,128)(2,1)} %refs_3_.3, f32[2,160]{1,0:T(2,128)} %refs_4_.3), custom_call_target="tpu_custom_call" | custom-call | flops 3000000000 | bytes 131072 | tf_op jit(solution)/shard_map/pallas_call | solution.py:36
  5.4 1.9 %collective-permute-start = (f32[128,256]{1,0:T(8,128)}, f32[128,256]{1,0:T(8,128)S(1)}, u32[]{:S(2)}, u32[]{:S(2)}) collective-permute-start(f32[128,256]{1,0:T(8,128)} %get-tuple-element.30), channel_id=1, source_target_pairs={{0,16},{16,0},{1,17},{17,1},{2,18},{18,2},{3,19},{19,3},{4,20},{20... | collective-permute-start | bytes 393224 | tf_op jit(solution)/shard_map/ppermute | solution.py:200
  7.3 1.5 %collective-permute-done.refs_2_.refs_3_ = f32[128,256]{1,0:T(8,128)S(1)} collective-permute-done((f32[128,256]{1,0:T(8,128)}, f32[128,256]{1,0:T(8,128)S(1)}, u32[]{:S(2)}, u32[]{:S(2)}) %collective-permute-start) | collective-permute-done | bytes 131104 | tf_op jit(solution)/shard_map/ppermute | solution.py:200
  8.8 0.0 copy-done.1
  8.8 0.0 copy-start.4
  8.8 0.9 copy-done.4
  9.7 0.0 copy-start
  9.7 0.8 shard_map.65.later_ref.refs_1_
  10.5 4.4 %collective-permute-start.1 = (f32[128,256]{1,0:T(8,128)S(1)}, f32[128,256]{1,0:T(8,128)S(1)}, u32[]{:S(2)}, u32[]{:S(2)}) collective-permute-start(f32[128,256]{1,0:T(8,128)S(1)} %shard_map.65.later_ref.refs_1_), channel_id=1, source_target_pairs={{0,32},{32,0},{64,96},{96,64},{128,160},{160,128},{192,224},{224,1... | collective-permute-start | bytes 393224 | tf_op jit(solution)/shard_map/ppermute | solution.py:223
  15.0 0.0 copy-done
  15.0 0.7 shard_map.66
  15.6 3.1 %collective-permute-done.1.refs_2_ = f32[128,256]{1,0:T(8,128)S(1)} collective-permute-done((f32[128,256]{1,0:T(8,128)S(1)}, f32[128,256]{1,0:T(8,128)S(1)}, u32[]{:S(2)}, u32[]{:S(2)}) %collective-permute-start.1) | collective-permute-done | bytes 131104 | tf_op jit(solution)/shard_map/ppermute | solution.py:223
  18.8 0.8 shard_map.67
  19.6 6.1 %collective-permute-start.2 = (f32[128,256]{1,0:T(8,128)S(1)}, f32[128,256]{1,0:T(8,128)S(1)}, u32[]{:S(2)}, u32[]{:S(2)}) collective-permute-start(f32[128,256]{1,0:T(8,128)S(1)} %get-tuple-element.32.refs_1_), channel_id=1, source_target_pairs={{0,64},{32,96},{64,0},{96,32},{128,192},{160,224},{192,128},{224,1... | collective-permute-start | bytes 393224 | tf_op jit(solution)/shard_map/ppermute | solution.py:223
  25.7 3.1 %collective-permute-start.7 = (f32[128,3072]{1,0:T(8,128)S(1)}, f32[128,3072]{1,0:T(8,128)S(1)}, u32[]{:S(2)}, u32[]{:S(2)}) collective-permute-start(f32[128,3072]{1,0:T(8,128)S(1)} %get-tuple-element.31.refs_3_), channel_id=1, source_target_pairs={{0,8},{8,0},{1,9},{9,1},{2,10},{10,2},{3,11},{11,3},{4,12},{12,4},... | collective-permute-start | bytes 4718600 | tf_op jit(solution)/shard_map/ppermute | solution.py:200
  28.8 2.3 %collective-permute-start.8 = (f32[128,3072]{1,0:T(8,128)S(1)}, f32[128,3072]{1,0:T(8,128)S(1)}, u32[]{:S(2)}, u32[]{:S(2)}) collective-permute-start(f32[128,3072]{1,0:T(8,128)S(1)} %get-tuple-element.43), channel_id=1, source_target_pairs={{0,264},{8,256},{256,8},{264,0},{1,265},{9,257},{257,9},{265,1},{2... | collective-permute-start | bytes 4718600 | tf_op jit(solution)/shard_map/ppermute | solution.py:200
  31.1 0.6 collective-permute-done.2.refs_2_
  31.8 0.0 copy-start.2
  31.8 0.9 shard_map.68
  32.7 8.4 %collective-permute-start.3 = (f32[128,256]{1,0:T(8,128)S(1)}, f32[128,256]{1,0:T(8,128)S(1)}, u32[]{:S(2)}, u32[]{:S(2)}) collective-permute-start(f32[128,256]{1,0:T(8,128)S(1)} %get-tuple-element.34.refs_1_), channel_id=1, source_target_pairs={{0,224},{32,192},{64,160},{96,128},{128,96},{160,64},{192,32},{224... | collective-permute-start | bytes 393224 | tf_op jit(solution)/shard_map/ppermute | solution.py:223
  41.1 3.8 %collective-permute-done.3.refs_2_ = f32[128,256]{1,0:T(8,128)S(1)} collective-permute-done((f32[128,256]{1,0:T(8,128)S(1)}, f32[128,256]{1,0:T(8,128)S(1)}, u32[]{:S(2)}, u32[]{:S(2)}) %collective-permute-start.3) | collective-permute-done | bytes 131104 | tf_op jit(solution)/shard_map/ppermute | solution.py:223
  45.0 0.0 copy-done.2
  45.0 0.0 copy-start.5
  45.0 1.1 shard_map.69
  46.1 1.3 %collective-permute-start.4 = (f32[128,128]{1,0:T(8,128)S(1)}, f32[128,128]{1,0:T(8,128)S(1)}, u32[]{:S(2)}, u32[]{:S(2)}) collective-permute-start(f32[128,128]{1,0:T(8,128)S(1)} %get-tuple-element.39), channel_id=1, source_target_pairs={{0,256},{1,257},{2,258},{3,259},{4,260},{5,261},{6,262},{7,263},{8... | collective-permute-start | bytes 196616 | tf_op jit(solution)/shard_map/ppermute | solution.py:247
  47.4 0.0 copy-done.5
  47.4 0.8 shard_map.70
  48.2 16.5 %collective-permute-done.4.refs_3_ = f32[128,128]{1,0:T(8,128)S(1)} collective-permute-done((f32[128,128]{1,0:T(8,128)S(1)}, f32[128,128]{1,0:T(8,128)S(1)}, u32[]{:S(2)}, u32[]{:S(2)}) %collective-permute-start.4) | collective-permute-done | bytes 65568 | tf_op jit(solution)/shard_map/ppermute | solution.py:247
  64.7 0.0 copy-start.3
  64.7 0.8 shard_map.71
  65.5 1.9 %collective-permute-start.5 = (f32[128,128]{1,0:T(8,128)S(1)}, f32[128,128]{1,0:T(8,128)S(1)}, u32[]{:S(2)}, u32[]{:S(2)}) collective-permute-start(f32[128,128]{1,0:T(8,128)S(1)} %get-tuple-element.41), channel_id=1, source_target_pairs={{0,16},{16,0},{1,17},{17,1},{2,18},{18,2},{3,19},{19,3},{4,20},{20... | collective-permute-start | bytes 196616 | tf_op jit(solution)/shard_map/ppermute | solution.py:200
  67.5 1.2 %collective-permute-done.5.refs_2_ = f32[128,128]{1,0:T(8,128)S(1)} collective-permute-done((f32[128,128]{1,0:T(8,128)S(1)}, f32[128,128]{1,0:T(8,128)S(1)}, u32[]{:S(2)}, u32[]{:S(2)}) %collective-permute-start.5) | collective-permute-done | bytes 65568 | tf_op jit(solution)/shard_map/ppermute | solution.py:200
  68.7 0.0 copy-done.3
  68.7 0.8 shard_map.72.refs_1_
  69.5 3.6 %collective-permute-start.6 = (f32[160,256]{1,0:T(8,128)S(1)}, f32[160,256]{1,0:T(8,128)S(1)}, u32[]{:S(2)}, u32[]{:S(2)}) collective-permute-start(f32[160,256]{1,0:T(8,128)S(1)} %shard_map.72.refs_1_), channel_id=1, source_target_pairs={{0,8},{8,0},{1,9},{9,1},{2,10},{10,2},{3,11},{11,3},{4,12},{12,4},... | collective-permute-start | bytes 491528 | tf_op jit(solution)/shard_map/ppermute | solution.py:200
  73.1 4.6 %collective-permute-done.6.refs_2_ = f32[160,256]{1,0:T(8,128)S(1)} collective-permute-done((f32[160,256]{1,0:T(8,128)S(1)}, f32[160,256]{1,0:T(8,128)S(1)}, u32[]{:S(2)}, u32[]{:S(2)}) %collective-permute-start.6) | collective-permute-done | bytes 163872 | tf_op jit(solution)/shard_map/ppermute | solution.py:200
  77.7 0.0 collective-permute-done.8.refs_5_
  77.7 0.0 collective-permute-done.7.refs_4_
  77.7 0.8 shard_map.73
  78.5 5.4 %collective-permute-start.9 = (f32[80,384]{1,0:T(8,128)S(1)}, f32[80,384]{1,0:T(8,128)S(1)}, u32[]{:S(2)}, u32[]{:S(2)}) collective-permute-start(f32[80,384]{1,0:T(8,128)S(1)} %get-tuple-element.44.refs_6_), channel_id=1, source_target_pairs={{0,7},{1,0},{2,1},{3,2},{4,3},{5,4},{6,5},{7,6},{8,15},{9,8},{10,9... | collective-permute-start | bytes 368648 | tf_op jit(solution)/shard_map/ppermute | solution.py:205
  83.9 1.9 %collective-permute-start.13 = (f32[80,384]{1,0:T(8,128)S(1)}, f32[80,384]{1,0:T(8,128)S(1)}, u32[]{:S(2)}, u32[]{:S(2)}) collective-permute-start(f32[80,384]{1,0:T(8,128)S(1)} %get-tuple-element.49), channel_id=1, source_target_pairs={{0,1},{1,2},{2,3},{3,4},{4,5},{5,6},{6,7},{7,0},{8,9},{9,10},{10,1... | collective-permute-start | bytes 368648 | tf_op jit(solution)/shard_map/ppermute | solution.py:205
  85.8 1.5 %shard_map.74 = (f32[160,384]{1,0:T(8,128)S(1)}, f32[160,384]{1,0:T(8,128)S(1)}, f32[160,384]{1,0:T(8,128)S(1)}, f32[160,384]{1,0:T(8,128)S(1)}, f32[160,384]{1,...) custom-call(s32[5]{0:T(128)S(1)} %copy-done.1, f32[160,256]{1,0:T(8,128)S(1)} %shard_map.72.refs_1_, ...), custom_call_target="tpu_custom_call" | custom-call | flops 1000000000 | bytes 131072 | tf_op jit(solution)/shard_map/pallas_call | solution.py:36
  87.3 0.0 collective-permute-done.9
  87.3 5.1 %collective-permute-start.10 = (f32[160,384]{1,0:T(8,128)S(1)}, f32[160,384]{1,0:T(8,128)S(1)}, u32[]{:S(2)}, u32[]{:S(2)}) collective-permute-start(f32[160,384]{1,0:T(8,128)S(1)} %pad_add_fusion.1), channel_id=1, source_target_pairs={{0,7},{1,0},{2,1},{3,2},{4,3},{5,4},{6,5},{7,6},{8,15},{9,8},{10,9... | collective-permute-start | bytes 737288 | tf_op jit(solution)/shard_map/ppermute | solution.py:205
  92.5 0.0 collective-permute-done.13
  92.5 1.9 %collective-permute-start.14 = (f32[160,384]{1,0:T(8,128)S(1)}, f32[160,384]{1,0:T(8,128)S(1)}, u32[]{:S(2)}, u32[]{:S(2)}) collective-permute-start(f32[160,384]{1,0:T(8,128)S(1)} %pad_add_fusion), channel_id=1, source_target_pairs={{0,1},{1,2},{2,3},{3,4},{4,5},{5,6},{6,7},{7,0},{8,9},{9,10},{10,1... | collective-permute-start | bytes 737288 | tf_op jit(solution)/shard_map/ppermute | solution.py:205
  94.5 2.2 %collective-permute-done.10 = f32[160,384]{1,0:T(8,128)S(1)} collective-permute-done((f32[160,384]{1,0:T(8,128)S(1)}, f32[160,384]{1,0:T(8,128)S(1)}, u32[]{:S(2)}, u32[]{:S(2)}) %collective-permute-start.10) | collective-permute-done | bytes 245792 | tf_op jit(solution)/shard_map/ppermute | solution.py:205
  96.7 5.6 %collective-permute-start.11 = (f32[160,384]{1,0:T(8,128)S(1)}, f32[160,384]{1,0:T(8,128)S(1)}, u32[]{:S(2)}, u32[]{:S(2)}) collective-permute-start(f32[160,384]{1,0:T(8,128)S(1)} %add.29), channel_id=1, source_target_pairs={{0,7},{1,0},{2,1},{3,2},{4,3},{5,4},{6,5},{7,6},{8,15},{9,8},{10,9... | collective-permute-start | bytes 737288 | tf_op jit(solution)/shard_map/ppermute | solution.py:205
  102.3 0.0 collective-permute-done.14
  102.3 1.9 %collective-permute-start.15 = (f32[160,384]{1,0:T(8,128)S(1)}, f32[160,384]{1,0:T(8,128)S(1)}, u32[]{:S(2)}, u32[]{:S(2)}) collective-permute-start(f32[160,384]{1,0:T(8,128)S(1)} %add.32), channel_id=1, source_target_pairs={{0,1},{1,2},{2,3},{3,4},{4,5},{5,6},{6,7},{7,0},{8,9},{9,10},{10,1... | collective-permute-start | bytes 737288 | tf_op jit(solution)/shard_map/ppermute | solution.py:205
  104.2 1.7 %collective-permute-done.11 = f32[160,384]{1,0:T(8,128)S(1)} collective-permute-done((f32[160,384]{1,0:T(8,128)S(1)}, f32[160,384]{1,0:T(8,128)S(1)}, u32[]{:S(2)}, u32[]{:S(2)}) %collective-permute-start.11) | collective-permute-done | bytes 245792 | tf_op jit(solution)/shard_map/ppermute | solution.py:205
  106.0 5.6 %collective-permute-start.12 = (f32[160,384]{1,0:T(8,128)S(1)}, f32[160,384]{1,0:T(8,128)S(1)}, u32[]{:S(2)}, u32[]{:S(2)}) collective-permute-start(f32[160,384]{1,0:T(8,128)S(1)} %add.30), channel_id=1, source_target_pairs={{0,7},{1,0},{2,1},{3,2},{4,3},{5,4},{6,5},{7,6},{8,15},{9,8},{10,9... | collective-permute-start | bytes 737288 | tf_op jit(solution)/shard_map/ppermute | solution.py:205
  111.6 0.0 collective-permute-done.15
  111.6 1.9 %collective-permute-start.16 = (f32[160,384]{1,0:T(8,128)S(1)}, f32[160,384]{1,0:T(8,128)S(1)}, u32[]{:S(2)}, u32[]{:S(2)}) collective-permute-start(f32[160,384]{1,0:T(8,128)S(1)} %add.33), channel_id=1, source_target_pairs={{0,1},{1,2},{2,3},{3,4},{4,5},{5,6},{6,7},{7,0},{8,9},{9,10},{10,1... | collective-permute-start | bytes 737288 | tf_op jit(solution)/shard_map/ppermute | solution.py:205
  113.6 1.7 %collective-permute-done.12 = f32[160,384]{1,0:T(8,128)S(1)} collective-permute-done((f32[160,384]{1,0:T(8,128)S(1)}, f32[160,384]{1,0:T(8,128)S(1)}, u32[]{:S(2)}, u32[]{:S(2)}) %collective-permute-start.12) | collective-permute-done | bytes 245792 | tf_op jit(solution)/shard_map/ppermute | solution.py:205
  115.3 5.7 %collective-permute-done.16 = f32[160,384]{1,0:T(8,128)S(1)} collective-permute-done((f32[160,384]{1,0:T(8,128)S(1)}, f32[160,384]{1,0:T(8,128)S(1)}, u32[]{:S(2)}, u32[]{:S(2)}) %collective-permute-start.16) | collective-permute-done | bytes 245792 | tf_op jit(solution)/shard_map/ppermute | solution.py:205
  120.9 0.7 add_convert_fusion
  (6 shorter events, 0.2 us)
Async XLA Ops:
  0.7 8.1 %copy-start.1 = (s32[5]{0:T(128)S(1)}, s32[5]{0:T(128)}, u32[]{:S(2)}) copy-start(s32[5]{0:T(128)} %stack.23.refs_0_) | copy-start | bytes 64
  5.4 3.4 %collective-permute-start = (f32[128,256]{1,0:T(8,128)}, f32[128,256]{1,0:T(8,128)S(1)}, u32[]{:S(2)}, u32[]{:S(2)}) collective-permute-start(f32[128,256]{1,0:T(8,128)} %get-tuple-element.30), channel_id=1, source_target_pairs={{0,16},{16,0},{1,17},{17,1},{2,18},{18,2},{3,19},{19,3},{4,20},{20... | collective-permute-start | bytes 393224 | tf_op jit(solution)/shard_map/ppermute | solution.py:200
  8.8 0.9 copy-start.4
  9.7 5.3 %copy-start = (bf16[256,6144]{1,0:T(8,128)(2,1)S(1)}, bf16[256,6144]{1,0:T(8,128)(2,1)}, u32[]{:S(2)}) copy-start(bf16[256,6144]{1,0:T(8,128)(2,1)} %refs_3_.5) | copy-start | bytes 9437188
  10.5 8.2 %collective-permute-start.1 = (f32[128,256]{1,0:T(8,128)S(1)}, f32[128,256]{1,0:T(8,128)S(1)}, u32[]{:S(2)}, u32[]{:S(2)}) collective-permute-start(f32[128,256]{1,0:T(8,128)S(1)} %shard_map.65.later_ref.refs_1_), channel_id=1, source_target_pairs={{0,32},{32,0},{64,96},{96,64},{128,160},{160,128},{192,224},{224,1... | collective-permute-start | bytes 393224 | tf_op jit(solution)/shard_map/ppermute | solution.py:223
  19.6 12.2 %collective-permute-start.2 = (f32[128,256]{1,0:T(8,128)S(1)}, f32[128,256]{1,0:T(8,128)S(1)}, u32[]{:S(2)}, u32[]{:S(2)}) collective-permute-start(f32[128,256]{1,0:T(8,128)S(1)} %get-tuple-element.32.refs_1_), channel_id=1, source_target_pairs={{0,64},{32,96},{64,0},{96,32},{128,192},{160,224},{192,128},{224,1... | collective-permute-start | bytes 393224 | tf_op jit(solution)/shard_map/ppermute | solution.py:223
  25.7 52.0 %collective-permute-start.7 = (f32[128,3072]{1,0:T(8,128)S(1)}, f32[128,3072]{1,0:T(8,128)S(1)}, u32[]{:S(2)}, u32[]{:S(2)}) collective-permute-start(f32[128,3072]{1,0:T(8,128)S(1)} %get-tuple-element.31.refs_3_), channel_id=1, source_target_pairs={{0,8},{8,0},{1,9},{9,1},{2,10},{10,2},{3,11},{11,3},{4,12},{12,4},... | collective-permute-start | bytes 4718600 | tf_op jit(solution)/shard_map/ppermute | solution.py:200
  28.8 48.9 %collective-permute-start.8 = (f32[128,3072]{1,0:T(8,128)S(1)}, f32[128,3072]{1,0:T(8,128)S(1)}, u32[]{:S(2)}, u32[]{:S(2)}) collective-permute-start(f32[128,3072]{1,0:T(8,128)S(1)} %get-tuple-element.43), channel_id=1, source_target_pairs={{0,264},{8,256},{256,8},{264,0},{1,265},{9,257},{257,9},{265,1},{2... | collective-permute-start | bytes 4718600 | tf_op jit(solution)/shard_map/ppermute | solution.py:200
  31.8 13.2 %copy-start.2 = (f32[2,128,128]{2,1,0:T(8,128)S(1)}, f32[2,128,128]{2,1,0:T(8,128)}, u32[]{:S(2)}) copy-start(f32[2,128,128]{2,1,0:T(8,128)} %refs_4_.5) | copy-start | bytes 393220
  32.7 12.3 %collective-permute-start.3 = (f32[128,256]{1,0:T(8,128)S(1)}, f32[128,256]{1,0:T(8,128)S(1)}, u32[]{:S(2)}, u32[]{:S(2)}) collective-permute-start(f32[128,256]{1,0:T(8,128)S(1)} %get-tuple-element.34.refs_1_), channel_id=1, source_target_pairs={{0,224},{32,192},{64,160},{96,128},{128,96},{160,64},{192,32},{224... | collective-permute-start | bytes 393224 | tf_op jit(solution)/shard_map/ppermute | solution.py:223
  45.0 2.4 %copy-start.5 = (f32[128,256]{1,0:T(8,128)S(1)}, f32[128,256]{1,0:T(8,128)}, u32[]{:S(2)}) copy-start(f32[128,256]{1,0:T(8,128)} %get-tuple-element.29.refs_1_.refs_2_) | copy-start | bytes 393220
  46.1 18.6 %collective-permute-start.4 = (f32[128,128]{1,0:T(8,128)S(1)}, f32[128,128]{1,0:T(8,128)S(1)}, u32[]{:S(2)}, u32[]{:S(2)}) collective-permute-start(f32[128,128]{1,0:T(8,128)S(1)} %get-tuple-element.39), channel_id=1, source_target_pairs={{0,256},{1,257},{2,258},{3,259},{4,260},{5,261},{6,262},{7,263},{8... | collective-permute-start | bytes 196616 | tf_op jit(solution)/shard_map/ppermute | solution.py:247
  64.7 4.0 %copy-start.3 = (f32[160,512]{1,0:T(8,128)S(1)}, f32[160,512]{1,0:T(8,128)}, u32[]{:S(2)}) copy-start(f32[160,512]{1,0:T(8,128)} %get-tuple-element.42.refs_3_) | copy-start | bytes 983044
  65.5 3.1 %collective-permute-start.5 = (f32[128,128]{1,0:T(8,128)S(1)}, f32[128,128]{1,0:T(8,128)S(1)}, u32[]{:S(2)}, u32[]{:S(2)}) collective-permute-start(f32[128,128]{1,0:T(8,128)S(1)} %get-tuple-element.41), channel_id=1, source_target_pairs={{0,16},{16,0},{1,17},{17,1},{2,18},{18,2},{3,19},{19,3},{4,20},{20... | collective-permute-start | bytes 196616 | tf_op jit(solution)/shard_map/ppermute | solution.py:200
  69.5 8.2 %collective-permute-start.6 = (f32[160,256]{1,0:T(8,128)S(1)}, f32[160,256]{1,0:T(8,128)S(1)}, u32[]{:S(2)}, u32[]{:S(2)}) collective-permute-start(f32[160,256]{1,0:T(8,128)S(1)} %shard_map.72.refs_1_), channel_id=1, source_target_pairs={{0,8},{8,0},{1,9},{9,1},{2,10},{10,2},{3,11},{11,3},{4,12},{12,4},... | collective-permute-start | bytes 491528 | tf_op jit(solution)/shard_map/ppermute | solution.py:200
  78.5 8.8 %collective-permute-start.9 = (f32[80,384]{1,0:T(8,128)S(1)}, f32[80,384]{1,0:T(8,128)S(1)}, u32[]{:S(2)}, u32[]{:S(2)}) collective-permute-start(f32[80,384]{1,0:T(8,128)S(1)} %get-tuple-element.44.refs_6_), channel_id=1, source_target_pairs={{0,7},{1,0},{2,1},{3,2},{4,3},{5,4},{6,5},{7,6},{8,15},{9,8},{10,9... | collective-permute-start | bytes 368648 | tf_op jit(solution)/shard_map/ppermute | solution.py:205
  83.9 8.6 %collective-permute-start.13 = (f32[80,384]{1,0:T(8,128)S(1)}, f32[80,384]{1,0:T(8,128)S(1)}, u32[]{:S(2)}, u32[]{:S(2)}) collective-permute-start(f32[80,384]{1,0:T(8,128)S(1)} %get-tuple-element.49), channel_id=1, source_target_pairs={{0,1},{1,2},{2,3},{3,4},{4,5},{5,6},{6,7},{7,0},{8,9},{9,10},{10,1... | collective-permute-start | bytes 368648 | tf_op jit(solution)/shard_map/ppermute | solution.py:205
  87.3 9.3 %collective-permute-start.10 = (f32[160,384]{1,0:T(8,128)S(1)}, f32[160,384]{1,0:T(8,128)S(1)}, u32[]{:S(2)}, u32[]{:S(2)}) collective-permute-start(f32[160,384]{1,0:T(8,128)S(1)} %pad_add_fusion.1), channel_id=1, source_target_pairs={{0,7},{1,0},{2,1},{3,2},{4,3},{5,4},{6,5},{7,6},{8,15},{9,8},{10,9... | collective-permute-start | bytes 737288 | tf_op jit(solution)/shard_map/ppermute | solution.py:205
  92.5 9.7 %collective-permute-start.14 = (f32[160,384]{1,0:T(8,128)S(1)}, f32[160,384]{1,0:T(8,128)S(1)}, u32[]{:S(2)}, u32[]{:S(2)}) collective-permute-start(f32[160,384]{1,0:T(8,128)S(1)} %pad_add_fusion), channel_id=1, source_target_pairs={{0,1},{1,2},{2,3},{3,4},{4,5},{5,6},{6,7},{7,0},{8,9},{9,10},{10,1... | collective-permute-start | bytes 737288 | tf_op jit(solution)/shard_map/ppermute | solution.py:205
  96.7 9.3 %collective-permute-start.11 = (f32[160,384]{1,0:T(8,128)S(1)}, f32[160,384]{1,0:T(8,128)S(1)}, u32[]{:S(2)}, u32[]{:S(2)}) collective-permute-start(f32[160,384]{1,0:T(8,128)S(1)} %add.29), channel_id=1, source_target_pairs={{0,7},{1,0},{2,1},{3,2},{4,3},{5,4},{6,5},{7,6},{8,15},{9,8},{10,9... | collective-permute-start | bytes 737288 | tf_op jit(solution)/shard_map/ppermute | solution.py:205
  102.3 9.3 %collective-permute-start.15 = (f32[160,384]{1,0:T(8,128)S(1)}, f32[160,384]{1,0:T(8,128)S(1)}, u32[]{:S(2)}, u32[]{:S(2)}) collective-permute-start(f32[160,384]{1,0:T(8,128)S(1)} %add.32), channel_id=1, source_target_pairs={{0,1},{1,2},{2,3},{3,4},{4,5},{5,6},{6,7},{7,0},{8,9},{9,10},{10,1... | collective-permute-start | bytes 737288 | tf_op jit(solution)/shard_map/ppermute | solution.py:205
  106.0 9.3 %collective-permute-start.12 = (f32[160,384]{1,0:T(8,128)S(1)}, f32[160,384]{1,0:T(8,128)S(1)}, u32[]{:S(2)}, u32[]{:S(2)}) collective-permute-start(f32[160,384]{1,0:T(8,128)S(1)} %add.30), channel_id=1, source_target_pairs={{0,7},{1,0},{2,1},{3,2},{4,3},{5,4},{6,5},{7,6},{8,15},{9,8},{10,9... | collective-permute-start | bytes 737288 | tf_op jit(solution)/shard_map/ppermute | solution.py:205
  111.6 9.3 %collective-permute-start.16 = (f32[160,384]{1,0:T(8,128)S(1)}, f32[160,384]{1,0:T(8,128)S(1)}, u32[]{:S(2)}, u32[]{:S(2)}) collective-permute-start(f32[160,384]{1,0:T(8,128)S(1)} %add.33), channel_id=1, source_target_pairs={{0,1},{1,2},{2,3},{3,4},{4,5},{5,6},{6,7},{7,0},{8,9},{9,10},{10,1... | collective-permute-start | bytes 737288 | tf_op jit(solution)/shard_map/ppermute | solution.py:205

commit v3 on v2

--- a/solution.py
+++ b/solution.py
@@ -26,9 +26,9 @@
     return lax.dot_general(a, b, (contract, ((), ())), preferred_element_type=f32)
 
 
-def call(kernel, out_shapes, at, *args, later=(), scratch=(), limit=4, us=1.0):
+def call(kernel, out_shapes, place, *args, later=(), scratch=(), limit=4, us=1.0, space=VM):
     outs = [jax.ShapeDtypeStruct(s, d) for s, d in out_shapes]
-    n = 1 + len(args)
+    n = len(place) + len(args)
 
     def body(*refs):
         kernel(*refs[:n], *refs[n + len(later) :])
@@ -36,16 +36,12 @@
     return pl.pallas_call(
         body,
         out_shape=outs,
-        in_specs=[SM] + [VM] * len(args) + [pl.BlockSpec(memory_space=pl.ANY)] * len(later),
+        in_specs=[SM] * len(place) + [space] * len(args) + [pl.BlockSpec(memory_space=pl.ANY)] * len(later),
         out_specs=[VM] * len(outs),
         scratch_shapes=list(scratch),
         compiler_params=pltpu.CompilerParams(vmem_limit_bytes=limit * MIB),
         cost_estimate=pl.CostEstimate(flops=int(us * 1e9), bytes_accessed=1 << 17, transcendentals=0),
-    )(at, *args, *later)
-
-
-def place(at_ref):
-    return at_ref[0], at_ref[1], at_ref[2]
+    )(*place, *args, *later)
 
 
 def left_half(shape):
@@ -65,15 +61,24 @@
     return exact(pair[:, :HW], state) + pair[:, HW:]
 
 
-def shard_maps(at_ref, q_ref, k_ref, v_ref, r_ref, keep_ref, send_ref, rows_ref, x_ref):
+def shard_maps(core_ref, q_hbm, k_hbm, v_hbm, r_hbm, keep_ref, send_ref, rows_ref, *scratch):
+    q_ref, k_ref, v_ref, r_ref, x_ref, *done = scratch
+    copies = [
+        pltpu.make_async_copy(source, target, semaphore)
+        for source, target, semaphore in zip((q_hbm, k_hbm, v_hbm, r_hbm), scratch, done)
+    ]
+    for copy in copies:
+        copy.start()
     rows = q_ref.shape[0]
-    _, _, core = place(at_ref)
+    core = core_ref[0]
     s_at = lax.broadcasted_iota(jnp.int32, (rows, rows), 0)
     t_at = lax.broadcasted_iota(jnp.int32, (rows, rows), 1)
     earlier_block = (t_at // MB) < (s_at // MB)
     causal = t_at <= s_at
     diagonal = t_at == s_at
     mix, key_gram, columns = [], [], []
+    for copy in copies:
+        copy.wait()
     for h in range(2):
         at = slice(h * HW, (h + 1) * HW)
         q, k, v = q_ref[:, at], k_ref[:, at], v_ref[:, at]
@@ -101,23 +106,23 @@
     send_ref[...] = jnp.where(first, maps[1], maps[0])
 
 
-def chip_map(at_ref, keep_ref, got_ref, out_ref):
-    first = place(at_ref)[2] == 0
+def chip_map(core_ref, keep_ref, got_ref, out_ref):
+    first = core_ref[0] == 0
     early = jnp.where(first, keep_ref[...], got_ref[...])
     late = jnp.where(first, got_ref[...], keep_ref[...])
     out_ref[...] = after(late, early)
 
 
-def join_chips(at_ref, own_ref, got_ref, both_ref, pre_ref):
-    upper = lax.rem(place(at_ref)[0], 2) == 1
+def join_chips(z_ref, own_ref, got_ref, both_ref, pre_ref):
+    upper = lax.rem(z_ref[0], 2) == 1
     low = jnp.where(upper, got_ref[...], own_ref[...])
     high = jnp.where(upper, own_ref[...], got_ref[...])
     both_ref[...] = after(high, low)
     pre_ref[...] = jnp.where(upper, low, identity(2 * HW))
 
 
-def join_pairs(at_ref, own_ref, got_ref, pre_in_ref, both_ref, pre_ref):
-    upper = lax.rem(place(at_ref)[0], 4) >= 2
+def join_pairs(z_ref, own_ref, got_ref, pre_in_ref, both_ref, pre_ref):
+    upper = lax.rem(z_ref[0], 4) >= 2
     low = jnp.where(upper, got_ref[...], own_ref[...])
     high = jnp.where(upper, own_ref[...], got_ref[...])
     both_ref[...] = after(high, low)
@@ -125,33 +130,31 @@
     pre_ref[...] = jnp.where(upper, after(pre, low), pre)
 
 
-def join_ring(at_ref, own_ref, got_ref, pre_in_ref, first_ref, end_ref, pre_ref):
-    z, _, core = place(at_ref)
-    upper = z >= 4
+def join_ring(z_ref, core_ref, own_ref, got_ref, pre_in_ref, first_ref, end_ref, pre_ref):
+    upper = z_ref[0] >= 4
     low = jnp.where(upper, got_ref[...], own_ref[...])
     high = jnp.where(upper, own_ref[...], got_ref[...])
-    end_ref[...] = applied(high, applied(low, first_ref[core]))
+    end_ref[...] = applied(high, applied(low, first_ref[core_ref[0]]))
     pre = pre_in_ref[...]
     pre_ref[...] = jnp.where(upper, after(pre, low), pre)
 
 
-def shard_prefixes(at_ref, pre_ref, keep_ref, got_ref, mine_ref, other_ref):
-    first = place(at_ref)[2] == 0
+def shard_prefixes(core_ref, pre_ref, keep_ref, got_ref, mine_ref, other_ref):
+    first = core_ref[0] == 0
     pre = pre_ref[...]
     middle = after(jnp.where(first, keep_ref[...], got_ref[...]), pre)
     mine_ref[...] = jnp.where(first, pre, middle)
     other_ref[...] = jnp.where(first, middle, pre)
 
 
-def shard_states(at_ref, mine_ref, other_ref, arrived_ref, first_ref, keep_ref, send_ref):
-    _, x_hi, core = place(at_ref)
-    state = jnp.where(x_hi == 0, first_ref[core], arrived_ref[...])
+def shard_states(x_hi_ref, core_ref, mine_ref, other_ref, arrived_ref, first_ref, keep_ref, send_ref):
+    state = jnp.where(x_hi_ref[0] == 0, first_ref[core_ref[0]], arrived_ref[...])
     send_ref[...] = applied(other_ref[...], state)
     keep_ref[...] = applied(mine_ref[...], state)
 
 
-def outputs(at_ref, keep_ref, got_ref, rows_ref, z_ref):
-    core = place(at_ref)[2]
+def outputs(core_ref, keep_ref, got_ref, rows_ref, z_ref):
+    core = core_ref[0]
     for h in range(2):
         state = jnp.where(core == h, keep_ref[...], got_ref[...])
         at = slice(h * HW, (h + 1) * HW)
@@ -177,9 +180,9 @@
     )
 
 
-def farthest(at_ref, z_ref, zx_ref, w_ref, near_ref, far_ref, low_ref, high_ref):
+def farthest(x_lo_ref, y_ref, z_ref, zx_ref, w_ref, near_ref, far_ref, low_ref, high_ref):
     half = low_ref.shape[0]
-    to = (at_ref[3], lax.rem(at_ref[4] + 4, SIZES[4]))
+    to = (x_lo_ref[0], lax.rem(y_ref[0] + 4, SIZES[4]))
     out = piece(z_ref[...].astype(bf16), zx_ref[...].astype(bf16), to, w_ref, near_ref, far_ref)
     low_ref[...] = out[:half]
     high_ref[...] = out[half:]
@@ -188,10 +191,10 @@
 OFFSETS = (-3, 3, -2, 2, -1, 1, 0)
 
 
-def nearer(at_ref, z_ref, zx_ref, w_ref, near_ref, far_ref, *out_refs):
+def nearer(x_lo_ref, y_ref, z_ref, zx_ref, w_ref, near_ref, far_ref, *out_refs):
     z, zx = z_ref[...].astype(bf16), zx_ref[...].astype(bf16)
     for offset, out_ref in zip(OFFSETS, out_refs):
-        to = (at_ref[3], lax.rem(at_ref[4] + (offset + SIZES[4]), SIZES[4]))
+        to = (x_lo_ref[0], lax.rem(y_ref[0] + (offset + SIZES[4]), SIZES[4]))
         out_ref[...] = piece(z, zx, to, w_ref, near_ref, far_ref)
 
 
@@ -207,22 +210,25 @@
 
 def local(queries, keys, values, rates, init_weight, out_weight):
     rows = queries.shape[0]
-    x_hi, z, core, x_lo, y = (lax.axis_index(a) for a in (XH, Z, CORE, XL, Y))
-    at = jnp.stack([z, x_hi, core, x_lo, y]).astype(jnp.int32)
+    x_hi, z, core, x_lo, y = (lax.axis_index(a).reshape(1) for a in (XH, Z, CORE, XL, Y))
     columns = out_weight.shape[1] // SIZES[3]
     chunk = columns // SIZES[4]
     square, wide, out_piece = ((HW, HW), f32), ((HW, 2 * HW), f32), ((rows, chunk), f32)
 
     keep, send, own_rows = call(
-        shard_maps, [wide, wide, ((rows, 4 * HW), f32)], at, queries, keys, values, rates,
-        scratch=[pltpu.VMEM((2, rows, 2 * HW), f32)], limit=56, us=3,
+        shard_maps, [wide, wide, ((rows, 4 * HW), f32)], [core],
+        *(pltpu.with_memory_space_constraint(x, pltpu.HBM) for x in (queries, keys, values, rates)),
+        scratch=[pltpu.VMEM((rows, 2 * HW), bf16)] * 3
+        + [pltpu.VMEM((2, rows), f32), pltpu.VMEM((2, rows, 2 * HW), f32)]
+        + [pltpu.SemaphoreType.DMA] * 4,
+        space=pl.BlockSpec(memory_space=pltpu.HBM), limit=8, us=3,
     )
     got = swapped(send, (CORE,))
 
     def across_z(x, to):
         return lax.ppermute(x, Z, [(i, to(i)) for i in range(SIZES[1])])
 
-    (chip,) = call(chip_map, [wide], at, keep, got)
+    (chip,) = call(chip_map, [wide], [core], keep, got)
     parts = 4
     near_out, far_out = pl.pallas_call(
         pair_weights,
@@ -237,23 +243,23 @@
         ),
         out_shape=[jax.ShapeDtypeStruct((HW, columns), f32)] * 2,
         compiler_params=pltpu.CompilerParams(vmem_limit_bytes=6 * MIB),
-    )((1 - x_lo).reshape(1).astype(jnp.int32), out_weight, chip)
+    )(1 - x_lo, out_weight, chip)
     near = swapped(near_out, (XL,))
     far = swapped(far_out, (XH, XL))
 
-    both, pre = call(join_chips, [wide, wide], at, chip, across_z(chip, lambda i: i ^ 1), later=[near_out], us=3)
-    four, pre = call(join_pairs, [wide, wide], at, both, across_z(both, lambda i: i ^ 2), pre, us=3)
-    end, pre = call(join_ring, [square, wide], at, four, across_z(four, lambda i: 7 - i), pre, init_weight, us=3)
+    both, pre = call(join_chips, [wide, wide], [z], chip, across_z(chip, lambda i: i ^ 1), later=[near_out], us=2)
+    four, pre = call(join_pairs, [wide, wide], [z], both, across_z(both, lambda i: i ^ 2), pre, us=2)
+    end, pre = call(join_ring, [square, wide], [z, core], four, across_z(four, lambda i: 7 - i), pre, init_weight, us=2)
     arrived = lax.ppermute(end, XH, [(0, 1)])
-    mine, other = call(shard_prefixes, [wide, wide], at, pre, keep, got, us=3)
-    kept, leaving = call(shard_states, [square, square], at, mine, other, arrived, init_weight, us=3)
-    (z_rows,) = call(outputs, [((rows, 2 * HW), f32)], at, kept, swapped(leaving, (CORE,)), own_rows)
+    mine, other = call(shard_prefixes, [wide, wide], [core], pre, keep, got, us=2)
+    kept, leaving = call(shard_states, [square, square], [x_hi, core], mine, other, arrived, init_weight, us=2)
+    (z_rows,) = call(outputs, [((rows, 2 * HW), f32)], [core], kept, swapped(leaving, (CORE,)), own_rows)
     z_pair = swapped(z_rows, (XL,))
 
     factors = (z_rows, z_pair, out_weight, near, far)
-    low, high = call(farthest, [((rows // 2, chunk), f32)] * 2, at, *factors, limit=16)
+    low, high = call(farthest, [((rows // 2, chunk), f32)] * 2, [x_lo, y], *factors, limit=16)
     down, up = passed(low, Y, -1), passed(high, Y, 1)
-    pieces = call(nearer, [out_piece] * len(OFFSETS), at, *factors, later=[low], limit=16)
+    pieces = call(nearer, [out_piece] * len(OFFSETS), [x_lo, y], *factors, later=[low], limit=16)
     down = pieces[0] + jnp.concatenate([down, jnp.zeros_like(down)], axis=0)
     up = pieces[1] + jnp.concatenate([jnp.zeros_like(up), up], axis=0)
     for i in (2, 4):

time: 122 us -> 117 us (0.959)
  the two profiles are of different devices: /device:TPU:4 before, /device:TPU:6 now
where the time goes in v3:
time: 117 us
  starting transfers between devices  57.7 us (49%)
  waiting for transfers between devices  41.8 us (36%)
  Pallas kernels  14.4 us (12%)
  local copies, waits for them, and re-layouts  1.56 us (1%)
    ppermute x8, starting transfers between devices, passed(): return lax.ppermute(x, axis, [(i, (i + by) % n) for i in range(n)])  28.6 us
    ppermute x3, starting transfers between devices, across_z(): return lax.ppermute(x, Z, [(i, to(i)) for i in range(SIZES[1])])  14.8 us
    ppermute x5, starting transfers between devices, swapped(): return lax.ppermute(x, axes, [(i, n - 1 - i) for i in range(n)])  13.1 us
    pallas_call x10, Pallas kernels, call(): pl.pallas_call(body, out_shape=outs, in_specs=[SM] * len(place) + [space]...  12.1 us
    ppermute x3, waiting for transfers between devices, across_z(): return lax.ppermute(x, Z, [(i, to(i)) for i in range(SIZES[1])])  11.4 us
    ppermute x8, waiting for transfers between devices, passed(): return lax.ppermute(x, axis, [(i, (i + by) % n) for i in range(n)])  11.3 us
    ppermute x1, waiting for transfers between devices, local(): arrived = lax.ppermute(end, XH, [(0, 1)])  10.3 us
    ppermute x5, waiting for transfers between devices, swapped(): return lax.ppermute(x, axes, [(i, n - 1 - i) for i in range(n)])  8.77 us
  transfers between devices with their start and end apart: 17, of which 10 were waited for; matrix products, arithmetic and copies ran while one was open for 0% of the time, Pallas kernels for 7%

profile of v3, /device:TPU:6, one launch (start us, length us, event | category | flops | bytes accessed | tf_op | source)
XLA Modules:
  0.0 116.7 jit_solution(13757478289856117691)
XLA Ops:
  0.0 3.9 %shard_map.64 = (f32[128,256]{1,0:T(8,128)S(1)}, f32[128,256]{1,0:T(8,128)S(1)}, f32[160,512]{1,0:T(8,128)S(1)}) custom-call(s32[1]{0:T(128)} %bitcast.2.refs_0_.refs_1_, bf16[160,256]{1,0:T(8,128)(2,1)} %refs_1_.1, bf16[160,256]{1,0:T(8,128)(2,1)} %refs_2_.1, bf16[160,256]{1,0:T(8,128)(2,1)} %refs_3_.1, f32[2,160]{1,0:T(2,128)} %refs_4_.3), custom_call_target="tpu_custom_call" | custom-call | flops 3000000000 | bytes 131072 | tf_op jit(solution)/shard_map/pallas_call | solution.py:36
  3.9 0.0 copy-start.2
  3.9 0.0 copy-start.4
  3.9 1.9 %collective-permute-start = (f32[128,256]{1,0:T(8,128)S(1)}, f32[128,256]{1,0:T(8,128)S(1)}, u32[]{:S(2)}, u32[]{:S(2)}) collective-permute-start(f32[128,256]{1,0:T(8,128)S(1)} %get-tuple-element.30), channel_id=1, source_target_pairs={{0,16},{16,0},{1,17},{17,1},{2,18},{18,2},{3,19},{19,3},{4,20},{20... | collective-permute-start | bytes 393224 | tf_op jit(solution)/shard_map/ppermute | solution.py:203
  5.8 1.3 %collective-permute-done.refs_2_.refs_3_ = f32[128,256]{1,0:T(8,128)S(1)} collective-permute-done((f32[128,256]{1,0:T(8,128)S(1)}, f32[128,256]{1,0:T(8,128)S(1)}, u32[]{:S(2)}, u32[]{:S(2)}) %collective-permute-start) | collective-permute-done | bytes 131104 | tf_op jit(solution)/shard_map/ppermute | solution.py:203
  7.2 0.0 copy-start
  7.2 0.3 shard_map.65.later_ref.refs_1_
  7.4 0.0 copy-done.2
  7.5 0.0 copy-done.4
  7.5 4.4 %collective-permute-start.1 = (f32[128,256]{1,0:T(8,128)S(1)}, f32[128,256]{1,0:T(8,128)S(1)}, u32[]{:S(2)}, u32[]{:S(2)}) collective-permute-start(f32[128,256]{1,0:T(8,128)S(1)} %shard_map.65.later_ref.refs_1_), channel_id=1, source_target_pairs={{0,32},{32,0},{64,96},{96,64},{128,160},{160,128},{192,224},{224,1... | collective-permute-start | bytes 393224 | tf_op jit(solution)/shard_map/ppermute | solution.py:229
  11.9 0.0 copy-done
  11.9 2.3 %shard_map.66 = (f32[128,3072]{1,0:T(8,128)}, f32[128,3072]{1,0:T(8,128)}) custom-call(s32[1]{0:T(128)S(6)} %sub.3.to_ref, bf16[256,6144]{1,0:T(8,128)(2,1)S(1)} %copy-done, f32[128,256]{1,0:T(8,128)S(1)} %shard_map.65.later_ref.refs_1_), custom_call_target="tpu_custom_call" | custom-call | tf_op jit(solution)/shard_map/pallas_call | solution.py:233
  14.2 5.4 %collective-permute-start.8 = (f32[128,3072]{1,0:T(8,128)}, f32[128,3072]{1,0:T(8,128)}, u32[]{:S(2)}, u32[]{:S(2)}) collective-permute-start(f32[128,3072]{1,0:T(8,128)} %get-tuple-element.43), channel_id=1, source_target_pairs={{0,264},{8,256},{256,8},{264,0},{1,265},{9,257},{257,9},{265,1},{2... | collective-permute-start | bytes 4718600 | tf_op jit(solution)/shard_map/ppermute | solution.py:203
  19.6 1.9 %collective-permute-start.7 = (f32[128,3072]{1,0:T(8,128)}, f32[128,3072]{1,0:T(8,128)}, u32[]{:S(2)}, u32[]{:S(2)}) collective-permute-start(f32[128,3072]{1,0:T(8,128)} %get-tuple-element.31.refs_3_), channel_id=1, source_target_pairs={{0,8},{8,0},{1,9},{9,1},{2,10},{10,2},{3,11},{11,3},{4,12},{12,4},... | collective-permute-start | bytes 4718600 | tf_op jit(solution)/shard_map/ppermute | solution.py:203
  21.5 0.0 collective-permute-done.1.refs_2_
  21.5 0.3 shard_map.67
  21.8 4.0 %collective-permute-start.2 = (f32[128,256]{1,0:T(8,128)S(1)}, f32[128,256]{1,0:T(8,128)S(1)}, u32[]{:S(2)}, u32[]{:S(2)}) collective-permute-start(f32[128,256]{1,0:T(8,128)S(1)} %get-tuple-element.32.refs_1_), channel_id=1, source_target_pairs={{0,64},{32,96},{64,0},{96,32},{128,192},{160,224},{192,128},{224,1... | collective-permute-start | bytes 393224 | tf_op jit(solution)/shard_map/ppermute | solution.py:229
  25.7 6.9 %collective-permute-done.2.refs_2_ = f32[128,256]{1,0:T(8,128)S(1)} collective-permute-done((f32[128,256]{1,0:T(8,128)S(1)}, f32[128,256]{1,0:T(8,128)S(1)}, u32[]{:S(2)}, u32[]{:S(2)}) %collective-permute-start.2) | collective-permute-done | bytes 131104 | tf_op jit(solution)/shard_map/ppermute | solution.py:229
  32.7 0.0 copy-start.1
  32.7 0.4 shard_map.68
  33.1 0.0 copy-start.6
  33.1 0.6 copy-done.6
  33.7 6.4 %collective-permute-start.3 = (f32[128,256]{1,0:T(8,128)S(1)}, f32[128,256]{1,0:T(8,128)}, u32[]{:S(2)}, u32[]{:S(2)}) collective-permute-start(f32[128,256]{1,0:T(8,128)S(1)} %get-tuple-element.34.refs_2_), channel_id=1, source_target_pairs={{0,224},{32,192},{64,160},{96,128},{128,96},{160,64},{192,32},{224... | collective-permute-start | bytes 393224 | tf_op jit(solution)/shard_map/ppermute | solution.py:229
  40.1 4.5 %collective-permute-done.3.refs_3_ = f32[128,256]{1,0:T(8,128)} collective-permute-done((f32[128,256]{1,0:T(8,128)S(1)}, f32[128,256]{1,0:T(8,128)}, u32[]{:S(2)}, u32[]{:S(2)}) %collective-permute-start.3) | collective-permute-done | bytes 131104 | tf_op jit(solution)/shard_map/ppermute | solution.py:229
  44.6 0.0 copy-done.1
  44.7 0.0 copy-start.7
  44.7 0.9 copy-done.7
  45.6 0.0 copy-start.5
  45.6 1.5 %shard_map.69 = (f32[128,128]{1,0:T(8,128)S(1)}, f32[128,256]{1,0:T(8,128)S(1)}) custom-call(s32[1]{0:T(128)} %bitcast.4.refs_0_, s32[1]{0:T(128)} %bitcast.2.refs_0_.refs_1_, f32[128,256]{1,0:T(8,128)S(1)} %get-tuple-element.34.refs_2_, f32[128,256]{1,0:T(8,128)} %collective-permute-done.3.refs_3_, f32[128,256]{1,0:T(8,128)S(1)} %copy-done.7, ...), custom_call_target="tpu_custom_call" | custom-call | flops 2000000000 | bytes 131072 | tf_op jit(solution)/shard_map/pallas_call | solution.py:36
  47.1 1.3 %collective-permute-start.4 = (f32[128,128]{1,0:T(8,128)S(1)}, f32[128,128]{1,0:T(8,128)S(1)}, u32[]{:S(2)}, u32[]{:S(2)}) collective-permute-start(f32[128,128]{1,0:T(8,128)S(1)} %get-tuple-element.39), channel_id=1, source_target_pairs={{0,256},{1,257},{2,258},{3,259},{4,260},{5,261},{6,262},{7,263},{8... | collective-permute-start | bytes 196616 | tf_op jit(solution)/shard_map/ppermute | solution.py:253
  48.4 0.0 copy-done.5
  48.4 0.3 shard_map.70
  48.7 10.3 %collective-permute-done.4.refs_4_ = f32[128,128]{1,0:T(8,128)S(1)} collective-permute-done((f32[128,128]{1,0:T(8,128)S(1)}, f32[128,128]{1,0:T(8,128)S(1)}, u32[]{:S(2)}, u32[]{:S(2)}) %collective-permute-start.4) | collective-permute-done | bytes 65568 | tf_op jit(solution)/shard_map/ppermute | solution.py:253
  59.0 0.0 copy-start.3
  59.0 0.3 shard_map.71
  59.2 1.9 %collective-permute-start.5 = (f32[128,128]{1,0:T(8,128)S(1)}, f32[128,128]{1,0:T(8,128)S(1)}, u32[]{:S(2)}, u32[]{:S(2)}) collective-permute-start(f32[128,128]{1,0:T(8,128)S(1)} %get-tuple-element.41), channel_id=1, source_target_pairs={{0,16},{16,0},{1,17},{17,1},{2,18},{18,2},{3,19},{19,3},{4,20},{20... | collective-permute-start | bytes 196616 | tf_op jit(solution)/shard_map/ppermute | solution.py:203
  61.2 1.2 %collective-permute-done.5.refs_2_ = f32[128,128]{1,0:T(8,128)S(1)} collective-permute-done((f32[128,128]{1,0:T(8,128)S(1)}, f32[128,128]{1,0:T(8,128)S(1)}, u32[]{:S(2)}, u32[]{:S(2)}) %collective-permute-start.5) | collective-permute-done | bytes 65568 | tf_op jit(solution)/shard_map/ppermute | solution.py:203
  62.4 0.0 copy-done.3
  62.4 0.3 shard_map.72.refs_2_
  62.7 1.9 %collective-permute-start.6 = (f32[160,256]{1,0:T(8,128)S(1)}, f32[160,256]{1,0:T(8,128)S(1)}, u32[]{:S(2)}, u32[]{:S(2)}) collective-permute-start(f32[160,256]{1,0:T(8,128)S(1)} %shard_map.72.refs_2_), channel_id=1, source_target_pairs={{0,8},{8,0},{1,9},{9,1},{2,10},{10,2},{3,11},{11,3},{4,12},{12,4},... | collective-permute-start | bytes 491528 | tf_op jit(solution)/shard_map/ppermute | solution.py:203
  64.6 6.2 %collective-permute-done.6.refs_3_ = f32[160,256]{1,0:T(8,128)S(1)} collective-permute-done((f32[160,256]{1,0:T(8,128)S(1)}, f32[160,256]{1,0:T(8,128)S(1)}, u32[]{:S(2)}, u32[]{:S(2)}) %collective-permute-start.6) | collective-permute-done | bytes 163872 | tf_op jit(solution)/shard_map/ppermute | solution.py:203
  70.9 0.0 collective-permute-done.8.refs_6_
  70.9 0.0 collective-permute-done.7.refs_5_
  70.9 2.1 %shard_map.73 = (f32[80,384]{1,0:T(8,128)S(1)}, f32[80,384]{1,0:T(8,128)S(1)}) custom-call(s32[1]{0:T(128)} %bitcast.refs_0_, s32[1]{0:T(128)} %bitcast.1.refs_1_, f32[160,256]{1,0:T(8,128)S(1)} %shard_map.72.refs_2_, f32[160,256]{1,0:T(8,128)S(1)} %collective-permute-done.6.refs_3_, bf16[256,6144]{1,0:T(8,128)(2,1)S(1)} %copy-done, ...), custom_call_target="tpu_custom_call" | custom-call | flops 1000000000 | bytes 131072 | tf_op jit(solution)/shard_map/pallas_call | solution.py:36
  73.0 4.6 %collective-permute-start.9 = (f32[80,384]{1,0:T(8,128)S(1)}, f32[80,384]{1,0:T(8,128)S(1)}, u32[]{:S(2)}, u32[]{:S(2)}) collective-permute-start(f32[80,384]{1,0:T(8,128)S(1)} %get-tuple-element.44.refs_7_), channel_id=1, source_target_pairs={{0,7},{1,0},{2,1},{3,2},{4,3},{5,4},{6,5},{7,6},{8,15},{9,8},{10,9... | collective-permute-start | bytes 368648 | tf_op jit(solution)/shard_map/ppermute | solution.py:208
  77.6 1.9 %collective-permute-start.13 = (f32[80,384]{1,0:T(8,128)S(1)}, f32[80,384]{1,0:T(8,128)S(1)}, u32[]{:S(2)}, u32[]{:S(2)}) collective-permute-start(f32[80,384]{1,0:T(8,128)S(1)} %get-tuple-element.49), channel_id=1, source_target_pairs={{0,1},{1,2},{2,3},{3,4},{4,5},{5,6},{6,7},{7,0},{8,9},{9,10},{10,1... | collective-permute-start | bytes 368648 | tf_op jit(solution)/shard_map/ppermute | solution.py:208
  79.5 2.8 %shard_map.74 = (f32[160,384]{1,0:T(8,128)S(1)}, f32[160,384]{1,0:T(8,128)S(1)}, f32[160,384]{1,0:T(8,128)S(1)}, f32[160,384]{1,0:T(8,128)S(1)}, f32[160,384]{1,...) custom-call(s32[1]{0:T(128)} %bitcast.refs_0_, s32[1]{0:T(128)} %bitcast.1.refs_1_, ...), custom_call_target="tpu_custom_call" | custom-call | flops 1000000000 | bytes 131072 | tf_op jit(solution)/shard_map/pallas_call | solution.py:36
  82.3 0.0 collective-permute-done.9
  82.4 5.1 %collective-permute-start.10 = (f32[160,384]{1,0:T(8,128)S(1)}, f32[160,384]{1,0:T(8,128)S(1)}, u32[]{:S(2)}, u32[]{:S(2)}) collective-permute-start(f32[160,384]{1,0:T(8,128)S(1)} %pad_add_fusion.1), channel_id=1, source_target_pairs={{0,7},{1,0},{2,1},{3,2},{4,3},{5,4},{6,5},{7,6},{8,15},{9,8},{10,9... | collective-permute-start | bytes 737288 | tf_op jit(solution)/shard_map/ppermute | solution.py:208
  87.5 0.0 collective-permute-done.13
  87.6 1.9 %collective-permute-start.14 = (f32[160,384]{1,0:T(8,128)S(1)}, f32[160,384]{1,0:T(8,128)S(1)}, u32[]{:S(2)}, u32[]{:S(2)}) collective-permute-start(f32[160,384]{1,0:T(8,128)S(1)} %pad_add_fusion), channel_id=1, source_target_pairs={{0,1},{1,2},{2,3},{3,4},{4,5},{5,6},{6,7},{7,0},{8,9},{9,10},{10,1... | collective-permute-start | bytes 737288 | tf_op jit(solution)/shard_map/ppermute | solution.py:208
  89.5 2.2 %collective-permute-done.10 = f32[160,384]{1,0:T(8,128)S(1)} collective-permute-done((f32[160,384]{1,0:T(8,128)S(1)}, f32[160,384]{1,0:T(8,128)S(1)}, u32[]{:S(2)}, u32[]{:S(2)}) %collective-permute-start.10) | collective-permute-done | bytes 245792 | tf_op jit(solution)/shard_map/ppermute | solution.py:208
  91.7 5.6 %collective-permute-start.11 = (f32[160,384]{1,0:T(8,128)S(1)}, f32[160,384]{1,0:T(8,128)S(1)}, u32[]{:S(2)}, u32[]{:S(2)}) collective-permute-start(f32[160,384]{1,0:T(8,128)S(1)} %add.29), channel_id=1, source_target_pairs={{0,7},{1,0},{2,1},{3,2},{4,3},{5,4},{6,5},{7,6},{8,15},{9,8},{10,9... | collective-permute-start | bytes 737288 | tf_op jit(solution)/shard_map/ppermute | solution.py:208
  97.3 0.0 collective-permute-done.14
  97.3 1.9 %collective-permute-start.15 = (f32[160,384]{1,0:T(8,128)S(1)}, f32[160,384]{1,0:T(8,128)S(1)}, u32[]{:S(2)}, u32[]{:S(2)}) collective-permute-start(f32[160,384]{1,0:T(8,128)S(1)} %add.32), channel_id=1, source_target_pairs={{0,1},{1,2},{2,3},{3,4},{4,5},{5,6},{6,7},{7,0},{8,9},{9,10},{10,1... | collective-permute-start | bytes 737288 | tf_op jit(solution)/shard_map/ppermute | solution.py:208
  99.3 1.7 %collective-permute-done.11 = f32[160,384]{1,0:T(8,128)S(1)} collective-permute-done((f32[160,384]{1,0:T(8,128)S(1)}, f32[160,384]{1,0:T(8,128)S(1)}, u32[]{:S(2)}, u32[]{:S(2)}) %collective-permute-start.11) | collective-permute-done | bytes 245792 | tf_op jit(solution)/shard_map/ppermute | solution.py:208
  101.0 5.6 %collective-permute-start.12 = (f32[160,384]{1,0:T(8,128)S(1)}, f32[160,384]{1,0:T(8,128)S(1)}, u32[]{:S(2)}, u32[]{:S(2)}) collective-permute-start(f32[160,384]{1,0:T(8,128)S(1)} %add.30), channel_id=1, source_target_pairs={{0,7},{1,0},{2,1},{3,2},{4,3},{5,4},{6,5},{7,6},{8,15},{9,8},{10,9... | collective-permute-start | bytes 737288 | tf_op jit(solution)/shard_map/ppermute | solution.py:208
  106.6 0.0 collective-permute-done.15
  106.7 1.9 %collective-permute-start.16 = (f32[160,384]{1,0:T(8,128)S(1)}, f32[160,384]{1,0:T(8,128)S(1)}, u32[]{:S(2)}, u32[]{:S(2)}) collective-permute-start(f32[160,384]{1,0:T(8,128)S(1)} %add.33), channel_id=1, source_target_pairs={{0,1},{1,2},{2,3},{3,4},{4,5},{5,6},{6,7},{7,0},{8,9},{9,10},{10,1... | collective-permute-start | bytes 737288 | tf_op jit(solution)/shard_map/ppermute | solution.py:208
  108.6 1.7 %collective-permute-done.12 = f32[160,384]{1,0:T(8,128)S(1)} collective-permute-done((f32[160,384]{1,0:T(8,128)S(1)}, f32[160,384]{1,0:T(8,128)S(1)}, u32[]{:S(2)}, u32[]{:S(2)}) %collective-permute-start.12) | collective-permute-done | bytes 245792 | tf_op jit(solution)/shard_map/ppermute | solution.py:208
  110.3 5.7 %collective-permute-done.16 = f32[160,384]{1,0:T(8,128)S(1)} collective-permute-done((f32[160,384]{1,0:T(8,128)S(1)}, f32[160,384]{1,0:T(8,128)S(1)}, u32[]{:S(2)}, u32[]{:S(2)}) %collective-permute-start.16) | collective-permute-done | bytes 245792 | tf_op jit(solution)/shard_map/ppermute | solution.py:208
  116.0 0.7 add_convert_fusion
  (6 shorter events, 0.2 us)
Async XLA Ops:
  3.9 3.5 %copy-start.2 = (f32[160,512]{1,0:T(8,128)}, f32[160,512]{1,0:T(8,128)S(1)}, u32[]{:S(2)}) copy-start(f32[160,512]{1,0:T(8,128)S(1)} %get-tuple-element.42.refs_3_) | copy-start | bytes 983044
  3.9 3.5 %copy-start.4 = (f32[128,256]{1,0:T(8,128)}, f32[128,256]{1,0:T(8,128)S(1)}, u32[]{:S(2)}) copy-start(f32[128,256]{1,0:T(8,128)S(1)} %get-tuple-element.29.refs_1_.refs_2_) | copy-start | bytes 393220
  3.9 3.2 %collective-permute-start = (f32[128,256]{1,0:T(8,128)S(1)}, f32[128,256]{1,0:T(8,128)S(1)}, u32[]{:S(2)}, u32[]{:S(2)}) collective-permute-start(f32[128,256]{1,0:T(8,128)S(1)} %get-tuple-element.30), channel_id=1, source_target_pairs={{0,16},{16,0},{1,17},{17,1},{2,18},{18,2},{3,19},{19,3},{4,20},{20... | collective-permute-start | bytes 393224 | tf_op jit(solution)/shard_map/ppermute | solution.py:203
  7.2 4.7 %copy-start = (bf16[256,6144]{1,0:T(8,128)(2,1)S(1)}, bf16[256,6144]{1,0:T(8,128)(2,1)}, u32[]{:S(2)}) copy-start(bf16[256,6144]{1,0:T(8,128)(2,1)} %refs_4_.5) | copy-start | bytes 9437188
  7.5 14.0 %collective-permute-start.1 = (f32[128,256]{1,0:T(8,128)S(1)}, f32[128,256]{1,0:T(8,128)S(1)}, u32[]{:S(2)}, u32[]{:S(2)}) collective-permute-start(f32[128,256]{1,0:T(8,128)S(1)} %shard_map.65.later_ref.refs_1_), channel_id=1, source_target_pairs={{0,32},{32,0},{64,96},{96,64},{128,160},{160,128},{192,224},{224,1... | collective-permute-start | bytes 393224 | tf_op jit(solution)/shard_map/ppermute | solution.py:229
  14.2 56.7 %collective-permute-start.8 = (f32[128,3072]{1,0:T(8,128)}, f32[128,3072]{1,0:T(8,128)}, u32[]{:S(2)}, u32[]{:S(2)}) collective-permute-start(f32[128,3072]{1,0:T(8,128)} %get-tuple-element.43), channel_id=1, source_target_pairs={{0,264},{8,256},{256,8},{264,0},{1,265},{9,257},{257,9},{265,1},{2... | collective-permute-start | bytes 4718600 | tf_op jit(solution)/shard_map/ppermute | solution.py:203
  19.6 51.3 %collective-permute-start.7 = (f32[128,3072]{1,0:T(8,128)}, f32[128,3072]{1,0:T(8,128)}, u32[]{:S(2)}, u32[]{:S(2)}) collective-permute-start(f32[128,3072]{1,0:T(8,128)} %get-tuple-element.31.refs_3_), channel_id=1, source_target_pairs={{0,8},{8,0},{1,9},{9,1},{2,10},{10,2},{3,11},{11,3},{4,12},{12,4},... | collective-permute-start | bytes 4718600 | tf_op jit(solution)/shard_map/ppermute | solution.py:203
  21.8 10.9 %collective-permute-start.2 = (f32[128,256]{1,0:T(8,128)S(1)}, f32[128,256]{1,0:T(8,128)S(1)}, u32[]{:S(2)}, u32[]{:S(2)}) collective-permute-start(f32[128,256]{1,0:T(8,128)S(1)} %get-tuple-element.32.refs_1_), channel_id=1, source_target_pairs={{0,64},{32,96},{64,0},{96,32},{128,192},{160,224},{192,128},{224,1... | collective-permute-start | bytes 393224 | tf_op jit(solution)/shard_map/ppermute | solution.py:229
  32.7 12.0 %copy-start.1 = (f32[2,128,128]{2,1,0:T(8,128)S(1)}, f32[2,128,128]{2,1,0:T(8,128)}, u32[]{:S(2)}) copy-start(f32[2,128,128]{2,1,0:T(8,128)} %refs_5_.3) | copy-start | bytes 393220
  33.1 0.6 copy-start.6
  33.7 10.9 %collective-permute-start.3 = (f32[128,256]{1,0:T(8,128)S(1)}, f32[128,256]{1,0:T(8,128)}, u32[]{:S(2)}, u32[]{:S(2)}) collective-permute-start(f32[128,256]{1,0:T(8,128)S(1)} %get-tuple-element.34.refs_2_), channel_id=1, source_target_pairs={{0,224},{32,192},{64,160},{96,128},{128,96},{160,64},{192,32},{224... | collective-permute-start | bytes 393224 | tf_op jit(solution)/shard_map/ppermute | solution.py:229
  44.7 0.9 copy-start.7
  45.6 2.8 %copy-start.5 = (f32[128,256]{1,0:T(8,128)S(1)}, f32[128,256]{1,0:T(8,128)}, u32[]{:S(2)}) copy-start(f32[128,256]{1,0:T(8,128)} %copy-done.4) | copy-start | bytes 393220
  47.1 11.9 %collective-permute-start.4 = (f32[128,128]{1,0:T(8,128)S(1)}, f32[128,128]{1,0:T(8,128)S(1)}, u32[]{:S(2)}, u32[]{:S(2)}) collective-permute-start(f32[128,128]{1,0:T(8,128)S(1)} %get-tuple-element.39), channel_id=1, source_target_pairs={{0,256},{1,257},{2,258},{3,259},{4,260},{5,261},{6,262},{7,263},{8... | collective-permute-start | bytes 196616 | tf_op jit(solution)/shard_map/ppermute | solution.py:253
  59.0 3.4 %copy-start.3 = (f32[160,512]{1,0:T(8,128)S(1)}, f32[160,512]{1,0:T(8,128)}, u32[]{:S(2)}) copy-start(f32[160,512]{1,0:T(8,128)} %copy-done.2) | copy-start | bytes 983044
  59.2 3.1 %collective-permute-start.5 = (f32[128,128]{1,0:T(8,128)S(1)}, f32[128,128]{1,0:T(8,128)S(1)}, u32[]{:S(2)}, u32[]{:S(2)}) collective-permute-start(f32[128,128]{1,0:T(8,128)S(1)} %get-tuple-element.41), channel_id=1, source_target_pairs={{0,16},{16,0},{1,17},{17,1},{2,18},{18,2},{3,19},{19,3},{4,20},{20... | collective-permute-start | bytes 196616 | tf_op jit(solution)/shard_map/ppermute | solution.py:203
  62.7 8.2 %collective-permute-start.6 = (f32[160,256]{1,0:T(8,128)S(1)}, f32[160,256]{1,0:T(8,128)S(1)}, u32[]{:S(2)}, u32[]{:S(2)}) collective-permute-start(f32[160,256]{1,0:T(8,128)S(1)} %shard_map.72.refs_2_), channel_id=1, source_target_pairs={{0,8},{8,0},{1,9},{9,1},{2,10},{10,2},{3,11},{11,3},{4,12},{12,4},... | collective-permute-start | bytes 491528 | tf_op jit(solution)/shard_map/ppermute | solution.py:203
  73.0 9.3 %collective-permute-start.9 = (f32[80,384]{1,0:T(8,128)S(1)}, f32[80,384]{1,0:T(8,128)S(1)}, u32[]{:S(2)}, u32[]{:S(2)}) collective-permute-start(f32[80,384]{1,0:T(8,128)S(1)} %get-tuple-element.44.refs_7_), channel_id=1, source_target_pairs={{0,7},{1,0},{2,1},{3,2},{4,3},{5,4},{6,5},{7,6},{8,15},{9,8},{10,9... | collective-permute-start | bytes 368648 | tf_op jit(solution)/shard_map/ppermute | solution.py:208
  77.6 9.9 %collective-permute-start.13 = (f32[80,384]{1,0:T(8,128)S(1)}, f32[80,384]{1,0:T(8,128)S(1)}, u32[]{:S(2)}, u32[]{:S(2)}) collective-permute-start(f32[80,384]{1,0:T(8,128)S(1)} %get-tuple-element.49), channel_id=1, source_target_pairs={{0,1},{1,2},{2,3},{3,4},{4,5},{5,6},{6,7},{7,0},{8,9},{9,10},{10,1... | collective-permute-start | bytes 368648 | tf_op jit(solution)/shard_map/ppermute | solution.py:208
  82.4 9.3 %collective-permute-start.10 = (f32[160,384]{1,0:T(8,128)S(1)}, f32[160,384]{1,0:T(8,128)S(1)}, u32[]{:S(2)}, u32[]{:S(2)}) collective-permute-start(f32[160,384]{1,0:T(8,128)S(1)} %pad_add_fusion.1), channel_id=1, source_target_pairs={{0,7},{1,0},{2,1},{3,2},{4,3},{5,4},{6,5},{7,6},{8,15},{9,8},{10,9... | collective-permute-start | bytes 737288 | tf_op jit(solution)/shard_map/ppermute | solution.py:208
  87.6 9.7 %collective-permute-start.14 = (f32[160,384]{1,0:T(8,128)S(1)}, f32[160,384]{1,0:T(8,128)S(1)}, u32[]{:S(2)}, u32[]{:S(2)}) collective-permute-start(f32[160,384]{1,0:T(8,128)S(1)} %pad_add_fusion), channel_id=1, source_target_pairs={{0,1},{1,2},{2,3},{3,4},{4,5},{5,6},{6,7},{7,0},{8,9},{9,10},{10,1... | collective-permute-start | bytes 737288 | tf_op jit(solution)/shard_map/ppermute | solution.py:208
  91.7 9.3 %collective-permute-start.11 = (f32[160,384]{1,0:T(8,128)S(1)}, f32[160,384]{1,0:T(8,128)S(1)}, u32[]{:S(2)}, u32[]{:S(2)}) collective-permute-start(f32[160,384]{1,0:T(8,128)S(1)} %add.29), channel_id=1, source_target_pairs={{0,7},{1,0},{2,1},{3,2},{4,3},{5,4},{6,5},{7,6},{8,15},{9,8},{10,9... | collective-permute-start | bytes 737288 | tf_op jit(solution)/shard_map/ppermute | solution.py:208
  97.3 9.3 %collective-permute-start.15 = (f32[160,384]{1,0:T(8,128)S(1)}, f32[160,384]{1,0:T(8,128)S(1)}, u32[]{:S(2)}, u32[]{:S(2)}) collective-permute-start(f32[160,384]{1,0:T(8,128)S(1)} %add.32), channel_id=1, source_target_pairs={{0,1},{1,2},{2,3},{3,4},{4,5},{5,6},{6,7},{7,0},{8,9},{9,10},{10,1... | collective-permute-start | bytes 737288 | tf_op jit(solution)/shard_map/ppermute | solution.py:208
  101.0 9.3 %collective-permute-start.12 = (f32[160,384]{1,0:T(8,128)S(1)}, f32[160,384]{1,0:T(8,128)S(1)}, u32[]{:S(2)}, u32[]{:S(2)}) collective-permute-start(f32[160,384]{1,0:T(8,128)S(1)} %add.30), channel_id=1, source_target_pairs={{0,7},{1,0},{2,1},{3,2},{4,3},{5,4},{6,5},{7,6},{8,15},{9,8},{10,9... | collective-permute-start | bytes 737288 | tf_op jit(solution)/shard_map/ppermute | solution.py:208
  106.7 9.3 %collective-permute-start.16 = (f32[160,384]{1,0:T(8,128)S(1)}, f32[160,384]{1,0:T(8,128)S(1)}, u32[]{:S(2)}, u32[]{:S(2)}) collective-permute-start(f32[160,384]{1,0:T(8,128)S(1)} %add.33), channel_id=1, source_target_pairs={{0,1},{1,2},{2,3},{3,4},{4,5},{5,6},{6,7},{7,0},{8,9},{9,10},{10,1... | collective-permute-start | bytes 737288 | tf_op jit(solution)/shard_map/ppermute | solution.py:208

commit v4 on v3

--- a/solution.py
+++ b/solution.py
@@ -18,7 +18,7 @@
 
 def exact(a, b, contract=((1,), (0,))):
     return lax.dot_general(
-        a, b, (contract, ((), ())), precision=lax.Precision.HIGHEST, preferred_element_type=f32
+        a, b, (contract, ((), ())), precision=lax.Precision.HIGH, preferred_element_type=f32
     )
 
 
@@ -26,8 +26,8 @@
     return lax.dot_general(a, b, (contract, ((), ())), preferred_element_type=f32)
 
 
-def call(kernel, out_shapes, place, *args, later=(), scratch=(), limit=4, us=1.0, space=VM):
-    outs = [jax.ShapeDtypeStruct(s, d) for s, d in out_shapes]
+def call(kernel, out_shapes, place, *args, later=(), scratch=(), limit=4, us=1.0, space=pltpu.VMEM, pinned=False):
+    outs = [pltpu.VMEM(s, d) if pinned else jax.ShapeDtypeStruct(s, d) for s, d in out_shapes]
     n = len(place) + len(args)
 
     def body(*refs):
@@ -36,12 +36,12 @@
     return pl.pallas_call(
         body,
         out_shape=outs,
-        in_specs=[SM] * len(place) + [space] * len(args) + [pl.BlockSpec(memory_space=pl.ANY)] * len(later),
+        in_specs=[SM] * len(place) + [pl.BlockSpec(memory_space=space)] * len(args) + [pl.BlockSpec(memory_space=pl.ANY)] * len(later),
         out_specs=[VM] * len(outs),
         scratch_shapes=list(scratch),
         compiler_params=pltpu.CompilerParams(vmem_limit_bytes=limit * MIB),
         cost_estimate=pl.CostEstimate(flops=int(us * 1e9), bytes_accessed=1 << 17, transcendentals=0),
-    )(*place, *args, *later)
+    )(*place, *(pltpu.with_memory_space_constraint(x, space) for x in args), *later)
 
 
 def left_half(shape):
@@ -61,12 +61,13 @@
     return exact(pair[:, :HW], state) + pair[:, HW:]
 
 
-def shard_maps(core_ref, q_hbm, k_hbm, v_hbm, r_hbm, keep_ref, send_ref, rows_ref, *scratch):
+def shard_maps(core_ref, q_hbm, k_hbm, v_hbm, r_hbm, w_hbm, keep_ref, send_ref, rows_ref, first_ref, *scratch):
     q_ref, k_ref, v_ref, r_ref, x_ref, *done = scratch
     copies = [
         pltpu.make_async_copy(source, target, semaphore)
         for source, target, semaphore in zip((q_hbm, k_hbm, v_hbm, r_hbm), scratch, done)
     ]
+    copies.append(pltpu.make_async_copy(w_hbm.at[core_ref[0]], first_ref, done[4]))
     for copy in copies:
         copy.start()
     rows = q_ref.shape[0]
@@ -77,7 +78,7 @@
     causal = t_at <= s_at
     diagonal = t_at == s_at
     mix, key_gram, columns = [], [], []
-    for copy in copies:
+    for copy in copies[:4]:
         copy.wait()
     for h in range(2):
         at = slice(h * HW, (h + 1) * HW)
@@ -104,6 +105,7 @@
     first = core == 0
     keep_ref[...] = jnp.where(first, maps[0], maps[1])
     send_ref[...] = jnp.where(first, maps[1], maps[0])
+    copies[4].wait()
 
 
 def chip_map(core_ref, keep_ref, got_ref, out_ref):
@@ -130,11 +132,11 @@
     pre_ref[...] = jnp.where(upper, after(pre, low), pre)
 
 
-def join_ring(z_ref, core_ref, own_ref, got_ref, pre_in_ref, first_ref, end_ref, pre_ref):
+def join_ring(z_ref, own_ref, got_ref, pre_in_ref, first_ref, end_ref, pre_ref):
     upper = z_ref[0] >= 4
     low = jnp.where(upper, got_ref[...], own_ref[...])
     high = jnp.where(upper, own_ref[...], got_ref[...])
-    end_ref[...] = applied(high, applied(low, first_ref[core_ref[0]]))
+    end_ref[...] = applied(high, applied(low, first_ref[...]))
     pre = pre_in_ref[...]
     pre_ref[...] = jnp.where(upper, after(pre, low), pre)
 
@@ -147,8 +149,8 @@
     other_ref[...] = jnp.where(first, middle, pre)
 
 
-def shard_states(x_hi_ref, core_ref, mine_ref, other_ref, arrived_ref, first_ref, keep_ref, send_ref):
-    state = jnp.where(x_hi_ref[0] == 0, first_ref[core_ref[0]], arrived_ref[...])
+def shard_states(x_hi_ref, mine_ref, other_ref, arrived_ref, first_ref, keep_ref, send_ref):
+    state = jnp.where(x_hi_ref[0] == 0, first_ref[...], arrived_ref[...])
     send_ref[...] = applied(other_ref[...], state)
     keep_ref[...] = applied(mine_ref[...], state)
 
@@ -162,28 +164,33 @@
         z_ref[:, at] = z.astype(bf16).astype(f32)
 
 
-def pair_weights(to_ref, w_ref, later_ref, near_ref, far_ref):
+def pair_weights(to_ref, near_in, far_in, later_ref, near_ref, far_ref):
     del to_ref, later_ref
-    near_ref[...] = w_ref[:HW, :].astype(f32)
-    far_ref[...] = w_ref[HW:, :].astype(f32)
-
-
-def piece(z, z_pair, to, w_ref, near_ref, far_ref):
-    chunk = w_ref.shape[1] // (SIZES[3] * SIZES[4])
-    x_lo, y = to
-    at = pl.ds(pl.multiple_of(y * chunk, HW), chunk)
-    own_at = pl.ds(pl.multiple_of((x_lo * SIZES[4] + y) * chunk, HW), chunk)
-    return (
-        single(z, w_ref[:, own_at])
-        + single(z_pair[:, :HW], near_ref[:, at].astype(bf16))
-        + single(z_pair[:, HW:], far_ref[:, at].astype(bf16))
-    )
-
-
-def farthest(x_lo_ref, y_ref, z_ref, zx_ref, w_ref, near_ref, far_ref, low_ref, high_ref):
+    near_ref[...] = near_in[...].astype(f32)
+    far_ref[...] = far_in[...].astype(f32)
+
+
+def own_weights(to_ref, w_ref, later_ref, out_ref):
+    del to_ref, later_ref
+    out_ref[...] = w_ref[...]
+
+
+def piece(place, offset, z, z_pair, w_ref, *pair_refs):
+    core_ref, y_ref = place
+    chunk = w_ref.shape[1] // SIZES[4]
+    at = pl.ds(pl.multiple_of(lax.rem(y_ref[0] + (offset + SIZES[4]), SIZES[4]) * chunk, HW), chunk)
+    first = core_ref[0] == 0
+    parts = []
+    for mine, other in (pair_refs[:2], pair_refs[2:]):
+        a, b = mine[:, at], other[:, at]
+        parts += [jnp.where(first, a, b), jnp.where(first, b, a)]
+    return single(z, w_ref[:, at]) + single(z_pair, jnp.concatenate(parts, axis=0).astype(bf16))
+
+
+def farthest(core_ref, y_ref, z_ref, zx_ref, w_ref, p0, p1, p2, p3, low_ref, high_ref):
     half = low_ref.shape[0]
-    to = (x_lo_ref[0], lax.rem(y_ref[0] + 4, SIZES[4]))
-    out = piece(z_ref[...].astype(bf16), zx_ref[...].astype(bf16), to, w_ref, near_ref, far_ref)
+    z, zx = z_ref[...].astype(bf16), zx_ref[...].astype(bf16)
+    out = piece((core_ref, y_ref), 4, z, zx, w_ref, p0, p1, p2, p3)
     low_ref[...] = out[:half]
     high_ref[...] = out[half:]
 
@@ -191,11 +198,10 @@
 OFFSETS = (-3, 3, -2, 2, -1, 1, 0)
 
 
-def nearer(x_lo_ref, y_ref, z_ref, zx_ref, w_ref, near_ref, far_ref, *out_refs):
+def nearer(core_ref, y_ref, z_ref, zx_ref, w_ref, p0, p1, p2, p3, *out_refs):
     z, zx = z_ref[...].astype(bf16), zx_ref[...].astype(bf16)
     for offset, out_ref in zip(OFFSETS, out_refs):
-        to = (x_lo_ref[0], lax.rem(y_ref[0] + (offset + SIZES[4]), SIZES[4]))
-        out_ref[...] = piece(z, zx, to, w_ref, near_ref, far_ref)
+        out_ref[...] = piece((core_ref, y_ref), offset, z, zx, w_ref, p0, p1, p2, p3)
 
 
 def swapped(x, axes):
@@ -215,13 +221,13 @@
     chunk = columns // SIZES[4]
     square, wide, out_piece = ((HW, HW), f32), ((HW, 2 * HW), f32), ((rows, chunk), f32)
 
-    keep, send, own_rows = call(
-        shard_maps, [wide, wide, ((rows, 4 * HW), f32)], [core],
-        *(pltpu.with_memory_space_constraint(x, pltpu.HBM) for x in (queries, keys, values, rates)),
+    keep, send, own_rows, first = call(
+        shard_maps, [wide, wide, ((rows, 4 * HW), f32), square], [core],
+        queries, keys, values, rates, init_weight,
         scratch=[pltpu.VMEM((rows, 2 * HW), bf16)] * 3
         + [pltpu.VMEM((2, rows), f32), pltpu.VMEM((2, rows, 2 * HW), f32)]
-        + [pltpu.SemaphoreType.DMA] * 4,
-        space=pl.BlockSpec(memory_space=pltpu.HBM), limit=8, us=3,
+        + [pltpu.SemaphoreType.DMA] * 5,
+        space=pltpu.HBM, limit=8, us=3,
     )
     got = swapped(send, (CORE,))
 
@@ -229,37 +235,54 @@
         return lax.ppermute(x, Z, [(i, to(i)) for i in range(SIZES[1])])
 
     (chip,) = call(chip_map, [wide], [core], keep, got)
-    parts = 4
+    parts = 2
+    share = HW // 2
     near_out, far_out = pl.pallas_call(
         pair_weights,
         grid_spec=pltpu.PrefetchScalarGridSpec(
             num_scalar_prefetch=1,
             grid=(parts,),
             in_specs=[
-                pl.BlockSpec((2 * HW, columns // parts), lambda i, to: (0, to[0] * parts + i)),
+                pl.BlockSpec((share, columns // parts), lambda i, to: (to[1], to[0] * parts + i)),
+                pl.BlockSpec((share, columns // parts), lambda i, to: (to[1] + 2, to[0] * parts + i)),
                 pl.BlockSpec(memory_space=pl.ANY),
             ],
-            out_specs=[pl.BlockSpec((HW, columns // parts), lambda i, to: (0, i))] * 2,
+            out_specs=[pl.BlockSpec((share, columns // parts), lambda i, to: (0, i))] * 2,
         ),
-        out_shape=[jax.ShapeDtypeStruct((HW, columns), f32)] * 2,
+        out_shape=[jax.ShapeDtypeStruct((share, columns), f32)] * 2,
         compiler_params=pltpu.CompilerParams(vmem_limit_bytes=6 * MIB),
-    )(1 - x_lo, out_weight, chip)
+    )(jnp.concatenate([1 - x_lo, core]), out_weight, out_weight, chip)
     near = swapped(near_out, (XL,))
     far = swapped(far_out, (XH, XL))
-
-    both, pre = call(join_chips, [wide, wide], [z], chip, across_z(chip, lambda i: i ^ 1), later=[near_out], us=2)
-    four, pre = call(join_pairs, [wide, wide], [z], both, across_z(both, lambda i: i ^ 2), pre, us=2)
-    end, pre = call(join_ring, [square, wide], [z, core], four, across_z(four, lambda i: 7 - i), pre, init_weight, us=2)
+    near_other, far_other = swapped(near, (CORE,)), swapped(far, (CORE,))
+    own_half = pl.pallas_call(
+        own_weights,
+        grid_spec=pltpu.PrefetchScalarGridSpec(
+            num_scalar_prefetch=1,
+            grid=(4,),
+            in_specs=[
+                pl.BlockSpec((2 * HW, columns // 4), lambda i, to: (0, to[0] * 4 + i)),
+                pl.BlockSpec(memory_space=pl.ANY),
+            ],
+            out_specs=pl.BlockSpec((2 * HW, columns // 4), lambda i, to: (0, i)),
+        ),
+        out_shape=jax.ShapeDtypeStruct((2 * HW, columns), bf16),
+        compiler_params=pltpu.CompilerParams(vmem_limit_bytes=6 * MIB),
+    )(x_lo, out_weight, near_out)
+
+    both, pre = call(join_chips, [wide, wide], [z], chip, across_z(chip, lambda i: i ^ 1), later=[near_out], us=2.5)
+    four, pre = call(join_pairs, [wide, wide], [z], both, across_z(both, lambda i: i ^ 2), pre, later=[own_half], us=2.5)
+    end, pre = call(join_ring, [square, wide], [z], four, across_z(four, lambda i: 7 - i), pre, first, us=2.5)
     arrived = lax.ppermute(end, XH, [(0, 1)])
-    mine, other = call(shard_prefixes, [wide, wide], [core], pre, keep, got, us=2)
-    kept, leaving = call(shard_states, [square, square], [x_hi, core], mine, other, arrived, init_weight, us=2)
+    mine, other = call(shard_prefixes, [wide, wide], [core], pre, keep, got, us=2.5)
+    kept, leaving = call(shard_states, [square, square], [x_hi], mine, other, arrived, first, us=2.5)
     (z_rows,) = call(outputs, [((rows, 2 * HW), f32)], [core], kept, swapped(leaving, (CORE,)), own_rows)
     z_pair = swapped(z_rows, (XL,))
 
-    factors = (z_rows, z_pair, out_weight, near, far)
-    low, high = call(farthest, [((rows // 2, chunk), f32)] * 2, [x_lo, y], *factors, limit=16)
+    factors = (z_rows, z_pair, own_half, near, near_other, far, far_other)
+    low, high = call(farthest, [((rows // 2, chunk), f32)] * 2, [core, y], *factors, limit=16)
     down, up = passed(low, Y, -1), passed(high, Y, 1)
-    pieces = call(nearer, [out_piece] * len(OFFSETS), [x_lo, y], *factors, later=[low], limit=16)
+    pieces = call(nearer, [out_piece] * len(OFFSETS), [core, y], *factors, later=[low], limit=16)
     down = pieces[0] + jnp.concatenate([down, jnp.zeros_like(down)], axis=0)
     up = pieces[1] + jnp.concatenate([jnp.zeros_like(up), up], axis=0)
     for i in (2, 4):

time: 117 us -> 111 us (0.949)
  the two profiles are of different devices: /device:TPU:6 before, /device:TPU:2 now
where the time goes in v4:
time: 111 us
  starting transfers between devices  68.7 us (62%)
  waiting for transfers between devices  28.1 us (25%)
  Pallas kernels  10.9 us (10%)
  local copies, waits for them, and re-layouts  1.41 us (1%)
    ppermute x8, starting transfers between devices, passed(): return lax.ppermute(x, axis, [(i, (i + by) % n) for i in range(n)])  29.4 us
    ppermute x7, starting transfers between devices, swapped(): return lax.ppermute(x, axes, [(i, n - 1 - i) for i in range(n)])  19.6 us
    ppermute x3, starting transfers between devices, across_z(): return lax.ppermute(x, Z, [(i, to(i)) for i in range(SIZES[1])])  17.7 us
    ppermute x8, waiting for transfers between devices, passed(): return lax.ppermute(x, axis, [(i, (i + by) % n) for i in range(n)])  11.3 us
    ppermute x3, waiting for transfers between devices, across_z(): return lax.ppermute(x, Z, [(i, to(i)) for i in range(SIZES[1])])  9.82 us
    pallas_call x10, Pallas kernels, call(): pl.pallas_call(body, out_shape=outs, in_specs=[SM] * len(place) + [pl.Blo...  8.61 us
    ppermute x7, waiting for transfers between devices, swapped(): return lax.ppermute(x, axes, [(i, n - 1 - i) for i in range(n)])  7.05 us
  transfers between devices with their start and end apart: 19, of which 9 were waited for; matrix products, arithmetic and copies ran while one was open for 0% of the time, Pallas kernels for 5%

profile of v4, /device:TPU:2, one launch (start us, length us, event | category | flops | bytes accessed | tf_op | source)
XLA Modules:
  0.0 110.5 jit_solution(3277669966466551405)
XLA Ops:
  0.0 3.1 %shard_map.64 = (f32[128,256]{1,0:T(8,128)S(1)}, f32[128,256]{1,0:T(8,128)S(1)}, f32[160,512]{1,0:T(8,128)S(1)}, f32[128,128]{1,0:T(8,128)S(1)}) custom-call(s32[1]{0:T(128)} %bitcast.refs_0_, bf16[160,256]{1,0:T(8,128)(2,1)} %refs_1_.1, bf16[160,256]{1,0:T(8,128)(2,1)} %refs_2_.1, bf16[160,256]{1,0:T(8,128)(2,1)} %refs_3_.1, f32[2,160]{1,0:T(2,128)} %refs_4_.1, ...), custom_call_target="tpu_custom_call" | custom-call | flops 3000000000 | bytes 131072 | tf_op jit(solution)/shard_map/pallas_call | solution.py:36
  3.1 0.0 copy-start.3
  3.1 0.7 copy-done.3
  3.9 2.2 %collective-permute-start = (f32[128,256]{1,0:T(8,128)S(1)}, f32[128,256]{1,0:T(8,128)S(1)}, u32[]{:S(2)}, u32[]{:S(2)}) collective-permute-start(f32[128,256]{1,0:T(8,128)S(1)} %get-tuple-element.31), channel_id=1, source_target_pairs={{0,16},{16,0},{1,17},{17,1},{2,18},{18,2},{3,19},{19,3},{4,20},{20... | collective-permute-start | bytes 393224 | tf_op jit(solution)/shard_map/ppermute | solution.py:209
  6.0 1.3 %collective-permute-done.refs_2_.refs_3_ = f32[128,256]{1,0:T(8,128)S(1)} collective-permute-done((f32[128,256]{1,0:T(8,128)S(1)}, f32[128,256]{1,0:T(8,128)S(1)}, u32[]{:S(2)}, u32[]{:S(2)}) %collective-permute-start) | collective-permute-done | bytes 131104 | tf_op jit(solution)/shard_map/ppermute | solution.py:209
  7.4 0.2 shard_map.65.later_ref.refs_1_
  7.6 0.0 copy-done.7
  7.6 0.0 copy-start.5
  7.6 0.6 copy-done.5
  8.2 4.3 %collective-permute-start.1 = (f32[128,256]{1,0:T(8,128)S(1)}, f32[128,256]{1,0:T(8,128)S(1)}, u32[]{:S(2)}, u32[]{:S(2)}) collective-permute-start(f32[128,256]{1,0:T(8,128)S(1)} %shard_map.65.later_ref.refs_1_), channel_id=1, source_target_pairs={{0,32},{32,0},{64,96},{96,64},{128,160},{160,128},{192,224},{224,1... | collective-permute-start | bytes 393224 | tf_op jit(solution)/shard_map/ppermute | solution.py:235
  12.5 0.1 pad_add_fusion.2.to_ref
  12.6 0.0 copy-done
  12.6 1.9 %shard_map.66 = (f32[64,3072]{1,0:T(8,128)}, f32[64,3072]{1,0:T(8,128)}) custom-call(s32[2]{0:T(128)S(1)} %pad_add_fusion.2.to_ref, bf16[256,6144]{1,0:T(8,128)(2,1)S(1)} %copy-done, bf16[256,6144]{1,0:T(8,128)(2,1)S(1)} %copy-done, f32[128,256]{1,0:T(8,128)S(1)} %shard_map.65.later_ref.refs_1_), custom_call_target="tpu_custom_call" | custom-call | tf_op jit(solution)/shard_map/pallas_call | solution.py:240
  14.5 3.4 %collective-permute-start.9 = (f32[64,3072]{1,0:T(8,128)}, f32[64,3072]{1,0:T(8,128)}, u32[]{:S(2)}, u32[]{:S(2)}) collective-permute-start(f32[64,3072]{1,0:T(8,128)} %get-tuple-element.45), channel_id=1, source_target_pairs={{0,264},{8,256},{256,8},{264,0},{1,265},{9,257},{257,9},{265,1},{2... | collective-permute-start | bytes 2359304 | tf_op jit(solution)/shard_map/ppermute | solution.py:209
  17.9 4.0 %collective-permute-start.7 = (f32[64,3072]{1,0:T(8,128)}, f32[64,3072]{1,0:T(8,128)}, u32[]{:S(2)}, u32[]{:S(2)}) collective-permute-start(f32[64,3072]{1,0:T(8,128)} %get-tuple-element.32.refs_3_.later_ref), channel_id=1, source_target_pairs={{0,8},{8,0},{1,9},{9,1},{2,10},{10,2},{3,11},{11,3},{4,12},{12,4},... | collective-permute-start | bytes 2359304 | tf_op jit(solution)/shard_map/ppermute | solution.py:209
  21.9 0.0 collective-permute-done.1.refs_2_
  21.9 0.2 shard_map.67
  22.1 5.8 %collective-permute-start.2 = (f32[128,256]{1,0:T(8,128)S(1)}, f32[128,256]{1,0:T(8,128)S(1)}, u32[]{:S(2)}, u32[]{:S(2)}) collective-permute-start(f32[128,256]{1,0:T(8,128)S(1)} %get-tuple-element.33.refs_1_), channel_id=1, source_target_pairs={{0,64},{32,96},{64,0},{96,32},{128,192},{160,224},{192,128},{224,1... | collective-permute-start | bytes 393224 | tf_op jit(solution)/shard_map/ppermute | solution.py:235
  27.9 0.4 shard_map.68.refs_4_
  28.4 0.0 copy-start.1
  28.4 5.3 %collective-permute-done.2.refs_2_ = f32[128,256]{1,0:T(8,128)S(1)} collective-permute-done((f32[128,256]{1,0:T(8,128)S(1)}, f32[128,256]{1,0:T(8,128)S(1)}, u32[]{:S(2)}, u32[]{:S(2)}) %collective-permute-start.2) | collective-permute-done | bytes 131104 | tf_op jit(solution)/shard_map/ppermute | solution.py:235
  33.7 0.3 shard_map.69
  34.0 0.0 copy-done.1
  34.0 7.6 %collective-permute-start.3 = (f32[128,256]{1,0:T(8,128)S(1)}, f32[128,256]{1,0:T(8,128)S(1)}, u32[]{:S(2)}, u32[]{:S(2)}) collective-permute-start(f32[128,256]{1,0:T(8,128)S(1)} %get-tuple-element.35.refs_1_), channel_id=1, source_target_pairs={{0,224},{32,192},{64,160},{96,128},{128,96},{160,64},{192,32},{224... | collective-permute-start | bytes 393224 | tf_op jit(solution)/shard_map/ppermute | solution.py:235
  41.6 4.5 %collective-permute-done.3.refs_2_ = f32[128,256]{1,0:T(8,128)S(1)} collective-permute-done((f32[128,256]{1,0:T(8,128)S(1)}, f32[128,256]{1,0:T(8,128)S(1)}, u32[]{:S(2)}, u32[]{:S(2)}) %collective-permute-start.3) | collective-permute-done | bytes 131104 | tf_op jit(solution)/shard_map/ppermute | solution.py:235
  46.1 0.0 copy-done.8
  46.1 0.4 shard_map.70
  46.5 2.1 %collective-permute-start.4 = (f32[128,128]{1,0:T(8,128)S(1)}, f32[128,128]{1,0:T(8,128)S(1)}, u32[]{:S(2)}, u32[]{:S(2)}) collective-permute-start(f32[128,128]{1,0:T(8,128)S(1)} %get-tuple-element.41), channel_id=1, source_target_pairs={{0,256},{1,257},{2,258},{3,259},{4,260},{5,261},{6,262},{7,263},{8... | collective-permute-start | bytes 196616 | tf_op jit(solution)/shard_map/ppermute | solution.py:276
  48.6 0.0 collective-permute-done.9.refs_7_
  48.6 1.9 %collective-permute-start.10 = (f32[64,3072]{1,0:T(8,128)}, f32[64,3072]{1,0:T(8,128)S(1)}, u32[]{:S(2)}, u32[]{:S(2)}) collective-permute-start(f32[64,3072]{1,0:T(8,128)} %collective-permute-done.9.refs_7_), channel_id=1, source_target_pairs={{0,16},{16,0},{1,17},{17,1},{2,18},{18,2},{3,19},{19,3},{4,20},{20... | collective-permute-start | bytes 2359304 | tf_op jit(solution)/shard_map/ppermute | solution.py:209
  50.5 0.0 collective-permute-done.7.refs_5_
  50.5 2.4 %collective-permute-start.8 = (f32[64,3072]{1,0:T(8,128)}, f32[64,3072]{1,0:T(8,128)S(1)}, u32[]{:S(2)}, u32[]{:S(2)}) collective-permute-start(f32[64,3072]{1,0:T(8,128)} %collective-permute-done.7.refs_5_), channel_id=1, source_target_pairs={{0,16},{16,0},{1,17},{17,1},{2,18},{18,2},{3,19},{19,3},{4,20},{20... | collective-permute-start | bytes 2359304 | tf_op jit(solution)/shard_map/ppermute | solution.py:209
  53.0 0.0 copy-done.6
  53.0 0.2 shard_map.71
  53.2 0.0 collective-permute-done.4.refs_3_
  53.2 0.0 copy-start.4
  53.2 0.2 shard_map.72
  53.4 2.1 %collective-permute-start.5 = (f32[128,128]{1,0:T(8,128)S(1)}, f32[128,128]{1,0:T(8,128)S(1)}, u32[]{:S(2)}, u32[]{:S(2)}) collective-permute-start(f32[128,128]{1,0:T(8,128)S(1)} %get-tuple-element.43), channel_id=1, source_target_pairs={{0,16},{16,0},{1,17},{17,1},{2,18},{18,2},{3,19},{19,3},{4,20},{20... | collective-permute-start | bytes 196616 | tf_op jit(solution)/shard_map/ppermute | solution.py:209
  55.5 1.2 %collective-permute-done.5.refs_2_ = f32[128,128]{1,0:T(8,128)S(1)} collective-permute-done((f32[128,128]{1,0:T(8,128)S(1)}, f32[128,128]{1,0:T(8,128)S(1)}, u32[]{:S(2)}, u32[]{:S(2)}) %collective-permute-start.5) | collective-permute-done | bytes 65568 | tf_op jit(solution)/shard_map/ppermute | solution.py:209
  56.7 0.0 copy-done.4
  56.7 0.2 shard_map.73.refs_2_
  56.9 3.7 %collective-permute-start.6 = (f32[160,256]{1,0:T(8,128)S(1)}, f32[160,256]{1,0:T(8,128)S(1)}, u32[]{:S(2)}, u32[]{:S(2)}) collective-permute-start(f32[160,256]{1,0:T(8,128)S(1)} %shard_map.73.refs_2_), channel_id=1, source_target_pairs={{0,8},{8,0},{1,9},{9,1},{2,10},{10,2},{3,11},{11,3},{4,12},{12,4},... | collective-permute-start | bytes 491528 | tf_op jit(solution)/shard_map/ppermute | solution.py:209
  60.6 4.5 %collective-permute-done.6.refs_3_ = f32[160,256]{1,0:T(8,128)S(1)} collective-permute-done((f32[160,256]{1,0:T(8,128)S(1)}, f32[160,256]{1,0:T(8,128)S(1)}, u32[]{:S(2)}, u32[]{:S(2)}) %collective-permute-start.6) | collective-permute-done | bytes 163872 | tf_op jit(solution)/shard_map/ppermute | solution.py:209
  65.1 0.0 collective-permute-done.10.refs_8_
  65.1 0.0 collective-permute-done.8.refs_6_
  65.1 1.6 %shard_map.74 = (f32[80,384]{1,0:T(8,128)S(1)}, f32[80,384]{1,0:T(8,128)S(1)}) custom-call(s32[1]{0:T(128)} %bitcast.refs_0_, s32[1]{0:T(128)} %bitcast.1.refs_1_, f32[160,256]{1,0:T(8,128)S(1)} %shard_map.73.refs_2_, f32[160,256]{1,0:T(8,128)S(1)} %collective-permute-done.6.refs_3_, bf16[256,3072]{1,0:T(8,128)(2,1)S(1)} %copy-done.2, ...), custom_call_target="tpu_custom_call" | custom-call | flops 1000000000 | bytes 131072 | tf_op jit(solution)/shard_map/pallas_call | solution.py:36
  66.7 5.4 %collective-permute-start.11 = (f32[80,384]{1,0:T(8,128)S(1)}, f32[80,384]{1,0:T(8,128)S(1)}, u32[]{:S(2)}, u32[]{:S(2)}) collective-permute-start(f32[80,384]{1,0:T(8,128)S(1)} %get-tuple-element.46.refs_9_), channel_id=1, source_target_pairs={{0,7},{1,0},{2,1},{3,2},{4,3},{5,4},{6,5},{7,6},{8,15},{9,8},{10,9... | collective-permute-start | bytes 368648 | tf_op jit(solution)/shard_map/ppermute | solution.py:214
  72.1 1.9 %collective-permute-start.15 = (f32[80,384]{1,0:T(8,128)S(1)}, f32[80,384]{1,0:T(8,128)S(1)}, u32[]{:S(2)}, u32[]{:S(2)}) collective-permute-start(f32[80,384]{1,0:T(8,128)S(1)} %get-tuple-element.51), channel_id=1, source_target_pairs={{0,1},{1,2},{2,3},{3,4},{4,5},{5,6},{6,7},{7,0},{8,9},{9,10},{10,1... | collective-permute-start | bytes 368648 | tf_op jit(solution)/shard_map/ppermute | solution.py:214
  74.0 2.2 %shard_map.75 = (f32[160,384]{1,0:T(8,128)S(1)}, f32[160,384]{1,0:T(8,128)S(1)}, f32[160,384]{1,0:T(8,128)S(1)}, f32[160,384]{1,0:T(8,128)S(1)}, f32[160,384]{1,...) custom-call(s32[1]{0:T(128)} %bitcast.refs_0_, s32[1]{0:T(128)} %bitcast.1.refs_1_, ...), custom_call_target="tpu_custom_call" | custom-call | flops 1000000000 | bytes 131072 | tf_op jit(solution)/shard_map/pallas_call | solution.py:36
  76.2 0.0 collective-permute-done.11
  76.3 5.1 %collective-permute-start.12 = (f32[160,384]{1,0:T(8,128)S(1)}, f32[160,384]{1,0:T(8,128)S(1)}, u32[]{:S(2)}, u32[]{:S(2)}) collective-permute-start(f32[160,384]{1,0:T(8,128)S(1)} %pad_add_fusion.1), channel_id=1, source_target_pairs={{0,7},{1,0},{2,1},{3,2},{4,3},{5,4},{6,5},{7,6},{8,15},{9,8},{10,9... | collective-permute-start | bytes 737288 | tf_op jit(solution)/shard_map/ppermute | solution.py:214
  81.4 0.0 collective-permute-done.15
  81.4 1.9 %collective-permute-start.16 = (f32[160,384]{1,0:T(8,128)S(1)}, f32[160,384]{1,0:T(8,128)S(1)}, u32[]{:S(2)}, u32[]{:S(2)}) collective-permute-start(f32[160,384]{1,0:T(8,128)S(1)} %pad_add_fusion), channel_id=1, source_target_pairs={{0,1},{1,2},{2,3},{3,4},{4,5},{5,6},{6,7},{7,0},{8,9},{9,10},{10,1... | collective-permute-start | bytes 737288 | tf_op jit(solution)/shard_map/ppermute | solution.py:214
  83.4 2.2 %collective-permute-done.12 = f32[160,384]{1,0:T(8,128)S(1)} collective-permute-done((f32[160,384]{1,0:T(8,128)S(1)}, f32[160,384]{1,0:T(8,128)S(1)}, u32[]{:S(2)}, u32[]{:S(2)}) %collective-permute-start.12) | collective-permute-done | bytes 245792 | tf_op jit(solution)/shard_map/ppermute | solution.py:214
  85.5 5.6 %collective-permute-start.13 = (f32[160,384]{1,0:T(8,128)S(1)}, f32[160,384]{1,0:T(8,128)S(1)}, u32[]{:S(2)}, u32[]{:S(2)}) collective-permute-start(f32[160,384]{1,0:T(8,128)S(1)} %add.29), channel_id=1, source_target_pairs={{0,7},{1,0},{2,1},{3,2},{4,3},{5,4},{6,5},{7,6},{8,15},{9,8},{10,9... | collective-permute-start | bytes 737288 | tf_op jit(solution)/shard_map/ppermute | solution.py:214
  91.2 0.0 collective-permute-done.16
  91.2 1.9 %collective-permute-start.17 = (f32[160,384]{1,0:T(8,128)S(1)}, f32[160,384]{1,0:T(8,128)S(1)}, u32[]{:S(2)}, u32[]{:S(2)}) collective-permute-start(f32[160,384]{1,0:T(8,128)S(1)} %add.32), channel_id=1, source_target_pairs={{0,1},{1,2},{2,3},{3,4},{4,5},{5,6},{6,7},{7,0},{8,9},{9,10},{10,1... | collective-permute-start | bytes 737288 | tf_op jit(solution)/shard_map/ppermute | solution.py:214
  93.1 1.7 %collective-permute-done.13 = f32[160,384]{1,0:T(8,128)S(1)} collective-permute-done((f32[160,384]{1,0:T(8,128)S(1)}, f32[160,384]{1,0:T(8,128)S(1)}, u32[]{:S(2)}, u32[]{:S(2)}) %collective-permute-start.13) | collective-permute-done | bytes 245792 | tf_op jit(solution)/shard_map/ppermute | solution.py:214
  94.9 5.6 %collective-permute-start.14 = (f32[160,384]{1,0:T(8,128)S(1)}, f32[160,384]{1,0:T(8,128)S(1)}, u32[]{:S(2)}, u32[]{:S(2)}) collective-permute-start(f32[160,384]{1,0:T(8,128)S(1)} %add.30), channel_id=1, source_target_pairs={{0,7},{1,0},{2,1},{3,2},{4,3},{5,4},{6,5},{7,6},{8,15},{9,8},{10,9... | collective-permute-start | bytes 737288 | tf_op jit(solution)/shard_map/ppermute | solution.py:214
  100.5 0.0 collective-permute-done.17
  100.5 1.9 %collective-permute-start.18 = (f32[160,384]{1,0:T(8,128)S(1)}, f32[160,384]{1,0:T(8,128)S(1)}, u32[]{:S(2)}, u32[]{:S(2)}) collective-permute-start(f32[160,384]{1,0:T(8,128)S(1)} %add.33), channel_id=1, source_target_pairs={{0,1},{1,2},{2,3},{3,4},{4,5},{5,6},{6,7},{7,0},{8,9},{9,10},{10,1... | collective-permute-start | bytes 737288 | tf_op jit(solution)/shard_map/ppermute | solution.py:214
  102.5 1.7 %collective-permute-done.14 = f32[160,384]{1,0:T(8,128)S(1)} collective-permute-done((f32[160,384]{1,0:T(8,128)S(1)}, f32[160,384]{1,0:T(8,128)S(1)}, u32[]{:S(2)}, u32[]{:S(2)}) %collective-permute-start.14) | collective-permute-done | bytes 245792 | tf_op jit(solution)/shard_map/ppermute | solution.py:214
  104.2 5.7 %collective-permute-done.18 = f32[160,384]{1,0:T(8,128)S(1)} collective-permute-done((f32[160,384]{1,0:T(8,128)S(1)}, f32[160,384]{1,0:T(8,128)S(1)}, u32[]{:S(2)}, u32[]{:S(2)}) %collective-permute-start.18) | collective-permute-done | bytes 245792 | tf_op jit(solution)/shard_map/ppermute | solution.py:214
  109.8 0.7 add_convert_fusion
  (12 shorter events, 0.2 us)
Async XLA Ops:
  3.1 0.7 copy-start.3
  3.9 3.7 %copy-start.7 = (f32[128,128]{1,0:T(8,128)}, f32[128,128]{1,0:T(8,128)S(1)}, u32[]{:S(2)}) copy-start(f32[128,128]{1,0:T(8,128)S(1)} %get-tuple-element.37.refs_4_) | copy-start | bytes 196612
  3.9 8.7 %copy-start = (bf16[256,6144]{1,0:T(8,128)(2,1)S(1)}, bf16[256,6144]{1,0:T(8,128)(2,1)}, u32[]{:S(2)}) copy-start(bf16[256,6144]{1,0:T(8,128)(2,1)} %w_ref.1) | copy-start | bytes 9437188
  3.9 3.5 %collective-permute-start = (f32[128,256]{1,0:T(8,128)S(1)}, f32[128,256]{1,0:T(8,128)S(1)}, u32[]{:S(2)}, u32[]{:S(2)}) collective-permute-start(f32[128,256]{1,0:T(8,128)S(1)} %get-tuple-element.31), channel_id=1, source_target_pairs={{0,16},{16,0},{1,17},{17,1},{2,18},{18,2},{3,19},{19,3},{4,20},{20... | collective-permute-start | bytes 393224 | tf_op jit(solution)/shard_map/ppermute | solution.py:209
  7.6 0.7 copy-start.5
  8.2 13.6 %collective-permute-start.1 = (f32[128,256]{1,0:T(8,128)S(1)}, f32[128,256]{1,0:T(8,128)S(1)}, u32[]{:S(2)}, u32[]{:S(2)}) collective-permute-start(f32[128,256]{1,0:T(8,128)S(1)} %shard_map.65.later_ref.refs_1_), channel_id=1, source_target_pairs={{0,32},{32,0},{64,96},{96,64},{128,160},{160,128},{192,224},{224,1... | collective-permute-start | bytes 393224 | tf_op jit(solution)/shard_map/ppermute | solution.py:235
  14.5 34.1 %collective-permute-start.9 = (f32[64,3072]{1,0:T(8,128)}, f32[64,3072]{1,0:T(8,128)}, u32[]{:S(2)}, u32[]{:S(2)}) collective-permute-start(f32[64,3072]{1,0:T(8,128)} %get-tuple-element.45), channel_id=1, source_target_pairs={{0,264},{8,256},{256,8},{264,0},{1,265},{9,257},{257,9},{265,1},{2... | collective-permute-start | bytes 2359304 | tf_op jit(solution)/shard_map/ppermute | solution.py:209
  17.9 32.7 %collective-permute-start.7 = (f32[64,3072]{1,0:T(8,128)}, f32[64,3072]{1,0:T(8,128)}, u32[]{:S(2)}, u32[]{:S(2)}) collective-permute-start(f32[64,3072]{1,0:T(8,128)} %get-tuple-element.32.refs_3_.later_ref), channel_id=1, source_target_pairs={{0,8},{8,0},{1,9},{9,1},{2,10},{10,2},{3,11},{11,3},{4,12},{12,4},... | collective-permute-start | bytes 2359304 | tf_op jit(solution)/shard_map/ppermute | solution.py:209
  22.1 11.6 %collective-permute-start.2 = (f32[128,256]{1,0:T(8,128)S(1)}, f32[128,256]{1,0:T(8,128)S(1)}, u32[]{:S(2)}, u32[]{:S(2)}) collective-permute-start(f32[128,256]{1,0:T(8,128)S(1)} %get-tuple-element.33.refs_1_), channel_id=1, source_target_pairs={{0,64},{32,96},{64,0},{96,32},{128,192},{160,224},{192,128},{224,1... | collective-permute-start | bytes 393224 | tf_op jit(solution)/shard_map/ppermute | solution.py:235
  28.4 5.6 %copy-start.1 = (bf16[256,3072]{1,0:T(8,128)(2,1)}, bf16[256,3072]{1,0:T(8,128)(2,1)S(1)}, u32[]{:S(2)}) copy-start(bf16[256,3072]{1,0:T(8,128)(2,1)S(1)} %shard_map.68.refs_4_) | copy-start | bytes 4718596
  33.7 12.4 %copy-start.8 = (f32[128,128]{1,0:T(8,128)S(1)}, f32[128,128]{1,0:T(8,128)}, u32[]{:S(2)}) copy-start(f32[128,128]{1,0:T(8,128)} %copy-done.7) | copy-start | bytes 196612
  34.0 12.1 %collective-permute-start.3 = (f32[128,256]{1,0:T(8,128)S(1)}, f32[128,256]{1,0:T(8,128)S(1)}, u32[]{:S(2)}, u32[]{:S(2)}) collective-permute-start(f32[128,256]{1,0:T(8,128)S(1)} %get-tuple-element.35.refs_1_), channel_id=1, source_target_pairs={{0,224},{32,192},{64,160},{96,128},{128,96},{160,64},{192,32},{224... | collective-permute-start | bytes 393224 | tf_op jit(solution)/shard_map/ppermute | solution.py:235
  46.1 6.9 %copy-start.6 = (f32[128,256]{1,0:T(8,128)S(1)}, f32[128,256]{1,0:T(8,128)}, u32[]{:S(2)}) copy-start(f32[128,256]{1,0:T(8,128)} %copy-done.5) | copy-start | bytes 393220
  46.5 6.7 %collective-permute-start.4 = (f32[128,128]{1,0:T(8,128)S(1)}, f32[128,128]{1,0:T(8,128)S(1)}, u32[]{:S(2)}, u32[]{:S(2)}) collective-permute-start(f32[128,128]{1,0:T(8,128)S(1)} %get-tuple-element.41), channel_id=1, source_target_pairs={{0,256},{1,257},{2,258},{3,259},{4,260},{5,261},{6,262},{7,263},{8... | collective-permute-start | bytes 196616 | tf_op jit(solution)/shard_map/ppermute | solution.py:276
  48.6 16.5 %collective-permute-start.10 = (f32[64,3072]{1,0:T(8,128)}, f32[64,3072]{1,0:T(8,128)S(1)}, u32[]{:S(2)}, u32[]{:S(2)}) collective-permute-start(f32[64,3072]{1,0:T(8,128)} %collective-permute-done.9.refs_7_), channel_id=1, source_target_pairs={{0,16},{16,0},{1,17},{17,1},{2,18},{18,2},{3,19},{19,3},{4,20},{20... | collective-permute-start | bytes 2359304 | tf_op jit(solution)/shard_map/ppermute | solution.py:209
  50.5 14.6 %collective-permute-start.8 = (f32[64,3072]{1,0:T(8,128)}, f32[64,3072]{1,0:T(8,128)S(1)}, u32[]{:S(2)}, u32[]{:S(2)}) collective-permute-start(f32[64,3072]{1,0:T(8,128)} %collective-permute-done.7.refs_5_), channel_id=1, source_target_pairs={{0,16},{16,0},{1,17},{17,1},{2,18},{18,2},{3,19},{19,3},{4,20},{20... | collective-permute-start | bytes 2359304 | tf_op jit(solution)/shard_map/ppermute | solution.py:209
  53.2 3.5 %copy-start.4 = (f32[160,512]{1,0:T(8,128)S(1)}, f32[160,512]{1,0:T(8,128)}, u32[]{:S(2)}) copy-start(f32[160,512]{1,0:T(8,128)} %copy-done.3) | copy-start | bytes 983044
  53.4 11.7 %copy-start.2 = (bf16[256,3072]{1,0:T(8,128)(2,1)S(1)}, bf16[256,3072]{1,0:T(8,128)(2,1)}, u32[]{:S(2)}) copy-start(bf16[256,3072]{1,0:T(8,128)(2,1)} %copy-done.1) | copy-start | bytes 4718596
  53.4 3.3 %collective-permute-start.5 = (f32[128,128]{1,0:T(8,128)S(1)}, f32[128,128]{1,0:T(8,128)S(1)}, u32[]{:S(2)}, u32[]{:S(2)}) collective-permute-start(f32[128,128]{1,0:T(8,128)S(1)} %get-tuple-element.43), channel_id=1, source_target_pairs={{0,16},{16,0},{1,17},{17,1},{2,18},{18,2},{3,19},{19,3},{4,20},{20... | collective-permute-start | bytes 196616 | tf_op jit(solution)/shard_map/ppermute | solution.py:209
  56.9 8.2 %collective-permute-start.6 = (f32[160,256]{1,0:T(8,128)S(1)}, f32[160,256]{1,0:T(8,128)S(1)}, u32[]{:S(2)}, u32[]{:S(2)}) collective-permute-start(f32[160,256]{1,0:T(8,128)S(1)} %shard_map.73.refs_2_), channel_id=1, source_target_pairs={{0,8},{8,0},{1,9},{9,1},{2,10},{10,2},{3,11},{11,3},{4,12},{12,4},... | collective-permute-start | bytes 491528 | tf_op jit(solution)/shard_map/ppermute | solution.py:209
  66.7 9.5 %collective-permute-start.11 = (f32[80,384]{1,0:T(8,128)S(1)}, f32[80,384]{1,0:T(8,128)S(1)}, u32[]{:S(2)}, u32[]{:S(2)}) collective-permute-start(f32[80,384]{1,0:T(8,128)S(1)} %get-tuple-element.46.refs_9_), channel_id=1, source_target_pairs={{0,7},{1,0},{2,1},{3,2},{4,3},{5,4},{6,5},{7,6},{8,15},{9,8},{10,9... | collective-permute-start | bytes 368648 | tf_op jit(solution)/shard_map/ppermute | solution.py:214
  72.1 9.3 %collective-permute-start.15 = (f32[80,384]{1,0:T(8,128)S(1)}, f32[80,384]{1,0:T(8,128)S(1)}, u32[]{:S(2)}, u32[]{:S(2)}) collective-permute-start(f32[80,384]{1,0:T(8,128)S(1)} %get-tuple-element.51), channel_id=1, source_target_pairs={{0,1},{1,2},{2,3},{3,4},{4,5},{5,6},{6,7},{7,0},{8,9},{9,10},{10,1... | collective-permute-start | bytes 368648 | tf_op jit(solution)/shard_map/ppermute | solution.py:214
  76.3 9.3 %collective-permute-start.12 = (f32[160,384]{1,0:T(8,128)S(1)}, f32[160,384]{1,0:T(8,128)S(1)}, u32[]{:S(2)}, u32[]{:S(2)}) collective-permute-start(f32[160,384]{1,0:T(8,128)S(1)} %pad_add_fusion.1), channel_id=1, source_target_pairs={{0,7},{1,0},{2,1},{3,2},{4,3},{5,4},{6,5},{7,6},{8,15},{9,8},{10,9... | collective-permute-start | bytes 737288 | tf_op jit(solution)/shard_map/ppermute | solution.py:214
  81.4 9.7 %collective-permute-start.16 = (f32[160,384]{1,0:T(8,128)S(1)}, f32[160,384]{1,0:T(8,128)S(1)}, u32[]{:S(2)}, u32[]{:S(2)}) collective-permute-start(f32[160,384]{1,0:T(8,128)S(1)} %pad_add_fusion), channel_id=1, source_target_pairs={{0,1},{1,2},{2,3},{3,4},{4,5},{5,6},{6,7},{7,0},{8,9},{9,10},{10,1... | collective-permute-start | bytes 737288 | tf_op jit(solution)/shard_map/ppermute | solution.py:214
  85.5 9.3 %collective-permute-start.13 = (f32[160,384]{1,0:T(8,128)S(1)}, f32[160,384]{1,0:T(8,128)S(1)}, u32[]{:S(2)}, u32[]{:S(2)}) collective-permute-start(f32[160,384]{1,0:T(8,128)S(1)} %add.29), channel_id=1, source_target_pairs={{0,7},{1,0},{2,1},{3,2},{4,3},{5,4},{6,5},{7,6},{8,15},{9,8},{10,9... | collective-permute-start | bytes 737288 | tf_op jit(solution)/shard_map/ppermute | solution.py:214
  91.2 9.3 %collective-permute-start.17 = (f32[160,384]{1,0:T(8,128)S(1)}, f32[160,384]{1,0:T(8,128)S(1)}, u32[]{:S(2)}, u32[]{:S(2)}) collective-permute-start(f32[160,384]{1,0:T(8,128)S(1)} %add.32), channel_id=1, source_target_pairs={{0,1},{1,2},{2,3},{3,4},{4,5},{5,6},{6,7},{7,0},{8,9},{9,10},{10,1... | collective-permute-start | bytes 737288 | tf_op jit(solution)/shard_map/ppermute | solution.py:214
  94.9 9.3 %collective-permute-start.14 = (f32[160,384]{1,0:T(8,128)S(1)}, f32[160,384]{1,0:T(8,128)S(1)}, u32[]{:S(2)}, u32[]{:S(2)}) collective-permute-start(f32[160,384]{1,0:T(8,128)S(1)} %add.30), channel_id=1, source_target_pairs={{0,7},{1,0},{2,1},{3,2},{4,3},{5,4},{6,5},{7,6},{8,15},{9,8},{10,9... | collective-permute-start | bytes 737288 | tf_op jit(solution)/shard_map/ppermute | solution.py:214
  100.5 9.3 %collective-permute-start.18 = (f32[160,384]{1,0:T(8,128)S(1)}, f32[160,384]{1,0:T(8,128)S(1)}, u32[]{:S(2)}, u32[]{:S(2)}) collective-permute-start(f32[160,384]{1,0:T(8,128)S(1)} %add.33), channel_id=1, source_target_pairs={{0,1},{1,2},{2,3},{3,4},{4,5},{5,6},{6,7},{7,0},{8,9},{9,10},{10,1... | collective-permute-start | bytes 737288 | tf_op jit(solution)/shard_map/ppermute | solution.py:214

commit v5 on v4

--- a/solution.py
+++ b/solution.py
@@ -61,34 +61,36 @@
     return exact(pair[:, :HW], state) + pair[:, HW:]
 
 
-def shard_maps(core_ref, q_hbm, k_hbm, v_hbm, r_hbm, w_hbm, keep_ref, send_ref, rows_ref, first_ref, *scratch):
-    q_ref, k_ref, v_ref, r_ref, x_ref, *done = scratch
-    copies = [
-        pltpu.make_async_copy(source, target, semaphore)
-        for source, target, semaphore in zip((q_hbm, k_hbm, v_hbm, r_hbm), scratch, done)
-    ]
-    copies.append(pltpu.make_async_copy(w_hbm.at[core_ref[0]], first_ref, done[4]))
+def gathered(copies):
     for copy in copies:
         copy.start()
-    rows = q_ref.shape[0]
-    core = core_ref[0]
+    return copies
+
+
+def shard_maps(core_ref, k_hbm, v_hbm, r_hbm, w_hbm, keep_ref, send_ref, x_ref, first_ref, k_ref, v_ref, r_ref, *done):
+    copies = gathered(
+        [
+            pltpu.make_async_copy(source, target, semaphore)
+            for source, target, semaphore in zip(
+                (k_hbm, v_hbm, r_hbm, w_hbm), (k_ref, v_ref, r_ref, first_ref), done
+            )
+        ]
+    )
+    rows = k_ref.shape[0]
     s_at = lax.broadcasted_iota(jnp.int32, (rows, rows), 0)
     t_at = lax.broadcasted_iota(jnp.int32, (rows, rows), 1)
     earlier_block = (t_at // MB) < (s_at // MB)
-    causal = t_at <= s_at
     diagonal = t_at == s_at
-    mix, key_gram, columns = [], [], []
-    for copy in copies[:4]:
+    key_gram, columns = [], []
+    for copy in copies[:3]:
         copy.wait()
     for h in range(2):
         at = slice(h * HW, (h + 1) * HW)
-        q, k, v = q_ref[:, at], k_ref[:, at], v_ref[:, at]
-        r = r_ref[h : h + 1, :]
+        k, r = k_ref[:, at], r_ref[h : h + 1, :]
         columns.append(jnp.sum(jnp.where(diagonal, r, 0.0), axis=1, keepdims=True))
         key_gram.append(jnp.where(earlier_block, single(k, k, ((1,), (1,))) * r, 0.0))
-        mix.append(jnp.where(causal, single(q, k, ((1,), (1,))) * r, 0.0))
         x_ref[h, :, :HW] = k.astype(f32)
-        x_ref[h, :, HW:] = v.astype(f32)
+        x_ref[h, :, HW:] = v_ref[:, at].astype(f32)
     for i in range(1, rows // MB):
         at = slice(i * MB, (i + 1) * MB)
         for h in range(2):
@@ -96,16 +98,25 @@
     maps = []
     for h in range(2):
         at = slice(h * HW, (h + 1) * HW)
-        x = x_ref[h]
-        y = exact(mix[h], x)
-        rows_ref[:, at] = q_ref[:, at].astype(f32) - y[:, :HW]
-        rows_ref[:, (2 + h) * HW : (3 + h) * HW] = y[:, HW:]
-        ab = exact(k_ref[:, at].astype(f32) * columns[h], x, ((0,), (0,)))
+        ab = exact(k_ref[:, at].astype(f32) * columns[h], x_ref[h], ((0,), (0,)))
         maps.append(identity(2 * HW) + jnp.where(left_half(ab.shape), -ab, ab))
-    first = core == 0
+    first = core_ref[0] == 0
     keep_ref[...] = jnp.where(first, maps[0], maps[1])
     send_ref[...] = jnp.where(first, maps[1], maps[0])
-    copies[4].wait()
+    copies[3].wait()
+
+
+def shard_rows(q_ref, k_ref, r_ref, x_ref, rows_ref):
+    rows = q_ref.shape[0]
+    s_at = lax.broadcasted_iota(jnp.int32, (rows, rows), 0)
+    t_at = lax.broadcasted_iota(jnp.int32, (rows, rows), 1)
+    for h in range(2):
+        at = slice(h * HW, (h + 1) * HW)
+        q = q_ref[:, at]
+        mix = jnp.where(t_at <= s_at, single(q, k_ref[:, at], ((1,), (1,))) * r_ref[h : h + 1, :], 0.0)
+        y = exact(mix, x_ref[h])
+        rows_ref[:, at] = q.astype(f32) - y[:, :HW]
+        rows_ref[:, (2 + h) * HW : (3 + h) * HW] = y[:, HW:]
 
 
 def chip_map(core_ref, keep_ref, got_ref, out_ref):
@@ -132,11 +143,11 @@
     pre_ref[...] = jnp.where(upper, after(pre, low), pre)
 
 
-def join_ring(z_ref, own_ref, got_ref, pre_in_ref, first_ref, end_ref, pre_ref):
+def join_ring(z_ref, core_ref, own_ref, got_ref, pre_in_ref, first_ref, end_ref, pre_ref):
     upper = z_ref[0] >= 4
     low = jnp.where(upper, got_ref[...], own_ref[...])
     high = jnp.where(upper, own_ref[...], got_ref[...])
-    end_ref[...] = applied(high, applied(low, first_ref[...]))
+    end_ref[...] = applied(high, applied(low, first_ref[core_ref[0]]))
     pre = pre_in_ref[...]
     pre_ref[...] = jnp.where(upper, after(pre, low), pre)
 
@@ -149,30 +160,41 @@
     other_ref[...] = jnp.where(first, middle, pre)
 
 
-def shard_states(x_hi_ref, mine_ref, other_ref, arrived_ref, first_ref, keep_ref, send_ref):
-    state = jnp.where(x_hi_ref[0] == 0, first_ref[...], arrived_ref[...])
-    send_ref[...] = applied(other_ref[...], state)
-    keep_ref[...] = applied(mine_ref[...], state)
-
-
-def outputs(core_ref, keep_ref, got_ref, rows_ref, z_ref):
-    core = core_ref[0]
-    for h in range(2):
-        state = jnp.where(core == h, keep_ref[...], got_ref[...])
+def ring_states(x_hi_ref, core_ref, here_ref, there_ref, first_ref, out_ref):
+    for h in range(2):
+        arrived = jnp.where(core_ref[0] == h, here_ref[...], there_ref[...])
+        out_ref[h] = jnp.where(x_hi_ref[0] == 0, first_ref[h], arrived)
+
+
+def outputs(core_ref, mine_ref, got_ref, begin_ref, rows_ref, z_ref):
+    for h in range(2):
+        state = applied(jnp.where(core_ref[0] == h, mine_ref[...], got_ref[...]), begin_ref[h])
         at = slice(h * HW, (h + 1) * HW)
         z = exact(rows_ref[:, at], state) + rows_ref[:, (2 + h) * HW : (3 + h) * HW]
         z_ref[:, at] = z.astype(bf16).astype(f32)
 
 
-def pair_weights(to_ref, near_in, far_in, later_ref, near_ref, far_ref):
-    del to_ref, later_ref
-    near_ref[...] = near_in[...].astype(f32)
-    far_ref[...] = far_in[...].astype(f32)
-
-
-def own_weights(to_ref, w_ref, later_ref, out_ref):
-    del to_ref, later_ref
-    out_ref[...] = w_ref[...]
+def copied(column_ref, row_ref, w_ref, later_ref, out_ref):
+    del column_ref, row_ref, later_ref
+    out_ref[...] = w_ref[...].astype(out_ref.dtype)
+
+
+def weight_share(weight, column, row, rows, dtype, later):
+    columns, parts = weight.shape[1] // SIZES[3], 2
+    return pl.pallas_call(
+        copied,
+        grid_spec=pltpu.PrefetchScalarGridSpec(
+            num_scalar_prefetch=2,
+            grid=(parts,),
+            in_specs=[
+                pl.BlockSpec((rows, columns // parts), lambda i, c, r: (r[0], c[0] * parts + i)),
+                pl.BlockSpec(memory_space=pl.ANY),
+            ],
+            out_specs=pl.BlockSpec((rows, columns // parts), lambda i, c, r: (0, i)),
+        ),
+        out_shape=jax.ShapeDtypeStruct((rows, columns), dtype),
+        compiler_params=pltpu.CompilerParams(vmem_limit_bytes=8 * MIB),
+    )(column, row, weight, later)
 
 
 def piece(place, offset, z, z_pair, w_ref, *pair_refs):
@@ -221,12 +243,12 @@
     chunk = columns // SIZES[4]
     square, wide, out_piece = ((HW, HW), f32), ((HW, 2 * HW), f32), ((rows, chunk), f32)
 
-    keep, send, own_rows, first = call(
-        shard_maps, [wide, wide, ((rows, 4 * HW), f32), square], [core],
-        queries, keys, values, rates, init_weight,
-        scratch=[pltpu.VMEM((rows, 2 * HW), bf16)] * 3
-        + [pltpu.VMEM((2, rows), f32), pltpu.VMEM((2, rows, 2 * HW), f32)]
-        + [pltpu.SemaphoreType.DMA] * 5,
+    share = HW // 2
+    keep, send, solved, first = call(
+        shard_maps, [wide, wide, ((2, rows, 2 * HW), f32), ((2, HW, HW), f32)], [core],
+        keys, values, rates, init_weight,
+        scratch=[pltpu.VMEM((rows, 2 * HW), bf16)] * 2
+        + [pltpu.VMEM((2, rows), f32)] + [pltpu.SemaphoreType.DMA] * 4,
         space=pltpu.HBM, limit=8, us=3,
     )
     got = swapped(send, (CORE,))
@@ -235,48 +257,29 @@
         return lax.ppermute(x, Z, [(i, to(i)) for i in range(SIZES[1])])
 
     (chip,) = call(chip_map, [wide], [core], keep, got)
-    parts = 2
-    share = HW // 2
-    near_out, far_out = pl.pallas_call(
-        pair_weights,
-        grid_spec=pltpu.PrefetchScalarGridSpec(
-            num_scalar_prefetch=1,
-            grid=(parts,),
-            in_specs=[
-                pl.BlockSpec((share, columns // parts), lambda i, to: (to[1], to[0] * parts + i)),
-                pl.BlockSpec((share, columns // parts), lambda i, to: (to[1] + 2, to[0] * parts + i)),
-                pl.BlockSpec(memory_space=pl.ANY),
-            ],
-            out_specs=[pl.BlockSpec((share, columns // parts), lambda i, to: (0, i))] * 2,
-        ),
-        out_shape=[jax.ShapeDtypeStruct((share, columns), f32)] * 2,
-        compiler_params=pltpu.CompilerParams(vmem_limit_bytes=6 * MIB),
-    )(jnp.concatenate([1 - x_lo, core]), out_weight, out_weight, chip)
+    (own_rows,) = call(shard_rows, [((rows, 4 * HW), f32)], [], queries, keys, rates, solved, later=[chip])
+    near_out = weight_share(out_weight, 1 - x_lo, core, share, f32, chip)
     near = swapped(near_out, (XL,))
+    both, pre = call(
+        join_chips, [wide, wide], [z], chip, across_z(chip, lambda i: i ^ 1), later=[near_out, own_rows], us=2.5
+    )
+    far_out = weight_share(out_weight, 1 - x_lo, core + 2, share, f32, both)
     far = swapped(far_out, (XH, XL))
+    four, pre = call(
+        join_pairs, [wide, wide], [z], both, across_z(both, lambda i: i ^ 2), pre, later=[far_out], us=3
+    )
+    own_half = weight_share(out_weight, x_lo, 0 * core, 2 * HW, bf16, four)
+    end, pre = call(
+        join_ring, [square, wide], [z, core], four, across_z(four, lambda i: 7 - i), pre, first, later=[own_half], us=6
+    )
     near_other, far_other = swapped(near, (CORE,)), swapped(far, (CORE,))
-    own_half = pl.pallas_call(
-        own_weights,
-        grid_spec=pltpu.PrefetchScalarGridSpec(
-            num_scalar_prefetch=1,
-            grid=(4,),
-            in_specs=[
-                pl.BlockSpec((2 * HW, columns // 4), lambda i, to: (0, to[0] * 4 + i)),
-                pl.BlockSpec(memory_space=pl.ANY),
-            ],
-            out_specs=pl.BlockSpec((2 * HW, columns // 4), lambda i, to: (0, i)),
-        ),
-        out_shape=jax.ShapeDtypeStruct((2 * HW, columns), bf16),
-        compiler_params=pltpu.CompilerParams(vmem_limit_bytes=6 * MIB),
-    )(x_lo, out_weight, near_out)
-
-    both, pre = call(join_chips, [wide, wide], [z], chip, across_z(chip, lambda i: i ^ 1), later=[near_out], us=2.5)
-    four, pre = call(join_pairs, [wide, wide], [z], both, across_z(both, lambda i: i ^ 2), pre, later=[own_half], us=2.5)
-    end, pre = call(join_ring, [square, wide], [z], four, across_z(four, lambda i: 7 - i), pre, first, us=2.5)
-    arrived = lax.ppermute(end, XH, [(0, 1)])
-    mine, other = call(shard_prefixes, [wide, wide], [core], pre, keep, got, us=2.5)
-    kept, leaving = call(shard_states, [square, square], [x_hi], mine, other, arrived, first, us=2.5)
-    (z_rows,) = call(outputs, [((rows, 2 * HW), f32)], [core], kept, swapped(leaving, (CORE,)), own_rows)
+    here = lax.ppermute(end, (XH, CORE), [(0, 2), (1, 3)])
+    there = lax.ppermute(end, (XH, CORE), [(0, 3), (1, 2)])
+    mine, other = call(shard_prefixes, [wide, wide], [core], pre, keep, got, us=0.1)
+    (begin,) = call(ring_states, [((2, HW, HW), f32)], [x_hi, core], here, there, first, us=5)
+    (z_rows,) = call(
+        outputs, [((rows, 2 * HW), f32)], [core], mine, swapped(other, (CORE,)), begin, own_rows, us=5
+    )
     z_pair = swapped(z_rows, (XL,))
 
     factors = (z_rows, z_pair, own_half, near, near_other, far, far_other)

time: 111 us -> 112 us (level)
  waiting for transfers between devices: 28.1 us -> 25.2 us
  starting transfers between devices: 68.7 us -> 70.2 us
  Pallas kernels: 10.9 us -> 12.2 us
    ppermute x1 -> x2, starting transfers between devices: 2.1 us -> 5.34 us  [the longest x1 3.5 us: local(): there = lax.ppermute(end, (XH, CORE), [(0, 3), (1, 2)])]
    ppermute x3, waiting for transfers between devices: 9.82 us -> 6.86 us  [across_z(): return lax.ppermute(x, Z, [(i, to(i)) for i in range(SIZES[1])])]
    ppermute x7, starting transfers between devices: 19.6 us -> 18 us  [swapped(): return lax.ppermute(x, axes, [(i, n - 1 - i) for i in range(n)])]
    pallas_call x10 -> x11, Pallas kernels: 8.61 us -> 9.8 us  [call(): pl.pallas_call(body, out_shape=outs, in_specs=[SM] * len(place) + [pl.Blo...]
    unnamed x18 -> x26, local copies, waits for them, and re-layouts: 1.41 us -> 2.39 us
    pallas_call x2 -> x3, Pallas kernels: 2.32 us -> 2.38 us  [weight_share(): pl.pallas_call(copied, grid_spec=pltpu.PrefetchScalarGridSpec(num_scalar_...]
  transfers between devices with their start and end apart: 19 -> 20, of which waited for: 9 -> 8; matrix products, arithmetic and copies ran while one was open for 0% -> 0% of each run, Pallas kernels for 5% -> 6%
where the time goes in v5:
time: 112 us; the launch traced here: 111 us
  starting transfers between devices  70.2 us (63%)
  waiting for transfers between devices  25.2 us (22%)
  Pallas kernels  12.2 us (11%)
  local copies, waits for them, and re-layouts  2.39 us (2%)
    ppermute x8, starting transfers between devices, passed(): return lax.ppermute(x, axis, [(i, (i + by) % n) for i in range(n)])  29.4 us
    ppermute x7, starting transfers between devices, swapped(): return lax.ppermute(x, axes, [(i, n - 1 - i) for i in range(n)])  18 us
    ppermute x3, starting transfers between devices, across_z(): return lax.ppermute(x, Z, [(i, to(i)) for i in range(SIZES[1])])  17.5 us
    ppermute x8, waiting for transfers between devices, passed(): return lax.ppermute(x, axis, [(i, (i + by) % n) for i in range(n)])  11.5 us
    pallas_call x11, Pallas kernels, call(): pl.pallas_call(body, out_shape=outs, in_specs=[SM] * len(place) + [pl.Blo...  9.8 us
    ppermute x3, waiting for transfers between devices, across_z(): return lax.ppermute(x, Z, [(i, to(i)) for i in range(SIZES[1])])  6.86 us
    ppermute x7, waiting for transfers between devices, swapped(): return lax.ppermute(x, axes, [(i, n - 1 - i) for i in range(n)])  6.83 us
    ppermute x1, starting transfers between devices, local(): there = lax.ppermute(end, (XH, CORE), [(0, 3), (1, 2)])  3.5 us
  transfers between devices with their start and end apart: 20, of which 8 were waited for; matrix products, arithmetic and copies ran while one was open for 0% of the time, Pallas kernels for 6%

profile of v5, /device:TPU:2, one launch (start us, length us, event | category | flops | bytes accessed | tf_op | source)
XLA Modules:
  0.0 111.3 jit_solution(16322838323926540720)
XLA Ops:
  0.0 3.0 %shard_map.64 = (f32[128,256]{1,0:T(8,128)S(1)}, f32[128,256]{1,0:T(8,128)S(1)}, f32[2,160,256]{2,1,0:T(8,128)S(1)}, f32[2,128,128]{2,1,0:T(8,128)S(1)}) custom-call(s32[1]{0:T(128)} %bitcast.refs_0_.row_ref.refs_1_, bf16[160,256]{1,0:T(8,128)(2,1)} %refs_1_.3, bf16[160,256]{1,0:T(8,128)(2,1)} %refs_2_.2, f32[2,160]{1,0:T(2,128)} %refs_2_.3, ...), custom_call_target="tpu_custom_call" | custom-call | flops 3000000000 | bytes 131072 | tf_op jit(solution)/shard_map/pallas_call | solution.py:36
  3.0 0.0 copy-start.8
  3.0 0.7 copy-done.8
  3.7 0.6 copy-done.10
  4.4 2.2 %collective-permute-start = (f32[128,256]{1,0:T(8,128)S(1)}, f32[128,256]{1,0:T(8,128)S(1)}, u32[]{:S(2)}, u32[]{:S(2)}) collective-permute-start(f32[128,256]{1,0:T(8,128)S(1)} %get-tuple-element.27), channel_id=1, source_target_pairs={{0,16},{16,0},{1,17},{17,1},{2,18},{18,2},{3,19},{19,3},{4,20},{20... | collective-permute-start | bytes 393224 | tf_op jit(solution)/shard_map/ppermute | solution.py:231
  6.6 1.3 %collective-permute-done.refs_2_.refs_3_ = f32[128,256]{1,0:T(8,128)S(1)} collective-permute-done((f32[128,256]{1,0:T(8,128)S(1)}, f32[128,256]{1,0:T(8,128)S(1)}, u32[]{:S(2)}, u32[]{:S(2)}) %collective-permute-start) | collective-permute-done | bytes 131104 | tf_op jit(solution)/shard_map/ppermute | solution.py:231
  7.9 0.2 shard_map.65.later_ref.refs_4_.refs_1_
  8.1 4.3 %collective-permute-start.1 = (f32[128,256]{1,0:T(8,128)S(1)}, f32[128,256]{1,0:T(8,128)}, u32[]{:S(2)}, u32[]{:S(2)}) collective-permute-start(f32[128,256]{1,0:T(8,128)S(1)} %shard_map.65.later_ref.refs_4_.refs_1_), channel_id=1, source_target_pairs={{0,32},{32,0},{64,96},{96,64},{128,160},{160,128},{192,224},{224,1... | collective-permute-start | bytes 393224 | tf_op jit(solution)/shard_map/ppermute | solution.py:257
  12.4 0.0 copy-start.3
  12.4 0.0 copy-start.4
  12.4 0.0 copy-start.9
  12.4 1.0 shard_map.66.refs_3_
  13.4 0.0 copy-done.4
  13.4 0.1 copy-done.9
  13.5 0.4 shard_map.67.refs_4_
  13.9 0.0 copy-start.6
  13.9 2.4 %collective-permute-done.1.refs_2_ = f32[128,256]{1,0:T(8,128)} collective-permute-done((f32[128,256]{1,0:T(8,128)S(1)}, f32[128,256]{1,0:T(8,128)}, u32[]{:S(2)}, u32[]{:S(2)}) %collective-permute-start.1) | collective-permute-done | bytes 131104 | tf_op jit(solution)/shard_map/ppermute | solution.py:257
  16.3 1.1 %shard_map.68 = (f32[128,256]{1,0:T(8,128)S(1)}, f32[128,256]{1,0:T(8,128)S(1)}) custom-call(s32[1]{0:T(128)} %bitcast.2.refs_0_, f32[128,256]{1,0:T(8,128)S(1)} %shard_map.65.later_ref.refs_4_.refs_1_, f32[128,256]{1,0:T(8,128)} %collective-permute-done.1.refs_2_, f32[64,3072]{1,0:T(8,128)} %shard_map.66.refs_3_, f32[160,512]{1,0:T(8,128)S(1)} %shard_map.67.refs_4_), custom_call_target="tpu_custom_call" | custom-call | flops 2500000000 | bytes 131072 | tf_op jit(solution)/shard_map/pallas_call | solution.py:36
  17.4 6.1 %collective-permute-start.2 = (f32[128,256]{1,0:T(8,128)S(1)}, f32[128,256]{1,0:T(8,128)S(1)}, u32[]{:S(2)}, u32[]{:S(2)}) collective-permute-start(f32[128,256]{1,0:T(8,128)S(1)} %get-tuple-element.29.later_ref.refs_1_), channel_id=1, source_target_pairs={{0,64},{32,96},{64,0},{96,32},{128,192},{160,224},{192,128},{224,1... | collective-permute-start | bytes 393224 | tf_op jit(solution)/shard_map/ppermute | solution.py:257
  23.5 3.0 %collective-permute-start.8 = (f32[64,3072]{1,0:T(8,128)}, f32[64,3072]{1,0:T(8,128)}, u32[]{:S(2)}, u32[]{:S(2)}) collective-permute-start(f32[64,3072]{1,0:T(8,128)} %shard_map.66.refs_3_), channel_id=1, source_target_pairs={{0,8},{8,0},{1,9},{9,1},{2,10},{10,2},{3,11},{11,3},{4,12},{12,4},... | collective-permute-start | bytes 2359304 | tf_op jit(solution)/shard_map/ppermute | solution.py:231
  26.5 1.0 shard_map.69.refs_4_
  27.5 3.5 %collective-permute-start.10 = (f32[64,3072]{1,0:T(8,128)}, f32[64,3072]{1,0:T(8,128)}, u32[]{:S(2)}, u32[]{:S(2)}) collective-permute-start(f32[64,3072]{1,0:T(8,128)} %shard_map.69.refs_4_), channel_id=1, source_target_pairs={{0,264},{8,256},{256,8},{264,0},{1,265},{9,257},{257,9},{265,1},{2... | collective-permute-start | bytes 2359304 | tf_op jit(solution)/shard_map/ppermute | solution.py:231
  31.0 0.0 collective-permute-done.2.refs_2_
  31.0 0.3 shard_map.70
  31.3 7.1 %collective-permute-start.3 = (f32[128,256]{1,0:T(8,128)S(1)}, f32[128,256]{1,0:T(8,128)S(1)}, u32[]{:S(2)}, u32[]{:S(2)}) collective-permute-start(f32[128,256]{1,0:T(8,128)S(1)} %get-tuple-element.31.later_ref.refs_2_), channel_id=1, source_target_pairs={{0,224},{32,192},{64,160},{96,128},{128,96},{160,64},{192,32},{224... | collective-permute-start | bytes 393224 | tf_op jit(solution)/shard_map/ppermute | solution.py:257
  38.4 0.4 shard_map.71.refs_6_.refs_4_
  38.9 4.5 %collective-permute-done.3.refs_3_ = f32[128,256]{1,0:T(8,128)S(1)} collective-permute-done((f32[128,256]{1,0:T(8,128)S(1)}, f32[128,256]{1,0:T(8,128)S(1)}, u32[]{:S(2)}, u32[]{:S(2)}) %collective-permute-start.3) | collective-permute-done | bytes 131104 | tf_op jit(solution)/shard_map/ppermute | solution.py:257
  43.4 0.4 shard_map.72
  43.8 3.5 %collective-permute-start.6 = (f32[128,128]{1,0:T(8,128)S(1)}, f32[128,128]{1,0:T(8,128)S(1)}, u32[]{:S(2)}, u32[]{:S(2)}) collective-permute-start(f32[128,128]{1,0:T(8,128)S(1)} %get-tuple-element.37), channel_id=1, source_target_pairs={{0,272},{16,256},{1,273},{17,257},{2,274},{18,258},{3,275},{19,259... | collective-permute-start | bytes 196616 | tf_op jit(solution)/shard_map/ppermute | solution.py:277
  47.3 1.8 %collective-permute-start.5 = (f32[128,128]{1,0:T(8,128)S(1)}, f32[128,128]{1,0:T(8,128)S(1)}, u32[]{:S(2)}, u32[]{:S(2)}) collective-permute-start(f32[128,128]{1,0:T(8,128)S(1)} %get-tuple-element.37), channel_id=1, source_target_pairs={{0,256},{16,272},{1,257},{17,273},{2,258},{18,274},{3,259},{19,275... | collective-permute-start | bytes 196616 | tf_op jit(solution)/shard_map/ppermute | solution.py:276
  49.1 0.2 shard_map.73
  49.3 2.0 %collective-permute-start.4 = (f32[128,256]{1,0:T(8,128)S(1)}, f32[128,256]{1,0:T(8,128)S(1)}, u32[]{:S(2)}, u32[]{:S(2)}) collective-permute-start(f32[128,256]{1,0:T(8,128)S(1)} %get-tuple-element.36), channel_id=1, source_target_pairs={{0,16},{16,0},{1,17},{17,1},{2,18},{18,2},{3,19},{19,3},{4,20},{20... | collective-permute-start | bytes 393224 | tf_op jit(solution)/shard_map/ppermute | solution.py:231
  51.4 0.0 collective-permute-done.8.refs_5_
  51.4 2.3 %collective-permute-start.9 = (f32[64,3072]{1,0:T(8,128)}, f32[64,3072]{1,0:T(8,128)S(1)}, u32[]{:S(2)}, u32[]{:S(2)}) collective-permute-start(f32[64,3072]{1,0:T(8,128)} %collective-permute-done.8.refs_5_), channel_id=1, source_target_pairs={{0,16},{16,0},{1,17},{17,1},{2,18},{18,2},{3,19},{19,3},{4,20},{20... | collective-permute-start | bytes 2359304 | tf_op jit(solution)/shard_map/ppermute | solution.py:231
  53.7 0.0 collective-permute-done.10.refs_7_
  53.7 2.0 %collective-permute-start.11 = (f32[64,3072]{1,0:T(8,128)}, f32[64,3072]{1,0:T(8,128)S(1)}, u32[]{:S(2)}, u32[]{:S(2)}) collective-permute-start(f32[64,3072]{1,0:T(8,128)} %collective-permute-done.10.refs_7_), channel_id=1, source_target_pairs={{0,16},{16,0},{1,17},{17,1},{2,18},{18,2},{3,19},{19,3},{4,20},{20... | collective-permute-start | bytes 2359304 | tf_op jit(solution)/shard_map/ppermute | solution.py:231
  55.7 0.0 collective-permute-done.6.refs_3_
  55.7 0.0 collective-permute-done.5.refs_2_
  55.8 0.0 collective-permute-done.4.refs_2_
  55.8 0.9 copy-done.7
  56.7 0.4 shard_map.75.refs_2_
  57.1 3.0 %collective-permute-start.7 = (f32[160,256]{1,0:T(8,128)S(1)}, f32[160,256]{1,0:T(8,128)S(1)}, u32[]{:S(2)}, u32[]{:S(2)}) collective-permute-start(f32[160,256]{1,0:T(8,128)S(1)} %shard_map.75.refs_2_), channel_id=1, source_target_pairs={{0,8},{8,0},{1,9},{9,1},{2,10},{10,2},{3,11},{11,3},{4,12},{12,4},... | collective-permute-start | bytes 491528 | tf_op jit(solution)/shard_map/ppermute | solution.py:231
  60.2 5.5 %collective-permute-done.7.refs_3_ = f32[160,256]{1,0:T(8,128)S(1)} collective-permute-done((f32[160,256]{1,0:T(8,128)S(1)}, f32[160,256]{1,0:T(8,128)S(1)}, u32[]{:S(2)}, u32[]{:S(2)}) %collective-permute-start.7) | collective-permute-done | bytes 163872 | tf_op jit(solution)/shard_map/ppermute | solution.py:231
  65.7 0.0 collective-permute-done.9.refs_6_
  65.7 0.0 collective-permute-done.11.refs_8_
  65.7 1.6 %shard_map.76 = (f32[80,384]{1,0:T(8,128)S(1)}, f32[80,384]{1,0:T(8,128)S(1)}) custom-call(s32[1]{0:T(128)} %bitcast.refs_0_.row_ref.refs_1_, s32[1]{0:T(128)} %bitcast.1.refs_1_, f32[160,256]{1,0:T(8,128)S(1)} %shard_map.75.refs_2_, f32[160,256]{1,0:T(8,128)S(1)} %collective-permute-done.7.refs_3_, bf16[256,3072]{1,0:T(8,128)(2,1)S(1)} %copy-done.2, ...), custom_call_target="tpu_custom_call" | custom-call | flops 1000000000 | bytes 131072 | tf_op jit(solution)/shard_map/pallas_call | solution.py:36
  67.3 5.4 %collective-permute-start.12 = (f32[80,384]{1,0:T(8,128)S(1)}, f32[80,384]{1,0:T(8,128)S(1)}, u32[]{:S(2)}, u32[]{:S(2)}) collective-permute-start(f32[80,384]{1,0:T(8,128)S(1)} %get-tuple-element.38.refs_9_), channel_id=1, source_target_pairs={{0,7},{1,0},{2,1},{3,2},{4,3},{5,4},{6,5},{7,6},{8,15},{9,8},{10,9... | collective-permute-start | bytes 368648 | tf_op jit(solution)/shard_map/ppermute | solution.py:236
  72.7 1.9 %collective-permute-start.16 = (f32[80,384]{1,0:T(8,128)S(1)}, f32[80,384]{1,0:T(8,128)S(1)}, u32[]{:S(2)}, u32[]{:S(2)}) collective-permute-start(f32[80,384]{1,0:T(8,128)S(1)} %get-tuple-element.43), channel_id=1, source_target_pairs={{0,1},{1,2},{2,3},{3,4},{4,5},{5,6},{6,7},{7,0},{8,9},{9,10},{10,1... | collective-permute-start | bytes 368648 | tf_op jit(solution)/shard_map/ppermute | solution.py:236
  74.6 2.2 %shard_map.77 = (f32[160,384]{1,0:T(8,128)S(1)}, f32[160,384]{1,0:T(8,128)S(1)}, f32[160,384]{1,0:T(8,128)S(1)}, f32[160,384]{1,0:T(8,128)S(1)}, f32[160,384]{1,...) custom-call(s32[1]{0:T(128)} %bitcast.refs_0_.row_ref.refs_1_, s32[1]{0:T(128)} %bitcast.1.refs_1_, ...), custom_call_target="tpu_custom_call" | custom-call | flops 1000000000 | bytes 131072 | tf_op jit(solution)/shard_map/pallas_call | solution.py:36
  76.8 0.0 collective-permute-done.12
  76.8 5.1 %collective-permute-start.13 = (f32[160,384]{1,0:T(8,128)S(1)}, f32[160,384]{1,0:T(8,128)S(1)}, u32[]{:S(2)}, u32[]{:S(2)}) collective-permute-start(f32[160,384]{1,0:T(8,128)S(1)} %pad_add_fusion.1), channel_id=1, source_target_pairs={{0,7},{1,0},{2,1},{3,2},{4,3},{5,4},{6,5},{7,6},{8,15},{9,8},{10,9... | collective-permute-start | bytes 737288 | tf_op jit(solution)/shard_map/ppermute | solution.py:236
  82.0 0.0 collective-permute-done.16
  82.0 1.9 %collective-permute-start.17 = (f32[160,384]{1,0:T(8,128)S(1)}, f32[160,384]{1,0:T(8,128)S(1)}, u32[]{:S(2)}, u32[]{:S(2)}) collective-permute-start(f32[160,384]{1,0:T(8,128)S(1)} %pad_add_fusion), channel_id=1, source_target_pairs={{0,1},{1,2},{2,3},{3,4},{4,5},{5,6},{6,7},{7,0},{8,9},{9,10},{10,1... | collective-permute-start | bytes 737288 | tf_op jit(solution)/shard_map/ppermute | solution.py:236
  83.9 2.4 %collective-permute-done.13 = f32[160,384]{1,0:T(8,128)S(1)} collective-permute-done((f32[160,384]{1,0:T(8,128)S(1)}, f32[160,384]{1,0:T(8,128)S(1)}, u32[]{:S(2)}, u32[]{:S(2)}) %collective-permute-start.13) | collective-permute-done | bytes 245792 | tf_op jit(solution)/shard_map/ppermute | solution.py:236
  86.3 5.6 %collective-permute-start.14 = (f32[160,384]{1,0:T(8,128)S(1)}, f32[160,384]{1,0:T(8,128)S(1)}, u32[]{:S(2)}, u32[]{:S(2)}) collective-permute-start(f32[160,384]{1,0:T(8,128)S(1)} %add.33), channel_id=1, source_target_pairs={{0,7},{1,0},{2,1},{3,2},{4,3},{5,4},{6,5},{7,6},{8,15},{9,8},{10,9... | collective-permute-start | bytes 737288 | tf_op jit(solution)/shard_map/ppermute | solution.py:236
  92.0 0.0 collective-permute-done.17
  92.0 1.9 %collective-permute-start.18 = (f32[160,384]{1,0:T(8,128)S(1)}, f32[160,384]{1,0:T(8,128)S(1)}, u32[]{:S(2)}, u32[]{:S(2)}) collective-permute-start(f32[160,384]{1,0:T(8,128)S(1)} %add.36), channel_id=1, source_target_pairs={{0,1},{1,2},{2,3},{3,4},{4,5},{5,6},{6,7},{7,0},{8,9},{9,10},{10,1... | collective-permute-start | bytes 737288 | tf_op jit(solution)/shard_map/ppermute | solution.py:236
  93.9 1.7 %collective-permute-done.14 = f32[160,384]{1,0:T(8,128)S(1)} collective-permute-done((f32[160,384]{1,0:T(8,128)S(1)}, f32[160,384]{1,0:T(8,128)S(1)}, u32[]{:S(2)}, u32[]{:S(2)}) %collective-permute-start.14) | collective-permute-done | bytes 245792 | tf_op jit(solution)/shard_map/ppermute | solution.py:236
  95.7 5.6 %collective-permute-start.15 = (f32[160,384]{1,0:T(8,128)S(1)}, f32[160,384]{1,0:T(8,128)S(1)}, u32[]{:S(2)}, u32[]{:S(2)}) collective-permute-start(f32[160,384]{1,0:T(8,128)S(1)} %add.34), channel_id=1, source_target_pairs={{0,7},{1,0},{2,1},{3,2},{4,3},{5,4},{6,5},{7,6},{8,15},{9,8},{10,9... | collective-permute-start | bytes 737288 | tf_op jit(solution)/shard_map/ppermute | solution.py:236
  101.3 0.0 collective-permute-done.18
  101.3 1.9 %collective-permute-start.19 = (f32[160,384]{1,0:T(8,128)S(1)}, f32[160,384]{1,0:T(8,128)S(1)}, u32[]{:S(2)}, u32[]{:S(2)}) collective-permute-start(f32[160,384]{1,0:T(8,128)S(1)} %add.37), channel_id=1, source_target_pairs={{0,1},{1,2},{2,3},{3,4},{4,5},{5,6},{6,7},{7,0},{8,9},{9,10},{10,1... | collective-permute-start | bytes 737288 | tf_op jit(solution)/shard_map/ppermute | solution.py:236
  103.3 1.7 %collective-permute-done.15 = f32[160,384]{1,0:T(8,128)S(1)} collective-permute-done((f32[160,384]{1,0:T(8,128)S(1)}, f32[160,384]{1,0:T(8,128)S(1)}, u32[]{:S(2)}, u32[]{:S(2)}) %collective-permute-start.15) | collective-permute-done | bytes 245792 | tf_op jit(solution)/shard_map/ppermute | solution.py:236
  105.0 5.7 %collective-permute-done.19 = f32[160,384]{1,0:T(8,128)S(1)} collective-permute-done((f32[160,384]{1,0:T(8,128)S(1)}, f32[160,384]{1,0:T(8,128)S(1)}, u32[]{:S(2)}, u32[]{:S(2)}) %collective-permute-start.19) | collective-permute-done | bytes 245792 | tf_op jit(solution)/shard_map/ppermute | solution.py:236
  110.6 0.7 add_convert_fusion
  (23 shorter events, 0.2 us)
Async XLA Ops:
  3.0 0.7 copy-start.8
  3.7 0.6 copy-start.10
  4.4 8.0 %copy-start = (bf16[256,6144]{1,0:T(8,128)(2,1)S(1)}, bf16[256,6144]{1,0:T(8,128)(2,1)}, u32[]{:S(2)}) copy-start(bf16[256,6144]{1,0:T(8,128)(2,1)} %w_ref.5) | copy-start | bytes 9437188
  4.4 3.5 %collective-permute-start = (f32[128,256]{1,0:T(8,128)S(1)}, f32[128,256]{1,0:T(8,128)S(1)}, u32[]{:S(2)}, u32[]{:S(2)}) collective-permute-start(f32[128,256]{1,0:T(8,128)S(1)} %get-tuple-element.27), channel_id=1, source_target_pairs={{0,16},{16,0},{1,17},{17,1},{2,18},{18,2},{3,19},{19,3},{4,20},{20... | collective-permute-start | bytes 393224 | tf_op jit(solution)/shard_map/ppermute | solution.py:231
  7.9 5.5 %copy-start.5 = (f32[2,160]{1,0:T(2,128)S(1)}, f32[2,160]{1,0:T(2,128)}, u32[]{:S(2)}) copy-start(f32[2,160]{1,0:T(2,128)} %refs_2_.3) | copy-start | bytes 3844
  8.1 8.2 %collective-permute-start.1 = (f32[128,256]{1,0:T(8,128)S(1)}, f32[128,256]{1,0:T(8,128)}, u32[]{:S(2)}, u32[]{:S(2)}) collective-permute-start(f32[128,256]{1,0:T(8,128)S(1)} %shard_map.65.later_ref.refs_4_.refs_1_), channel_id=1, source_target_pairs={{0,32},{32,0},{64,96},{96,64},{128,160},{160,128},{192,224},{224,1... | collective-permute-start | bytes 393224 | tf_op jit(solution)/shard_map/ppermute | solution.py:257
  12.4 1.0 copy-start.3
  12.4 1.0 copy-start.4
  12.4 1.1 copy-start.9
  13.9 3.5 %copy-start.6 = (f32[160,512]{1,0:T(8,128)}, f32[160,512]{1,0:T(8,128)S(1)}, u32[]{:S(2)}) copy-start(f32[160,512]{1,0:T(8,128)S(1)} %shard_map.67.refs_4_) | copy-start | bytes 983044
  17.4 13.6 %collective-permute-start.2 = (f32[128,256]{1,0:T(8,128)S(1)}, f32[128,256]{1,0:T(8,128)S(1)}, u32[]{:S(2)}, u32[]{:S(2)}) collective-permute-start(f32[128,256]{1,0:T(8,128)S(1)} %get-tuple-element.29.later_ref.refs_1_), channel_id=1, source_target_pairs={{0,64},{32,96},{64,0},{96,32},{128,192},{160,224},{192,128},{224,1... | collective-permute-start | bytes 393224 | tf_op jit(solution)/shard_map/ppermute | solution.py:257
  23.5 27.9 %collective-permute-start.8 = (f32[64,3072]{1,0:T(8,128)}, f32[64,3072]{1,0:T(8,128)}, u32[]{:S(2)}, u32[]{:S(2)}) collective-permute-start(f32[64,3072]{1,0:T(8,128)} %shard_map.66.refs_3_), channel_id=1, source_target_pairs={{0,8},{8,0},{1,9},{9,1},{2,10},{10,2},{3,11},{11,3},{4,12},{12,4},... | collective-permute-start | bytes 2359304 | tf_op jit(solution)/shard_map/ppermute | solution.py:231
  27.5 26.2 %collective-permute-start.10 = (f32[64,3072]{1,0:T(8,128)}, f32[64,3072]{1,0:T(8,128)}, u32[]{:S(2)}, u32[]{:S(2)}) collective-permute-start(f32[64,3072]{1,0:T(8,128)} %shard_map.69.refs_4_), channel_id=1, source_target_pairs={{0,264},{8,256},{256,8},{264,0},{1,265},{9,257},{257,9},{265,1},{2... | collective-permute-start | bytes 2359304 | tf_op jit(solution)/shard_map/ppermute | solution.py:231
  31.3 12.1 %copy-start.11 = (f32[2,128,128]{2,1,0:T(8,128)S(1)}, f32[2,128,128]{2,1,0:T(8,128)}, u32[]{:S(2)}) copy-start(f32[2,128,128]{2,1,0:T(8,128)} %copy-done.10) | copy-start | bytes 393220
  31.3 12.0 %collective-permute-start.3 = (f32[128,256]{1,0:T(8,128)S(1)}, f32[128,256]{1,0:T(8,128)S(1)}, u32[]{:S(2)}, u32[]{:S(2)}) collective-permute-start(f32[128,256]{1,0:T(8,128)S(1)} %get-tuple-element.31.later_ref.refs_2_), channel_id=1, source_target_pairs={{0,224},{32,192},{64,160},{96,128},{128,96},{160,64},{192,32},{224... | collective-permute-start | bytes 393224 | tf_op jit(solution)/shard_map/ppermute | solution.py:257
  38.8 4.9 %copy-start.1 = (bf16[256,3072]{1,0:T(8,128)(2,1)}, bf16[256,3072]{1,0:T(8,128)(2,1)S(1)}, u32[]{:S(2)}) copy-start(bf16[256,3072]{1,0:T(8,128)(2,1)S(1)} %shard_map.71.refs_6_.refs_4_) | copy-start | bytes 4718596
  43.4 12.4 %copy-start.12 = (f32[2,128,128]{2,1,0:T(8,128)S(1)}, f32[2,128,128]{2,1,0:T(8,128)}, u32[]{:S(2)}) copy-start(f32[2,128,128]{2,1,0:T(8,128)} %copy-done.10) | copy-start | bytes 393220
  43.8 12.0 %collective-permute-start.6 = (f32[128,128]{1,0:T(8,128)S(1)}, f32[128,128]{1,0:T(8,128)S(1)}, u32[]{:S(2)}, u32[]{:S(2)}) collective-permute-start(f32[128,128]{1,0:T(8,128)S(1)} %get-tuple-element.37), channel_id=1, source_target_pairs={{0,272},{16,256},{1,273},{17,257},{2,274},{18,258},{3,275},{19,259... | collective-permute-start | bytes 196616 | tf_op jit(solution)/shard_map/ppermute | solution.py:277
  47.3 8.5 %collective-permute-start.5 = (f32[128,128]{1,0:T(8,128)S(1)}, f32[128,128]{1,0:T(8,128)S(1)}, u32[]{:S(2)}, u32[]{:S(2)}) collective-permute-start(f32[128,128]{1,0:T(8,128)S(1)} %get-tuple-element.37), channel_id=1, source_target_pairs={{0,256},{16,272},{1,257},{17,273},{2,258},{18,274},{3,259},{19,275... | collective-permute-start | bytes 196616 | tf_op jit(solution)/shard_map/ppermute | solution.py:276
  49.3 6.5 %collective-permute-start.4 = (f32[128,256]{1,0:T(8,128)S(1)}, f32[128,256]{1,0:T(8,128)S(1)}, u32[]{:S(2)}, u32[]{:S(2)}) collective-permute-start(f32[128,256]{1,0:T(8,128)S(1)} %get-tuple-element.36), channel_id=1, source_target_pairs={{0,16},{16,0},{1,17},{17,1},{2,18},{18,2},{3,19},{19,3},{4,20},{20... | collective-permute-start | bytes 393224 | tf_op jit(solution)/shard_map/ppermute | solution.py:231
  51.4 14.3 %collective-permute-start.9 = (f32[64,3072]{1,0:T(8,128)}, f32[64,3072]{1,0:T(8,128)S(1)}, u32[]{:S(2)}, u32[]{:S(2)}) collective-permute-start(f32[64,3072]{1,0:T(8,128)} %collective-permute-done.8.refs_5_), channel_id=1, source_target_pairs={{0,16},{16,0},{1,17},{17,1},{2,18},{18,2},{3,19},{19,3},{4,20},{20... | collective-permute-start | bytes 2359304 | tf_op jit(solution)/shard_map/ppermute | solution.py:231
  53.7 12.0 %collective-permute-start.11 = (f32[64,3072]{1,0:T(8,128)}, f32[64,3072]{1,0:T(8,128)S(1)}, u32[]{:S(2)}, u32[]{:S(2)}) collective-permute-start(f32[64,3072]{1,0:T(8,128)} %collective-permute-done.10.refs_7_), channel_id=1, source_target_pairs={{0,16},{16,0},{1,17},{17,1},{2,18},{18,2},{3,19},{19,3},{4,20},{20... | collective-permute-start | bytes 2359304 | tf_op jit(solution)/shard_map/ppermute | solution.py:231
  55.8 1.0 copy-start.7
  56.7 8.9 %copy-start.2 = (bf16[256,3072]{1,0:T(8,128)(2,1)S(1)}, bf16[256,3072]{1,0:T(8,128)(2,1)}, u32[]{:S(2)}) copy-start(bf16[256,3072]{1,0:T(8,128)(2,1)} %copy-done.1) | copy-start | bytes 4718596
  57.1 8.5 %collective-permute-start.7 = (f32[160,256]{1,0:T(8,128)S(1)}, f32[160,256]{1,0:T(8,128)S(1)}, u32[]{:S(2)}, u32[]{:S(2)}) collective-permute-start(f32[160,256]{1,0:T(8,128)S(1)} %shard_map.75.refs_2_), channel_id=1, source_target_pairs={{0,8},{8,0},{1,9},{9,1},{2,10},{10,2},{3,11},{11,3},{4,12},{12,4},... | collective-permute-start | bytes 491528 | tf_op jit(solution)/shard_map/ppermute | solution.py:231
  67.3 9.5 %collective-permute-start.12 = (f32[80,384]{1,0:T(8,128)S(1)}, f32[80,384]{1,0:T(8,128)S(1)}, u32[]{:S(2)}, u32[]{:S(2)}) collective-permute-start(f32[80,384]{1,0:T(8,128)S(1)} %get-tuple-element.38.refs_9_), channel_id=1, source_target_pairs={{0,7},{1,0},{2,1},{3,2},{4,3},{5,4},{6,5},{7,6},{8,15},{9,8},{10,9... | collective-permute-start | bytes 368648 | tf_op jit(solution)/shard_map/ppermute | solution.py:236
  72.7 9.3 %collective-permute-start.16 = (f32[80,384]{1,0:T(8,128)S(1)}, f32[80,384]{1,0:T(8,128)S(1)}, u32[]{:S(2)}, u32[]{:S(2)}) collective-permute-start(f32[80,384]{1,0:T(8,128)S(1)} %get-tuple-element.43), channel_id=1, source_target_pairs={{0,1},{1,2},{2,3},{3,4},{4,5},{5,6},{6,7},{7,0},{8,9},{9,10},{10,1... | collective-permute-start | bytes 368648 | tf_op jit(solution)/shard_map/ppermute | solution.py:236
  76.8 9.5 %collective-permute-start.13 = (f32[160,384]{1,0:T(8,128)S(1)}, f32[160,384]{1,0:T(8,128)S(1)}, u32[]{:S(2)}, u32[]{:S(2)}) collective-permute-start(f32[160,384]{1,0:T(8,128)S(1)} %pad_add_fusion.1), channel_id=1, source_target_pairs={{0,7},{1,0},{2,1},{3,2},{4,3},{5,4},{6,5},{7,6},{8,15},{9,8},{10,9... | collective-permute-start | bytes 737288 | tf_op jit(solution)/shard_map/ppermute | solution.py:236
  82.0 10.0 %collective-permute-start.17 = (f32[160,384]{1,0:T(8,128)S(1)}, f32[160,384]{1,0:T(8,128)S(1)}, u32[]{:S(2)}, u32[]{:S(2)}) collective-permute-start(f32[160,384]{1,0:T(8,128)S(1)} %pad_add_fusion), channel_id=1, source_target_pairs={{0,1},{1,2},{2,3},{3,4},{4,5},{5,6},{6,7},{7,0},{8,9},{9,10},{10,1... | collective-permute-start | bytes 737288 | tf_op jit(solution)/shard_map/ppermute | solution.py:236
  86.3 9.3 %collective-permute-start.14 = (f32[160,384]{1,0:T(8,128)S(1)}, f32[160,384]{1,0:T(8,128)S(1)}, u32[]{:S(2)}, u32[]{:S(2)}) collective-permute-start(f32[160,384]{1,0:T(8,128)S(1)} %add.33), channel_id=1, source_target_pairs={{0,7},{1,0},{2,1},{3,2},{4,3},{5,4},{6,5},{7,6},{8,15},{9,8},{10,9... | collective-permute-start | bytes 737288 | tf_op jit(solution)/shard_map/ppermute | solution.py:236
  92.0 9.3 %collective-permute-start.18 = (f32[160,384]{1,0:T(8,128)S(1)}, f32[160,384]{1,0:T(8,128)S(1)}, u32[]{:S(2)}, u32[]{:S(2)}) collective-permute-start(f32[160,384]{1,0:T(8,128)S(1)} %add.36), channel_id=1, source_target_pairs={{0,1},{1,2},{2,3},{3,4},{4,5},{5,6},{6,7},{7,0},{8,9},{9,10},{10,1... | collective-permute-start | bytes 737288 | tf_op jit(solution)/shard_map/ppermute | solution.py:236
  95.7 9.3 %collective-permute-start.15 = (f32[160,384]{1,0:T(8,128)S(1)}, f32[160,384]{1,0:T(8,128)S(1)}, u32[]{:S(2)}, u32[]{:S(2)}) collective-permute-start(f32[160,384]{1,0:T(8,128)S(1)} %add.34), channel_id=1, source_target_pairs={{0,7},{1,0},{2,1},{3,2},{4,3},{5,4},{6,5},{7,6},{8,15},{9,8},{10,9... | collective-permute-start | bytes 737288 | tf_op jit(solution)/shard_map/ppermute | solution.py:236
  101.3 9.3 %collective-permute-start.19 = (f32[160,384]{1,0:T(8,128)S(1)}, f32[160,384]{1,0:T(8,128)S(1)}, u32[]{:S(2)}, u32[]{:S(2)}) collective-permute-start(f32[160,384]{1,0:T(8,128)S(1)} %add.37), channel_id=1, source_target_pairs={{0,1},{1,2},{2,3},{3,4},{4,5},{5,6},{6,7},{7,0},{8,9},{9,10},{10,1... | collective-permute-start | bytes 737288 | tf_op jit(solution)/shard_map/ppermute | solution.py:236

commit v6 on v5

v6 whole, which is shorter than its diff:
```python
import jax
import jax.numpy as jnp
from jax import lax
from jax.experimental import pallas as pl
from jax.experimental.pallas import tpu as pltpu
from jax.sharding import Mesh, PartitionSpec as P

MB = 16
HW = 128
XH, Z, CORE, XL, Y = "xh", "z", "core", "xl", "y"
SIZES = (2, 8, 2, 2, 8)
f32 = jnp.float32
bf16 = jnp.bfloat16
VM = pl.BlockSpec(memory_space=pltpu.VMEM)
SM = pl.BlockSpec(memory_space=pltpu.SMEM)
MIB = 2**20


def exact(a, b, contract=((1,), (0,))):
    return lax.dot_general(
        a, b, (contract, ((), ())), precision=lax.Precision.HIGH, preferred_element_type=f32
    )


def single(a, b, contract=((1,), (0,))):
    return lax.dot_general(a, b, (contract, ((), ())), preferred_element_type=f32)


def call(kernel, out_shapes, place, *args, later=(), scratch=(), limit=4, us=1.0, space=pltpu.VMEM, pinned=False):
    outs = [pltpu.VMEM(s, d) if pinned else jax.ShapeDtypeStruct(s, d) for s, d in out_shapes]
    n = len(place) + len(args)

    def body(*refs):
        kernel(*refs[:n], *refs[n + len(later) :])

    return pl.pallas_call(
        body,
        name=kernel.__name__,
        out_shape=outs,
        in_specs=[SM] * len(place) + [pl.BlockSpec(memory_space=space)] * len(args) + [pl.BlockSpec(memory_space=pl.ANY)] * len(later),
        out_specs=[VM] * len(outs),
        scratch_shapes=list(scratch),
        compiler_params=pltpu.CompilerParams(vmem_limit_bytes=limit * MIB),
        cost_estimate=pl.CostEstimate(flops=int(us * 1e9), bytes_accessed=1 << 17, transcendentals=0),
    )(*place, *(pltpu.with_memory_space_constraint(x, space) for x in args), *later)


def left_half(shape):
    return lax.broadcasted_iota(jnp.int32, shape, 1) < HW


def identity(columns):
    rows_at = lax.broadcasted_iota(jnp.int32, (HW, columns), 0)
    return (rows_at == lax.broadcasted_iota(jnp.int32, (HW, columns), 1)).astype(f32)


def after(second, first):
    return exact(second[:, :HW], first) + jnp.where(left_half(second.shape), 0.0, second)


def applied(pair, state):
    return exact(pair[:, :HW], state) + pair[:, HW:]


def gathered(copies):
    for copy in copies:
        copy.start()
    return copies


def shard_maps(core_ref, k_hbm, v_hbm, r_hbm, keep_ref, send_ref, x_ref, k_ref, v_ref, r_ref, *done):
    copies = gathered(
        [
            pltpu.make_async_copy(source, target, semaphore)
            for source, target, semaphore in zip(
                (k_hbm, v_hbm, r_hbm), (k_ref, v_ref, r_ref), done
            )
        ]
    )
    rows = k_ref.shape[0]
    s_at = lax.broadcasted_iota(jnp.int32, (rows, rows), 0)
    t_at = lax.broadcasted_iota(jnp.int32, (rows, rows), 1)
    earlier_block = (t_at // MB) < (s_at // MB)
    diagonal = t_at == s_at
    key_gram, columns = [], []
    for copy in copies:
        copy.wait()
    for h in range(2):
        at = slice(h * HW, (h + 1) * HW)
        k, r = k_ref[:, at], r_ref[h : h + 1, :]
        columns.append(jnp.sum(jnp.where(diagonal, r, 0.0), axis=1, keepdims=True))
        key_gram.append(jnp.where(earlier_block, single(k, k, ((1,), (1,))) * r, 0.0))
        x_ref[h, :, :HW] = k.astype(f32)
        x_ref[h, :, HW:] = v_ref[:, at].astype(f32)
    for i in range(1, rows // MB):
        at = slice(i * MB, (i + 1) * MB)
        for h in range(2):
            x_ref[h, at, :] = x_ref[h, at, :] - exact(key_gram[h][at, :], x_ref[h])
    maps = []
    for h in range(2):
        at = slice(h * HW, (h + 1) * HW)
        ab = exact(k_ref[:, at].astype(f32) * columns[h], x_ref[h], ((0,), (0,)))
        maps.append(identity(2 * HW) + jnp.where(left_half(ab.shape), -ab, ab))
    first = core_ref[0] == 0
    keep_ref[...] = jnp.where(first, maps[0], maps[1])
    send_ref[...] = jnp.where(first, maps[1], maps[0])


def shard_rows(q_ref, k_ref, r_ref, x_ref, rows_ref, token_ref):
    token_ref[...] = jnp.zeros_like(token_ref)
    rows = q_ref.shape[0]
    s_at = lax.broadcasted_iota(jnp.int32, (rows, rows), 0)
    t_at = lax.broadcasted_iota(jnp.int32, (rows, rows), 1)
    for h in range(2):
        at = slice(h * HW, (h + 1) * HW)
        q = q_ref[:, at]
        mix = jnp.where(t_at <= s_at, single(q, k_ref[:, at], ((1,), (1,))) * r_ref[h : h + 1, :], 0.0)
        y = exact(mix, x_ref[h])
        rows_ref[:, at] = q.astype(f32) - y[:, :HW]
        rows_ref[:, (2 + h) * HW : (3 + h) * HW] = y[:, HW:]


def in_order(first_core, keep_ref, got_ref):
    keep, got = keep_ref[...], got_ref[...]
    return jnp.where(first_core, keep, got), jnp.where(first_core, got, keep)


def chip_map(core_ref, keep_ref, got_ref, out_ref):
    early, late = in_order(core_ref[0] == 0, keep_ref, got_ref)
    out_ref[...] = after(late, early)


def first_map(core_ref, keep_ref, got_ref, out_ref):
    out_ref[...] = in_order(core_ref[0] == 0, keep_ref, got_ref)[0]


def is_upper(z, span):
    return lax.rem(z, 2 * span) >= span


def halves(upper, own_ref, got_ref):
    own, got = own_ref[...], got_ref[...]
    return jnp.where(upper, got, own), jnp.where(upper, own, got)


def prefixed(upper, low, pre):
    return jnp.where(upper, after(pre, low), pre)


def join_chips(z_ref, own_ref, got_ref, both_ref):
    low, high = halves(is_upper(z_ref[0], 1), own_ref, got_ref)
    both_ref[...] = after(high, low)


def join_pairs(z_ref, own_ref, got_ref, both_ref):
    low, high = halves(is_upper(z_ref[0], 2), own_ref, got_ref)
    both_ref[...] = after(high, low)


def join_ring(z_ref, core_ref, own_ref, got_ref, first_ref, end_ref):
    low, high = halves(is_upper(z_ref[0], 4), own_ref, got_ref)
    end_ref[...] = applied(high, applied(low, first_ref[core_ref[0]]))


def before_chips(z_ref, own_ref, got_ref, pre_ref):
    upper = is_upper(z_ref[0], 1)
    low, _ = halves(upper, own_ref, got_ref)
    pre_ref[...] = jnp.where(upper, low, identity(2 * HW))


def before_pairs(z_ref, own_ref, got_ref, pre_in_ref, pre_ref):
    upper = is_upper(z_ref[0], 2)
    low, _ = halves(upper, own_ref, got_ref)
    pre_ref[...] = prefixed(upper, low, pre_in_ref[...])


def shard_prefixes(z_ref, core_ref, own_ref, got_ref, pre_in_ref, early_ref, mine_ref, other_ref):
    upper = is_upper(z_ref[0], 4)
    low, _ = halves(upper, own_ref, got_ref)
    pre = prefixed(upper, low, pre_in_ref[...])
    middle = after(early_ref[...], pre)
    first = core_ref[0] == 0
    mine_ref[...] = jnp.where(first, pre, middle)
    other_ref[...] = jnp.where(first, middle, pre)


def ring_states(x_hi_ref, core_ref, here_ref, there_ref, first_ref, out_ref):
    for h in range(2):
        arrived = jnp.where(core_ref[0] == h, here_ref[...], there_ref[...])
        out_ref[h] = jnp.where(x_hi_ref[0] == 0, first_ref[h], arrived)


def fetched(in_ref, out_ref):
    out_ref[...] = in_ref[...]


def outputs(core_ref, mine_ref, got_ref, begin_ref, rows_ref, z_ref):
    for h in range(2):
        state = applied(jnp.where(core_ref[0] == h, mine_ref[...], got_ref[...]), begin_ref[h])
        at = slice(h * HW, (h + 1) * HW)
        z = exact(rows_ref[:, at], state) + rows_ref[:, (2 + h) * HW : (3 + h) * HW]
        z_ref[:, at] = z.astype(bf16).astype(f32)


def copied(column_ref, row_ref, w_ref, later_ref, out_ref):
    del column_ref, row_ref, later_ref
    out_ref[...] = w_ref[...].astype(out_ref.dtype)


def weight_share(weight, column, row, rows, dtype, later, name):
    columns, parts = weight.shape[1] // SIZES[3], 2
    return pl.pallas_call(
        copied,
        name=name,
        grid_spec=pltpu.PrefetchScalarGridSpec(
            num_scalar_prefetch=2,
            grid=(parts,),
            in_specs=[
                pl.BlockSpec((rows, columns // parts), lambda i, c, r: (r[0], c[0] * parts + i)),
                pl.BlockSpec(memory_space=pl.ANY),
            ],
            out_specs=pl.BlockSpec((rows, columns // parts), lambda i, c, r: (0, i)),
        ),
        out_shape=jax.ShapeDtypeStruct((rows, columns), dtype),
        compiler_params=pltpu.CompilerParams(vmem_limit_bytes=8 * MIB),
    )(column, row, weight, later)


OFFSETS = (4, -3, 3, -2, 2, -1, 1, 0)


def piece_weights(x_lo_ref, y_ref, core_ref, w_hbm, n0, n1, f0, f1, later_ref, out_ref, own_ref, done):
    del later_ref
    chunk = out_ref.shape[2]
    columns = own_ref.shape[1]
    copy = pltpu.make_async_copy(
        w_hbm.at[:, pl.ds(pl.multiple_of(x_lo_ref[0] * columns, HW), columns)], own_ref, done
    )
    copy.start()
    first = core_ref[0] == 0
    share = HW // 2
    places = [
        pl.ds(pl.multiple_of(lax.rem(y_ref[0] + (o + SIZES[4]), SIZES[4]) * chunk, HW), chunk) for o in OFFSETS
    ]
    for i, at in enumerate(places):
        for j, (mine, other) in enumerate(((n0, n1), (f0, f1))):
            a, b = mine[:, at], other[:, at]
            row = 2 * HW + j * HW
            out_ref[i, row : row + share, :] = jnp.where(first, a, b).astype(bf16)
            out_ref[i, row + share : row + HW, :] = jnp.where(first, b, a).astype(bf16)
    copy.wait()
    for i, at in enumerate(places):
        out_ref[i, : 2 * HW, :] = own_ref[:, at]


def piece(z_ref, zx_ref, w_ref, i):
    return single(z_ref[...].astype(bf16), w_ref[i, : 2 * HW, :]) + single(
        zx_ref[...].astype(bf16), w_ref[i, 2 * HW :, :]
    )


def farthest(z_ref, zx_ref, w_ref, low_ref, high_ref):
    half = low_ref.shape[0]
    out = piece(z_ref, zx_ref, w_ref, 0)
    low_ref[...] = out[:half]
    high_ref[...] = out[half:]


def nearer(z_ref, zx_ref, w_ref, *out_refs):
    for i, out_ref in enumerate(out_refs):
        out_ref[...] = piece(z_ref, zx_ref, w_ref, i + 1)


def swapped(x, axes):
    n = 2 ** len(axes)
    return lax.ppermute(x, axes, [(i, n - 1 - i) for i in range(n)])


def passed(x, axis, by):
    n = lax.axis_size(axis)
    return lax.ppermute(x, axis, [(i, (i + by) % n) for i in range(n)])


def local(queries, keys, values, rates, init_weight, out_weight):
    rows = queries.shape[0]
    x_hi, z, core, x_lo, y = (lax.axis_index(a).reshape(1) for a in (XH, Z, CORE, XL, Y))
    columns = out_weight.shape[1] // SIZES[3]
    chunk = columns // SIZES[4]
    square, wide, out_piece = ((HW, HW), f32), ((HW, 2 * HW), f32), ((rows, chunk), f32)

    share = HW // 2
    keep, send, solved = call(
        shard_maps, [wide, wide, ((2, rows, 2 * HW), f32)], [core],
        keys, values, rates,
        scratch=[pltpu.VMEM((rows, 2 * HW), bf16)] * 2
        + [pltpu.VMEM((2, rows), f32)] + [pltpu.SemaphoreType.DMA] * 3,
        space=pltpu.HBM, limit=8, us=3,
    )
    got = swapped(send, (CORE,))

    def across_z(x, to):
        return lax.ppermute(x, Z, [(i, to(i)) for i in range(SIZES[1])])

    own_rows, token = call(shard_rows, [((rows, 4 * HW), f32), ((8, HW), f32)], [], queries, keys, rates, solved, us=0.1)
    (chip,) = call(chip_map, [wide], [core], keep, got, later=[token])
    (early,) = call(first_map, [wide], [core], keep, got, later=[chip], us=0.1)
    near_out = weight_share(out_weight, 1 - x_lo, core, share, f32, early, "near")
    near = swapped(near_out, (XL,))
    got_chip = across_z(chip, lambda i: i ^ 1)
    (both,) = call(join_chips, [wide], [z], chip, got_chip, later=[near_out, early], us=0.5)
    (pre,) = call(before_chips, [wide], [z], chip, got_chip, later=[both], us=0.1)
    far_out = weight_share(out_weight, 1 - x_lo, core + 2, share, f32, both, "far")
    far = swapped(far_out, (XH, XL))
    got_both = across_z(both, lambda i: i ^ 2)
    (four,) = call(join_pairs, [wide], [z], both, got_both, later=[far_out, pre], us=6)
    (pre,) = call(before_pairs, [wide], [z], both, got_both, pre, later=[four], us=0.1)
    near_other = swapped(near, (CORE,))
    (first,) = call(fetched, [((2, HW, HW), f32)], [], init_weight, later=[four], us=0.1)
    got_four = across_z(four, lambda i: 7 - i)
    (end,) = call(join_ring, [square], [z, core], four, got_four, first, later=[pre], us=6)
    far_other = swapped(far, (CORE,))
    here = lax.ppermute(end, (XH, CORE), [(0, 2), (1, 3)])
    there = lax.ppermute(end, (XH, CORE), [(0, 3), (1, 2)])
    mine, other = call(shard_prefixes, [wide, wide], [z, core], four, got_four, pre, early, later=[end], us=0.1)
    (begin,) = call(ring_states, [((2, HW, HW), f32)], [x_hi, core], here, there, first, us=5)
    (late_rows,) = call(fetched, [((rows, 4 * HW), f32)], [], own_rows, later=[end], us=0.1)
    (z_rows,) = call(
        outputs, [((rows, 2 * HW), f32)], [core], mine, swapped(other, (CORE,)), begin, late_rows, us=1
    )
    z_pair = swapped(z_rows, (XL,))
    weights = pl.pallas_call(
        piece_weights,
        name="piece_weights",
        out_shape=jax.ShapeDtypeStruct((SIZES[4], 4 * HW, chunk), bf16),
        in_specs=[SM] * 3 + [pl.BlockSpec(memory_space=pltpu.HBM)] + [VM] * 4 + [pl.BlockSpec(memory_space=pl.ANY)],
        out_specs=VM,
        scratch_shapes=[pltpu.VMEM((2 * HW, columns), bf16), pltpu.SemaphoreType.DMA],
        compiler_params=pltpu.CompilerParams(vmem_limit_bytes=16 * MIB),
        cost_estimate=pl.CostEstimate(flops=int(0.5 * 1e9), bytes_accessed=1 << 17, transcendentals=0),
    )(
        x_lo, y, core, pltpu.with_memory_space_constraint(out_weight, pltpu.HBM),
        near, near_other, far, far_other, z_rows,
    )

    factors = (z_rows, z_pair, weights)
    low, high = call(farthest, [((rows // 2, chunk), f32)] * 2, [], *factors, limit=16)
    down, up = passed(low, Y, -1), passed(high, Y, 1)
    pieces = call(nearer, [out_piece] * (len(OFFSETS) - 1), [], *factors, later=[low], limit=16)
    down = pieces[0] + jnp.concatenate([down, jnp.zeros_like(down)], axis=0)
    up = pieces[1] + jnp.concatenate([jnp.zeros_like(up), up], axis=0)
    for i in (2, 4):
        down = passed(down, Y, -1) + pieces[i]
        up = passed(up, Y, 1) + pieces[i + 1]
    return (passed(down, Y, -1) + passed(up, Y, 1) + pieces[6]).astype(bf16)


def solution(mesh):
    fine = Mesh(mesh.devices.reshape(SIZES), (XH, Z, CORE, XL, Y))
    ctx, tp = (XH, Z, CORE), (XL, Y)
    in_specs = (P(ctx, tp), P(ctx, tp), P(ctx, tp), P(tp, ctx), P(tp, None, None), P(tp, None))
    return jax.shard_map(local, mesh=fine, in_specs=in_specs, out_specs=P(ctx, tp), check_vma=False)
```

time: 112 us -> 109 us (0.973)
  the two profiles are of different devices: /device:TPU:2 before, /device:TPU:24 now
where the time goes in v6:
time: 109 us
  starting transfers between devices  69.8 us (64%)
  waiting for transfers between devices  24.7 us (23%)
  Pallas kernels  9.74 us (9%)
  local copies, waits for them, and re-layouts  2.98 us (3%)
    ppermute x8, starting transfers between devices, passed(): return lax.ppermute(x, axis, [(i, (i + by) % n) for i in range(n)])  28.8 us
    ppermute x7, starting transfers between devices, swapped(): return lax.ppermute(x, axes, [(i, n - 1 - i) for i in range(n)])  18.7 us
    ppermute x3, starting transfers between devices, across_z(): return lax.ppermute(x, Z, [(i, to(i)) for i in range(SIZES[1])])  17.4 us
    ppermute x7, waiting for transfers between devices, swapped(): return lax.ppermute(x, axes, [(i, n - 1 - i) for i in range(n)])  11.6 us
    ppermute x8, waiting for transfers between devices, passed(): return lax.ppermute(x, axis, [(i, (i + by) % n) for i in range(n)])  11.2 us
    pallas_call x16, Pallas kernels, call(): pl.pallas_call(body, name=kernel.__name__, out_shape=outs, in_specs=[SM]...  6.59 us
    ppermute x1, starting transfers between devices, local(): here = lax.ppermute(end, (XH, CORE), [(0, 2), (1, 3)])  3.43 us
    unnamed x22, local copies, waits for them, and re-layouts  2.98 us
  transfers between devices with their start and end apart: 20, of which 10 were waited for; matrix products, arithmetic and copies ran while one was open for 0% of the time, Pallas kernels for 6%

profile of v6, /device:TPU:24, one launch (start us, length us, event | category | flops | bytes accessed | tf_op | source)
XLA Modules:
  0.0 108.6 jit_solution(5689324652942782106)
XLA Ops:
  0.0 3.0 %shard_maps.1 = (f32[128,256]{1,0:T(8,128)S(1)}, f32[128,256]{1,0:T(8,128)S(1)}, f32[2,160,256]{2,1,0:T(8,128)S(1)}) custom-call(s32[1]{0:T(128)} %bitcast.refs_0_.row_ref.refs_1_.core_ref, bf16[160,256]{1,0:T(8,128)(2,1)} %refs_1_.3, bf16[160,256]{1,0:T(8,128)(2,1)} %refs_2_.2, f32[2,160]{1,0:T(2,128)} %refs_2_.3), custom_call_target="tpu_custom_call" | custom-call | flops 3000000000 | bytes 131072 | tf_op jit(solution)/shard_map/shard_maps/pallas_call | solution.py:36
  3.0 0.0 copy-start.4
  3.0 0.0 copy-start
  3.1 2.2 %collective-permute-start = (f32[128,256]{1,0:T(8,128)S(1)}, f32[128,256]{1,0:T(8,128)S(1)}, u32[]{:S(2)}, u32[]{:S(2)}) collective-permute-start(f32[128,256]{1,0:T(8,128)S(1)} %get-tuple-element.22), channel_id=1, source_target_pairs={{0,16},{16,0},{1,17},{17,1},{2,18},{18,2},{3,19},{19,3},{4,20},{20... | collective-permute-start | bytes 393224 | tf_op jit(solution)/shard_map/ppermute | solution.py:276
  5.2 0.0 copy-done.8
  5.3 0.4 shard_rows.1
  5.7 0.7 copy-done.1
  6.4 0.1 collective-permute-done.refs_2_
  6.6 0.2 chip_map.1.refs_3_.refs_1_
  6.8 0.4 copy-done.6
  7.2 4.3 %collective-permute-start.1 = (f32[128,256]{1,0:T(8,128)S(1)}, f32[128,256]{1,0:T(8,128)S(1)}, u32[]{:S(2)}, u32[]{:S(2)}) collective-permute-start(f32[128,256]{1,0:T(8,128)S(1)} %chip_map.1.refs_3_.refs_1_), channel_id=1, source_target_pairs={{0,32},{32,0},{64,96},{96,64},{128,160},{160,128},{192,224},{224,1... | collective-permute-start | bytes 393224 | tf_op jit(solution)/shard_map/ppermute | solution.py:302
  11.5 0.0 copy-start.5
  11.5 0.9 copy-done.5
  12.4 0.9 copy-done.7
  13.3 0.2 near.1.refs_3_
  13.6 1.9 %collective-permute-done.1.refs_2_ = f32[128,256]{1,0:T(8,128)S(1)} collective-permute-done((f32[128,256]{1,0:T(8,128)S(1)}, f32[128,256]{1,0:T(8,128)S(1)}, u32[]{:S(2)}, u32[]{:S(2)}) %collective-permute-start.1) | collective-permute-done | bytes 131104 | tf_op jit(solution)/shard_map/ppermute | solution.py:302
  15.5 0.2 join_chips.1.later_ref.refs_3_.refs_1_
  15.7 6.1 %collective-permute-start.2 = (f32[128,256]{1,0:T(8,128)S(1)}, f32[128,256]{1,0:T(8,128)S(1)}, u32[]{:S(2)}, u32[]{:S(2)}) collective-permute-start(f32[128,256]{1,0:T(8,128)S(1)} %join_chips.1.later_ref.refs_3_.refs_1_), channel_id=1, source_target_pairs={{0,64},{32,96},{64,0},{96,32},{128,192},{160,224},{192,128},{224,1... | collective-permute-start | bytes 393224 | tf_op jit(solution)/shard_map/ppermute | solution.py:302
  21.8 3.4 %collective-permute-start.8 = (f32[64,3072]{1,0:T(8,128)S(1)}, f32[64,3072]{1,0:T(8,128)}, u32[]{:S(2)}, u32[]{:S(2)}) collective-permute-start(f32[64,3072]{1,0:T(8,128)S(1)} %near.1.refs_3_), channel_id=1, source_target_pairs={{0,8},{8,0},{1,9},{9,1},{2,10},{10,2},{3,11},{11,3},{4,12},{12,4},... | collective-permute-start | bytes 2359304 | tf_op jit(solution)/shard_map/ppermute | solution.py:276
  25.2 0.2 far.1.refs_3_
  25.5 4.0 %collective-permute-start.10 = (f32[64,3072]{1,0:T(8,128)S(1)}, f32[64,3072]{1,0:T(8,128)S(1)}, u32[]{:S(2)}, u32[]{:S(2)}) collective-permute-start(f32[64,3072]{1,0:T(8,128)S(1)} %far.1.refs_3_), channel_id=1, source_target_pairs={{0,264},{8,256},{256,8},{264,0},{1,265},{9,257},{257,9},{265,1},{2... | collective-permute-start | bytes 2359304 | tf_op jit(solution)/shard_map/ppermute | solution.py:276
  29.5 0.0 copy-start.3
  29.5 0.0 collective-permute-done.2.refs_2_
  29.5 0.2 join_pairs.1.refs_4_.refs_1_.refs_2_
  29.7 7.1 %collective-permute-start.3 = (f32[128,256]{1,0:T(8,128)S(1)}, f32[128,256]{1,0:T(8,128)S(1)}, u32[]{:S(2)}, u32[]{:S(2)}) collective-permute-start(f32[128,256]{1,0:T(8,128)S(1)} %join_pairs.1.refs_4_.refs_1_.refs_2_), channel_id=1, source_target_pairs={{0,224},{32,192},{64,160},{96,128},{128,96},{160,64},{192,32},{224... | collective-permute-start | bytes 393224 | tf_op jit(solution)/shard_map/ppermute | solution.py:302
  36.8 0.2 before_pairs.1.refs_5_.refs_4_
  37.1 5.8 %collective-permute-done.8.n0 = f32[64,3072]{1,0:T(8,128)} collective-permute-done((f32[64,3072]{1,0:T(8,128)S(1)}, f32[64,3072]{1,0:T(8,128)}, u32[]{:S(2)}, u32[]{:S(2)}) %collective-permute-start.8) | collective-permute-done | bytes 786464 | tf_op jit(solution)/shard_map/ppermute | solution.py:276
  42.8 1.9 %collective-permute-start.9 = (f32[64,3072]{1,0:T(8,128)}, f32[64,3072]{1,0:T(8,128)S(1)}, u32[]{:S(2)}, u32[]{:S(2)}) collective-permute-start(f32[64,3072]{1,0:T(8,128)} %collective-permute-done.8.n0), channel_id=1, source_target_pairs={{0,16},{16,0},{1,17},{17,1},{2,18},{18,2},{3,19},{19,3},{4,20},{20... | collective-permute-start | bytes 2359304 | tf_op jit(solution)/shard_map/ppermute | solution.py:276
  44.7 2.5 %collective-permute-done.10.f0 = f32[64,3072]{1,0:T(8,128)S(1)} collective-permute-done((f32[64,3072]{1,0:T(8,128)S(1)}, f32[64,3072]{1,0:T(8,128)S(1)}, u32[]{:S(2)}, u32[]{:S(2)}) %collective-permute-start.10) | collective-permute-done | bytes 786464 | tf_op jit(solution)/shard_map/ppermute | solution.py:276
  47.3 1.9 %collective-permute-start.11 = (f32[64,3072]{1,0:T(8,128)S(1)}, f32[64,3072]{1,0:T(8,128)S(1)}, u32[]{:S(2)}, u32[]{:S(2)}) collective-permute-start(f32[64,3072]{1,0:T(8,128)S(1)} %collective-permute-done.10.f0), channel_id=1, source_target_pairs={{0,16},{16,0},{1,17},{17,1},{2,18},{18,2},{3,19},{19,3},{4,20},{20... | collective-permute-start | bytes 2359304 | tf_op jit(solution)/shard_map/ppermute | solution.py:276
  49.2 0.0 collective-permute-done.3.refs_3_
  49.2 0.4 join_ring.1.refs_6_.refs_1_
  49.6 3.4 %collective-permute-start.5 = (f32[128,128]{1,0:T(8,128)S(1)}, f32[128,128]{1,0:T(8,128)S(1)}, u32[]{:S(2)}, u32[]{:S(2)}) collective-permute-start(f32[128,128]{1,0:T(8,128)S(1)} %join_ring.1.refs_6_.refs_1_), channel_id=1, source_target_pairs={{0,256},{16,272},{1,257},{17,273},{2,258},{18,274},{3,259},{19,275... | collective-permute-start | bytes 196616 | tf_op jit(solution)/shard_map/ppermute | solution.py:322
  53.0 1.4 %collective-permute-start.6 = (f32[128,128]{1,0:T(8,128)S(1)}, f32[128,128]{1,0:T(8,128)S(1)}, u32[]{:S(2)}, u32[]{:S(2)}) collective-permute-start(f32[128,128]{1,0:T(8,128)S(1)} %join_ring.1.refs_6_.refs_1_), channel_id=1, source_target_pairs={{0,272},{16,256},{1,273},{17,257},{2,274},{18,258},{3,275},{19,259... | collective-permute-start | bytes 196616 | tf_op jit(solution)/shard_map/ppermute | solution.py:323
  54.4 0.4 shard_prefixes.1
  54.8 2.0 %collective-permute-start.4 = (f32[128,256]{1,0:T(8,128)S(1)}, f32[128,256]{1,0:T(8,128)S(1)}, u32[]{:S(2)}, u32[]{:S(2)}) collective-permute-start(f32[128,256]{1,0:T(8,128)S(1)} %get-tuple-element.26), channel_id=1, source_target_pairs={{0,16},{16,0},{1,17},{17,1},{2,18},{18,2},{3,19},{19,3},{4,20},{20... | collective-permute-start | bytes 393224 | tf_op jit(solution)/shard_map/ppermute | solution.py:276
  56.9 0.0 collective-permute-done.5.refs_2_
  56.9 0.0 collective-permute-done.6.refs_3_
  57.0 1.1 %collective-permute-done.4.refs_2_ = f32[128,256]{1,0:T(8,128)S(1)} collective-permute-done((f32[128,256]{1,0:T(8,128)S(1)}, f32[128,256]{1,0:T(8,128)S(1)}, u32[]{:S(2)}, u32[]{:S(2)}) %collective-permute-start.4) | collective-permute-done | bytes 131104 | tf_op jit(solution)/shard_map/ppermute | solution.py:276
  58.1 0.4 outputs.1.later_ref.refs_0_
  58.5 3.3 %collective-permute-start.7 = (f32[160,256]{1,0:T(8,128)S(1)}, f32[160,256]{1,0:T(8,128)S(1)}, u32[]{:S(2)}, u32[]{:S(2)}) collective-permute-start(f32[160,256]{1,0:T(8,128)S(1)} %outputs.1.later_ref.refs_0_), channel_id=1, source_target_pairs={{0,8},{8,0},{1,9},{9,1},{2,10},{10,2},{3,11},{11,3},{4,12},{12,4},... | collective-permute-start | bytes 491528 | tf_op jit(solution)/shard_map/ppermute | solution.py:276
  61.8 0.0 collective-permute-done.9.n1
  61.8 0.0 collective-permute-done.11.f1
  61.8 2.7 %piece_weights.1.refs_2_ = bf16[8,512,384]{2,1,0:T(8,128)(2,1)S(1)} custom-call(s32[1]{0:T(128)} %bitcast.2.x_lo_ref, s32[1]{0:T(128)} %bitcast.4.y_ref, s32[1]{0:T(128)} %bitcast.refs_0_.row_ref.refs_1_.core_ref, bf16[256,6144]{1,0:T(8,128)(2,1)} %w_hbm.1, f32[64,3072]{1,0:T(8,128)} %collective-permute-done.8.n0, f32[64,3072]{1,0:T(8,128)S(1)} %collective-permute-done.9.n1, ...), custom_call_target="tpu_custom_call" | custom-call | flops 500000000 | bytes 131072 | tf_op jit(solution)/shard_map/piece_weights/pallas_call | solution.py:331
  64.5 2.1 %collective-permute-done.7.refs_1_ = f32[160,256]{1,0:T(8,128)S(1)} collective-permute-done((f32[160,256]{1,0:T(8,128)S(1)}, f32[160,256]{1,0:T(8,128)S(1)}, u32[]{:S(2)}, u32[]{:S(2)}) %collective-permute-start.7) | collective-permute-done | bytes 163872 | tf_op jit(solution)/shard_map/ppermute | solution.py:276
  66.6 0.2 farthest.1
  66.9 4.7 %collective-permute-start.16 = (f32[80,384]{1,0:T(8,128)S(1)}, f32[80,384]{1,0:T(8,128)S(1)}, u32[]{:S(2)}, u32[]{:S(2)}) collective-permute-start(f32[80,384]{1,0:T(8,128)S(1)} %get-tuple-element.33), channel_id=1, source_target_pairs={{0,1},{1,2},{2,3},{3,4},{4,5},{5,6},{6,7},{7,0},{8,9},{9,10},{10,1... | collective-permute-start | bytes 368648 | tf_op jit(solution)/shard_map/ppermute | solution.py:281
  71.6 1.9 %collective-permute-start.12 = (f32[80,384]{1,0:T(8,128)S(1)}, f32[80,384]{1,0:T(8,128)S(1)}, u32[]{:S(2)}, u32[]{:S(2)}) collective-permute-start(f32[80,384]{1,0:T(8,128)S(1)} %get-tuple-element.28.refs_3_), channel_id=1, source_target_pairs={{0,7},{1,0},{2,1},{3,2},{4,3},{5,4},{6,5},{7,6},{8,15},{9,8},{10,9... | collective-permute-start | bytes 368648 | tf_op jit(solution)/shard_map/ppermute | solution.py:281
  73.5 0.8 nearer.1
  74.3 0.0 collective-permute-done.16
  74.4 5.2 %collective-permute-start.17 = (f32[160,384]{1,0:T(8,128)S(1)}, f32[160,384]{1,0:T(8,128)S(1)}, u32[]{:S(2)}, u32[]{:S(2)}) collective-permute-start(f32[160,384]{1,0:T(8,128)S(1)} %pad_add_fusion), channel_id=1, source_target_pairs={{0,1},{1,2},{2,3},{3,4},{4,5},{5,6},{6,7},{7,0},{8,9},{9,10},{10,1... | collective-permute-start | bytes 737288 | tf_op jit(solution)/shard_map/ppermute | solution.py:281
  79.6 0.0 collective-permute-done.12
  79.6 1.9 %collective-permute-start.13 = (f32[160,384]{1,0:T(8,128)S(1)}, f32[160,384]{1,0:T(8,128)S(1)}, u32[]{:S(2)}, u32[]{:S(2)}) collective-permute-start(f32[160,384]{1,0:T(8,128)S(1)} %pad_add_fusion.1), channel_id=1, source_target_pairs={{0,7},{1,0},{2,1},{3,2},{4,3},{5,4},{6,5},{7,6},{8,15},{9,8},{10,9... | collective-permute-start | bytes 737288 | tf_op jit(solution)/shard_map/ppermute | solution.py:281
  81.6 2.1 %collective-permute-done.17 = f32[160,384]{1,0:T(8,128)S(1)} collective-permute-done((f32[160,384]{1,0:T(8,128)S(1)}, f32[160,384]{1,0:T(8,128)S(1)}, u32[]{:S(2)}, u32[]{:S(2)}) %collective-permute-start.17) | collective-permute-done | bytes 245792 | tf_op jit(solution)/shard_map/ppermute | solution.py:281
  83.6 5.6 %collective-permute-start.18 = (f32[160,384]{1,0:T(8,128)S(1)}, f32[160,384]{1,0:T(8,128)S(1)}, u32[]{:S(2)}, u32[]{:S(2)}) collective-permute-start(f32[160,384]{1,0:T(8,128)S(1)} %add.36), channel_id=1, source_target_pairs={{0,1},{1,2},{2,3},{3,4},{4,5},{5,6},{6,7},{7,0},{8,9},{9,10},{10,1... | collective-permute-start | bytes 737288 | tf_op jit(solution)/shard_map/ppermute | solution.py:281
  89.3 0.0 collective-permute-done.13
  89.3 1.9 %collective-permute-start.14 = (f32[160,384]{1,0:T(8,128)S(1)}, f32[160,384]{1,0:T(8,128)S(1)}, u32[]{:S(2)}, u32[]{:S(2)}) collective-permute-start(f32[160,384]{1,0:T(8,128)S(1)} %add.33), channel_id=1, source_target_pairs={{0,7},{1,0},{2,1},{3,2},{4,3},{5,4},{6,5},{7,6},{8,15},{9,8},{10,9... | collective-permute-start | bytes 737288 | tf_op jit(solution)/shard_map/ppermute | solution.py:281
  91.2 1.7 %collective-permute-done.18 = f32[160,384]{1,0:T(8,128)S(1)} collective-permute-done((f32[160,384]{1,0:T(8,128)S(1)}, f32[160,384]{1,0:T(8,128)S(1)}, u32[]{:S(2)}, u32[]{:S(2)}) %collective-permute-start.18) | collective-permute-done | bytes 245792 | tf_op jit(solution)/shard_map/ppermute | solution.py:281
  93.0 5.6 %collective-permute-start.19 = (f32[160,384]{1,0:T(8,128)S(1)}, f32[160,384]{1,0:T(8,128)S(1)}, u32[]{:S(2)}, u32[]{:S(2)}) collective-permute-start(f32[160,384]{1,0:T(8,128)S(1)} %add.37), channel_id=1, source_target_pairs={{0,1},{1,2},{2,3},{3,4},{4,5},{5,6},{6,7},{7,0},{8,9},{9,10},{10,1... | collective-permute-start | bytes 737288 | tf_op jit(solution)/shard_map/ppermute | solution.py:281
  98.6 0.0 collective-permute-done.14
  98.6 1.9 %collective-permute-start.15 = (f32[160,384]{1,0:T(8,128)S(1)}, f32[160,384]{1,0:T(8,128)S(1)}, u32[]{:S(2)}, u32[]{:S(2)}) collective-permute-start(f32[160,384]{1,0:T(8,128)S(1)} %add.34), channel_id=1, source_target_pairs={{0,7},{1,0},{2,1},{3,2},{4,3},{5,4},{6,5},{7,6},{8,15},{9,8},{10,9... | collective-permute-start | bytes 737288 | tf_op jit(solution)/shard_map/ppermute | solution.py:281
  100.6 1.7 %collective-permute-done.19 = f32[160,384]{1,0:T(8,128)S(1)} collective-permute-done((f32[160,384]{1,0:T(8,128)S(1)}, f32[160,384]{1,0:T(8,128)S(1)}, u32[]{:S(2)}, u32[]{:S(2)}) %collective-permute-start.19) | collective-permute-done | bytes 245792 | tf_op jit(solution)/shard_map/ppermute | solution.py:281
  102.3 5.7 %collective-permute-done.15 = f32[160,384]{1,0:T(8,128)S(1)} collective-permute-done((f32[160,384]{1,0:T(8,128)S(1)}, f32[160,384]{1,0:T(8,128)S(1)}, u32[]{:S(2)}, u32[]{:S(2)}) %collective-permute-start.15) | collective-permute-done | bytes 245792 | tf_op jit(solution)/shard_map/ppermute | solution.py:281
  107.9 0.7 add_convert_fusion
  (24 shorter events, 0.3 us)
Async XLA Ops:
  0.0 5.2 %copy-start.8 = (bf16[160,256]{1,0:T(8,128)(2,1)S(1)}, bf16[160,256]{1,0:T(8,128)(2,1)}, u32[]{:S(2)}) copy-start(bf16[160,256]{1,0:T(8,128)(2,1)} %refs_1_.3) | copy-start | bytes 245764
  0.0 5.3 %copy-start.9 = (bf16[160,256]{1,0:T(8,128)(2,1)S(1)}, bf16[160,256]{1,0:T(8,128)(2,1)}, u32[]{:S(2)}) copy-start(bf16[160,256]{1,0:T(8,128)(2,1)} %refs_0_.2) | copy-start | bytes 245764
  0.0 5.3 %copy-start.10 = (f32[2,160]{1,0:T(2,128)S(1)}, f32[2,160]{1,0:T(2,128)}, u32[]{:S(2)}) copy-start(f32[2,160]{1,0:T(2,128)} %refs_2_.3) | copy-start | bytes 3844
  3.0 3.5 %copy-start.4 = (f32[128,256]{1,0:T(8,128)}, f32[128,256]{1,0:T(8,128)S(1)}, u32[]{:S(2)}) copy-start(f32[128,256]{1,0:T(8,128)S(1)} %get-tuple-element.21.refs_1_) | copy-start | bytes 393220
  3.0 10.3 %copy-start = (bf16[256,6144]{1,0:T(8,128)(2,1)S(1)}, bf16[256,6144]{1,0:T(8,128)(2,1)}, u32[]{:S(2)}) copy-start(bf16[256,6144]{1,0:T(8,128)(2,1)} %w_hbm.1) | copy-start | bytes 9437188
  3.1 3.5 %collective-permute-start = (f32[128,256]{1,0:T(8,128)S(1)}, f32[128,256]{1,0:T(8,128)S(1)}, u32[]{:S(2)}, u32[]{:S(2)}) collective-permute-start(f32[128,256]{1,0:T(8,128)S(1)} %get-tuple-element.22), channel_id=1, source_target_pairs={{0,16},{16,0},{1,17},{17,1},{2,18},{18,2},{3,19},{19,3},{4,20},{20... | collective-permute-start | bytes 393224 | tf_op jit(solution)/shard_map/ppermute | solution.py:276
  5.7 0.7 copy-start.1
  6.6 0.6 copy-start.6
  7.2 8.3 %collective-permute-start.1 = (f32[128,256]{1,0:T(8,128)S(1)}, f32[128,256]{1,0:T(8,128)S(1)}, u32[]{:S(2)}, u32[]{:S(2)}) collective-permute-start(f32[128,256]{1,0:T(8,128)S(1)} %chip_map.1.refs_3_.refs_1_), channel_id=1, source_target_pairs={{0,32},{32,0},{64,96},{96,64},{128,160},{160,128},{192,224},{224,1... | collective-permute-start | bytes 393224 | tf_op jit(solution)/shard_map/ppermute | solution.py:302
  11.5 0.9 copy-start.5
  12.4 0.9 copy-start.7
  15.7 13.8 %collective-permute-start.2 = (f32[128,256]{1,0:T(8,128)S(1)}, f32[128,256]{1,0:T(8,128)S(1)}, u32[]{:S(2)}, u32[]{:S(2)}) collective-permute-start(f32[128,256]{1,0:T(8,128)S(1)} %join_chips.1.later_ref.refs_3_.refs_1_), channel_id=1, source_target_pairs={{0,64},{32,96},{64,0},{96,32},{128,192},{160,224},{192,128},{224,1... | collective-permute-start | bytes 393224 | tf_op jit(solution)/shard_map/ppermute | solution.py:302
  21.8 21.0 %collective-permute-start.8 = (f32[64,3072]{1,0:T(8,128)S(1)}, f32[64,3072]{1,0:T(8,128)}, u32[]{:S(2)}, u32[]{:S(2)}) collective-permute-start(f32[64,3072]{1,0:T(8,128)S(1)} %near.1.refs_3_), channel_id=1, source_target_pairs={{0,8},{8,0},{1,9},{9,1},{2,10},{10,2},{3,11},{11,3},{4,12},{12,4},... | collective-permute-start | bytes 2359304 | tf_op jit(solution)/shard_map/ppermute | solution.py:276
  25.5 21.8 %collective-permute-start.10 = (f32[64,3072]{1,0:T(8,128)S(1)}, f32[64,3072]{1,0:T(8,128)S(1)}, u32[]{:S(2)}, u32[]{:S(2)}) collective-permute-start(f32[64,3072]{1,0:T(8,128)S(1)} %far.1.refs_3_), channel_id=1, source_target_pairs={{0,264},{8,256},{256,8},{264,0},{1,265},{9,257},{257,9},{265,1},{2... | collective-permute-start | bytes 2359304 | tf_op jit(solution)/shard_map/ppermute | solution.py:276
  29.5 7.3 %copy-start.3 = (f32[2,128,128]{2,1,0:T(8,128)S(1)}, f32[2,128,128]{2,1,0:T(8,128)}, u32[]{:S(2)}) copy-start(f32[2,128,128]{2,1,0:T(8,128)} %refs_0_.3) | copy-start | bytes 393220
  29.7 19.5 %collective-permute-start.3 = (f32[128,256]{1,0:T(8,128)S(1)}, f32[128,256]{1,0:T(8,128)S(1)}, u32[]{:S(2)}, u32[]{:S(2)}) collective-permute-start(f32[128,256]{1,0:T(8,128)S(1)} %join_pairs.1.refs_4_.refs_1_.refs_2_), channel_id=1, source_target_pairs={{0,224},{32,192},{64,160},{96,128},{128,96},{160,64},{192,32},{224... | collective-permute-start | bytes 393224 | tf_op jit(solution)/shard_map/ppermute | solution.py:302
  37.0 19.8 %copy-start.2 = (f32[160,512]{1,0:T(8,128)S(1)}, f32[160,512]{1,0:T(8,128)}, u32[]{:S(2)}) copy-start(f32[160,512]{1,0:T(8,128)} %copy-done.1) | copy-start | bytes 983044
  42.8 19.0 %collective-permute-start.9 = (f32[64,3072]{1,0:T(8,128)}, f32[64,3072]{1,0:T(8,128)S(1)}, u32[]{:S(2)}, u32[]{:S(2)}) collective-permute-start(f32[64,3072]{1,0:T(8,128)} %collective-permute-done.8.n0), channel_id=1, source_target_pairs={{0,16},{16,0},{1,17},{17,1},{2,18},{18,2},{3,19},{19,3},{4,20},{20... | collective-permute-start | bytes 2359304 | tf_op jit(solution)/shard_map/ppermute | solution.py:276
  47.3 14.6 %collective-permute-start.11 = (f32[64,3072]{1,0:T(8,128)S(1)}, f32[64,3072]{1,0:T(8,128)S(1)}, u32[]{:S(2)}, u32[]{:S(2)}) collective-permute-start(f32[64,3072]{1,0:T(8,128)S(1)} %collective-permute-done.10.f0), channel_id=1, source_target_pairs={{0,16},{16,0},{1,17},{17,1},{2,18},{18,2},{3,19},{19,3},{4,20},{20... | collective-permute-start | bytes 2359304 | tf_op jit(solution)/shard_map/ppermute | solution.py:276
  49.6 7.4 %collective-permute-start.5 = (f32[128,128]{1,0:T(8,128)S(1)}, f32[128,128]{1,0:T(8,128)S(1)}, u32[]{:S(2)}, u32[]{:S(2)}) collective-permute-start(f32[128,128]{1,0:T(8,128)S(1)} %join_ring.1.refs_6_.refs_1_), channel_id=1, source_target_pairs={{0,256},{16,272},{1,257},{17,273},{2,258},{18,274},{3,259},{19,275... | collective-permute-start | bytes 196616 | tf_op jit(solution)/shard_map/ppermute | solution.py:322
  53.0 3.9 %collective-permute-start.6 = (f32[128,128]{1,0:T(8,128)S(1)}, f32[128,128]{1,0:T(8,128)S(1)}, u32[]{:S(2)}, u32[]{:S(2)}) collective-permute-start(f32[128,128]{1,0:T(8,128)S(1)} %join_ring.1.refs_6_.refs_1_), channel_id=1, source_target_pairs={{0,272},{16,256},{1,273},{17,257},{2,274},{18,258},{3,275},{19,259... | collective-permute-start | bytes 196616 | tf_op jit(solution)/shard_map/ppermute | solution.py:323
  54.8 3.2 %collective-permute-start.4 = (f32[128,256]{1,0:T(8,128)S(1)}, f32[128,256]{1,0:T(8,128)S(1)}, u32[]{:S(2)}, u32[]{:S(2)}) collective-permute-start(f32[128,256]{1,0:T(8,128)S(1)} %get-tuple-element.26), channel_id=1, source_target_pairs={{0,16},{16,0},{1,17},{17,1},{2,18},{18,2},{3,19},{19,3},{4,20},{20... | collective-permute-start | bytes 393224 | tf_op jit(solution)/shard_map/ppermute | solution.py:276
  58.5 8.1 %collective-permute-start.7 = (f32[160,256]{1,0:T(8,128)S(1)}, f32[160,256]{1,0:T(8,128)S(1)}, u32[]{:S(2)}, u32[]{:S(2)}) collective-permute-start(f32[160,256]{1,0:T(8,128)S(1)} %outputs.1.later_ref.refs_0_), channel_id=1, source_target_pairs={{0,8},{8,0},{1,9},{9,1},{2,10},{10,2},{3,11},{11,3},{4,12},{12,4},... | collective-permute-start | bytes 491528 | tf_op jit(solution)/shard_map/ppermute | solution.py:276
  66.9 7.4 %collective-permute-start.16 = (f32[80,384]{1,0:T(8,128)S(1)}, f32[80,384]{1,0:T(8,128)S(1)}, u32[]{:S(2)}, u32[]{:S(2)}) collective-permute-start(f32[80,384]{1,0:T(8,128)S(1)} %get-tuple-element.33), channel_id=1, source_target_pairs={{0,1},{1,2},{2,3},{3,4},{4,5},{5,6},{6,7},{7,0},{8,9},{9,10},{10,1... | collective-permute-start | bytes 368648 | tf_op jit(solution)/shard_map/ppermute | solution.py:281
  71.6 8.0 %collective-permute-start.12 = (f32[80,384]{1,0:T(8,128)S(1)}, f32[80,384]{1,0:T(8,128)S(1)}, u32[]{:S(2)}, u32[]{:S(2)}) collective-permute-start(f32[80,384]{1,0:T(8,128)S(1)} %get-tuple-element.28.refs_3_), channel_id=1, source_target_pairs={{0,7},{1,0},{2,1},{3,2},{4,3},{5,4},{6,5},{7,6},{8,15},{9,8},{10,9... | collective-permute-start | bytes 368648 | tf_op jit(solution)/shard_map/ppermute | solution.py:281
  74.4 9.3 %collective-permute-start.17 = (f32[160,384]{1,0:T(8,128)S(1)}, f32[160,384]{1,0:T(8,128)S(1)}, u32[]{:S(2)}, u32[]{:S(2)}) collective-permute-start(f32[160,384]{1,0:T(8,128)S(1)} %pad_add_fusion), channel_id=1, source_target_pairs={{0,1},{1,2},{2,3},{3,4},{4,5},{5,6},{6,7},{7,0},{8,9},{9,10},{10,1... | collective-permute-start | bytes 737288 | tf_op jit(solution)/shard_map/ppermute | solution.py:281
  79.6 9.6 %collective-permute-start.13 = (f32[160,384]{1,0:T(8,128)S(1)}, f32[160,384]{1,0:T(8,128)S(1)}, u32[]{:S(2)}, u32[]{:S(2)}) collective-permute-start(f32[160,384]{1,0:T(8,128)S(1)} %pad_add_fusion.1), channel_id=1, source_target_pairs={{0,7},{1,0},{2,1},{3,2},{4,3},{5,4},{6,5},{7,6},{8,15},{9,8},{10,9... | collective-permute-start | bytes 737288 | tf_op jit(solution)/shard_map/ppermute | solution.py:281
  83.6 9.3 %collective-permute-start.18 = (f32[160,384]{1,0:T(8,128)S(1)}, f32[160,384]{1,0:T(8,128)S(1)}, u32[]{:S(2)}, u32[]{:S(2)}) collective-permute-start(f32[160,384]{1,0:T(8,128)S(1)} %add.36), channel_id=1, source_target_pairs={{0,1},{1,2},{2,3},{3,4},{4,5},{5,6},{6,7},{7,0},{8,9},{9,10},{10,1... | collective-permute-start | bytes 737288 | tf_op jit(solution)/shard_map/ppermute | solution.py:281
  89.3 9.3 %collective-permute-start.14 = (f32[160,384]{1,0:T(8,128)S(1)}, f32[160,384]{1,0:T(8,128)S(1)}, u32[]{:S(2)}, u32[]{:S(2)}) collective-permute-start(f32[160,384]{1,0:T(8,128)S(1)} %add.33), channel_id=1, source_target_pairs={{0,7},{1,0},{2,1},{3,2},{4,3},{5,4},{6,5},{7,6},{8,15},{9,8},{10,9... | collective-permute-start | bytes 737288 | tf_op jit(solution)/shard_map/ppermute | solution.py:281
  93.0 9.3 %collective-permute-start.19 = (f32[160,384]{1,0:T(8,128)S(1)}, f32[160,384]{1,0:T(8,128)S(1)}, u32[]{:S(2)}, u32[]{:S(2)}) collective-permute-start(f32[160,384]{1,0:T(8,128)S(1)} %add.37), channel_id=1, source_target_pairs={{0,1},{1,2},{2,3},{3,4},{4,5},{5,6},{6,7},{7,0},{8,9},{9,10},{10,1... | collective-permute-start | bytes 737288 | tf_op jit(solution)/shard_map/ppermute | solution.py:281
  98.6 9.3 %collective-permute-start.15 = (f32[160,384]{1,0:T(8,128)S(1)}, f32[160,384]{1,0:T(8,128)S(1)}, u32[]{:S(2)}, u32[]{:S(2)}) collective-permute-start(f32[160,384]{1,0:T(8,128)S(1)} %add.34), channel_id=1, source_target_pairs={{0,7},{1,0},{2,1},{3,2},{4,3},{5,4},{6,5},{7,6},{8,15},{9,8},{10,9... | collective-permute-start | bytes 737288 | tf_op jit(solution)/shard_map/ppermute | solution.py:281

commit v7 on v6

--- a/solution.py
+++ b/solution.py
@@ -305,27 +305,27 @@
     (chip,) = call(chip_map, [wide], [core], keep, got, later=[token])
     (early,) = call(first_map, [wide], [core], keep, got, later=[chip], us=0.1)
     near_out = weight_share(out_weight, 1 - x_lo, core, share, f32, early, "near")
+    far_out = weight_share(out_weight, 1 - x_lo, core + 2, share, f32, early, "far")
     near = swapped(near_out, (XL,))
     got_chip = across_z(chip, lambda i: i ^ 1)
-    (both,) = call(join_chips, [wide], [z], chip, got_chip, later=[near_out, early], us=0.5)
+    (both,) = call(join_chips, [wide], [z], chip, got_chip, later=[near_out, far_out, early], us=0.6)
     (pre,) = call(before_chips, [wide], [z], chip, got_chip, later=[both], us=0.1)
-    far_out = weight_share(out_weight, 1 - x_lo, core + 2, share, f32, both, "far")
     far = swapped(far_out, (XH, XL))
     got_both = across_z(both, lambda i: i ^ 2)
-    (four,) = call(join_pairs, [wide], [z], both, got_both, later=[far_out, pre], us=6)
+    (four,) = call(join_pairs, [wide], [z], both, got_both, later=[pre], us=4)
     (pre,) = call(before_pairs, [wide], [z], both, got_both, pre, later=[four], us=0.1)
     near_other = swapped(near, (CORE,))
     (first,) = call(fetched, [((2, HW, HW), f32)], [], init_weight, later=[four], us=0.1)
     got_four = across_z(four, lambda i: 7 - i)
-    (end,) = call(join_ring, [square], [z, core], four, got_four, first, later=[pre], us=6)
+    (end,) = call(join_ring, [square], [z, core], four, got_four, first, later=[pre], us=3)
     far_other = swapped(far, (CORE,))
     here = lax.ppermute(end, (XH, CORE), [(0, 2), (1, 3)])
     there = lax.ppermute(end, (XH, CORE), [(0, 3), (1, 2)])
     mine, other = call(shard_prefixes, [wide, wide], [z, core], four, got_four, pre, early, later=[end], us=0.1)
-    (begin,) = call(ring_states, [((2, HW, HW), f32)], [x_hi, core], here, there, first, us=5)
+    (begin,) = call(ring_states, [((2, HW, HW), f32)], [x_hi, core], here, there, first, us=12)
     (late_rows,) = call(fetched, [((rows, 4 * HW), f32)], [], own_rows, later=[end], us=0.1)
     (z_rows,) = call(
-        outputs, [((rows, 2 * HW), f32)], [core], mine, swapped(other, (CORE,)), begin, late_rows, us=1
+        outputs, [((rows, 2 * HW), f32)], [core], mine, swapped(other, (CORE,)), begin, late_rows, us=8
     )
     z_pair = swapped(z_rows, (XL,))
     weights = pl.pallas_call(
@@ -336,7 +336,7 @@
         out_specs=VM,
         scratch_shapes=[pltpu.VMEM((2 * HW, columns), bf16), pltpu.SemaphoreType.DMA],
         compiler_params=pltpu.CompilerParams(vmem_limit_bytes=16 * MIB),
-        cost_estimate=pl.CostEstimate(flops=int(0.5 * 1e9), bytes_accessed=1 << 17, transcendentals=0),
+        cost_estimate=pl.CostEstimate(flops=int(3 * 1e9), bytes_accessed=1 << 17, transcendentals=0),
     )(
         x_lo, y, core, pltpu.with_memory_space_constraint(out_weight, pltpu.HBM),
         near, near_other, far, far_other, z_rows,

time: 109 us -> 106 us (0.972)
  waiting for transfers between devices: 24.7 us -> 20.8 us
    ppermute x7, waiting for transfers between devices: 11.6 us -> 4.45 us  [swapped(): return lax.ppermute(x, axes, [(i, n - 1 - i) for i in range(n)])]
    ppermute x3, waiting for transfers between devices: 1.93 us -> 4.87 us  [across_z(): return lax.ppermute(x, Z, [(i, to(i)) for i in range(SIZES[1])])]
    pallas_call x2, Pallas kernels: 0.46 us -> 2 us  [weight_share(): pl.pallas_call(copied, name=name, grid_spec=pltpu.PrefetchScalarGridSpec(...]
    pallas_call x1, Pallas kernels: 2.69 us -> 1.56 us  [local(): pl.pallas_call(piece_weights, name='piece_weights', out_shape=jax.ShapeDt...]
  transfers between devices with their start and end apart: 20 -> 20, of which waited for: 10 -> 8; matrix products, arithmetic and copies ran while one was open for 0% -> 0% of each run, Pallas kernels for 6% -> 6%
where the time goes in v7:
time: 106 us; the launch traced here: 105 us
  starting transfers between devices  70 us (66%)
  waiting for transfers between devices  20.8 us (20%)
  Pallas kernels  10.1 us (10%)
  local copies, waits for them, and re-layouts  2.97 us (3%)
    ppermute x8, starting transfers between devices, passed(): return lax.ppermute(x, axis, [(i, (i + by) % n) for i in range(n)])  28.9 us
    ppermute x3, starting transfers between devices, across_z(): return lax.ppermute(x, Z, [(i, to(i)) for i in range(SIZES[1])])  18.3 us
    ppermute x7, starting transfers between devices, swapped(): return lax.ppermute(x, axes, [(i, n - 1 - i) for i in range(n)])  17.8 us
    ppermute x8, waiting for transfers between devices, passed(): return lax.ppermute(x, axis, [(i, (i + by) % n) for i in range(n)])  11.4 us
    pallas_call x16, Pallas kernels, call(): pl.pallas_call(body, name=kernel.__name__, out_shape=outs, in_specs=[SM]...  6.56 us
    ppermute x3, waiting for transfers between devices, across_z(): return lax.ppermute(x, Z, [(i, to(i)) for i in range(SIZES[1])])  4.87 us
    ppermute x7, waiting for transfers between devices, swapped(): return lax.ppermute(x, axes, [(i, n - 1 - i) for i in range(n)])  4.45 us
    ppermute x1, starting transfers between devices, local(): here = lax.ppermute(end, (XH, CORE), [(0, 2), (1, 3)])  3.73 us
  transfers between devices with their start and end apart: 20, of which 8 were waited for; matrix products, arithmetic and copies ran while one was open for 0% of the time, Pallas kernels for 6%

profile of v7, /device:TPU:24, one launch (start us, length us, event | category | flops | bytes accessed | tf_op | source)
XLA Modules:
  0.0 105.2 jit_solution(5589110495831603452)
XLA Ops:
  0.0 3.0 %shard_maps.1 = (f32[128,256]{1,0:T(8,128)S(1)}, f32[128,256]{1,0:T(8,128)S(1)}, f32[2,160,256]{2,1,0:T(8,128)S(1)}) custom-call(s32[1]{0:T(128)} %bitcast.refs_0_.row_ref.refs_1_.core_ref, bf16[160,256]{1,0:T(8,128)(2,1)} %refs_1_.3, bf16[160,256]{1,0:T(8,128)(2,1)} %refs_2_.2, f32[2,160]{1,0:T(2,128)} %refs_2_.3), custom_call_target="tpu_custom_call" | custom-call | flops 3000000000 | bytes 131072 | tf_op jit(solution)/shard_map/shard_maps/pallas_call | solution.py:36
  3.0 0.0 copy-start
  3.1 2.2 %collective-permute-start = (f32[128,256]{1,0:T(8,128)S(1)}, f32[128,256]{1,0:T(8,128)S(1)}, u32[]{:S(2)}, u32[]{:S(2)}) collective-permute-start(f32[128,256]{1,0:T(8,128)S(1)} %get-tuple-element.22), channel_id=1, source_target_pairs={{0,16},{16,0},{1,17},{17,1},{2,18},{18,2},{3,19},{19,3},{4,20},{20... | collective-permute-start | bytes 393224 | tf_op jit(solution)/shard_map/ppermute | solution.py:276
  5.3 0.4 shard_rows.1
  5.7 0.7 copy-done.1
  6.4 0.1 collective-permute-done.refs_2_
  6.6 0.2 chip_map.1.refs_3_.refs_1_
  6.8 0.4 copy-done.6
  7.2 4.3 %collective-permute-start.1 = (f32[128,256]{1,0:T(8,128)S(1)}, f32[128,256]{1,0:T(8,128)S(1)}, u32[]{:S(2)}, u32[]{:S(2)}) collective-permute-start(f32[128,256]{1,0:T(8,128)S(1)} %chip_map.1.refs_3_.refs_1_), channel_id=1, source_target_pairs={{0,32},{32,0},{64,96},{96,64},{128,160},{160,128},{192,224},{224,1... | collective-permute-start | bytes 393224 | tf_op jit(solution)/shard_map/ppermute | solution.py:302
  11.5 0.0 copy-start.5
  11.5 0.9 copy-done.5
  12.4 0.9 copy-done.7
  13.3 1.0 near.1.refs_3_
  14.3 1.0 far.1.refs_4_
  15.3 0.2 collective-permute-done.1.refs_2_
  15.5 0.2 join_chips.1.refs_3_.refs_1_
  15.7 6.1 %collective-permute-start.2 = (f32[128,256]{1,0:T(8,128)S(1)}, f32[128,256]{1,0:T(8,128)S(1)}, u32[]{:S(2)}, u32[]{:S(2)}) collective-permute-start(f32[128,256]{1,0:T(8,128)S(1)} %join_chips.1.refs_3_.refs_1_), channel_id=1, source_target_pairs={{0,64},{32,96},{64,0},{96,32},{128,192},{160,224},{192,128},{224,1... | collective-permute-start | bytes 393224 | tf_op jit(solution)/shard_map/ppermute | solution.py:302
  21.8 4.7 %collective-permute-start.10 = (f32[64,3072]{1,0:T(8,128)}, f32[64,3072]{1,0:T(8,128)S(1)}, u32[]{:S(2)}, u32[]{:S(2)}) collective-permute-start(f32[64,3072]{1,0:T(8,128)} %far.1.refs_4_), channel_id=1, source_target_pairs={{0,264},{8,256},{256,8},{264,0},{1,265},{9,257},{257,9},{265,1},{2... | collective-permute-start | bytes 2359304 | tf_op jit(solution)/shard_map/ppermute | solution.py:276
  26.5 2.1 %collective-permute-start.8 = (f32[64,3072]{1,0:T(8,128)}, f32[64,3072]{1,0:T(8,128)S(1)}, u32[]{:S(2)}, u32[]{:S(2)}) collective-permute-start(f32[64,3072]{1,0:T(8,128)} %near.1.refs_3_), channel_id=1, source_target_pairs={{0,8},{8,0},{1,9},{9,1},{2,10},{10,2},{3,11},{11,3},{4,12},{12,4},... | collective-permute-start | bytes 2359304 | tf_op jit(solution)/shard_map/ppermute | solution.py:276
  28.6 0.0 copy-start.3
  28.6 0.0 collective-permute-done.2.refs_2_
  28.7 0.2 join_pairs.1.refs_4_.refs_1_.refs_2_
  28.9 7.9 %collective-permute-start.3 = (f32[128,256]{1,0:T(8,128)S(1)}, f32[128,256]{1,0:T(8,128)S(1)}, u32[]{:S(2)}, u32[]{:S(2)}) collective-permute-start(f32[128,256]{1,0:T(8,128)S(1)} %join_pairs.1.refs_4_.refs_1_.refs_2_), channel_id=1, source_target_pairs={{0,224},{32,192},{64,160},{96,128},{128,96},{160,64},{192,32},{224... | collective-permute-start | bytes 393224 | tf_op jit(solution)/shard_map/ppermute | solution.py:302
  36.8 0.0 copy-done.3
  36.8 0.2 before_pairs.1.refs_5_.refs_4_
  37.1 4.7 %collective-permute-done.3.refs_3_ = f32[128,256]{1,0:T(8,128)S(1)} collective-permute-done((f32[128,256]{1,0:T(8,128)S(1)}, f32[128,256]{1,0:T(8,128)S(1)}, u32[]{:S(2)}, u32[]{:S(2)}) %collective-permute-start.3) | collective-permute-done | bytes 131104 | tf_op jit(solution)/shard_map/ppermute | solution.py:302
  41.8 0.3 join_ring.1.refs_6_.refs_1_
  42.1 3.7 %collective-permute-start.5 = (f32[128,128]{1,0:T(8,128)S(1)}, f32[128,128]{1,0:T(8,128)S(1)}, u32[]{:S(2)}, u32[]{:S(2)}) collective-permute-start(f32[128,128]{1,0:T(8,128)S(1)} %join_ring.1.refs_6_.refs_1_), channel_id=1, source_target_pairs={{0,256},{16,272},{1,257},{17,273},{2,258},{18,274},{3,259},{19,275... | collective-permute-start | bytes 196616 | tf_op jit(solution)/shard_map/ppermute | solution.py:322
  45.9 1.3 %collective-permute-start.6 = (f32[128,128]{1,0:T(8,128)S(1)}, f32[128,128]{1,0:T(8,128)S(1)}, u32[]{:S(2)}, u32[]{:S(2)}) collective-permute-start(f32[128,128]{1,0:T(8,128)S(1)} %join_ring.1.refs_6_.refs_1_), channel_id=1, source_target_pairs={{0,272},{16,256},{1,273},{17,257},{2,274},{18,258},{3,275},{19,259... | collective-permute-start | bytes 196616 | tf_op jit(solution)/shard_map/ppermute | solution.py:323
  47.2 0.4 shard_prefixes.1
  47.6 2.0 %collective-permute-start.4 = (f32[128,256]{1,0:T(8,128)S(1)}, f32[128,256]{1,0:T(8,128)S(1)}, u32[]{:S(2)}, u32[]{:S(2)}) collective-permute-start(f32[128,256]{1,0:T(8,128)S(1)} %get-tuple-element.26), channel_id=1, source_target_pairs={{0,16},{16,0},{1,17},{17,1},{2,18},{18,2},{3,19},{19,3},{4,20},{20... | collective-permute-start | bytes 393224 | tf_op jit(solution)/shard_map/ppermute | solution.py:276
  49.6 0.0 copy-done.2
  49.7 0.0 collective-permute-done.10.f0
  49.7 2.3 %collective-permute-start.11 = (f32[64,3072]{1,0:T(8,128)S(1)}, f32[64,3072]{1,0:T(8,128)S(1)}, u32[]{:S(2)}, u32[]{:S(2)}) collective-permute-start(f32[64,3072]{1,0:T(8,128)S(1)} %collective-permute-done.10.f0), channel_id=1, source_target_pairs={{0,16},{16,0},{1,17},{17,1},{2,18},{18,2},{3,19},{19,3},{4,20},{20... | collective-permute-start | bytes 2359304 | tf_op jit(solution)/shard_map/ppermute | solution.py:276
  52.0 0.0 collective-permute-done.8.n0
  52.0 2.0 %collective-permute-start.9 = (f32[64,3072]{1,0:T(8,128)S(1)}, f32[64,3072]{1,0:T(8,128)S(1)}, u32[]{:S(2)}, u32[]{:S(2)}) collective-permute-start(f32[64,3072]{1,0:T(8,128)S(1)} %collective-permute-done.8.n0), channel_id=1, source_target_pairs={{0,16},{16,0},{1,17},{17,1},{2,18},{18,2},{3,19},{19,3},{4,20},{20... | collective-permute-start | bytes 2359304 | tf_op jit(solution)/shard_map/ppermute | solution.py:276
  54.1 0.0 collective-permute-done.5.refs_2_
  54.1 0.0 collective-permute-done.6.refs_3_
  54.1 0.0 collective-permute-done.4.refs_2_
  54.1 0.4 outputs.1.later_ref.refs_0_
  54.5 2.5 %collective-permute-start.7 = (f32[160,256]{1,0:T(8,128)S(1)}, f32[160,256]{1,0:T(8,128)S(1)}, u32[]{:S(2)}, u32[]{:S(2)}) collective-permute-start(f32[160,256]{1,0:T(8,128)S(1)} %outputs.1.later_ref.refs_0_), channel_id=1, source_target_pairs={{0,8},{8,0},{1,9},{9,1},{2,10},{10,2},{3,11},{11,3},{4,12},{12,4},... | collective-permute-start | bytes 491528 | tf_op jit(solution)/shard_map/ppermute | solution.py:276
  57.0 0.0 collective-permute-done.11.f1
  57.1 0.0 collective-permute-done.9.n1
  57.1 1.6 %piece_weights.1.refs_2_ = bf16[8,512,384]{2,1,0:T(8,128)(2,1)S(1)} custom-call(s32[1]{0:T(128)} %bitcast.2.x_lo_ref, s32[1]{0:T(128)} %bitcast.4.y_ref, s32[1]{0:T(128)} %bitcast.refs_0_.row_ref.refs_1_.core_ref, bf16[256,6144]{1,0:T(8,128)(2,1)} %w_hbm.1, f32[64,3072]{1,0:T(8,128)S(1)} %collective-permute-done.8.n0, ...), custom_call_target="tpu_custom_call" | custom-call | flops 3000000000 | bytes 131072 | tf_op jit(solution)/shard_map/piece_weights/pallas_call | solution.py:331
  58.6 4.3 %collective-permute-done.7.refs_1_ = f32[160,256]{1,0:T(8,128)S(1)} collective-permute-done((f32[160,256]{1,0:T(8,128)S(1)}, f32[160,256]{1,0:T(8,128)S(1)}, u32[]{:S(2)}, u32[]{:S(2)}) %collective-permute-start.7) | collective-permute-done | bytes 163872 | tf_op jit(solution)/shard_map/ppermute | solution.py:276
  63.0 0.2 farthest.1
  63.2 4.7 %collective-permute-start.16 = (f32[80,384]{1,0:T(8,128)S(1)}, f32[80,384]{1,0:T(8,128)S(1)}, u32[]{:S(2)}, u32[]{:S(2)}) collective-permute-start(f32[80,384]{1,0:T(8,128)S(1)} %get-tuple-element.33), channel_id=1, source_target_pairs={{0,1},{1,2},{2,3},{3,4},{4,5},{5,6},{6,7},{7,0},{8,9},{9,10},{10,1... | collective-permute-start | bytes 368648 | tf_op jit(solution)/shard_map/ppermute | solution.py:281
  67.9 1.9 %collective-permute-start.12 = (f32[80,384]{1,0:T(8,128)S(1)}, f32[80,384]{1,0:T(8,128)S(1)}, u32[]{:S(2)}, u32[]{:S(2)}) collective-permute-start(f32[80,384]{1,0:T(8,128)S(1)} %get-tuple-element.28.refs_3_), channel_id=1, source_target_pairs={{0,7},{1,0},{2,1},{3,2},{4,3},{5,4},{6,5},{7,6},{8,15},{9,8},{10,9... | collective-permute-start | bytes 368648 | tf_op jit(solution)/shard_map/ppermute | solution.py:281
  69.8 0.8 nearer.1
  70.6 0.0 collective-permute-done.16
  70.7 5.3 %collective-permute-start.17 = (f32[160,384]{1,0:T(8,128)S(1)}, f32[160,384]{1,0:T(8,128)S(1)}, u32[]{:S(2)}, u32[]{:S(2)}) collective-permute-start(f32[160,384]{1,0:T(8,128)S(1)} %pad_add_fusion), channel_id=1, source_target_pairs={{0,1},{1,2},{2,3},{3,4},{4,5},{5,6},{6,7},{7,0},{8,9},{9,10},{10,1... | collective-permute-start | bytes 737288 | tf_op jit(solution)/shard_map/ppermute | solution.py:281
  75.9 0.0 collective-permute-done.12
  76.0 1.9 %collective-permute-start.13 = (f32[160,384]{1,0:T(8,128)S(1)}, f32[160,384]{1,0:T(8,128)S(1)}, u32[]{:S(2)}, u32[]{:S(2)}) collective-permute-start(f32[160,384]{1,0:T(8,128)S(1)} %pad_add_fusion.1), channel_id=1, source_target_pairs={{0,7},{1,0},{2,1},{3,2},{4,3},{5,4},{6,5},{7,6},{8,15},{9,8},{10,9... | collective-permute-start | bytes 737288 | tf_op jit(solution)/shard_map/ppermute | solution.py:281
  77.9 2.3 %collective-permute-done.17 = f32[160,384]{1,0:T(8,128)S(1)} collective-permute-done((f32[160,384]{1,0:T(8,128)S(1)}, f32[160,384]{1,0:T(8,128)S(1)}, u32[]{:S(2)}, u32[]{:S(2)}) %collective-permute-start.17) | collective-permute-done | bytes 245792 | tf_op jit(solution)/shard_map/ppermute | solution.py:281
  80.3 5.6 %collective-permute-start.18 = (f32[160,384]{1,0:T(8,128)S(1)}, f32[160,384]{1,0:T(8,128)S(1)}, u32[]{:S(2)}, u32[]{:S(2)}) collective-permute-start(f32[160,384]{1,0:T(8,128)S(1)} %add.36), channel_id=1, source_target_pairs={{0,1},{1,2},{2,3},{3,4},{4,5},{5,6},{6,7},{7,0},{8,9},{9,10},{10,1... | collective-permute-start | bytes 737288 | tf_op jit(solution)/shard_map/ppermute | solution.py:281
  85.9 0.0 collective-permute-done.13
  85.9 1.9 %collective-permute-start.14 = (f32[160,384]{1,0:T(8,128)S(1)}, f32[160,384]{1,0:T(8,128)S(1)}, u32[]{:S(2)}, u32[]{:S(2)}) collective-permute-start(f32[160,384]{1,0:T(8,128)S(1)} %add.33), channel_id=1, source_target_pairs={{0,7},{1,0},{2,1},{3,2},{4,3},{5,4},{6,5},{7,6},{8,15},{9,8},{10,9... | collective-permute-start | bytes 737288 | tf_op jit(solution)/shard_map/ppermute | solution.py:281
  87.8 1.7 %collective-permute-done.18 = f32[160,384]{1,0:T(8,128)S(1)} collective-permute-done((f32[160,384]{1,0:T(8,128)S(1)}, f32[160,384]{1,0:T(8,128)S(1)}, u32[]{:S(2)}, u32[]{:S(2)}) %collective-permute-start.18) | collective-permute-done | bytes 245792 | tf_op jit(solution)/shard_map/ppermute | solution.py:281
  89.6 5.6 %collective-permute-start.19 = (f32[160,384]{1,0:T(8,128)S(1)}, f32[160,384]{1,0:T(8,128)S(1)}, u32[]{:S(2)}, u32[]{:S(2)}) collective-permute-start(f32[160,384]{1,0:T(8,128)S(1)} %add.37), channel_id=1, source_target_pairs={{0,1},{1,2},{2,3},{3,4},{4,5},{5,6},{6,7},{7,0},{8,9},{9,10},{10,1... | collective-permute-start | bytes 737288 | tf_op jit(solution)/shard_map/ppermute | solution.py:281
  95.2 0.0 collective-permute-done.14
  95.2 1.9 %collective-permute-start.15 = (f32[160,384]{1,0:T(8,128)S(1)}, f32[160,384]{1,0:T(8,128)S(1)}, u32[]{:S(2)}, u32[]{:S(2)}) collective-permute-start(f32[160,384]{1,0:T(8,128)S(1)} %add.34), channel_id=1, source_target_pairs={{0,7},{1,0},{2,1},{3,2},{4,3},{5,4},{6,5},{7,6},{8,15},{9,8},{10,9... | collective-permute-start | bytes 737288 | tf_op jit(solution)/shard_map/ppermute | solution.py:281
  97.2 1.7 %collective-permute-done.19 = f32[160,384]{1,0:T(8,128)S(1)} collective-permute-done((f32[160,384]{1,0:T(8,128)S(1)}, f32[160,384]{1,0:T(8,128)S(1)}, u32[]{:S(2)}, u32[]{:S(2)}) %collective-permute-start.19) | collective-permute-done | bytes 245792 | tf_op jit(solution)/shard_map/ppermute | solution.py:281
  98.9 5.7 %collective-permute-done.15 = f32[160,384]{1,0:T(8,128)S(1)} collective-permute-done((f32[160,384]{1,0:T(8,128)S(1)}, f32[160,384]{1,0:T(8,128)S(1)}, u32[]{:S(2)}, u32[]{:S(2)}) %collective-permute-start.15) | collective-permute-done | bytes 245792 | tf_op jit(solution)/shard_map/ppermute | solution.py:281
  104.5 0.7 add_convert_fusion
  (24 shorter events, 0.3 us)
Async XLA Ops:
  0.0 5.2 %copy-start.8 = (bf16[160,256]{1,0:T(8,128)(2,1)S(1)}, bf16[160,256]{1,0:T(8,128)(2,1)}, u32[]{:S(2)}) copy-start(bf16[160,256]{1,0:T(8,128)(2,1)} %refs_1_.3) | copy-start | bytes 245764
  0.0 5.3 %copy-start.9 = (bf16[160,256]{1,0:T(8,128)(2,1)S(1)}, bf16[160,256]{1,0:T(8,128)(2,1)}, u32[]{:S(2)}) copy-start(bf16[160,256]{1,0:T(8,128)(2,1)} %refs_0_.2) | copy-start | bytes 245764
  0.0 5.3 %copy-start.10 = (f32[2,160]{1,0:T(2,128)S(1)}, f32[2,160]{1,0:T(2,128)}, u32[]{:S(2)}) copy-start(f32[2,160]{1,0:T(2,128)} %refs_2_.3) | copy-start | bytes 3844
  3.0 3.5 %copy-start.4 = (f32[128,256]{1,0:T(8,128)}, f32[128,256]{1,0:T(8,128)S(1)}, u32[]{:S(2)}) copy-start(f32[128,256]{1,0:T(8,128)S(1)} %get-tuple-element.21.refs_1_) | copy-start | bytes 393220
  3.0 10.3 %copy-start = (bf16[256,6144]{1,0:T(8,128)(2,1)S(1)}, bf16[256,6144]{1,0:T(8,128)(2,1)}, u32[]{:S(2)}) copy-start(bf16[256,6144]{1,0:T(8,128)(2,1)} %w_hbm.1) | copy-start | bytes 9437188
  3.1 3.5 %collective-permute-start = (f32[128,256]{1,0:T(8,128)S(1)}, f32[128,256]{1,0:T(8,128)S(1)}, u32[]{:S(2)}, u32[]{:S(2)}) collective-permute-start(f32[128,256]{1,0:T(8,128)S(1)} %get-tuple-element.22), channel_id=1, source_target_pairs={{0,16},{16,0},{1,17},{17,1},{2,18},{18,2},{3,19},{19,3},{4,20},{20... | collective-permute-start | bytes 393224 | tf_op jit(solution)/shard_map/ppermute | solution.py:276
  5.7 0.7 copy-start.1
  6.6 0.6 copy-start.6
  7.2 8.3 %collective-permute-start.1 = (f32[128,256]{1,0:T(8,128)S(1)}, f32[128,256]{1,0:T(8,128)S(1)}, u32[]{:S(2)}, u32[]{:S(2)}) collective-permute-start(f32[128,256]{1,0:T(8,128)S(1)} %chip_map.1.refs_3_.refs_1_), channel_id=1, source_target_pairs={{0,32},{32,0},{64,96},{96,64},{128,160},{160,128},{192,224},{224,1... | collective-permute-start | bytes 393224 | tf_op jit(solution)/shard_map/ppermute | solution.py:302
  11.5 0.9 copy-start.5
  12.4 0.9 copy-start.7
  15.7 12.9 %collective-permute-start.2 = (f32[128,256]{1,0:T(8,128)S(1)}, f32[128,256]{1,0:T(8,128)S(1)}, u32[]{:S(2)}, u32[]{:S(2)}) collective-permute-start(f32[128,256]{1,0:T(8,128)S(1)} %join_chips.1.refs_3_.refs_1_), channel_id=1, source_target_pairs={{0,64},{32,96},{64,0},{96,32},{128,192},{160,224},{192,128},{224,1... | collective-permute-start | bytes 393224 | tf_op jit(solution)/shard_map/ppermute | solution.py:302
  21.8 27.9 %collective-permute-start.10 = (f32[64,3072]{1,0:T(8,128)}, f32[64,3072]{1,0:T(8,128)S(1)}, u32[]{:S(2)}, u32[]{:S(2)}) collective-permute-start(f32[64,3072]{1,0:T(8,128)} %far.1.refs_4_), channel_id=1, source_target_pairs={{0,264},{8,256},{256,8},{264,0},{1,265},{9,257},{257,9},{265,1},{2... | collective-permute-start | bytes 2359304 | tf_op jit(solution)/shard_map/ppermute | solution.py:276
  26.5 25.5 %collective-permute-start.8 = (f32[64,3072]{1,0:T(8,128)}, f32[64,3072]{1,0:T(8,128)S(1)}, u32[]{:S(2)}, u32[]{:S(2)}) collective-permute-start(f32[64,3072]{1,0:T(8,128)} %near.1.refs_3_), channel_id=1, source_target_pairs={{0,8},{8,0},{1,9},{9,1},{2,10},{10,2},{3,11},{11,3},{4,12},{12,4},... | collective-permute-start | bytes 2359304 | tf_op jit(solution)/shard_map/ppermute | solution.py:276
  28.6 8.2 %copy-start.3 = (f32[2,128,128]{2,1,0:T(8,128)S(1)}, f32[2,128,128]{2,1,0:T(8,128)}, u32[]{:S(2)}) copy-start(f32[2,128,128]{2,1,0:T(8,128)} %refs_0_.3) | copy-start | bytes 393220
  28.9 12.9 %collective-permute-start.3 = (f32[128,256]{1,0:T(8,128)S(1)}, f32[128,256]{1,0:T(8,128)S(1)}, u32[]{:S(2)}, u32[]{:S(2)}) collective-permute-start(f32[128,256]{1,0:T(8,128)S(1)} %join_pairs.1.refs_4_.refs_1_.refs_2_), channel_id=1, source_target_pairs={{0,224},{32,192},{64,160},{96,128},{128,96},{160,64},{192,32},{224... | collective-permute-start | bytes 393224 | tf_op jit(solution)/shard_map/ppermute | solution.py:302
  37.1 12.6 %copy-start.2 = (f32[160,512]{1,0:T(8,128)S(1)}, f32[160,512]{1,0:T(8,128)}, u32[]{:S(2)}) copy-start(f32[160,512]{1,0:T(8,128)} %copy-done.1) | copy-start | bytes 983044
  42.1 11.9 %collective-permute-start.5 = (f32[128,128]{1,0:T(8,128)S(1)}, f32[128,128]{1,0:T(8,128)S(1)}, u32[]{:S(2)}, u32[]{:S(2)}) collective-permute-start(f32[128,128]{1,0:T(8,128)S(1)} %join_ring.1.refs_6_.refs_1_), channel_id=1, source_target_pairs={{0,256},{16,272},{1,257},{17,273},{2,258},{18,274},{3,259},{19,275... | collective-permute-start | bytes 196616 | tf_op jit(solution)/shard_map/ppermute | solution.py:322
  45.9 8.2 %collective-permute-start.6 = (f32[128,128]{1,0:T(8,128)S(1)}, f32[128,128]{1,0:T(8,128)S(1)}, u32[]{:S(2)}, u32[]{:S(2)}) collective-permute-start(f32[128,128]{1,0:T(8,128)S(1)} %join_ring.1.refs_6_.refs_1_), channel_id=1, source_target_pairs={{0,272},{16,256},{1,273},{17,257},{2,274},{18,258},{3,275},{19,259... | collective-permute-start | bytes 196616 | tf_op jit(solution)/shard_map/ppermute | solution.py:323
  47.6 6.5 %collective-permute-start.4 = (f32[128,256]{1,0:T(8,128)S(1)}, f32[128,256]{1,0:T(8,128)S(1)}, u32[]{:S(2)}, u32[]{:S(2)}) collective-permute-start(f32[128,256]{1,0:T(8,128)S(1)} %get-tuple-element.26), channel_id=1, source_target_pairs={{0,16},{16,0},{1,17},{17,1},{2,18},{18,2},{3,19},{19,3},{4,20},{20... | collective-permute-start | bytes 393224 | tf_op jit(solution)/shard_map/ppermute | solution.py:276
  49.7 7.4 %collective-permute-start.11 = (f32[64,3072]{1,0:T(8,128)S(1)}, f32[64,3072]{1,0:T(8,128)S(1)}, u32[]{:S(2)}, u32[]{:S(2)}) collective-permute-start(f32[64,3072]{1,0:T(8,128)S(1)} %collective-permute-done.10.f0), channel_id=1, source_target_pairs={{0,16},{16,0},{1,17},{17,1},{2,18},{18,2},{3,19},{19,3},{4,20},{20... | collective-permute-start | bytes 2359304 | tf_op jit(solution)/shard_map/ppermute | solution.py:276
  52.0 5.0 %collective-permute-start.9 = (f32[64,3072]{1,0:T(8,128)S(1)}, f32[64,3072]{1,0:T(8,128)S(1)}, u32[]{:S(2)}, u32[]{:S(2)}) collective-permute-start(f32[64,3072]{1,0:T(8,128)S(1)} %collective-permute-done.8.n0), channel_id=1, source_target_pairs={{0,16},{16,0},{1,17},{17,1},{2,18},{18,2},{3,19},{19,3},{4,20},{20... | collective-permute-start | bytes 2359304 | tf_op jit(solution)/shard_map/ppermute | solution.py:276
  54.5 8.4 %collective-permute-start.7 = (f32[160,256]{1,0:T(8,128)S(1)}, f32[160,256]{1,0:T(8,128)S(1)}, u32[]{:S(2)}, u32[]{:S(2)}) collective-permute-start(f32[160,256]{1,0:T(8,128)S(1)} %outputs.1.later_ref.refs_0_), channel_id=1, source_target_pairs={{0,8},{8,0},{1,9},{9,1},{2,10},{10,2},{3,11},{11,3},{4,12},{12,4},... | collective-permute-start | bytes 491528 | tf_op jit(solution)/shard_map/ppermute | solution.py:276
  63.2 7.4 %collective-permute-start.16 = (f32[80,384]{1,0:T(8,128)S(1)}, f32[80,384]{1,0:T(8,128)S(1)}, u32[]{:S(2)}, u32[]{:S(2)}) collective-permute-start(f32[80,384]{1,0:T(8,128)S(1)} %get-tuple-element.33), channel_id=1, source_target_pairs={{0,1},{1,2},{2,3},{3,4},{4,5},{5,6},{6,7},{7,0},{8,9},{9,10},{10,1... | collective-permute-start | bytes 368648 | tf_op jit(solution)/shard_map/ppermute | solution.py:281
  67.9 8.0 %collective-permute-start.12 = (f32[80,384]{1,0:T(8,128)S(1)}, f32[80,384]{1,0:T(8,128)S(1)}, u32[]{:S(2)}, u32[]{:S(2)}) collective-permute-start(f32[80,384]{1,0:T(8,128)S(1)} %get-tuple-element.28.refs_3_), channel_id=1, source_target_pairs={{0,7},{1,0},{2,1},{3,2},{4,3},{5,4},{6,5},{7,6},{8,15},{9,8},{10,9... | collective-permute-start | bytes 368648 | tf_op jit(solution)/shard_map/ppermute | solution.py:281
  70.7 9.6 %collective-permute-start.17 = (f32[160,384]{1,0:T(8,128)S(1)}, f32[160,384]{1,0:T(8,128)S(1)}, u32[]{:S(2)}, u32[]{:S(2)}) collective-permute-start(f32[160,384]{1,0:T(8,128)S(1)} %pad_add_fusion), channel_id=1, source_target_pairs={{0,1},{1,2},{2,3},{3,4},{4,5},{5,6},{6,7},{7,0},{8,9},{9,10},{10,1... | collective-permute-start | bytes 737288 | tf_op jit(solution)/shard_map/ppermute | solution.py:281
  76.0 9.9 %collective-permute-start.13 = (f32[160,384]{1,0:T(8,128)S(1)}, f32[160,384]{1,0:T(8,128)S(1)}, u32[]{:S(2)}, u32[]{:S(2)}) collective-permute-start(f32[160,384]{1,0:T(8,128)S(1)} %pad_add_fusion.1), channel_id=1, source_target_pairs={{0,7},{1,0},{2,1},{3,2},{4,3},{5,4},{6,5},{7,6},{8,15},{9,8},{10,9... | collective-permute-start | bytes 737288 | tf_op jit(solution)/shard_map/ppermute | solution.py:281
  80.3 9.3 %collective-permute-start.18 = (f32[160,384]{1,0:T(8,128)S(1)}, f32[160,384]{1,0:T(8,128)S(1)}, u32[]{:S(2)}, u32[]{:S(2)}) collective-permute-start(f32[160,384]{1,0:T(8,128)S(1)} %add.36), channel_id=1, source_target_pairs={{0,1},{1,2},{2,3},{3,4},{4,5},{5,6},{6,7},{7,0},{8,9},{9,10},{10,1... | collective-permute-start | bytes 737288 | tf_op jit(solution)/shard_map/ppermute | solution.py:281
  85.9 9.3 %collective-permute-start.14 = (f32[160,384]{1,0:T(8,128)S(1)}, f32[160,384]{1,0:T(8,128)S(1)}, u32[]{:S(2)}, u32[]{:S(2)}) collective-permute-start(f32[160,384]{1,0:T(8,128)S(1)} %add.33), channel_id=1, source_target_pairs={{0,7},{1,0},{2,1},{3,2},{4,3},{5,4},{6,5},{7,6},{8,15},{9,8},{10,9... | collective-permute-start | bytes 737288 | tf_op jit(solution)/shard_map/ppermute | solution.py:281
  89.6 9.3 %collective-permute-start.19 = (f32[160,384]{1,0:T(8,128)S(1)}, f32[160,384]{1,0:T(8,128)S(1)}, u32[]{:S(2)}, u32[]{:S(2)}) collective-permute-start(f32[160,384]{1,0:T(8,128)S(1)} %add.37), channel_id=1, source_target_pairs={{0,1},{1,2},{2,3},{3,4},{4,5},{5,6},{6,7},{7,0},{8,9},{9,10},{10,1... | collective-permute-start | bytes 737288 | tf_op jit(solution)/shard_map/ppermute | solution.py:281
  95.2 9.3 %collective-permute-start.15 = (f32[160,384]{1,0:T(8,128)S(1)}, f32[160,384]{1,0:T(8,128)S(1)}, u32[]{:S(2)}, u32[]{:S(2)}) collective-permute-start(f32[160,384]{1,0:T(8,128)S(1)} %add.34), channel_id=1, source_target_pairs={{0,7},{1,0},{2,1},{3,2},{4,3},{5,4},{6,5},{7,6},{8,15},{9,8},{10,9... | collective-permute-start | bytes 737288 | tf_op jit(solution)/shard_map/ppermute | solution.py:281

commit v8 on v7

--- a/solution.py
+++ b/solution.py
@@ -125,13 +125,14 @@
     return jnp.where(first_core, keep, got), jnp.where(first_core, got, keep)
 
 
-def chip_map(core_ref, keep_ref, got_ref, out_ref):
+def chip_map(core_ref, keep_ref, got_ref, later_ref, out_ref, early_hbm, early_ref, done):
+    del later_ref
     early, late = in_order(core_ref[0] == 0, keep_ref, got_ref)
+    early_ref[...] = early
+    copy = pltpu.make_async_copy(early_ref, early_hbm, done)
+    copy.start()
     out_ref[...] = after(late, early)
-
-
-def first_map(core_ref, keep_ref, got_ref, out_ref):
-    out_ref[...] = in_order(core_ref[0] == 0, keep_ref, got_ref)[0]
+    copy.wait()
 
 
 def is_upper(z, span):
@@ -202,28 +203,30 @@
         z_ref[:, at] = z.astype(bf16).astype(f32)
 
 
-def copied(column_ref, row_ref, w_ref, later_ref, out_ref):
+def share_weights(column_ref, row_ref, near_in, far_in, later_ref, near_ref, far_ref):
     del column_ref, row_ref, later_ref
-    out_ref[...] = w_ref[...].astype(out_ref.dtype)
-
-
-def weight_share(weight, column, row, rows, dtype, later, name):
+    near_ref[...] = near_in[...].astype(f32)
+    far_ref[...] = far_in[...].astype(f32)
+
+
+def weight_shares(weight, column, row, rows, later):
     columns, parts = weight.shape[1] // SIZES[3], 2
     return pl.pallas_call(
-        copied,
-        name=name,
+        share_weights,
+        name="share_weights",
         grid_spec=pltpu.PrefetchScalarGridSpec(
             num_scalar_prefetch=2,
             grid=(parts,),
             in_specs=[
                 pl.BlockSpec((rows, columns // parts), lambda i, c, r: (r[0], c[0] * parts + i)),
+                pl.BlockSpec((rows, columns // parts), lambda i, c, r: (r[0] + 2, c[0] * parts + i)),
                 pl.BlockSpec(memory_space=pl.ANY),
             ],
-            out_specs=pl.BlockSpec((rows, columns // parts), lambda i, c, r: (0, i)),
+            out_specs=[pl.BlockSpec((rows, columns // parts), lambda i, c, r: (0, i))] * 2,
         ),
-        out_shape=jax.ShapeDtypeStruct((rows, columns), dtype),
+        out_shape=[jax.ShapeDtypeStruct((rows, columns), f32)] * 2,
         compiler_params=pltpu.CompilerParams(vmem_limit_bytes=8 * MIB),
-    )(column, row, weight, later)
+    )(column, row, weight, weight, later)
 
 
 OFFSETS = (4, -3, 3, -2, 2, -1, 1, 0)
@@ -302,17 +305,23 @@
         return lax.ppermute(x, Z, [(i, to(i)) for i in range(SIZES[1])])
 
     own_rows, token = call(shard_rows, [((rows, 4 * HW), f32), ((8, HW), f32)], [], queries, keys, rates, solved, us=0.1)
-    (chip,) = call(chip_map, [wide], [core], keep, got, later=[token])
-    (early,) = call(first_map, [wide], [core], keep, got, later=[chip], us=0.1)
-    near_out = weight_share(out_weight, 1 - x_lo, core, share, f32, early, "near")
-    far_out = weight_share(out_weight, 1 - x_lo, core + 2, share, f32, early, "far")
+    chip, early = pl.pallas_call(
+        chip_map,
+        name="chip_map",
+        out_shape=[jax.ShapeDtypeStruct((HW, 2 * HW), f32), pltpu.HBM((HW, 2 * HW), f32)],
+        in_specs=[SM, VM, VM, pl.BlockSpec(memory_space=pl.ANY)],
+        out_specs=[VM, pl.BlockSpec(memory_space=pltpu.HBM)],
+        scratch_shapes=[pltpu.VMEM((HW, 2 * HW), f32), pltpu.SemaphoreType.DMA],
+        compiler_params=pltpu.CompilerParams(vmem_limit_bytes=4 * MIB),
+    )(core, keep, got, token)
+    near_out, far_out = weight_shares(out_weight, 1 - x_lo, core, share, chip)
     near = swapped(near_out, (XL,))
     got_chip = across_z(chip, lambda i: i ^ 1)
-    (both,) = call(join_chips, [wide], [z], chip, got_chip, later=[near_out, far_out, early], us=0.6)
+    (both,) = call(join_chips, [wide], [z], chip, got_chip, later=[near_out], us=0.3)
     (pre,) = call(before_chips, [wide], [z], chip, got_chip, later=[both], us=0.1)
     far = swapped(far_out, (XH, XL))
     got_both = across_z(both, lambda i: i ^ 2)
-    (four,) = call(join_pairs, [wide], [z], both, got_both, later=[pre], us=4)
+    (four,) = call(join_pairs, [wide], [z], both, got_both, later=[pre], us=0.3)
     (pre,) = call(before_pairs, [wide], [z], both, got_both, pre, later=[four], us=0.1)
     near_other = swapped(near, (CORE,))
     (first,) = call(fetched, [((2, HW, HW), f32)], [], init_weight, later=[four], us=0.1)
@@ -325,7 +334,7 @@
     (begin,) = call(ring_states, [((2, HW, HW), f32)], [x_hi, core], here, there, first, us=12)
     (late_rows,) = call(fetched, [((rows, 4 * HW), f32)], [], own_rows, later=[end], us=0.1)
     (z_rows,) = call(
-        outputs, [((rows, 2 * HW), f32)], [core], mine, swapped(other, (CORE,)), begin, late_rows, us=8
+        outputs, [((rows, 2 * HW), f32)], [core], mine, swapped(other, (CORE,)), begin, late_rows, us=4
     )
     z_pair = swapped(z_rows, (XL,))
     weights = pl.pallas_call(

time: 106 us -> 108 us (1.019)
  waiting for transfers between devices: 20.8 us -> 25.6 us
  local copies, waits for them, and re-layouts: 2.97 us -> 0.76 us
    ppermute x3, waiting for transfers between devices: 4.87 us -> 10.2 us  [across_z(): return lax.ppermute(x, Z, [(i, to(i)) for i in range(SIZES[1])])]
    unnamed x22 -> x16, local copies, waits for them, and re-layouts: 2.97 us -> 0.76 us
    pallas_call x16 -> x14, Pallas kernels: 6.56 us -> 6.44 us  [call(): pl.pallas_call(body, name=kernel.__name__, out_shape=outs, in_specs=[SM]...]
where the time goes in v8:
time: 108 us
  starting transfers between devices  69.8 us (65%)
  waiting for transfers between devices  25.6 us (24%)
  Pallas kernels  10 us (9%)
    ppermute x8, starting transfers between devices, passed(): return lax.ppermute(x, axis, [(i, (i + by) % n) for i in range(n)])  28.8 us
    ppermute x7, starting transfers between devices, swapped(): return lax.ppermute(x, axes, [(i, n - 1 - i) for i in range(n)])  18.6 us
    ppermute x3, starting transfers between devices, across_z(): return lax.ppermute(x, Z, [(i, to(i)) for i in range(SIZES[1])])  18.2 us
    ppermute x8, waiting for transfers between devices, passed(): return lax.ppermute(x, axis, [(i, (i + by) % n) for i in range(n)])  11.4 us
    ppermute x3, waiting for transfers between devices, across_z(): return lax.ppermute(x, Z, [(i, to(i)) for i in range(SIZES[1])])  10.2 us
    pallas_call x14, Pallas kernels, call(): pl.pallas_call(body, name=kernel.__name__, out_shape=outs, in_specs=[SM]...  6.44 us
    ppermute x7, waiting for transfers between devices, swapped(): return lax.ppermute(x, axes, [(i, n - 1 - i) for i in range(n)])  3.97 us
    ppermute x1, starting transfers between devices, local(): here = lax.ppermute(end, (XH, CORE), [(0, 2), (1, 3)])  2.8 us
  transfers between devices with their start and end apart: 20, of which 8 were waited for; matrix products, arithmetic and copies ran while one was open for 0% of the time, Pallas kernels for 6%

profile of v8, /device:TPU:24, one launch (start us, length us, event | category | flops | bytes accessed | tf_op | source)
XLA Modules:
  0.0 107.5 jit_solution(3872633771973848067)
XLA Ops:
  0.0 0.0 copy-start
  0.0 3.1 %shard_maps.1 = (f32[128,256]{1,0:T(8,128)S(1)}, f32[128,256]{1,0:T(8,128)S(1)}, f32[2,160,256]{2,1,0:T(8,128)S(1)}) custom-call(s32[1]{0:T(128)} %bitcast.refs_0_.core_ref.row_ref.refs_1_, bf16[160,256]{1,0:T(8,128)(2,1)} %refs_1_.3, bf16[160,256]{1,0:T(8,128)(2,1)} %refs_2_.2, f32[2,160]{1,0:T(2,128)} %refs_2_.3), custom_call_target="tpu_custom_call" | custom-call | flops 3000000000 | bytes 131072 | tf_op jit(solution)/shard_map/shard_maps/pallas_call | solution.py:36
  3.2 1.9 %collective-permute-start = (f32[128,256]{1,0:T(8,128)S(1)}, f32[128,256]{1,0:T(8,128)S(1)}, u32[]{:S(2)}, u32[]{:S(2)}) collective-permute-start(f32[128,256]{1,0:T(8,128)S(1)} %get-tuple-element.26), channel_id=1, source_target_pairs={{0,16},{16,0},{1,17},{17,1},{2,18},{18,2},{3,19},{19,3},{4,20},{20... | collective-permute-start | bytes 393224 | tf_op jit(solution)/shard_map/ppermute | solution.py:279
  5.1 0.0 copy-done.5
  5.1 0.0 copy-done.6
  5.1 0.0 copy-done.7
  5.1 0.4 shard_rows.1
  5.5 0.0 copy-start.1
  5.6 0.7 copy-done.1
  6.3 0.1 collective-permute-done.got_ref
  6.4 0.7 chip_map.1
  7.1 4.3 %collective-permute-start.1 = (f32[128,256]{1,0:T(8,128)S(1)}, f32[128,256]{1,0:T(8,128)S(1)}, u32[]{:S(2)}, u32[]{:S(2)}) collective-permute-start(f32[128,256]{1,0:T(8,128)S(1)} %get-tuple-element.29.later_ref.refs_1_), channel_id=1, source_target_pairs={{0,32},{32,0},{64,96},{96,64},{128,160},{160,128},{192,224},{224,1... | collective-permute-start | bytes 393224 | tf_op jit(solution)/shard_map/ppermute | solution.py:305
  11.4 0.0 copy-done
  11.4 0.0 copy-start.3
  11.4 1.3 %share_weights.1 = (f32[64,3072]{1,0:T(8,128)}, f32[64,3072]{1,0:T(8,128)}) custom-call(s32[1]{0:T(128)S(6)} %sub.3.column_ref, s32[1]{0:T(128)} %bitcast.refs_0_.core_ref.row_ref.refs_1_, bf16[256,6144]{1,0:T(8,128)(2,1)S(1)} %copy-done, bf16[256,6144]{1,0:T(8,128)(2,1)S(1)} %copy-done, f32[128,256]{1,0:T(8,128)S(1)} %get-tuple-element.29.later_ref.refs_1_), custom_call_target="tpu_custom_call" | custom-call | tf_op jit(solution)/shard_map/share_weights/pallas_call | solution.py:214
  12.7 3.4 %collective-permute-start.8 = (f32[64,3072]{1,0:T(8,128)}, f32[64,3072]{1,0:T(8,128)S(1)}, u32[]{:S(2)}, u32[]{:S(2)}) collective-permute-start(f32[64,3072]{1,0:T(8,128)} %get-tuple-element.30.refs_3_), channel_id=1, source_target_pairs={{0,8},{8,0},{1,9},{9,1},{2,10},{10,2},{3,11},{11,3},{4,12},{12,4},... | collective-permute-start | bytes 2359304 | tf_op jit(solution)/shard_map/ppermute | solution.py:279
  16.1 4.0 %collective-permute-start.10 = (f32[64,3072]{1,0:T(8,128)}, f32[64,3072]{1,0:T(8,128)S(1)}, u32[]{:S(2)}, u32[]{:S(2)}) collective-permute-start(f32[64,3072]{1,0:T(8,128)} %get-tuple-element.35), channel_id=1, source_target_pairs={{0,264},{8,256},{256,8},{264,0},{1,265},{9,257},{257,9},{265,1},{2... | collective-permute-start | bytes 2359304 | tf_op jit(solution)/shard_map/ppermute | solution.py:279
  20.1 0.0 collective-permute-done.1.refs_2_
  20.2 0.2 join_chips.1.refs_3_.refs_1_
  20.4 6.1 %collective-permute-start.2 = (f32[128,256]{1,0:T(8,128)S(1)}, f32[128,256]{1,0:T(8,128)S(1)}, u32[]{:S(2)}, u32[]{:S(2)}) collective-permute-start(f32[128,256]{1,0:T(8,128)S(1)} %join_chips.1.refs_3_.refs_1_), channel_id=1, source_target_pairs={{0,64},{32,96},{64,0},{96,32},{128,192},{160,224},{192,128},{224,1... | collective-permute-start | bytes 393224 | tf_op jit(solution)/shard_map/ppermute | solution.py:305
  26.5 5.7 %collective-permute-done.2.refs_2_ = f32[128,256]{1,0:T(8,128)S(1)} collective-permute-done((f32[128,256]{1,0:T(8,128)S(1)}, f32[128,256]{1,0:T(8,128)S(1)}, u32[]{:S(2)}, u32[]{:S(2)}) %collective-permute-start.2) | collective-permute-done | bytes 131104 | tf_op jit(solution)/shard_map/ppermute | solution.py:305
  32.2 0.2 join_pairs.1.refs_4_.refs_1_.refs_2_
  32.4 7.9 %collective-permute-start.3 = (f32[128,256]{1,0:T(8,128)S(1)}, f32[128,256]{1,0:T(8,128)S(1)}, u32[]{:S(2)}, u32[]{:S(2)}) collective-permute-start(f32[128,256]{1,0:T(8,128)S(1)} %join_pairs.1.refs_4_.refs_1_.refs_2_), channel_id=1, source_target_pairs={{0,224},{32,192},{64,160},{96,128},{128,96},{160,64},{192,32},{224... | collective-permute-start | bytes 393224 | tf_op jit(solution)/shard_map/ppermute | solution.py:305
  40.3 0.0 copy-done.3
  40.3 0.2 before_pairs.1.refs_5_.refs_4_
  40.6 0.0 copy-start.4
  40.6 4.4 %collective-permute-done.3.refs_3_ = f32[128,256]{1,0:T(8,128)S(1)} collective-permute-done((f32[128,256]{1,0:T(8,128)S(1)}, f32[128,256]{1,0:T(8,128)S(1)}, u32[]{:S(2)}, u32[]{:S(2)}) %collective-permute-start.3) | collective-permute-done | bytes 131104 | tf_op jit(solution)/shard_map/ppermute | solution.py:305
  45.0 0.3 join_ring.1.refs_6_.refs_1_
  45.4 2.8 %collective-permute-start.5 = (f32[128,128]{1,0:T(8,128)S(1)}, f32[128,128]{1,0:T(8,128)S(1)}, u32[]{:S(2)}, u32[]{:S(2)}) collective-permute-start(f32[128,128]{1,0:T(8,128)S(1)} %join_ring.1.refs_6_.refs_1_), channel_id=1, source_target_pairs={{0,256},{16,272},{1,257},{17,273},{2,258},{18,274},{3,259},{19,275... | collective-permute-start | bytes 196616 | tf_op jit(solution)/shard_map/ppermute | solution.py:331
  48.2 1.3 %collective-permute-start.6 = (f32[128,128]{1,0:T(8,128)S(1)}, f32[128,128]{1,0:T(8,128)S(1)}, u32[]{:S(2)}, u32[]{:S(2)}) collective-permute-start(f32[128,128]{1,0:T(8,128)S(1)} %join_ring.1.refs_6_.refs_1_), channel_id=1, source_target_pairs={{0,272},{16,256},{1,273},{17,257},{2,274},{18,258},{3,275},{19,259... | collective-permute-start | bytes 196616 | tf_op jit(solution)/shard_map/ppermute | solution.py:332
  49.5 0.4 shard_prefixes.1
  49.9 2.0 %collective-permute-start.4 = (f32[128,256]{1,0:T(8,128)S(1)}, f32[128,256]{1,0:T(8,128)S(1)}, u32[]{:S(2)}, u32[]{:S(2)}) collective-permute-start(f32[128,256]{1,0:T(8,128)S(1)} %get-tuple-element.33), channel_id=1, source_target_pairs={{0,16},{16,0},{1,17},{17,1},{2,18},{18,2},{3,19},{19,3},{4,20},{20... | collective-permute-start | bytes 393224 | tf_op jit(solution)/shard_map/ppermute | solution.py:279
  52.0 0.0 collective-permute-done.8.n0
  52.0 2.3 %collective-permute-start.9 = (f32[64,3072]{1,0:T(8,128)S(1)}, f32[64,3072]{1,0:T(8,128)S(1)}, u32[]{:S(2)}, u32[]{:S(2)}) collective-permute-start(f32[64,3072]{1,0:T(8,128)S(1)} %collective-permute-done.8.n0), channel_id=1, source_target_pairs={{0,16},{16,0},{1,17},{17,1},{2,18},{18,2},{3,19},{19,3},{4,20},{20... | collective-permute-start | bytes 2359304 | tf_op jit(solution)/shard_map/ppermute | solution.py:279
  54.3 0.0 collective-permute-done.10.f0
  54.3 2.0 %collective-permute-start.11 = (f32[64,3072]{1,0:T(8,128)S(1)}, f32[64,3072]{1,0:T(8,128)S(1)}, u32[]{:S(2)}, u32[]{:S(2)}) collective-permute-start(f32[64,3072]{1,0:T(8,128)S(1)} %collective-permute-done.10.f0), channel_id=1, source_target_pairs={{0,16},{16,0},{1,17},{17,1},{2,18},{18,2},{3,19},{19,3},{4,20},{20... | collective-permute-start | bytes 2359304 | tf_op jit(solution)/shard_map/ppermute | solution.py:279
  56.4 0.0 collective-permute-done.5.refs_2_
  56.4 0.0 collective-permute-done.6.refs_3_
  56.4 0.0 collective-permute-done.4.refs_2_
  56.4 0.4 outputs.1.later_ref.refs_0_
  56.8 3.0 %collective-permute-start.7 = (f32[160,256]{1,0:T(8,128)S(1)}, f32[160,256]{1,0:T(8,128)S(1)}, u32[]{:S(2)}, u32[]{:S(2)}) collective-permute-start(f32[160,256]{1,0:T(8,128)S(1)} %outputs.1.later_ref.refs_0_), channel_id=1, source_target_pairs={{0,8},{8,0},{1,9},{9,1},{2,10},{10,2},{3,11},{11,3},{4,12},{12,4},... | collective-permute-start | bytes 491528 | tf_op jit(solution)/shard_map/ppermute | solution.py:279
  59.8 0.0 collective-permute-done.9.n1
  59.8 0.0 collective-permute-done.11.f1
  59.8 1.6 %piece_weights.1.refs_2_ = bf16[8,512,384]{2,1,0:T(8,128)(2,1)S(1)} custom-call(s32[1]{0:T(128)} %bitcast.2.x_lo_ref, s32[1]{0:T(128)} %bitcast.4.y_ref, s32[1]{0:T(128)} %bitcast.refs_0_.core_ref.row_ref.refs_1_, bf16[256,6144]{1,0:T(8,128)(2,1)} %w_hbm.1, f32[64,3072]{1,0:T(8,128)S(1)} %collective-permute-done.8.n0, ...), custom_call_target="tpu_custom_call" | custom-call | flops 3000000000 | bytes 131072 | tf_op jit(solution)/shard_map/piece_weights/pallas_call | solution.py:340
  61.4 3.8 %collective-permute-done.7.refs_1_ = f32[160,256]{1,0:T(8,128)S(1)} collective-permute-done((f32[160,256]{1,0:T(8,128)S(1)}, f32[160,256]{1,0:T(8,128)S(1)}, u32[]{:S(2)}, u32[]{:S(2)}) %collective-permute-start.7) | collective-permute-done | bytes 163872 | tf_op jit(solution)/shard_map/ppermute | solution.py:279
  65.3 0.2 farthest.1
  65.5 4.7 %collective-permute-start.16 = (f32[80,384]{1,0:T(8,128)S(1)}, f32[80,384]{1,0:T(8,128)S(1)}, u32[]{:S(2)}, u32[]{:S(2)}) collective-permute-start(f32[80,384]{1,0:T(8,128)S(1)} %get-tuple-element.41), channel_id=1, source_target_pairs={{0,1},{1,2},{2,3},{3,4},{4,5},{5,6},{6,7},{7,0},{8,9},{9,10},{10,1... | collective-permute-start | bytes 368648 | tf_op jit(solution)/shard_map/ppermute | solution.py:284
  70.2 1.9 %collective-permute-start.12 = (f32[80,384]{1,0:T(8,128)S(1)}, f32[80,384]{1,0:T(8,128)S(1)}, u32[]{:S(2)}, u32[]{:S(2)}) collective-permute-start(f32[80,384]{1,0:T(8,128)S(1)} %get-tuple-element.36.refs_3_), channel_id=1, source_target_pairs={{0,7},{1,0},{2,1},{3,2},{4,3},{5,4},{6,5},{7,6},{8,15},{9,8},{10,9... | collective-permute-start | bytes 368648 | tf_op jit(solution)/shard_map/ppermute | solution.py:284
  72.1 0.8 nearer.1
  72.9 0.0 collective-permute-done.16
  72.9 5.3 %collective-permute-start.17 = (f32[160,384]{1,0:T(8,128)S(1)}, f32[160,384]{1,0:T(8,128)S(1)}, u32[]{:S(2)}, u32[]{:S(2)}) collective-permute-start(f32[160,384]{1,0:T(8,128)S(1)} %pad_add_fusion), channel_id=1, source_target_pairs={{0,1},{1,2},{2,3},{3,4},{4,5},{5,6},{6,7},{7,0},{8,9},{9,10},{10,1... | collective-permute-start | bytes 737288 | tf_op jit(solution)/shard_map/ppermute | solution.py:284
  78.2 0.0 collective-permute-done.12
  78.3 1.9 %collective-permute-start.13 = (f32[160,384]{1,0:T(8,128)S(1)}, f32[160,384]{1,0:T(8,128)S(1)}, u32[]{:S(2)}, u32[]{:S(2)}) collective-permute-start(f32[160,384]{1,0:T(8,128)S(1)} %pad_add_fusion.1), channel_id=1, source_target_pairs={{0,7},{1,0},{2,1},{3,2},{4,3},{5,4},{6,5},{7,6},{8,15},{9,8},{10,9... | collective-permute-start | bytes 737288 | tf_op jit(solution)/shard_map/ppermute | solution.py:284
  80.2 2.3 %collective-permute-done.17 = f32[160,384]{1,0:T(8,128)S(1)} collective-permute-done((f32[160,384]{1,0:T(8,128)S(1)}, f32[160,384]{1,0:T(8,128)S(1)}, u32[]{:S(2)}, u32[]{:S(2)}) %collective-permute-start.17) | collective-permute-done | bytes 245792 | tf_op jit(solution)/shard_map/ppermute | solution.py:284
  82.5 5.6 %collective-permute-start.18 = (f32[160,384]{1,0:T(8,128)S(1)}, f32[160,384]{1,0:T(8,128)S(1)}, u32[]{:S(2)}, u32[]{:S(2)}) collective-permute-start(f32[160,384]{1,0:T(8,128)S(1)} %add.32), channel_id=1, source_target_pairs={{0,1},{1,2},{2,3},{3,4},{4,5},{5,6},{6,7},{7,0},{8,9},{9,10},{10,1... | collective-permute-start | bytes 737288 | tf_op jit(solution)/shard_map/ppermute | solution.py:284
  88.2 0.0 collective-permute-done.13
  88.2 1.9 %collective-permute-start.14 = (f32[160,384]{1,0:T(8,128)S(1)}, f32[160,384]{1,0:T(8,128)S(1)}, u32[]{:S(2)}, u32[]{:S(2)}) collective-permute-start(f32[160,384]{1,0:T(8,128)S(1)} %add.29), channel_id=1, source_target_pairs={{0,7},{1,0},{2,1},{3,2},{4,3},{5,4},{6,5},{7,6},{8,15},{9,8},{10,9... | collective-permute-start | bytes 737288 | tf_op jit(solution)/shard_map/ppermute | solution.py:284
  90.1 1.7 %collective-permute-done.18 = f32[160,384]{1,0:T(8,128)S(1)} collective-permute-done((f32[160,384]{1,0:T(8,128)S(1)}, f32[160,384]{1,0:T(8,128)S(1)}, u32[]{:S(2)}, u32[]{:S(2)}) %collective-permute-start.18) | collective-permute-done | bytes 245792 | tf_op jit(solution)/shard_map/ppermute | solution.py:284
  91.9 5.6 %collective-permute-start.19 = (f32[160,384]{1,0:T(8,128)S(1)}, f32[160,384]{1,0:T(8,128)S(1)}, u32[]{:S(2)}, u32[]{:S(2)}) collective-permute-start(f32[160,384]{1,0:T(8,128)S(1)} %add.33), channel_id=1, source_target_pairs={{0,1},{1,2},{2,3},{3,4},{4,5},{5,6},{6,7},{7,0},{8,9},{9,10},{10,1... | collective-permute-start | bytes 737288 | tf_op jit(solution)/shard_map/ppermute | solution.py:284
  97.5 0.0 collective-permute-done.14
  97.5 1.9 %collective-permute-start.15 = (f32[160,384]{1,0:T(8,128)S(1)}, f32[160,384]{1,0:T(8,128)S(1)}, u32[]{:S(2)}, u32[]{:S(2)}) collective-permute-start(f32[160,384]{1,0:T(8,128)S(1)} %add.30), channel_id=1, source_target_pairs={{0,7},{1,0},{2,1},{3,2},{4,3},{5,4},{6,5},{7,6},{8,15},{9,8},{10,9... | collective-permute-start | bytes 737288 | tf_op jit(solution)/shard_map/ppermute | solution.py:284
  99.5 1.7 %collective-permute-done.19 = f32[160,384]{1,0:T(8,128)S(1)} collective-permute-done((f32[160,384]{1,0:T(8,128)S(1)}, f32[160,384]{1,0:T(8,128)S(1)}, u32[]{:S(2)}, u32[]{:S(2)}) %collective-permute-start.19) | collective-permute-done | bytes 245792 | tf_op jit(solution)/shard_map/ppermute | solution.py:284
  101.2 5.7 %collective-permute-done.15 = f32[160,384]{1,0:T(8,128)S(1)} collective-permute-done((f32[160,384]{1,0:T(8,128)S(1)}, f32[160,384]{1,0:T(8,128)S(1)}, u32[]{:S(2)}, u32[]{:S(2)}) %collective-permute-start.15) | collective-permute-done | bytes 245792 | tf_op jit(solution)/shard_map/ppermute | solution.py:284
  106.8 0.7 add_convert_fusion
  (16 shorter events, 0.2 us)
Async XLA Ops:
  0.0 5.1 %copy-start.5 = (bf16[160,256]{1,0:T(8,128)(2,1)S(1)}, bf16[160,256]{1,0:T(8,128)(2,1)}, u32[]{:S(2)}) copy-start(bf16[160,256]{1,0:T(8,128)(2,1)} %refs_1_.3) | copy-start | bytes 245764
  0.0 5.1 %copy-start.6 = (bf16[160,256]{1,0:T(8,128)(2,1)S(1)}, bf16[160,256]{1,0:T(8,128)(2,1)}, u32[]{:S(2)}) copy-start(bf16[160,256]{1,0:T(8,128)(2,1)} %refs_0_.2) | copy-start | bytes 245764
  0.0 5.1 %copy-start.7 = (f32[2,160]{1,0:T(2,128)S(1)}, f32[2,160]{1,0:T(2,128)}, u32[]{:S(2)}) copy-start(f32[2,160]{1,0:T(2,128)} %refs_2_.3) | copy-start | bytes 3844
  0.0 11.4 %copy-start = (bf16[256,6144]{1,0:T(8,128)(2,1)S(1)}, bf16[256,6144]{1,0:T(8,128)(2,1)}, u32[]{:S(2)}) copy-start(bf16[256,6144]{1,0:T(8,128)(2,1)} %w_hbm.1) | copy-start | bytes 9437188
  3.2 3.2 %collective-permute-start = (f32[128,256]{1,0:T(8,128)S(1)}, f32[128,256]{1,0:T(8,128)S(1)}, u32[]{:S(2)}, u32[]{:S(2)}) collective-permute-start(f32[128,256]{1,0:T(8,128)S(1)} %get-tuple-element.26), channel_id=1, source_target_pairs={{0,16},{16,0},{1,17},{17,1},{2,18},{18,2},{3,19},{19,3},{4,20},{20... | collective-permute-start | bytes 393224 | tf_op jit(solution)/shard_map/ppermute | solution.py:279
  5.5 0.7 copy-start.1
  7.1 13.1 %collective-permute-start.1 = (f32[128,256]{1,0:T(8,128)S(1)}, f32[128,256]{1,0:T(8,128)S(1)}, u32[]{:S(2)}, u32[]{:S(2)}) collective-permute-start(f32[128,256]{1,0:T(8,128)S(1)} %get-tuple-element.29.later_ref.refs_1_), channel_id=1, source_target_pairs={{0,32},{32,0},{64,96},{96,64},{128,160},{160,128},{192,224},{224,1... | collective-permute-start | bytes 393224 | tf_op jit(solution)/shard_map/ppermute | solution.py:305
  11.4 28.9 %copy-start.3 = (f32[2,128,128]{2,1,0:T(8,128)S(1)}, f32[2,128,128]{2,1,0:T(8,128)}, u32[]{:S(2)}) copy-start(f32[2,128,128]{2,1,0:T(8,128)} %refs_0_.3) | copy-start | bytes 393220
  12.7 39.3 %collective-permute-start.8 = (f32[64,3072]{1,0:T(8,128)}, f32[64,3072]{1,0:T(8,128)S(1)}, u32[]{:S(2)}, u32[]{:S(2)}) collective-permute-start(f32[64,3072]{1,0:T(8,128)} %get-tuple-element.30.refs_3_), channel_id=1, source_target_pairs={{0,8},{8,0},{1,9},{9,1},{2,10},{10,2},{3,11},{11,3},{4,12},{12,4},... | collective-permute-start | bytes 2359304 | tf_op jit(solution)/shard_map/ppermute | solution.py:279
  16.1 38.2 %collective-permute-start.10 = (f32[64,3072]{1,0:T(8,128)}, f32[64,3072]{1,0:T(8,128)S(1)}, u32[]{:S(2)}, u32[]{:S(2)}) collective-permute-start(f32[64,3072]{1,0:T(8,128)} %get-tuple-element.35), channel_id=1, source_target_pairs={{0,264},{8,256},{256,8},{264,0},{1,265},{9,257},{257,9},{265,1},{2... | collective-permute-start | bytes 2359304 | tf_op jit(solution)/shard_map/ppermute | solution.py:279
  20.4 11.9 %collective-permute-start.2 = (f32[128,256]{1,0:T(8,128)S(1)}, f32[128,256]{1,0:T(8,128)S(1)}, u32[]{:S(2)}, u32[]{:S(2)}) collective-permute-start(f32[128,256]{1,0:T(8,128)S(1)} %join_chips.1.refs_3_.refs_1_), channel_id=1, source_target_pairs={{0,64},{32,96},{64,0},{96,32},{128,192},{160,224},{192,128},{224,1... | collective-permute-start | bytes 393224 | tf_op jit(solution)/shard_map/ppermute | solution.py:305
  32.4 12.6 %collective-permute-start.3 = (f32[128,256]{1,0:T(8,128)S(1)}, f32[128,256]{1,0:T(8,128)S(1)}, u32[]{:S(2)}, u32[]{:S(2)}) collective-permute-start(f32[128,256]{1,0:T(8,128)S(1)} %join_pairs.1.refs_4_.refs_1_.refs_2_), channel_id=1, source_target_pairs={{0,224},{32,192},{64,160},{96,128},{128,96},{160,64},{192,32},{224... | collective-permute-start | bytes 393224 | tf_op jit(solution)/shard_map/ppermute | solution.py:305
  40.6 8.9 %copy-start.4 = (f32[128,256]{1,0:T(8,128)S(1)}, f32[128,256]{1,0:T(8,128)}, u32[]{:S(2)}) copy-start(f32[128,256]{1,0:T(8,128)} %get-tuple-element.31.refs_5_) | copy-start | bytes 393220
  40.6 11.4 %copy-start.2 = (f32[160,512]{1,0:T(8,128)S(1)}, f32[160,512]{1,0:T(8,128)}, u32[]{:S(2)}) copy-start(f32[160,512]{1,0:T(8,128)} %copy-done.1) | copy-start | bytes 983044
  45.4 11.0 %collective-permute-start.5 = (f32[128,128]{1,0:T(8,128)S(1)}, f32[128,128]{1,0:T(8,128)S(1)}, u32[]{:S(2)}, u32[]{:S(2)}) collective-permute-start(f32[128,128]{1,0:T(8,128)S(1)} %join_ring.1.refs_6_.refs_1_), channel_id=1, source_target_pairs={{0,256},{16,272},{1,257},{17,273},{2,258},{18,274},{3,259},{19,275... | collective-permute-start | bytes 196616 | tf_op jit(solution)/shard_map/ppermute | solution.py:331
  48.2 8.2 %collective-permute-start.6 = (f32[128,128]{1,0:T(8,128)S(1)}, f32[128,128]{1,0:T(8,128)S(1)}, u32[]{:S(2)}, u32[]{:S(2)}) collective-permute-start(f32[128,128]{1,0:T(8,128)S(1)} %join_ring.1.refs_6_.refs_1_), channel_id=1, source_target_pairs={{0,272},{16,256},{1,273},{17,257},{2,274},{18,258},{3,275},{19,259... | collective-permute-start | bytes 196616 | tf_op jit(solution)/shard_map/ppermute | solution.py:332
  49.9 6.5 %collective-permute-start.4 = (f32[128,256]{1,0:T(8,128)S(1)}, f32[128,256]{1,0:T(8,128)S(1)}, u32[]{:S(2)}, u32[]{:S(2)}) collective-permute-start(f32[128,256]{1,0:T(8,128)S(1)} %get-tuple-element.33), channel_id=1, source_target_pairs={{0,16},{16,0},{1,17},{17,1},{2,18},{18,2},{3,19},{19,3},{4,20},{20... | collective-permute-start | bytes 393224 | tf_op jit(solution)/shard_map/ppermute | solution.py:279
  52.0 7.8 %collective-permute-start.9 = (f32[64,3072]{1,0:T(8,128)S(1)}, f32[64,3072]{1,0:T(8,128)S(1)}, u32[]{:S(2)}, u32[]{:S(2)}) collective-permute-start(f32[64,3072]{1,0:T(8,128)S(1)} %collective-permute-done.8.n0), channel_id=1, source_target_pairs={{0,16},{16,0},{1,17},{17,1},{2,18},{18,2},{3,19},{19,3},{4,20},{20... | collective-permute-start | bytes 2359304 | tf_op jit(solution)/shard_map/ppermute | solution.py:279
  54.3 5.5 %collective-permute-start.11 = (f32[64,3072]{1,0:T(8,128)S(1)}, f32[64,3072]{1,0:T(8,128)S(1)}, u32[]{:S(2)}, u32[]{:S(2)}) collective-permute-start(f32[64,3072]{1,0:T(8,128)S(1)} %collective-permute-done.10.f0), channel_id=1, source_target_pairs={{0,16},{16,0},{1,17},{17,1},{2,18},{18,2},{3,19},{19,3},{4,20},{20... | collective-permute-start | bytes 2359304 | tf_op jit(solution)/shard_map/ppermute | solution.py:279
  56.8 8.4 %collective-permute-start.7 = (f32[160,256]{1,0:T(8,128)S(1)}, f32[160,256]{1,0:T(8,128)S(1)}, u32[]{:S(2)}, u32[]{:S(2)}) collective-permute-start(f32[160,256]{1,0:T(8,128)S(1)} %outputs.1.later_ref.refs_0_), channel_id=1, source_target_pairs={{0,8},{8,0},{1,9},{9,1},{2,10},{10,2},{3,11},{11,3},{4,12},{12,4},... | collective-permute-start | bytes 491528 | tf_op jit(solution)/shard_map/ppermute | solution.py:279
  65.5 7.4 %collective-permute-start.16 = (f32[80,384]{1,0:T(8,128)S(1)}, f32[80,384]{1,0:T(8,128)S(1)}, u32[]{:S(2)}, u32[]{:S(2)}) collective-permute-start(f32[80,384]{1,0:T(8,128)S(1)} %get-tuple-element.41), channel_id=1, source_target_pairs={{0,1},{1,2},{2,3},{3,4},{4,5},{5,6},{6,7},{7,0},{8,9},{9,10},{10,1... | collective-permute-start | bytes 368648 | tf_op jit(solution)/shard_map/ppermute | solution.py:284
  70.2 8.0 %collective-permute-start.12 = (f32[80,384]{1,0:T(8,128)S(1)}, f32[80,384]{1,0:T(8,128)S(1)}, u32[]{:S(2)}, u32[]{:S(2)}) collective-permute-start(f32[80,384]{1,0:T(8,128)S(1)} %get-tuple-element.36.refs_3_), channel_id=1, source_target_pairs={{0,7},{1,0},{2,1},{3,2},{4,3},{5,4},{6,5},{7,6},{8,15},{9,8},{10,9... | collective-permute-start | bytes 368648 | tf_op jit(solution)/shard_map/ppermute | solution.py:284
  72.9 9.6 %collective-permute-start.17 = (f32[160,384]{1,0:T(8,128)S(1)}, f32[160,384]{1,0:T(8,128)S(1)}, u32[]{:S(2)}, u32[]{:S(2)}) collective-permute-start(f32[160,384]{1,0:T(8,128)S(1)} %pad_add_fusion), channel_id=1, source_target_pairs={{0,1},{1,2},{2,3},{3,4},{4,5},{5,6},{6,7},{7,0},{8,9},{9,10},{10,1... | collective-permute-start | bytes 737288 | tf_op jit(solution)/shard_map/ppermute | solution.py:284
  78.3 9.9 %collective-permute-start.13 = (f32[160,384]{1,0:T(8,128)S(1)}, f32[160,384]{1,0:T(8,128)S(1)}, u32[]{:S(2)}, u32[]{:S(2)}) collective-permute-start(f32[160,384]{1,0:T(8,128)S(1)} %pad_add_fusion.1), channel_id=1, source_target_pairs={{0,7},{1,0},{2,1},{3,2},{4,3},{5,4},{6,5},{7,6},{8,15},{9,8},{10,9... | collective-permute-start | bytes 737288 | tf_op jit(solution)/shard_map/ppermute | solution.py:284
  82.5 9.3 %collective-permute-start.18 = (f32[160,384]{1,0:T(8,128)S(1)}, f32[160,384]{1,0:T(8,128)S(1)}, u32[]{:S(2)}, u32[]{:S(2)}) collective-permute-start(f32[160,384]{1,0:T(8,128)S(1)} %add.32), channel_id=1, source_target_pairs={{0,1},{1,2},{2,3},{3,4},{4,5},{5,6},{6,7},{7,0},{8,9},{9,10},{10,1... | collective-permute-start | bytes 737288 | tf_op jit(solution)/shard_map/ppermute | solution.py:284
  88.2 9.3 %collective-permute-start.14 = (f32[160,384]{1,0:T(8,128)S(1)}, f32[160,384]{1,0:T(8,128)S(1)}, u32[]{:S(2)}, u32[]{:S(2)}) collective-permute-start(f32[160,384]{1,0:T(8,128)S(1)} %add.29), channel_id=1, source_target_pairs={{0,7},{1,0},{2,1},{3,2},{4,3},{5,4},{6,5},{7,6},{8,15},{9,8},{10,9... | collective-permute-start | bytes 737288 | tf_op jit(solution)/shard_map/ppermute | solution.py:284
  91.9 9.3 %collective-permute-start.19 = (f32[160,384]{1,0:T(8,128)S(1)}, f32[160,384]{1,0:T(8,128)S(1)}, u32[]{:S(2)}, u32[]{:S(2)}) collective-permute-start(f32[160,384]{1,0:T(8,128)S(1)} %add.33), channel_id=1, source_target_pairs={{0,1},{1,2},{2,3},{3,4},{4,5},{5,6},{6,7},{7,0},{8,9},{9,10},{10,1... | collective-permute-start | bytes 737288 | tf_op jit(solution)/shard_map/ppermute | solution.py:284
  97.5 9.3 %collective-permute-start.15 = (f32[160,384]{1,0:T(8,128)S(1)}, f32[160,384]{1,0:T(8,128)S(1)}, u32[]{:S(2)}, u32[]{:S(2)}) collective-permute-start(f32[160,384]{1,0:T(8,128)S(1)} %add.30), channel_id=1, source_target_pairs={{0,7},{1,0},{2,1},{3,2},{4,3},{5,4},{6,5},{7,6},{8,15},{9,8},{10,9... | collective-permute-start | bytes 737288 | tf_op jit(solution)/shard_map/ppermute | solution.py:284

commit v9 on v7

--- a/solution.py
+++ b/solution.py
@@ -226,7 +226,7 @@
     )(column, row, weight, later)
 
 
-OFFSETS = (4, -3, 3, -2, 2, -1, 1, 0)
+OFFSETS = (4, -2, 2, -3, 3, -1, 1, 0)
 
 
 def piece_weights(x_lo_ref, y_ref, core_ref, w_hbm, n0, n1, f0, f1, later_ref, out_ref, own_ref, done):
@@ -259,16 +259,18 @@
     )
 
 
-def farthest(z_ref, zx_ref, w_ref, low_ref, high_ref):
-    half = low_ref.shape[0]
-    out = piece(z_ref, zx_ref, w_ref, 0)
-    low_ref[...] = out[:half]
-    high_ref[...] = out[half:]
-
-
-def nearer(z_ref, zx_ref, w_ref, *out_refs):
+def leaving(z_ref, zx_ref, w_ref, down_ref, up_ref):
+    half = z_ref.shape[0] // 2
+    far = piece(z_ref, zx_ref, w_ref, 0)
+    down_ref[:half, :] = far[:half]
+    up_ref[:half, :] = far[half:]
+    down_ref[half:, :] = piece(z_ref, zx_ref, w_ref, 1)
+    up_ref[half:, :] = piece(z_ref, zx_ref, w_ref, 2)
+
+
+def remaining(z_ref, zx_ref, w_ref, *out_refs):
     for i, out_ref in enumerate(out_refs):
-        out_ref[...] = piece(z_ref, zx_ref, w_ref, i + 1)
+        out_ref[...] = piece(z_ref, zx_ref, w_ref, i + 3)
 
 
 def swapped(x, axes):
@@ -343,15 +345,16 @@
     )
 
     factors = (z_rows, z_pair, weights)
-    low, high = call(farthest, [((rows // 2, chunk), f32)] * 2, [], *factors, limit=16)
-    down, up = passed(low, Y, -1), passed(high, Y, 1)
-    pieces = call(nearer, [out_piece] * (len(OFFSETS) - 1), [], *factors, later=[low], limit=16)
-    down = pieces[0] + jnp.concatenate([down, jnp.zeros_like(down)], axis=0)
-    up = pieces[1] + jnp.concatenate([jnp.zeros_like(up), up], axis=0)
-    for i in (2, 4):
-        down = passed(down, Y, -1) + pieces[i]
-        up = passed(up, Y, 1) + pieces[i + 1]
-    return (passed(down, Y, -1) + passed(up, Y, 1) + pieces[6]).astype(bf16)
+    half = rows // 2
+    down, up = call(leaving, [((half + rows, chunk), f32)] * 2, [], *factors, limit=16)
+    down1, up1 = passed(down, Y, -1), passed(up, Y, 1)
+    down3, up3, down0, up0, own = call(remaining, [out_piece] * 5, [], *factors, later=[down], limit=16)
+    none = jnp.zeros((half, chunk), f32)
+    down2 = passed(down3 + jnp.concatenate([down1[:half], none], axis=0), Y, -2)
+    up2 = passed(up3 + jnp.concatenate([none, up1[:half]], axis=0), Y, 2)
+    down = passed(down0 + down1[half:] + down2, Y, -1)
+    up = passed(up0 + up1[half:] + up2, Y, 1)
+    return (down + up + own).astype(bf16)
 
 
 def solution(mesh):

time: 106 us -> 108 us (1.019)
  the two profiles are of different devices: /device:TPU:24 before, /device:TPU:1 now
where the time goes in v9:
time: 108 us; the launch traced here: 107 us
  starting transfers between devices  57.3 us (53%)
  waiting for transfers between devices  35.3 us (33%)
  Pallas kernels  10.2 us (9%)
  local copies, waits for them, and re-layouts  3.01 us (3%)
    ppermute x7, starting transfers between devices, swapped(): return lax.ppermute(x, axes, [(i, n - 1 - i) for i in range(n)])  24 us
    ppermute x6, waiting for transfers between devices, passed(): return lax.ppermute(x, axis, [(i, (i + by) % n) for i in range(n)])  22.5 us
    ppermute x6, starting transfers between devices, passed(): return lax.ppermute(x, axis, [(i, (i + by) % n) for i in range(n)])  19 us
    ppermute x3, starting transfers between devices, across_z(): return lax.ppermute(x, Z, [(i, to(i)) for i in range(SIZES[1])])  9.11 us
    ppermute x3, waiting for transfers between devices, across_z(): return lax.ppermute(x, Z, [(i, to(i)) for i in range(SIZES[1])])  9.09 us
    pallas_call x16, Pallas kernels, call(): pl.pallas_call(body, name=kernel.__name__, out_shape=outs, in_specs=[SM]...  6.58 us
    ppermute x7, waiting for transfers between devices, swapped(): return lax.ppermute(x, axes, [(i, n - 1 - i) for i in range(n)])  3.68 us
    ppermute x1, starting transfers between devices, local(): here = lax.ppermute(end, (XH, CORE), [(0, 2), (1, 3)])  3.22 us
  transfers between devices with their start and end apart: 18, of which 9 were waited for; matrix products, arithmetic and copies ran while one was open for 0% of the time, Pallas kernels for 6%

profile of v9, /device:TPU:1, one launch (start us, length us, event | category | flops | bytes accessed | tf_op | source)
XLA Modules:
  0.0 107.2 jit_solution(3274830584476301524)
XLA Ops:
  0.0 3.0 %shard_maps.1 = (f32[128,256]{1,0:T(8,128)S(1)}, f32[128,256]{1,0:T(8,128)S(1)}, f32[2,160,256]{2,1,0:T(8,128)S(1)}) custom-call(s32[1]{0:T(128)} %bitcast.refs_0_.row_ref.refs_1_.core_ref, bf16[160,256]{1,0:T(8,128)(2,1)} %refs_1_.3, bf16[160,256]{1,0:T(8,128)(2,1)} %refs_2_.2, f32[2,160]{1,0:T(2,128)} %refs_2_.3), custom_call_target="tpu_custom_call" | custom-call | flops 3000000000 | bytes 131072 | tf_op jit(solution)/shard_map/shard_maps/pallas_call | solution.py:36
  3.0 0.0 copy-start.4
  3.0 0.0 copy-start
  3.1 9.0 %collective-permute-start = (f32[128,256]{1,0:T(8,128)S(1)}, f32[128,256]{1,0:T(8,128)S(1)}, u32[]{:S(2)}, u32[]{:S(2)}) collective-permute-start(f32[128,256]{1,0:T(8,128)S(1)} %get-tuple-element.20), channel_id=1, source_target_pairs={{0,16},{16,0},{1,17},{17,1},{2,18},{18,2},{3,19},{19,3},{4,20},{20... | collective-permute-start | bytes 393224 | tf_op jit(solution)/shard_map/ppermute | solution.py:278
  12.1 0.0 copy-done.8
  12.1 0.0 copy-done.9
  12.1 0.4 shard_rows.1
  12.6 0.7 copy-done.1
  13.3 0.0 collective-permute-done.refs_2_
  13.3 0.2 chip_map.1.refs_3_.refs_1_
  13.5 0.4 copy-done.6
  14.0 1.9 %collective-permute-start.1 = (f32[128,256]{1,0:T(8,128)S(1)}, f32[128,256]{1,0:T(8,128)S(1)}, u32[]{:S(2)}, u32[]{:S(2)}) collective-permute-start(f32[128,256]{1,0:T(8,128)S(1)} %chip_map.1.refs_3_.refs_1_), channel_id=1, source_target_pairs={{0,32},{32,0},{64,96},{96,64},{128,160},{160,128},{192,224},{224,1... | collective-permute-start | bytes 393224 | tf_op jit(solution)/shard_map/ppermute | solution.py:304
  15.9 0.9 copy-done.5
  16.8 0.9 copy-done.7
  17.7 1.0 near.1.refs_3_
  18.7 1.0 far.1.refs_4_
  19.7 1.1 collective-permute-done.1.refs_2_
  20.8 0.2 join_chips.1.refs_3_.refs_1_
  21.0 1.9 %collective-permute-start.2 = (f32[128,256]{1,0:T(8,128)S(1)}, f32[128,256]{1,0:T(8,128)S(1)}, u32[]{:S(2)}, u32[]{:S(2)}) collective-permute-start(f32[128,256]{1,0:T(8,128)S(1)} %join_chips.1.refs_3_.refs_1_), channel_id=1, source_target_pairs={{0,64},{32,96},{64,0},{96,32},{128,192},{160,224},{192,128},{224,1... | collective-permute-start | bytes 393224 | tf_op jit(solution)/shard_map/ppermute | solution.py:304
  22.9 4.0 %collective-permute-start.10 = (f32[64,3072]{1,0:T(8,128)}, f32[64,3072]{1,0:T(8,128)S(1)}, u32[]{:S(2)}, u32[]{:S(2)}) collective-permute-start(f32[64,3072]{1,0:T(8,128)} %far.1.refs_4_), channel_id=1, source_target_pairs={{0,264},{8,256},{256,8},{264,0},{1,265},{9,257},{257,9},{265,1},{2... | collective-permute-start | bytes 2359304 | tf_op jit(solution)/shard_map/ppermute | solution.py:278
  26.9 1.9 %collective-permute-start.8 = (f32[64,3072]{1,0:T(8,128)}, f32[64,3072]{1,0:T(8,128)S(1)}, u32[]{:S(2)}, u32[]{:S(2)}) collective-permute-start(f32[64,3072]{1,0:T(8,128)} %near.1.refs_3_), channel_id=1, source_target_pairs={{0,8},{8,0},{1,9},{9,1},{2,10},{10,2},{3,11},{11,3},{4,12},{12,4},... | collective-permute-start | bytes 2359304 | tf_op jit(solution)/shard_map/ppermute | solution.py:278
  28.9 0.0 copy-start.3
  28.9 3.0 %collective-permute-done.2.refs_2_ = f32[128,256]{1,0:T(8,128)S(1)} collective-permute-done((f32[128,256]{1,0:T(8,128)S(1)}, f32[128,256]{1,0:T(8,128)S(1)}, u32[]{:S(2)}, u32[]{:S(2)}) %collective-permute-start.2) | collective-permute-done | bytes 131104 | tf_op jit(solution)/shard_map/ppermute | solution.py:304
  31.9 0.2 join_pairs.1.refs_4_.refs_1_.refs_2_
  32.1 5.3 %collective-permute-start.3 = (f32[128,256]{1,0:T(8,128)S(1)}, f32[128,256]{1,0:T(8,128)S(1)}, u32[]{:S(2)}, u32[]{:S(2)}) collective-permute-start(f32[128,256]{1,0:T(8,128)S(1)} %join_pairs.1.refs_4_.refs_1_.refs_2_), channel_id=1, source_target_pairs={{0,224},{32,192},{64,160},{96,128},{128,96},{160,64},{192,32},{224... | collective-permute-start | bytes 393224 | tf_op jit(solution)/shard_map/ppermute | solution.py:304
  37.5 0.2 before_pairs.1.refs_5_.refs_4_
  37.7 0.0 copy-start.2
  37.7 5.0 %collective-permute-done.3.refs_3_ = f32[128,256]{1,0:T(8,128)S(1)} collective-permute-done((f32[128,256]{1,0:T(8,128)S(1)}, f32[128,256]{1,0:T(8,128)S(1)}, u32[]{:S(2)}, u32[]{:S(2)}) %collective-permute-start.3) | collective-permute-done | bytes 131104 | tf_op jit(solution)/shard_map/ppermute | solution.py:304
  42.7 0.3 join_ring.1.refs_6_.refs_1_
  43.0 3.2 %collective-permute-start.5 = (f32[128,128]{1,0:T(8,128)S(1)}, f32[128,128]{1,0:T(8,128)S(1)}, u32[]{:S(2)}, u32[]{:S(2)}) collective-permute-start(f32[128,128]{1,0:T(8,128)S(1)} %join_ring.1.refs_6_.refs_1_), channel_id=1, source_target_pairs={{0,256},{16,272},{1,257},{17,273},{2,258},{18,274},{3,259},{19,275... | collective-permute-start | bytes 196616 | tf_op jit(solution)/shard_map/ppermute | solution.py:324
  46.3 2.0 %collective-permute-start.6 = (f32[128,128]{1,0:T(8,128)S(1)}, f32[128,128]{1,0:T(8,128)S(1)}, u32[]{:S(2)}, u32[]{:S(2)}) collective-permute-start(f32[128,128]{1,0:T(8,128)S(1)} %join_ring.1.refs_6_.refs_1_), channel_id=1, source_target_pairs={{0,272},{16,256},{1,273},{17,257},{2,274},{18,258},{3,275},{19,259... | collective-permute-start | bytes 196616 | tf_op jit(solution)/shard_map/ppermute | solution.py:325
  48.3 0.4 shard_prefixes.1
  48.7 2.3 %collective-permute-start.4 = (f32[128,256]{1,0:T(8,128)S(1)}, f32[128,256]{1,0:T(8,128)S(1)}, u32[]{:S(2)}, u32[]{:S(2)}) collective-permute-start(f32[128,256]{1,0:T(8,128)S(1)} %get-tuple-element.24), channel_id=1, source_target_pairs={{0,16},{16,0},{1,17},{17,1},{2,18},{18,2},{3,19},{19,3},{4,20},{20... | collective-permute-start | bytes 393224 | tf_op jit(solution)/shard_map/ppermute | solution.py:278
  51.1 0.0 collective-permute-done.10.f0
  51.1 2.0 %collective-permute-start.11 = (f32[64,3072]{1,0:T(8,128)S(1)}, f32[64,3072]{1,0:T(8,128)S(1)}, u32[]{:S(2)}, u32[]{:S(2)}) collective-permute-start(f32[64,3072]{1,0:T(8,128)S(1)} %collective-permute-done.10.f0), channel_id=1, source_target_pairs={{0,16},{16,0},{1,17},{17,1},{2,18},{18,2},{3,19},{19,3},{4,20},{20... | collective-permute-start | bytes 2359304 | tf_op jit(solution)/shard_map/ppermute | solution.py:278
  53.1 0.0 collective-permute-done.8.n0
  53.2 2.3 %collective-permute-start.9 = (f32[64,3072]{1,0:T(8,128)S(1)}, f32[64,3072]{1,0:T(8,128)S(1)}, u32[]{:S(2)}, u32[]{:S(2)}) collective-permute-start(f32[64,3072]{1,0:T(8,128)S(1)} %collective-permute-done.8.n0), channel_id=1, source_target_pairs={{0,16},{16,0},{1,17},{17,1},{2,18},{18,2},{3,19},{19,3},{4,20},{20... | collective-permute-start | bytes 2359304 | tf_op jit(solution)/shard_map/ppermute | solution.py:278
  55.5 0.0 collective-permute-done.5.refs_2_
  55.5 0.0 collective-permute-done.6.refs_3_
  55.5 0.0 collective-permute-done.4.refs_2_
  55.5 0.4 outputs.1.later_ref.refs_0_
  55.9 2.4 %collective-permute-start.7 = (f32[160,256]{1,0:T(8,128)S(1)}, f32[160,256]{1,0:T(8,128)S(1)}, u32[]{:S(2)}, u32[]{:S(2)}) collective-permute-start(f32[160,256]{1,0:T(8,128)S(1)} %outputs.1.later_ref.refs_0_), channel_id=1, source_target_pairs={{0,8},{8,0},{1,9},{9,1},{2,10},{10,2},{3,11},{11,3},{4,12},{12,4},... | collective-permute-start | bytes 491528 | tf_op jit(solution)/shard_map/ppermute | solution.py:278
  58.4 0.0 collective-permute-done.11.f1
  58.4 0.0 collective-permute-done.9.n1
  58.4 1.6 %piece_weights.1.refs_2_ = bf16[8,512,384]{2,1,0:T(8,128)(2,1)S(1)} custom-call(s32[1]{0:T(128)} %bitcast.2.x_lo_ref, s32[1]{0:T(128)} %bitcast.4.y_ref, s32[1]{0:T(128)} %bitcast.refs_0_.row_ref.refs_1_.core_ref, bf16[256,6144]{1,0:T(8,128)(2,1)} %w_hbm.1, f32[64,3072]{1,0:T(8,128)S(1)} %collective-permute-done.8.n0, ...), custom_call_target="tpu_custom_call" | custom-call | flops 3000000000 | bytes 131072 | tf_op jit(solution)/shard_map/piece_weights/pallas_call | solution.py:333
  59.9 3.7 %collective-permute-done.7.refs_1_ = f32[160,256]{1,0:T(8,128)S(1)} collective-permute-done((f32[160,256]{1,0:T(8,128)S(1)}, f32[160,256]{1,0:T(8,128)S(1)}, u32[]{:S(2)}, u32[]{:S(2)}) %collective-permute-start.7) | collective-permute-done | bytes 163872 | tf_op jit(solution)/shard_map/ppermute | solution.py:278
  63.6 0.4 leaving.1
  64.0 0.0 copy-start.11
  64.0 3.2 %collective-permute-start.15 = (f32[240,384]{1,0:T(8,128)S(1)}, f32[240,384]{1,0:T(8,128)S(1)}, u32[]{:S(2)}, u32[]{:S(2)}) collective-permute-start(f32[240,384]{1,0:T(8,128)S(1)} %get-tuple-element.30), channel_id=1, source_target_pairs={{0,1},{1,2},{2,3},{3,4},{4,5},{5,6},{6,7},{7,0},{8,9},{9,10},{10,1... | collective-permute-start | bytes 1105928 | tf_op jit(solution)/shard_map/ppermute | solution.py:283
  67.3 4.0 %collective-permute-start.12 = (f32[240,384]{1,0:T(8,128)S(1)}, f32[240,384]{1,0:T(8,128)S(1)}, u32[]{:S(2)}, u32[]{:S(2)}) collective-permute-start(f32[240,384]{1,0:T(8,128)S(1)} %get-tuple-element.26.refs_3_), channel_id=1, source_target_pairs={{0,7},{1,0},{2,1},{3,2},{4,3},{5,4},{6,5},{7,6},{8,15},{9,8},{10,9... | collective-permute-start | bytes 1105928 | tf_op jit(solution)/shard_map/ppermute | solution.py:283
  71.3 0.6 remaining.1
  71.9 5.5 %collective-permute-done.15 = f32[240,384]{1,0:T(8,128)S(1)} collective-permute-done((f32[240,384]{1,0:T(8,128)S(1)}, f32[240,384]{1,0:T(8,128)S(1)}, u32[]{:S(2)}, u32[]{:S(2)}) %collective-permute-start.15) | collective-permute-done | bytes 368672 | tf_op jit(solution)/shard_map/ppermute | solution.py:283
  77.5 2.2 %collective-permute-start.16 = (f32[160,384]{1,0:T(8,128)S(1)}, f32[160,384]{1,0:T(8,128)S(1)}, u32[]{:S(2)}, u32[]{:S(2)}) collective-permute-start(f32[160,384]{1,0:T(8,128)S(1)} %pad_add_fusion), channel_id=1, source_target_pairs={{0,2},{1,3},{2,4},{3,5},{4,6},{5,7},{6,0},{7,1},{8,10},{9,11},{10,... | collective-permute-start | bytes 737288 | tf_op jit(solution)/shard_map/ppermute | solution.py:283
  79.6 0.0 collective-permute-done.12
  79.7 0.1 fusion.1
  79.8 5.2 %collective-permute-start.13 = (f32[160,384]{1,0:T(8,128)S(1)}, f32[160,384]{1,0:T(8,128)S(1)}, u32[]{:S(2)}, u32[]{:S(2)}) collective-permute-start(f32[160,384]{1,0:T(8,128)S(1)} %fusion.1), channel_id=1, source_target_pairs={{0,6},{1,7},{2,0},{3,1},{4,2},{5,3},{6,4},{7,5},{8,14},{9,15},{10,... | collective-permute-start | bytes 737288 | tf_op jit(solution)/shard_map/ppermute | solution.py:283
  85.0 8.4 %collective-permute-done.16 = f32[160,384]{1,0:T(8,128)S(1)} collective-permute-done((f32[160,384]{1,0:T(8,128)S(1)}, f32[160,384]{1,0:T(8,128)S(1)}, u32[]{:S(2)}, u32[]{:S(2)}) %collective-permute-start.16) | collective-permute-done | bytes 245792 | tf_op jit(solution)/shard_map/ppermute | solution.py:283
  93.4 0.1 fusion
  93.5 1.9 %collective-permute-start.17 = (f32[160,384]{1,0:T(8,128)S(1)}, f32[160,384]{1,0:T(8,128)S(1)}, u32[]{:S(2)}, u32[]{:S(2)}) collective-permute-start(f32[160,384]{1,0:T(8,128)S(1)} %fusion), channel_id=1, source_target_pairs={{0,1},{1,2},{2,3},{3,4},{4,5},{5,6},{6,7},{7,0},{8,9},{9,10},{10,1... | collective-permute-start | bytes 737288 | tf_op jit(solution)/shard_map/ppermute | solution.py:283
  95.4 2.1 %collective-permute-done.13 = f32[160,384]{1,0:T(8,128)S(1)} collective-permute-done((f32[160,384]{1,0:T(8,128)S(1)}, f32[160,384]{1,0:T(8,128)S(1)}, u32[]{:S(2)}, u32[]{:S(2)}) %collective-permute-start.13) | collective-permute-done | bytes 245792 | tf_op jit(solution)/shard_map/ppermute | solution.py:283
  97.6 2.5 %collective-permute-start.14 = (f32[160,384]{1,0:T(8,128)S(1)}, f32[160,384]{1,0:T(8,128)S(1)}, u32[]{:S(2)}, u32[]{:S(2)}) collective-permute-start(f32[160,384]{1,0:T(8,128)S(1)} %fusion.2), channel_id=1, source_target_pairs={{0,7},{1,0},{2,1},{3,2},{4,3},{5,4},{6,5},{7,6},{8,15},{9,8},{10,9... | collective-permute-start | bytes 737288 | tf_op jit(solution)/shard_map/ppermute | solution.py:283
  100.1 2.7 %collective-permute-done.17 = f32[160,384]{1,0:T(8,128)S(1)} collective-permute-done((f32[160,384]{1,0:T(8,128)S(1)}, f32[160,384]{1,0:T(8,128)S(1)}, u32[]{:S(2)}, u32[]{:S(2)}) %collective-permute-start.17) | collective-permute-done | bytes 245792 | tf_op jit(solution)/shard_map/ppermute | solution.py:283
  102.7 3.8 %collective-permute-done.14 = f32[160,384]{1,0:T(8,128)S(1)} collective-permute-done((f32[160,384]{1,0:T(8,128)S(1)}, f32[160,384]{1,0:T(8,128)S(1)}, u32[]{:S(2)}, u32[]{:S(2)}) %collective-permute-start.14) | collective-permute-done | bytes 245792 | tf_op jit(solution)/shard_map/ppermute | solution.py:283
  106.5 0.7 add_convert_fusion
  (21 shorter events, 0.2 us)
Async XLA Ops:
  0.0 12.1 %copy-start.8 = (bf16[160,256]{1,0:T(8,128)(2,1)S(1)}, bf16[160,256]{1,0:T(8,128)(2,1)}, u32[]{:S(2)}) copy-start(bf16[160,256]{1,0:T(8,128)(2,1)} %refs_1_.3) | copy-start | bytes 245764
  0.0 12.1 %copy-start.9 = (bf16[160,256]{1,0:T(8,128)(2,1)S(1)}, bf16[160,256]{1,0:T(8,128)(2,1)}, u32[]{:S(2)}) copy-start(bf16[160,256]{1,0:T(8,128)(2,1)} %refs_0_.2) | copy-start | bytes 245764
  0.0 12.1 %copy-start.10 = (f32[2,160]{1,0:T(2,128)S(1)}, f32[2,160]{1,0:T(2,128)}, u32[]{:S(2)}) copy-start(f32[2,160]{1,0:T(2,128)} %refs_2_.3) | copy-start | bytes 3844
  3.0 10.3 %copy-start.4 = (f32[128,256]{1,0:T(8,128)}, f32[128,256]{1,0:T(8,128)S(1)}, u32[]{:S(2)}) copy-start(f32[128,256]{1,0:T(8,128)S(1)} %get-tuple-element.19.refs_1_) | copy-start | bytes 393220
  3.0 14.7 %copy-start = (bf16[256,6144]{1,0:T(8,128)(2,1)S(1)}, bf16[256,6144]{1,0:T(8,128)(2,1)}, u32[]{:S(2)}) copy-start(bf16[256,6144]{1,0:T(8,128)(2,1)} %w_hbm.1) | copy-start | bytes 9437188
  3.1 10.3 %collective-permute-start = (f32[128,256]{1,0:T(8,128)S(1)}, f32[128,256]{1,0:T(8,128)S(1)}, u32[]{:S(2)}, u32[]{:S(2)}) collective-permute-start(f32[128,256]{1,0:T(8,128)S(1)} %get-tuple-element.20), channel_id=1, source_target_pairs={{0,16},{16,0},{1,17},{17,1},{2,18},{18,2},{3,19},{19,3},{4,20},{20... | collective-permute-start | bytes 393224 | tf_op jit(solution)/shard_map/ppermute | solution.py:278
  12.6 0.7 copy-start.1
  13.3 0.6 copy-start.6
  14.0 6.8 %collective-permute-start.1 = (f32[128,256]{1,0:T(8,128)S(1)}, f32[128,256]{1,0:T(8,128)S(1)}, u32[]{:S(2)}, u32[]{:S(2)}) collective-permute-start(f32[128,256]{1,0:T(8,128)S(1)} %chip_map.1.refs_3_.refs_1_), channel_id=1, source_target_pairs={{0,32},{32,0},{64,96},{96,64},{128,160},{160,128},{192,224},{224,1... | collective-permute-start | bytes 393224 | tf_op jit(solution)/shard_map/ppermute | solution.py:304
  15.9 0.9 copy-start.5
  16.8 0.9 copy-start.7
  21.0 10.9 %collective-permute-start.2 = (f32[128,256]{1,0:T(8,128)S(1)}, f32[128,256]{1,0:T(8,128)S(1)}, u32[]{:S(2)}, u32[]{:S(2)}) collective-permute-start(f32[128,256]{1,0:T(8,128)S(1)} %join_chips.1.refs_3_.refs_1_), channel_id=1, source_target_pairs={{0,64},{32,96},{64,0},{96,32},{128,192},{160,224},{192,128},{224,1... | collective-permute-start | bytes 393224 | tf_op jit(solution)/shard_map/ppermute | solution.py:304
  22.9 28.2 %collective-permute-start.10 = (f32[64,3072]{1,0:T(8,128)}, f32[64,3072]{1,0:T(8,128)S(1)}, u32[]{:S(2)}, u32[]{:S(2)}) collective-permute-start(f32[64,3072]{1,0:T(8,128)} %far.1.refs_4_), channel_id=1, source_target_pairs={{0,264},{8,256},{256,8},{264,0},{1,265},{9,257},{257,9},{265,1},{2... | collective-permute-start | bytes 2359304 | tf_op jit(solution)/shard_map/ppermute | solution.py:278
  26.9 26.2 %collective-permute-start.8 = (f32[64,3072]{1,0:T(8,128)}, f32[64,3072]{1,0:T(8,128)S(1)}, u32[]{:S(2)}, u32[]{:S(2)}) collective-permute-start(f32[64,3072]{1,0:T(8,128)} %near.1.refs_3_), channel_id=1, source_target_pairs={{0,8},{8,0},{1,9},{9,1},{2,10},{10,2},{3,11},{11,3},{4,12},{12,4},... | collective-permute-start | bytes 2359304 | tf_op jit(solution)/shard_map/ppermute | solution.py:278
  28.9 8.6 %copy-start.3 = (f32[2,128,128]{2,1,0:T(8,128)S(1)}, f32[2,128,128]{2,1,0:T(8,128)}, u32[]{:S(2)}) copy-start(f32[2,128,128]{2,1,0:T(8,128)} %refs_0_.3) | copy-start | bytes 393220
  32.1 10.5 %collective-permute-start.3 = (f32[128,256]{1,0:T(8,128)S(1)}, f32[128,256]{1,0:T(8,128)S(1)}, u32[]{:S(2)}, u32[]{:S(2)}) collective-permute-start(f32[128,256]{1,0:T(8,128)S(1)} %join_pairs.1.refs_4_.refs_1_.refs_2_), channel_id=1, source_target_pairs={{0,224},{32,192},{64,160},{96,128},{128,96},{160,64},{192,32},{224... | collective-permute-start | bytes 393224 | tf_op jit(solution)/shard_map/ppermute | solution.py:304
  37.7 13.4 %copy-start.2 = (f32[160,512]{1,0:T(8,128)S(1)}, f32[160,512]{1,0:T(8,128)}, u32[]{:S(2)}) copy-start(f32[160,512]{1,0:T(8,128)} %copy-done.1) | copy-start | bytes 983044
  43.0 12.4 %collective-permute-start.5 = (f32[128,128]{1,0:T(8,128)S(1)}, f32[128,128]{1,0:T(8,128)S(1)}, u32[]{:S(2)}, u32[]{:S(2)}) collective-permute-start(f32[128,128]{1,0:T(8,128)S(1)} %join_ring.1.refs_6_.refs_1_), channel_id=1, source_target_pairs={{0,256},{16,272},{1,257},{17,273},{2,258},{18,274},{3,259},{19,275... | collective-permute-start | bytes 196616 | tf_op jit(solution)/shard_map/ppermute | solution.py:324
  46.3 9.2 %collective-permute-start.6 = (f32[128,128]{1,0:T(8,128)S(1)}, f32[128,128]{1,0:T(8,128)S(1)}, u32[]{:S(2)}, u32[]{:S(2)}) collective-permute-start(f32[128,128]{1,0:T(8,128)S(1)} %join_ring.1.refs_6_.refs_1_), channel_id=1, source_target_pairs={{0,272},{16,256},{1,273},{17,257},{2,274},{18,258},{3,275},{19,259... | collective-permute-start | bytes 196616 | tf_op jit(solution)/shard_map/ppermute | solution.py:325
  48.7 6.8 %collective-permute-start.4 = (f32[128,256]{1,0:T(8,128)S(1)}, f32[128,256]{1,0:T(8,128)S(1)}, u32[]{:S(2)}, u32[]{:S(2)}) collective-permute-start(f32[128,256]{1,0:T(8,128)S(1)} %get-tuple-element.24), channel_id=1, source_target_pairs={{0,16},{16,0},{1,17},{17,1},{2,18},{18,2},{3,19},{19,3},{4,20},{20... | collective-permute-start | bytes 393224 | tf_op jit(solution)/shard_map/ppermute | solution.py:278
  51.1 7.2 %collective-permute-start.11 = (f32[64,3072]{1,0:T(8,128)S(1)}, f32[64,3072]{1,0:T(8,128)S(1)}, u32[]{:S(2)}, u32[]{:S(2)}) collective-permute-start(f32[64,3072]{1,0:T(8,128)S(1)} %collective-permute-done.10.f0), channel_id=1, source_target_pairs={{0,16},{16,0},{1,17},{17,1},{2,18},{18,2},{3,19},{19,3},{4,20},{20... | collective-permute-start | bytes 2359304 | tf_op jit(solution)/shard_map/ppermute | solution.py:278
  53.2 5.2 %collective-permute-start.9 = (f32[64,3072]{1,0:T(8,128)S(1)}, f32[64,3072]{1,0:T(8,128)S(1)}, u32[]{:S(2)}, u32[]{:S(2)}) collective-permute-start(f32[64,3072]{1,0:T(8,128)S(1)} %collective-permute-done.8.n0), channel_id=1, source_target_pairs={{0,16},{16,0},{1,17},{17,1},{2,18},{18,2},{3,19},{19,3},{4,20},{20... | collective-permute-start | bytes 2359304 | tf_op jit(solution)/shard_map/ppermute | solution.py:278
  55.9 7.7 %collective-permute-start.7 = (f32[160,256]{1,0:T(8,128)S(1)}, f32[160,256]{1,0:T(8,128)S(1)}, u32[]{:S(2)}, u32[]{:S(2)}) collective-permute-start(f32[160,256]{1,0:T(8,128)S(1)} %outputs.1.later_ref.refs_0_), channel_id=1, source_target_pairs={{0,8},{8,0},{1,9},{9,1},{2,10},{10,2},{3,11},{11,3},{4,12},{12,4},... | collective-permute-start | bytes 491528 | tf_op jit(solution)/shard_map/ppermute | solution.py:278
  64.0 15.6 %copy-start.11 = (pred[160]{0:T(512)(128)(4,1)S(1)}, pred[160]{0:T(512)(128)(4,1)}, u32[]{:S(2)}) copy-start(pred[160]{0:T(512)(128)(4,1)} %constant.27.clone.1) | copy-start | bytes 484
  64.0 13.4 %collective-permute-start.15 = (f32[240,384]{1,0:T(8,128)S(1)}, f32[240,384]{1,0:T(8,128)S(1)}, u32[]{:S(2)}, u32[]{:S(2)}) collective-permute-start(f32[240,384]{1,0:T(8,128)S(1)} %get-tuple-element.30), channel_id=1, source_target_pairs={{0,1},{1,2},{2,3},{3,4},{4,5},{5,6},{6,7},{7,0},{8,9},{9,10},{10,1... | collective-permute-start | bytes 1105928 | tf_op jit(solution)/shard_map/ppermute | solution.py:283
  67.3 12.4 %collective-permute-start.12 = (f32[240,384]{1,0:T(8,128)S(1)}, f32[240,384]{1,0:T(8,128)S(1)}, u32[]{:S(2)}, u32[]{:S(2)}) collective-permute-start(f32[240,384]{1,0:T(8,128)S(1)} %get-tuple-element.26.refs_3_), channel_id=1, source_target_pairs={{0,7},{1,0},{2,1},{3,2},{4,3},{5,4},{6,5},{7,6},{8,15},{9,8},{10,9... | collective-permute-start | bytes 1105928 | tf_op jit(solution)/shard_map/ppermute | solution.py:283
  77.5 16.0 %collective-permute-start.16 = (f32[160,384]{1,0:T(8,128)S(1)}, f32[160,384]{1,0:T(8,128)S(1)}, u32[]{:S(2)}, u32[]{:S(2)}) collective-permute-start(f32[160,384]{1,0:T(8,128)S(1)} %pad_add_fusion), channel_id=1, source_target_pairs={{0,2},{1,3},{2,4},{3,5},{4,6},{5,7},{6,0},{7,1},{8,10},{9,11},{10,... | collective-permute-start | bytes 737288 | tf_op jit(solution)/shard_map/ppermute | solution.py:283
  79.8 17.8 %collective-permute-start.13 = (f32[160,384]{1,0:T(8,128)S(1)}, f32[160,384]{1,0:T(8,128)S(1)}, u32[]{:S(2)}, u32[]{:S(2)}) collective-permute-start(f32[160,384]{1,0:T(8,128)S(1)} %fusion.1), channel_id=1, source_target_pairs={{0,6},{1,7},{2,0},{3,1},{4,2},{5,3},{6,4},{7,5},{8,14},{9,15},{10,... | collective-permute-start | bytes 737288 | tf_op jit(solution)/shard_map/ppermute | solution.py:283
  93.5 9.2 %collective-permute-start.17 = (f32[160,384]{1,0:T(8,128)S(1)}, f32[160,384]{1,0:T(8,128)S(1)}, u32[]{:S(2)}, u32[]{:S(2)}) collective-permute-start(f32[160,384]{1,0:T(8,128)S(1)} %fusion), channel_id=1, source_target_pairs={{0,1},{1,2},{2,3},{3,4},{4,5},{5,6},{6,7},{7,0},{8,9},{9,10},{10,1... | collective-permute-start | bytes 737288 | tf_op jit(solution)/shard_map/ppermute | solution.py:283
  97.6 8.9 %collective-permute-start.14 = (f32[160,384]{1,0:T(8,128)S(1)}, f32[160,384]{1,0:T(8,128)S(1)}, u32[]{:S(2)}, u32[]{:S(2)}) collective-permute-start(f32[160,384]{1,0:T(8,128)S(1)} %fusion.2), channel_id=1, source_target_pairs={{0,7},{1,0},{2,1},{3,2},{4,3},{5,4},{6,5},{7,6},{8,15},{9,8},{10,9... | collective-permute-start | bytes 737288 | tf_op jit(solution)/shard_map/ppermute | solution.py:283

commit v10 on v8

--- a/solution.py
+++ b/solution.py
@@ -317,24 +317,24 @@
     near_out, far_out = weight_shares(out_weight, 1 - x_lo, core, share, chip)
     near = swapped(near_out, (XL,))
     got_chip = across_z(chip, lambda i: i ^ 1)
-    (both,) = call(join_chips, [wide], [z], chip, got_chip, later=[near_out], us=0.3)
+    (both,) = call(join_chips, [wide], [z], chip, got_chip, later=[near_out], us=2)
     (pre,) = call(before_chips, [wide], [z], chip, got_chip, later=[both], us=0.1)
     far = swapped(far_out, (XH, XL))
     got_both = across_z(both, lambda i: i ^ 2)
-    (four,) = call(join_pairs, [wide], [z], both, got_both, later=[pre], us=0.3)
+    (four,) = call(join_pairs, [wide], [z], both, got_both, later=[pre], us=3)
     (pre,) = call(before_pairs, [wide], [z], both, got_both, pre, later=[four], us=0.1)
     near_other = swapped(near, (CORE,))
     (first,) = call(fetched, [((2, HW, HW), f32)], [], init_weight, later=[four], us=0.1)
     got_four = across_z(four, lambda i: 7 - i)
-    (end,) = call(join_ring, [square], [z, core], four, got_four, first, later=[pre], us=3)
+    (end,) = call(join_ring, [square], [z, core], four, got_four, first, later=[pre], us=2)
     far_other = swapped(far, (CORE,))
     here = lax.ppermute(end, (XH, CORE), [(0, 2), (1, 3)])
     there = lax.ppermute(end, (XH, CORE), [(0, 3), (1, 2)])
     mine, other = call(shard_prefixes, [wide, wide], [z, core], four, got_four, pre, early, later=[end], us=0.1)
-    (begin,) = call(ring_states, [((2, HW, HW), f32)], [x_hi, core], here, there, first, us=12)
+    (begin,) = call(ring_states, [((2, HW, HW), f32)], [x_hi, core], here, there, first, us=6)
     (late_rows,) = call(fetched, [((rows, 4 * HW), f32)], [], own_rows, later=[end], us=0.1)
     (z_rows,) = call(
-        outputs, [((rows, 2 * HW), f32)], [core], mine, swapped(other, (CORE,)), begin, late_rows, us=4
+        outputs, [((rows, 2 * HW), f32)], [core], mine, swapped(other, (CORE,)), begin, late_rows, later=[near_other], us=4
     )
     z_pair = swapped(z_rows, (XL,))
     weights = pl.pallas_call(

time: 108 us -> 105 us (0.972)
  the two profiles are of different devices: /device:TPU:24 before, /device:TPU:2 now
where the time goes in v10:
time: 105 us; the launch traced here: 104 us
  starting transfers between devices  71 us (68%)
  waiting for transfers between devices  19.9 us (19%)
  Pallas kernels  10.8 us (10%)
    ppermute x8, starting transfers between devices, passed(): return lax.ppermute(x, axis, [(i, (i + by) % n) for i in range(n)])  29.5 us
    ppermute x7, starting transfers between devices, swapped(): return lax.ppermute(x, axes, [(i, n - 1 - i) for i in range(n)])  20.8 us
    ppermute x3, starting transfers between devices, across_z(): return lax.ppermute(x, Z, [(i, to(i)) for i in range(SIZES[1])])  14.7 us
    ppermute x8, waiting for transfers between devices, passed(): return lax.ppermute(x, axis, [(i, (i + by) % n) for i in range(n)])  11.1 us
    pallas_call x14, Pallas kernels, call(): pl.pallas_call(body, name=kernel.__name__, out_shape=outs, in_specs=[SM]...  7.27 us
    ppermute x3, waiting for transfers between devices, across_z(): return lax.ppermute(x, Z, [(i, to(i)) for i in range(SIZES[1])])  5.47 us
    ppermute x7, waiting for transfers between devices, swapped(): return lax.ppermute(x, axes, [(i, n - 1 - i) for i in range(n)])  3.32 us
    ppermute x1, starting transfers between devices, local(): there = lax.ppermute(end, (XH, CORE), [(0, 3), (1, 2)])  3.3 us
  transfers between devices with their start and end apart: 20, of which 8 were waited for; matrix products, arithmetic and copies ran while one was open for 0% of the time, Pallas kernels for 7%

profile of v10, /device:TPU:2, one launch (start us, length us, event | category | flops | bytes accessed | tf_op | source)
XLA Modules:
  0.0 103.8 jit_solution(268658747367130335)
XLA Ops:
  0.0 0.0 copy-start
  0.0 3.1 %shard_maps.1 = (f32[128,256]{1,0:T(8,128)S(1)}, f32[128,256]{1,0:T(8,128)S(1)}, f32[2,160,256]{2,1,0:T(8,128)S(1)}) custom-call(s32[1]{0:T(128)} %bitcast.refs_0_.core_ref.row_ref.refs_1_, bf16[160,256]{1,0:T(8,128)(2,1)} %refs_1_.3, bf16[160,256]{1,0:T(8,128)(2,1)} %refs_2_.2, f32[2,160]{1,0:T(2,128)} %refs_2_.3), custom_call_target="tpu_custom_call" | custom-call | flops 3000000000 | bytes 131072 | tf_op jit(solution)/shard_map/shard_maps/pallas_call | solution.py:36
  3.1 1.9 %collective-permute-start = (f32[128,256]{1,0:T(8,128)S(1)}, f32[128,256]{1,0:T(8,128)S(1)}, u32[]{:S(2)}, u32[]{:S(2)}) collective-permute-start(f32[128,256]{1,0:T(8,128)S(1)} %get-tuple-element.26), channel_id=1, source_target_pairs={{0,16},{16,0},{1,17},{17,1},{2,18},{18,2},{3,19},{19,3},{4,20},{20... | collective-permute-start | bytes 393224 | tf_op jit(solution)/shard_map/ppermute | solution.py:279
  5.1 0.0 copy-done.5
  5.1 0.0 copy-done.6
  5.1 0.0 copy-done.7
  5.1 0.4 shard_rows.1
  5.5 0.0 copy-start.1
  5.5 0.7 copy-done.1
  6.3 0.1 collective-permute-done.got_ref
  6.4 0.7 chip_map.1
  7.1 4.3 %collective-permute-start.1 = (f32[128,256]{1,0:T(8,128)S(1)}, f32[128,256]{1,0:T(8,128)S(1)}, u32[]{:S(2)}, u32[]{:S(2)}) collective-permute-start(f32[128,256]{1,0:T(8,128)S(1)} %get-tuple-element.29.later_ref.refs_1_), channel_id=1, source_target_pairs={{0,32},{32,0},{64,96},{96,64},{128,160},{160,128},{192,224},{224,1... | collective-permute-start | bytes 393224 | tf_op jit(solution)/shard_map/ppermute | solution.py:305
  11.4 0.0 copy-done
  11.4 1.3 %share_weights.1 = (f32[64,3072]{1,0:T(8,128)}, f32[64,3072]{1,0:T(8,128)}) custom-call(s32[1]{0:T(128)S(6)} %sub.3.column_ref, s32[1]{0:T(128)} %bitcast.refs_0_.core_ref.row_ref.refs_1_, bf16[256,6144]{1,0:T(8,128)(2,1)S(1)} %copy-done, bf16[256,6144]{1,0:T(8,128)(2,1)S(1)} %copy-done, f32[128,256]{1,0:T(8,128)S(1)} %get-tuple-element.29.later_ref.refs_1_), custom_call_target="tpu_custom_call" | custom-call | tf_op jit(solution)/shard_map/share_weights/pallas_call | solution.py:214
  12.7 5.4 %collective-permute-start.7 = (f32[64,3072]{1,0:T(8,128)}, f32[64,3072]{1,0:T(8,128)S(1)}, u32[]{:S(2)}, u32[]{:S(2)}) collective-permute-start(f32[64,3072]{1,0:T(8,128)} %get-tuple-element.30.refs_3_), channel_id=1, source_target_pairs={{0,8},{8,0},{1,9},{9,1},{2,10},{10,2},{3,11},{11,3},{4,12},{12,4},... | collective-permute-start | bytes 2359304 | tf_op jit(solution)/shard_map/ppermute | solution.py:279
  18.1 0.0 collective-permute-done.1.refs_2_
  18.1 0.2 join_chips.1.refs_3_.refs_1_
  18.4 3.4 %collective-permute-start.2 = (f32[128,256]{1,0:T(8,128)S(1)}, f32[128,256]{1,0:T(8,128)S(1)}, u32[]{:S(2)}, u32[]{:S(2)}) collective-permute-start(f32[128,256]{1,0:T(8,128)S(1)} %join_chips.1.refs_3_.refs_1_), channel_id=1, source_target_pairs={{0,64},{32,96},{64,0},{96,32},{128,192},{160,224},{192,128},{224,1... | collective-permute-start | bytes 393224 | tf_op jit(solution)/shard_map/ppermute | solution.py:305
  21.7 3.8 %collective-permute-start.10 = (f32[64,3072]{1,0:T(8,128)}, f32[64,3072]{1,0:T(8,128)S(1)}, u32[]{:S(2)}, u32[]{:S(2)}) collective-permute-start(f32[64,3072]{1,0:T(8,128)} %get-tuple-element.35), channel_id=1, source_target_pairs={{0,264},{8,256},{256,8},{264,0},{1,265},{9,257},{257,9},{265,1},{2... | collective-permute-start | bytes 2359304 | tf_op jit(solution)/shard_map/ppermute | solution.py:279
  25.5 0.0 copy-start.3
  25.6 3.9 %collective-permute-done.2.refs_2_ = f32[128,256]{1,0:T(8,128)S(1)} collective-permute-done((f32[128,256]{1,0:T(8,128)S(1)}, f32[128,256]{1,0:T(8,128)S(1)}, u32[]{:S(2)}, u32[]{:S(2)}) %collective-permute-start.2) | collective-permute-done | bytes 131104 | tf_op jit(solution)/shard_map/ppermute | solution.py:305
  29.5 0.2 join_pairs.1.refs_4_.refs_1_.refs_2_
  29.7 7.0 %collective-permute-start.3 = (f32[128,256]{1,0:T(8,128)S(1)}, f32[128,256]{1,0:T(8,128)S(1)}, u32[]{:S(2)}, u32[]{:S(2)}) collective-permute-start(f32[128,256]{1,0:T(8,128)S(1)} %join_pairs.1.refs_4_.refs_1_.refs_2_), channel_id=1, source_target_pairs={{0,224},{32,192},{64,160},{96,128},{128,96},{160,64},{192,32},{224... | collective-permute-start | bytes 393224 | tf_op jit(solution)/shard_map/ppermute | solution.py:305
  36.7 0.0 copy-done.3
  36.8 0.2 before_pairs.1.refs_5_.refs_4_
  37.0 0.0 collective-permute-done.7.n0
  37.0 2.1 %collective-permute-start.8 = (f32[64,3072]{1,0:T(8,128)S(1)}, f32[64,3072]{1,0:T(8,128)S(1)}, u32[]{:S(2)}, u32[]{:S(2)}) collective-permute-start(f32[64,3072]{1,0:T(8,128)S(1)} %collective-permute-done.7.n0), channel_id=1, source_target_pairs={{0,16},{16,0},{1,17},{17,1},{2,18},{18,2},{3,19},{19,3},{4,20},{20... | collective-permute-start | bytes 2359304 | tf_op jit(solution)/shard_map/ppermute | solution.py:279
  39.1 1.5 %collective-permute-done.3.refs_3_ = f32[128,256]{1,0:T(8,128)S(1)} collective-permute-done((f32[128,256]{1,0:T(8,128)S(1)}, f32[128,256]{1,0:T(8,128)S(1)}, u32[]{:S(2)}, u32[]{:S(2)}) %collective-permute-start.3) | collective-permute-done | bytes 131104 | tf_op jit(solution)/shard_map/ppermute | solution.py:305
  40.6 0.3 join_ring.1.refs_6_.refs_1_
  41.0 3.3 %collective-permute-start.6 = (f32[128,128]{1,0:T(8,128)S(1)}, f32[128,128]{1,0:T(8,128)S(1)}, u32[]{:S(2)}, u32[]{:S(2)}) collective-permute-start(f32[128,128]{1,0:T(8,128)S(1)} %join_ring.1.refs_6_.refs_1_), channel_id=1, source_target_pairs={{0,272},{16,256},{1,273},{17,257},{2,274},{18,258},{3,275},{19,259... | collective-permute-start | bytes 196616 | tf_op jit(solution)/shard_map/ppermute | solution.py:332
  44.3 2.7 %collective-permute-start.5 = (f32[128,128]{1,0:T(8,128)S(1)}, f32[128,128]{1,0:T(8,128)}, u32[]{:S(2)}, u32[]{:S(2)}) collective-permute-start(f32[128,128]{1,0:T(8,128)S(1)} %join_ring.1.refs_6_.refs_1_), channel_id=1, source_target_pairs={{0,256},{16,272},{1,257},{17,273},{2,258},{18,274},{3,259},{19,275... | collective-permute-start | bytes 196616 | tf_op jit(solution)/shard_map/ppermute | solution.py:331
  47.0 0.4 shard_prefixes.1
  47.4 2.0 %collective-permute-start.4 = (f32[128,256]{1,0:T(8,128)S(1)}, f32[128,256]{1,0:T(8,128)S(1)}, u32[]{:S(2)}, u32[]{:S(2)}) collective-permute-start(f32[128,256]{1,0:T(8,128)S(1)} %get-tuple-element.33), channel_id=1, source_target_pairs={{0,16},{16,0},{1,17},{17,1},{2,18},{18,2},{3,19},{19,3},{4,20},{20... | collective-permute-start | bytes 393224 | tf_op jit(solution)/shard_map/ppermute | solution.py:279
  49.5 0.0 collective-permute-done.10.f0
  49.5 2.3 %collective-permute-start.11 = (f32[64,3072]{1,0:T(8,128)S(1)}, f32[64,3072]{1,0:T(8,128)S(1)}, u32[]{:S(2)}, u32[]{:S(2)}) collective-permute-start(f32[64,3072]{1,0:T(8,128)S(1)} %collective-permute-done.10.f0), channel_id=1, source_target_pairs={{0,16},{16,0},{1,17},{17,1},{2,18},{18,2},{3,19},{19,3},{4,20},{20... | collective-permute-start | bytes 2359304 | tf_op jit(solution)/shard_map/ppermute | solution.py:279
  51.8 0.0 collective-permute-done.6.refs_3_
  51.8 0.0 collective-permute-done.5.refs_2_
  51.8 0.9 ring_states.1.refs_3_
  52.7 0.0 collective-permute-done.4.refs_2_
  52.7 0.0 collective-permute-done.8.refs_5_.n1
  52.7 0.4 outputs.1.later_ref.refs_0_
  53.1 3.3 %collective-permute-start.9 = (f32[160,256]{1,0:T(8,128)S(1)}, f32[160,256]{1,0:T(8,128)S(1)}, u32[]{:S(2)}, u32[]{:S(2)}) collective-permute-start(f32[160,256]{1,0:T(8,128)S(1)} %outputs.1.later_ref.refs_0_), channel_id=1, source_target_pairs={{0,8},{8,0},{1,9},{9,1},{2,10},{10,2},{3,11},{11,3},{4,12},{12,4},... | collective-permute-start | bytes 491528 | tf_op jit(solution)/shard_map/ppermute | solution.py:279
  56.4 0.0 collective-permute-done.11.f1
  56.4 1.6 %piece_weights.1.refs_2_ = bf16[8,512,384]{2,1,0:T(8,128)(2,1)S(1)} custom-call(s32[1]{0:T(128)} %bitcast.2.x_lo_ref, s32[1]{0:T(128)} %bitcast.4.y_ref, s32[1]{0:T(128)} %bitcast.refs_0_.core_ref.row_ref.refs_1_, bf16[256,6144]{1,0:T(8,128)(2,1)} %w_hbm.1, f32[64,3072]{1,0:T(8,128)S(1)} %collective-permute-done.7.n0, ...), custom_call_target="tpu_custom_call" | custom-call | flops 3000000000 | bytes 131072 | tf_op jit(solution)/shard_map/piece_weights/pallas_call | solution.py:340
  58.0 3.2 %collective-permute-done.9.refs_1_ = f32[160,256]{1,0:T(8,128)S(1)} collective-permute-done((f32[160,256]{1,0:T(8,128)S(1)}, f32[160,256]{1,0:T(8,128)S(1)}, u32[]{:S(2)}, u32[]{:S(2)}) %collective-permute-start.9) | collective-permute-done | bytes 163872 | tf_op jit(solution)/shard_map/ppermute | solution.py:279
  61.2 0.2 farthest.1
  61.5 5.4 %collective-permute-start.12 = (f32[80,384]{1,0:T(8,128)S(1)}, f32[80,384]{1,0:T(8,128)S(1)}, u32[]{:S(2)}, u32[]{:S(2)}) collective-permute-start(f32[80,384]{1,0:T(8,128)S(1)} %get-tuple-element.36.refs_3_), channel_id=1, source_target_pairs={{0,7},{1,0},{2,1},{3,2},{4,3},{5,4},{6,5},{7,6},{8,15},{9,8},{10,9... | collective-permute-start | bytes 368648 | tf_op jit(solution)/shard_map/ppermute | solution.py:284
  66.9 1.9 %collective-permute-start.16 = (f32[80,384]{1,0:T(8,128)S(1)}, f32[80,384]{1,0:T(8,128)S(1)}, u32[]{:S(2)}, u32[]{:S(2)}) collective-permute-start(f32[80,384]{1,0:T(8,128)S(1)} %get-tuple-element.41), channel_id=1, source_target_pairs={{0,1},{1,2},{2,3},{3,4},{4,5},{5,6},{6,7},{7,0},{8,9},{9,10},{10,1... | collective-permute-start | bytes 368648 | tf_op jit(solution)/shard_map/ppermute | solution.py:284
  68.8 0.8 nearer.1
  69.6 0.0 collective-permute-done.12
  69.6 5.3 %collective-permute-start.13 = (f32[160,384]{1,0:T(8,128)S(1)}, f32[160,384]{1,0:T(8,128)S(1)}, u32[]{:S(2)}, u32[]{:S(2)}) collective-permute-start(f32[160,384]{1,0:T(8,128)S(1)} %pad_add_fusion.1), channel_id=1, source_target_pairs={{0,7},{1,0},{2,1},{3,2},{4,3},{5,4},{6,5},{7,6},{8,15},{9,8},{10,9... | collective-permute-start | bytes 737288 | tf_op jit(solution)/shard_map/ppermute | solution.py:284
  74.9 0.0 collective-permute-done.16
  74.9 1.9 %collective-permute-start.17 = (f32[160,384]{1,0:T(8,128)S(1)}, f32[160,384]{1,0:T(8,128)S(1)}, u32[]{:S(2)}, u32[]{:S(2)}) collective-permute-start(f32[160,384]{1,0:T(8,128)S(1)} %pad_add_fusion), channel_id=1, source_target_pairs={{0,1},{1,2},{2,3},{3,4},{4,5},{5,6},{6,7},{7,0},{8,9},{9,10},{10,1... | collective-permute-start | bytes 737288 | tf_op jit(solution)/shard_map/ppermute | solution.py:284
  76.8 2.0 %collective-permute-done.13 = f32[160,384]{1,0:T(8,128)S(1)} collective-permute-done((f32[160,384]{1,0:T(8,128)S(1)}, f32[160,384]{1,0:T(8,128)S(1)}, u32[]{:S(2)}, u32[]{:S(2)}) %collective-permute-start.13) | collective-permute-done | bytes 245792 | tf_op jit(solution)/shard_map/ppermute | solution.py:284
  78.8 5.6 %collective-permute-start.14 = (f32[160,384]{1,0:T(8,128)S(1)}, f32[160,384]{1,0:T(8,128)S(1)}, u32[]{:S(2)}, u32[]{:S(2)}) collective-permute-start(f32[160,384]{1,0:T(8,128)S(1)} %add.29), channel_id=1, source_target_pairs={{0,7},{1,0},{2,1},{3,2},{4,3},{5,4},{6,5},{7,6},{8,15},{9,8},{10,9... | collective-permute-start | bytes 737288 | tf_op jit(solution)/shard_map/ppermute | solution.py:284
  84.5 0.0 collective-permute-done.17
  84.5 1.9 %collective-permute-start.18 = (f32[160,384]{1,0:T(8,128)S(1)}, f32[160,384]{1,0:T(8,128)S(1)}, u32[]{:S(2)}, u32[]{:S(2)}) collective-permute-start(f32[160,384]{1,0:T(8,128)S(1)} %add.32), channel_id=1, source_target_pairs={{0,1},{1,2},{2,3},{3,4},{4,5},{5,6},{6,7},{7,0},{8,9},{9,10},{10,1... | collective-permute-start | bytes 737288 | tf_op jit(solution)/shard_map/ppermute | solution.py:284
  86.4 1.7 %collective-permute-done.14 = f32[160,384]{1,0:T(8,128)S(1)} collective-permute-done((f32[160,384]{1,0:T(8,128)S(1)}, f32[160,384]{1,0:T(8,128)S(1)}, u32[]{:S(2)}, u32[]{:S(2)}) %collective-permute-start.14) | collective-permute-done | bytes 245792 | tf_op jit(solution)/shard_map/ppermute | solution.py:284
  88.2 5.6 %collective-permute-start.15 = (f32[160,384]{1,0:T(8,128)S(1)}, f32[160,384]{1,0:T(8,128)S(1)}, u32[]{:S(2)}, u32[]{:S(2)}) collective-permute-start(f32[160,384]{1,0:T(8,128)S(1)} %add.30), channel_id=1, source_target_pairs={{0,7},{1,0},{2,1},{3,2},{4,3},{5,4},{6,5},{7,6},{8,15},{9,8},{10,9... | collective-permute-start | bytes 737288 | tf_op jit(solution)/shard_map/ppermute | solution.py:284
  93.8 0.0 collective-permute-done.18
  93.8 1.9 %collective-permute-start.19 = (f32[160,384]{1,0:T(8,128)S(1)}, f32[160,384]{1,0:T(8,128)S(1)}, u32[]{:S(2)}, u32[]{:S(2)}) collective-permute-start(f32[160,384]{1,0:T(8,128)S(1)} %add.33), channel_id=1, source_target_pairs={{0,1},{1,2},{2,3},{3,4},{4,5},{5,6},{6,7},{7,0},{8,9},{9,10},{10,1... | collective-permute-start | bytes 737288 | tf_op jit(solution)/shard_map/ppermute | solution.py:284
  95.8 1.7 %collective-permute-done.15 = f32[160,384]{1,0:T(8,128)S(1)} collective-permute-done((f32[160,384]{1,0:T(8,128)S(1)}, f32[160,384]{1,0:T(8,128)S(1)}, u32[]{:S(2)}, u32[]{:S(2)}) %collective-permute-start.15) | collective-permute-done | bytes 245792 | tf_op jit(solution)/shard_map/ppermute | solution.py:284
  97.5 5.7 %collective-permute-done.19 = f32[160,384]{1,0:T(8,128)S(1)} collective-permute-done((f32[160,384]{1,0:T(8,128)S(1)}, f32[160,384]{1,0:T(8,128)S(1)}, u32[]{:S(2)}, u32[]{:S(2)}) %collective-permute-start.19) | collective-permute-done | bytes 245792 | tf_op jit(solution)/shard_map/ppermute | solution.py:284
  103.1 0.7 add_convert_fusion
  (16 shorter events, 0.2 us)
Async XLA Ops:
  0.0 5.1 %copy-start.5 = (bf16[160,256]{1,0:T(8,128)(2,1)S(1)}, bf16[160,256]{1,0:T(8,128)(2,1)}, u32[]{:S(2)}) copy-start(bf16[160,256]{1,0:T(8,128)(2,1)} %refs_1_.3) | copy-start | bytes 245764
  0.0 5.1 %copy-start.6 = (bf16[160,256]{1,0:T(8,128)(2,1)S(1)}, bf16[160,256]{1,0:T(8,128)(2,1)}, u32[]{:S(2)}) copy-start(bf16[160,256]{1,0:T(8,128)(2,1)} %refs_0_.2) | copy-start | bytes 245764
  0.0 5.1 %copy-start.7 = (f32[2,160]{1,0:T(2,128)S(1)}, f32[2,160]{1,0:T(2,128)}, u32[]{:S(2)}) copy-start(f32[2,160]{1,0:T(2,128)} %refs_2_.3) | copy-start | bytes 3844
  0.0 11.4 %copy-start = (bf16[256,6144]{1,0:T(8,128)(2,1)S(1)}, bf16[256,6144]{1,0:T(8,128)(2,1)}, u32[]{:S(2)}) copy-start(bf16[256,6144]{1,0:T(8,128)(2,1)} %w_hbm.1) | copy-start | bytes 9437188
  3.1 3.2 %collective-permute-start = (f32[128,256]{1,0:T(8,128)S(1)}, f32[128,256]{1,0:T(8,128)S(1)}, u32[]{:S(2)}, u32[]{:S(2)}) collective-permute-start(f32[128,256]{1,0:T(8,128)S(1)} %get-tuple-element.26), channel_id=1, source_target_pairs={{0,16},{16,0},{1,17},{17,1},{2,18},{18,2},{3,19},{19,3},{4,20},{20... | collective-permute-start | bytes 393224 | tf_op jit(solution)/shard_map/ppermute | solution.py:279
  5.5 0.7 copy-start.1
  7.1 11.1 %collective-permute-start.1 = (f32[128,256]{1,0:T(8,128)S(1)}, f32[128,256]{1,0:T(8,128)S(1)}, u32[]{:S(2)}, u32[]{:S(2)}) collective-permute-start(f32[128,256]{1,0:T(8,128)S(1)} %get-tuple-element.29.later_ref.refs_1_), channel_id=1, source_target_pairs={{0,32},{32,0},{64,96},{96,64},{128,160},{160,128},{192,224},{224,1... | collective-permute-start | bytes 393224 | tf_op jit(solution)/shard_map/ppermute | solution.py:305
  12.7 24.3 %collective-permute-start.7 = (f32[64,3072]{1,0:T(8,128)}, f32[64,3072]{1,0:T(8,128)S(1)}, u32[]{:S(2)}, u32[]{:S(2)}) collective-permute-start(f32[64,3072]{1,0:T(8,128)} %get-tuple-element.30.refs_3_), channel_id=1, source_target_pairs={{0,8},{8,0},{1,9},{9,1},{2,10},{10,2},{3,11},{11,3},{4,12},{12,4},... | collective-permute-start | bytes 2359304 | tf_op jit(solution)/shard_map/ppermute | solution.py:279
  18.4 11.2 %collective-permute-start.2 = (f32[128,256]{1,0:T(8,128)S(1)}, f32[128,256]{1,0:T(8,128)S(1)}, u32[]{:S(2)}, u32[]{:S(2)}) collective-permute-start(f32[128,256]{1,0:T(8,128)S(1)} %join_chips.1.refs_3_.refs_1_), channel_id=1, source_target_pairs={{0,64},{32,96},{64,0},{96,32},{128,192},{160,224},{192,128},{224,1... | collective-permute-start | bytes 393224 | tf_op jit(solution)/shard_map/ppermute | solution.py:305
  21.7 27.7 %collective-permute-start.10 = (f32[64,3072]{1,0:T(8,128)}, f32[64,3072]{1,0:T(8,128)S(1)}, u32[]{:S(2)}, u32[]{:S(2)}) collective-permute-start(f32[64,3072]{1,0:T(8,128)} %get-tuple-element.35), channel_id=1, source_target_pairs={{0,264},{8,256},{256,8},{264,0},{1,265},{9,257},{257,9},{265,1},{2... | collective-permute-start | bytes 2359304 | tf_op jit(solution)/shard_map/ppermute | solution.py:279
  25.5 11.2 %copy-start.3 = (f32[2,128,128]{2,1,0:T(8,128)S(1)}, f32[2,128,128]{2,1,0:T(8,128)}, u32[]{:S(2)}) copy-start(f32[2,128,128]{2,1,0:T(8,128)} %refs_0_.3) | copy-start | bytes 393220
  29.7 10.9 %collective-permute-start.3 = (f32[128,256]{1,0:T(8,128)S(1)}, f32[128,256]{1,0:T(8,128)S(1)}, u32[]{:S(2)}, u32[]{:S(2)}) collective-permute-start(f32[128,256]{1,0:T(8,128)S(1)} %join_pairs.1.refs_4_.refs_1_.refs_2_), channel_id=1, source_target_pairs={{0,224},{32,192},{64,160},{96,128},{128,96},{160,64},{192,32},{224... | collective-permute-start | bytes 393224 | tf_op jit(solution)/shard_map/ppermute | solution.py:305
  37.0 10.0 %copy-start.4 = (f32[128,256]{1,0:T(8,128)S(1)}, f32[128,256]{1,0:T(8,128)}, u32[]{:S(2)}) copy-start(f32[128,256]{1,0:T(8,128)} %get-tuple-element.31.refs_5_) | copy-start | bytes 393220
  37.0 12.4 %copy-start.2 = (f32[160,512]{1,0:T(8,128)S(1)}, f32[160,512]{1,0:T(8,128)}, u32[]{:S(2)}) copy-start(f32[160,512]{1,0:T(8,128)} %copy-done.1) | copy-start | bytes 983044
  37.0 15.7 %collective-permute-start.8 = (f32[64,3072]{1,0:T(8,128)S(1)}, f32[64,3072]{1,0:T(8,128)S(1)}, u32[]{:S(2)}, u32[]{:S(2)}) collective-permute-start(f32[64,3072]{1,0:T(8,128)S(1)} %collective-permute-done.7.n0), channel_id=1, source_target_pairs={{0,16},{16,0},{1,17},{17,1},{2,18},{18,2},{3,19},{19,3},{4,20},{20... | collective-permute-start | bytes 2359304 | tf_op jit(solution)/shard_map/ppermute | solution.py:279
  41.0 10.8 %collective-permute-start.6 = (f32[128,128]{1,0:T(8,128)S(1)}, f32[128,128]{1,0:T(8,128)S(1)}, u32[]{:S(2)}, u32[]{:S(2)}) collective-permute-start(f32[128,128]{1,0:T(8,128)S(1)} %join_ring.1.refs_6_.refs_1_), channel_id=1, source_target_pairs={{0,272},{16,256},{1,273},{17,257},{2,274},{18,258},{3,275},{19,259... | collective-permute-start | bytes 196616 | tf_op jit(solution)/shard_map/ppermute | solution.py:332
  44.3 7.5 %collective-permute-start.5 = (f32[128,128]{1,0:T(8,128)S(1)}, f32[128,128]{1,0:T(8,128)}, u32[]{:S(2)}, u32[]{:S(2)}) collective-permute-start(f32[128,128]{1,0:T(8,128)S(1)} %join_ring.1.refs_6_.refs_1_), channel_id=1, source_target_pairs={{0,256},{16,272},{1,257},{17,273},{2,258},{18,274},{3,259},{19,275... | collective-permute-start | bytes 196616 | tf_op jit(solution)/shard_map/ppermute | solution.py:331
  47.4 5.3 %collective-permute-start.4 = (f32[128,256]{1,0:T(8,128)S(1)}, f32[128,256]{1,0:T(8,128)S(1)}, u32[]{:S(2)}, u32[]{:S(2)}) collective-permute-start(f32[128,256]{1,0:T(8,128)S(1)} %get-tuple-element.33), channel_id=1, source_target_pairs={{0,16},{16,0},{1,17},{17,1},{2,18},{18,2},{3,19},{19,3},{4,20},{20... | collective-permute-start | bytes 393224 | tf_op jit(solution)/shard_map/ppermute | solution.py:279
  49.5 7.0 %collective-permute-start.11 = (f32[64,3072]{1,0:T(8,128)S(1)}, f32[64,3072]{1,0:T(8,128)S(1)}, u32[]{:S(2)}, u32[]{:S(2)}) collective-permute-start(f32[64,3072]{1,0:T(8,128)S(1)} %collective-permute-done.10.f0), channel_id=1, source_target_pairs={{0,16},{16,0},{1,17},{17,1},{2,18},{18,2},{3,19},{19,3},{4,20},{20... | collective-permute-start | bytes 2359304 | tf_op jit(solution)/shard_map/ppermute | solution.py:279
  53.1 8.1 %collective-permute-start.9 = (f32[160,256]{1,0:T(8,128)S(1)}, f32[160,256]{1,0:T(8,128)S(1)}, u32[]{:S(2)}, u32[]{:S(2)}) collective-permute-start(f32[160,256]{1,0:T(8,128)S(1)} %outputs.1.later_ref.refs_0_), channel_id=1, source_target_pairs={{0,8},{8,0},{1,9},{9,1},{2,10},{10,2},{3,11},{11,3},{4,12},{12,4},... | collective-permute-start | bytes 491528 | tf_op jit(solution)/shard_map/ppermute | solution.py:279
  61.5 8.1 %collective-permute-start.12 = (f32[80,384]{1,0:T(8,128)S(1)}, f32[80,384]{1,0:T(8,128)S(1)}, u32[]{:S(2)}, u32[]{:S(2)}) collective-permute-start(f32[80,384]{1,0:T(8,128)S(1)} %get-tuple-element.36.refs_3_), channel_id=1, source_target_pairs={{0,7},{1,0},{2,1},{3,2},{4,3},{5,4},{6,5},{7,6},{8,15},{9,8},{10,9... | collective-permute-start | bytes 368648 | tf_op jit(solution)/shard_map/ppermute | solution.py:284
  66.9 8.0 %collective-permute-start.16 = (f32[80,384]{1,0:T(8,128)S(1)}, f32[80,384]{1,0:T(8,128)S(1)}, u32[]{:S(2)}, u32[]{:S(2)}) collective-permute-start(f32[80,384]{1,0:T(8,128)S(1)} %get-tuple-element.41), channel_id=1, source_target_pairs={{0,1},{1,2},{2,3},{3,4},{4,5},{5,6},{6,7},{7,0},{8,9},{9,10},{10,1... | collective-permute-start | bytes 368648 | tf_op jit(solution)/shard_map/ppermute | solution.py:284
  69.6 9.2 %collective-permute-start.13 = (f32[160,384]{1,0:T(8,128)S(1)}, f32[160,384]{1,0:T(8,128)S(1)}, u32[]{:S(2)}, u32[]{:S(2)}) collective-permute-start(f32[160,384]{1,0:T(8,128)S(1)} %pad_add_fusion.1), channel_id=1, source_target_pairs={{0,7},{1,0},{2,1},{3,2},{4,3},{5,4},{6,5},{7,6},{8,15},{9,8},{10,9... | collective-permute-start | bytes 737288 | tf_op jit(solution)/shard_map/ppermute | solution.py:284
  74.9 9.5 %collective-permute-start.17 = (f32[160,384]{1,0:T(8,128)S(1)}, f32[160,384]{1,0:T(8,128)S(1)}, u32[]{:S(2)}, u32[]{:S(2)}) collective-permute-start(f32[160,384]{1,0:T(8,128)S(1)} %pad_add_fusion), channel_id=1, source_target_pairs={{0,1},{1,2},{2,3},{3,4},{4,5},{5,6},{6,7},{7,0},{8,9},{9,10},{10,1... | collective-permute-start | bytes 737288 | tf_op jit(solution)/shard_map/ppermute | solution.py:284
  78.8 9.3 %collective-permute-start.14 = (f32[160,384]{1,0:T(8,128)S(1)}, f32[160,384]{1,0:T(8,128)S(1)}, u32[]{:S(2)}, u32[]{:S(2)}) collective-permute-start(f32[160,384]{1,0:T(8,128)S(1)} %add.29), channel_id=1, source_target_pairs={{0,7},{1,0},{2,1},{3,2},{4,3},{5,4},{6,5},{7,6},{8,15},{9,8},{10,9... | collective-permute-start | bytes 737288 | tf_op jit(solution)/shard_map/ppermute | solution.py:284
  84.5 9.3 %collective-permute-start.18 = (f32[160,384]{1,0:T(8,128)S(1)}, f32[160,384]{1,0:T(8,128)S(1)}, u32[]{:S(2)}, u32[]{:S(2)}) collective-permute-start(f32[160,384]{1,0:T(8,128)S(1)} %add.32), channel_id=1, source_target_pairs={{0,1},{1,2},{2,3},{3,4},{4,5},{5,6},{6,7},{7,0},{8,9},{9,10},{10,1... | collective-permute-start | bytes 737288 | tf_op jit(solution)/shard_map/ppermute | solution.py:284
  88.2 9.3 %collective-permute-start.15 = (f32[160,384]{1,0:T(8,128)S(1)}, f32[160,384]{1,0:T(8,128)S(1)}, u32[]{:S(2)}, u32[]{:S(2)}) collective-permute-start(f32[160,384]{1,0:T(8,128)S(1)} %add.30), channel_id=1, source_target_pairs={{0,7},{1,0},{2,1},{3,2},{4,3},{5,4},{6,5},{7,6},{8,15},{9,8},{10,9... | collective-permute-start | bytes 737288 | tf_op jit(solution)/shard_map/ppermute | solution.py:284
  93.8 9.3 %collective-permute-start.19 = (f32[160,384]{1,0:T(8,128)S(1)}, f32[160,384]{1,0:T(8,128)S(1)}, u32[]{:S(2)}, u32[]{:S(2)}) collective-permute-start(f32[160,384]{1,0:T(8,128)S(1)} %add.33), channel_id=1, source_target_pairs={{0,1},{1,2},{2,3},{3,4},{4,5},{5,6},{6,7},{7,0},{8,9},{9,10},{10,1... | collective-permute-start | bytes 737288 | tf_op jit(solution)/shard_map/ppermute | solution.py:284

commit v11 on v10

--- a/solution.py
+++ b/solution.py
@@ -331,7 +331,7 @@
     here = lax.ppermute(end, (XH, CORE), [(0, 2), (1, 3)])
     there = lax.ppermute(end, (XH, CORE), [(0, 3), (1, 2)])
     mine, other = call(shard_prefixes, [wide, wide], [z, core], four, got_four, pre, early, later=[end], us=0.1)
-    (begin,) = call(ring_states, [((2, HW, HW), f32)], [x_hi, core], here, there, first, us=6)
+    (begin,) = call(ring_states, [((2, HW, HW), f32)], [x_hi, core], here, there, first, us=5)
     (late_rows,) = call(fetched, [((rows, 4 * HW), f32)], [], own_rows, later=[end], us=0.1)
     (z_rows,) = call(
         outputs, [((rows, 2 * HW), f32)], [core], mine, swapped(other, (CORE,)), begin, late_rows, later=[near_other], us=4

time: 105 us -> 105 us (level)
  no operation moved by 1% of the time
where the time goes in v11:
time: 105 us; the launch traced here: 104 us
  starting transfers between devices  70.9 us (68%)
  waiting for transfers between devices  20 us (19%)
  Pallas kernels  10.8 us (10%)
    ppermute x8, starting transfers between devices, passed(): return lax.ppermute(x, axis, [(i, (i + by) % n) for i in range(n)])  29.5 us
    ppermute x7, starting transfers between devices, swapped(): return lax.ppermute(x, axes, [(i, n - 1 - i) for i in range(n)])  20.7 us
    ppermute x3, starting transfers between devices, across_z(): return lax.ppermute(x, Z, [(i, to(i)) for i in range(SIZES[1])])  14.7 us
    ppermute x8, waiting for transfers between devices, passed(): return lax.ppermute(x, axis, [(i, (i + by) % n) for i in range(n)])  11.1 us
    pallas_call x14, Pallas kernels, call(): pl.pallas_call(body, name=kernel.__name__, out_shape=outs, in_specs=[SM]...  7.27 us
    ppermute x3, waiting for transfers between devices, across_z(): return lax.ppermute(x, Z, [(i, to(i)) for i in range(SIZES[1])])  5.6 us
    ppermute x7, waiting for transfers between devices, swapped(): return lax.ppermute(x, axes, [(i, n - 1 - i) for i in range(n)])  3.32 us
    ppermute x1, starting transfers between devices, local(): there = lax.ppermute(end, (XH, CORE), [(0, 3), (1, 2)])  3.3 us
  transfers between devices with their start and end apart: 20, of which 8 were waited for; matrix products, arithmetic and copies ran while one was open for 0% of the time, Pallas kernels for 7%

profile of v11, /device:TPU:2, one launch (start us, length us, event | category | flops | bytes accessed | tf_op | source)
XLA Modules:
  0.0 103.8 jit_solution(885417188082689494)
XLA Ops:
  0.0 0.0 copy-start
  0.0 3.1 %shard_maps.1 = (f32[128,256]{1,0:T(8,128)S(1)}, f32[128,256]{1,0:T(8,128)S(1)}, f32[2,160,256]{2,1,0:T(8,128)S(1)}) custom-call(s32[1]{0:T(128)} %bitcast.refs_0_.core_ref.row_ref.refs_1_, bf16[160,256]{1,0:T(8,128)(2,1)} %refs_1_.3, bf16[160,256]{1,0:T(8,128)(2,1)} %refs_2_.2, f32[2,160]{1,0:T(2,128)} %refs_2_.3), custom_call_target="tpu_custom_call" | custom-call | flops 3000000000 | bytes 131072 | tf_op jit(solution)/shard_map/shard_maps/pallas_call | solution.py:36
  3.1 1.9 %collective-permute-start = (f32[128,256]{1,0:T(8,128)S(1)}, f32[128,256]{1,0:T(8,128)S(1)}, u32[]{:S(2)}, u32[]{:S(2)}) collective-permute-start(f32[128,256]{1,0:T(8,128)S(1)} %get-tuple-element.26), channel_id=1, source_target_pairs={{0,16},{16,0},{1,17},{17,1},{2,18},{18,2},{3,19},{19,3},{4,20},{20... | collective-permute-start | bytes 393224 | tf_op jit(solution)/shard_map/ppermute | solution.py:279
  5.1 0.0 copy-done.5
  5.1 0.0 copy-done.6
  5.1 0.0 copy-done.7
  5.1 0.4 shard_rows.1
  5.5 0.0 copy-start.1
  5.5 0.7 copy-done.1
  6.3 0.1 collective-permute-done.got_ref
  6.4 0.7 chip_map.1
  7.1 4.3 %collective-permute-start.1 = (f32[128,256]{1,0:T(8,128)S(1)}, f32[128,256]{1,0:T(8,128)S(1)}, u32[]{:S(2)}, u32[]{:S(2)}) collective-permute-start(f32[128,256]{1,0:T(8,128)S(1)} %get-tuple-element.29.later_ref.refs_1_), channel_id=1, source_target_pairs={{0,32},{32,0},{64,96},{96,64},{128,160},{160,128},{192,224},{224,1... | collective-permute-start | bytes 393224 | tf_op jit(solution)/shard_map/ppermute | solution.py:305
  11.4 0.0 copy-done
  11.4 1.3 %share_weights.1 = (f32[64,3072]{1,0:T(8,128)}, f32[64,3072]{1,0:T(8,128)}) custom-call(s32[1]{0:T(128)S(6)} %sub.3.column_ref, s32[1]{0:T(128)} %bitcast.refs_0_.core_ref.row_ref.refs_1_, bf16[256,6144]{1,0:T(8,128)(2,1)S(1)} %copy-done, bf16[256,6144]{1,0:T(8,128)(2,1)S(1)} %copy-done, f32[128,256]{1,0:T(8,128)S(1)} %get-tuple-element.29.later_ref.refs_1_), custom_call_target="tpu_custom_call" | custom-call | tf_op jit(solution)/shard_map/share_weights/pallas_call | solution.py:214
  12.7 5.4 %collective-permute-start.7 = (f32[64,3072]{1,0:T(8,128)}, f32[64,3072]{1,0:T(8,128)S(1)}, u32[]{:S(2)}, u32[]{:S(2)}) collective-permute-start(f32[64,3072]{1,0:T(8,128)} %get-tuple-element.30.refs_3_), channel_id=1, source_target_pairs={{0,8},{8,0},{1,9},{9,1},{2,10},{10,2},{3,11},{11,3},{4,12},{12,4},... | collective-permute-start | bytes 2359304 | tf_op jit(solution)/shard_map/ppermute | solution.py:279
  18.1 0.0 collective-permute-done.1.refs_2_
  18.1 0.2 join_chips.1.refs_3_.refs_1_
  18.4 3.4 %collective-permute-start.2 = (f32[128,256]{1,0:T(8,128)S(1)}, f32[128,256]{1,0:T(8,128)S(1)}, u32[]{:S(2)}, u32[]{:S(2)}) collective-permute-start(f32[128,256]{1,0:T(8,128)S(1)} %join_chips.1.refs_3_.refs_1_), channel_id=1, source_target_pairs={{0,64},{32,96},{64,0},{96,32},{128,192},{160,224},{192,128},{224,1... | collective-permute-start | bytes 393224 | tf_op jit(solution)/shard_map/ppermute | solution.py:305
  21.7 3.8 %collective-permute-start.10 = (f32[64,3072]{1,0:T(8,128)}, f32[64,3072]{1,0:T(8,128)S(1)}, u32[]{:S(2)}, u32[]{:S(2)}) collective-permute-start(f32[64,3072]{1,0:T(8,128)} %get-tuple-element.35), channel_id=1, source_target_pairs={{0,264},{8,256},{256,8},{264,0},{1,265},{9,257},{257,9},{265,1},{2... | collective-permute-start | bytes 2359304 | tf_op jit(solution)/shard_map/ppermute | solution.py:279
  25.5 0.0 copy-start.3
  25.6 3.9 %collective-permute-done.2.refs_2_ = f32[128,256]{1,0:T(8,128)S(1)} collective-permute-done((f32[128,256]{1,0:T(8,128)S(1)}, f32[128,256]{1,0:T(8,128)S(1)}, u32[]{:S(2)}, u32[]{:S(2)}) %collective-permute-start.2) | collective-permute-done | bytes 131104 | tf_op jit(solution)/shard_map/ppermute | solution.py:305
  29.5 0.2 join_pairs.1.refs_4_.refs_1_.refs_2_
  29.7 7.0 %collective-permute-start.3 = (f32[128,256]{1,0:T(8,128)S(1)}, f32[128,256]{1,0:T(8,128)S(1)}, u32[]{:S(2)}, u32[]{:S(2)}) collective-permute-start(f32[128,256]{1,0:T(8,128)S(1)} %join_pairs.1.refs_4_.refs_1_.refs_2_), channel_id=1, source_target_pairs={{0,224},{32,192},{64,160},{96,128},{128,96},{160,64},{192,32},{224... | collective-permute-start | bytes 393224 | tf_op jit(solution)/shard_map/ppermute | solution.py:305
  36.7 0.0 collective-permute-done.7.n0
  36.7 1.9 %collective-permute-start.8 = (f32[64,3072]{1,0:T(8,128)S(1)}, f32[64,3072]{1,0:T(8,128)S(1)}, u32[]{:S(2)}, u32[]{:S(2)}) collective-permute-start(f32[64,3072]{1,0:T(8,128)S(1)} %collective-permute-done.7.n0), channel_id=1, source_target_pairs={{0,16},{16,0},{1,17},{17,1},{2,18},{18,2},{3,19},{19,3},{4,20},{20... | collective-permute-start | bytes 2359304 | tf_op jit(solution)/shard_map/ppermute | solution.py:279
  38.7 0.0 copy-done.3
  38.7 0.2 before_pairs.1.refs_5_.refs_4_
  38.9 1.7 %collective-permute-done.3.refs_3_ = f32[128,256]{1,0:T(8,128)S(1)} collective-permute-done((f32[128,256]{1,0:T(8,128)S(1)}, f32[128,256]{1,0:T(8,128)S(1)}, u32[]{:S(2)}, u32[]{:S(2)}) %collective-permute-start.3) | collective-permute-done | bytes 131104 | tf_op jit(solution)/shard_map/ppermute | solution.py:305
  40.6 0.3 join_ring.1.refs_6_.refs_1_
  41.0 3.3 %collective-permute-start.6 = (f32[128,128]{1,0:T(8,128)S(1)}, f32[128,128]{1,0:T(8,128)S(1)}, u32[]{:S(2)}, u32[]{:S(2)}) collective-permute-start(f32[128,128]{1,0:T(8,128)S(1)} %join_ring.1.refs_6_.refs_1_), channel_id=1, source_target_pairs={{0,272},{16,256},{1,273},{17,257},{2,274},{18,258},{3,275},{19,259... | collective-permute-start | bytes 196616 | tf_op jit(solution)/shard_map/ppermute | solution.py:332
  44.3 2.7 %collective-permute-start.5 = (f32[128,128]{1,0:T(8,128)S(1)}, f32[128,128]{1,0:T(8,128)}, u32[]{:S(2)}, u32[]{:S(2)}) collective-permute-start(f32[128,128]{1,0:T(8,128)S(1)} %join_ring.1.refs_6_.refs_1_), channel_id=1, source_target_pairs={{0,256},{16,272},{1,257},{17,273},{2,258},{18,274},{3,259},{19,275... | collective-permute-start | bytes 196616 | tf_op jit(solution)/shard_map/ppermute | solution.py:331
  47.0 0.4 shard_prefixes.1
  47.4 2.0 %collective-permute-start.4 = (f32[128,256]{1,0:T(8,128)S(1)}, f32[128,256]{1,0:T(8,128)S(1)}, u32[]{:S(2)}, u32[]{:S(2)}) collective-permute-start(f32[128,256]{1,0:T(8,128)S(1)} %get-tuple-element.33), channel_id=1, source_target_pairs={{0,16},{16,0},{1,17},{17,1},{2,18},{18,2},{3,19},{19,3},{4,20},{20... | collective-permute-start | bytes 393224 | tf_op jit(solution)/shard_map/ppermute | solution.py:279
  49.5 0.0 collective-permute-done.10.f0
  49.5 2.3 %collective-permute-start.11 = (f32[64,3072]{1,0:T(8,128)S(1)}, f32[64,3072]{1,0:T(8,128)S(1)}, u32[]{:S(2)}, u32[]{:S(2)}) collective-permute-start(f32[64,3072]{1,0:T(8,128)S(1)} %collective-permute-done.10.f0), channel_id=1, source_target_pairs={{0,16},{16,0},{1,17},{17,1},{2,18},{18,2},{3,19},{19,3},{4,20},{20... | collective-permute-start | bytes 2359304 | tf_op jit(solution)/shard_map/ppermute | solution.py:279
  51.8 0.0 collective-permute-done.6.refs_3_
  51.8 0.0 collective-permute-done.5.refs_2_
  51.8 0.9 ring_states.1.refs_3_
  52.7 0.0 collective-permute-done.4.refs_2_
  52.7 0.0 collective-permute-done.8.refs_5_.n1
  52.7 0.4 outputs.1.later_ref.refs_0_
  53.1 3.3 %collective-permute-start.9 = (f32[160,256]{1,0:T(8,128)S(1)}, f32[160,256]{1,0:T(8,128)S(1)}, u32[]{:S(2)}, u32[]{:S(2)}) collective-permute-start(f32[160,256]{1,0:T(8,128)S(1)} %outputs.1.later_ref.refs_0_), channel_id=1, source_target_pairs={{0,8},{8,0},{1,9},{9,1},{2,10},{10,2},{3,11},{11,3},{4,12},{12,4},... | collective-permute-start | bytes 491528 | tf_op jit(solution)/shard_map/ppermute | solution.py:279
  56.4 0.0 collective-permute-done.11.f1
  56.4 1.6 %piece_weights.1.refs_2_ = bf16[8,512,384]{2,1,0:T(8,128)(2,1)S(1)} custom-call(s32[1]{0:T(128)} %bitcast.2.x_lo_ref, s32[1]{0:T(128)} %bitcast.4.y_ref, s32[1]{0:T(128)} %bitcast.refs_0_.core_ref.row_ref.refs_1_, bf16[256,6144]{1,0:T(8,128)(2,1)} %w_hbm.1, f32[64,3072]{1,0:T(8,128)S(1)} %collective-permute-done.7.n0, ...), custom_call_target="tpu_custom_call" | custom-call | flops 3000000000 | bytes 131072 | tf_op jit(solution)/shard_map/piece_weights/pallas_call | solution.py:340
  58.0 3.2 %collective-permute-done.9.refs_1_ = f32[160,256]{1,0:T(8,128)S(1)} collective-permute-done((f32[160,256]{1,0:T(8,128)S(1)}, f32[160,256]{1,0:T(8,128)S(1)}, u32[]{:S(2)}, u32[]{:S(2)}) %collective-permute-start.9) | collective-permute-done | bytes 163872 | tf_op jit(solution)/shard_map/ppermute | solution.py:279
  61.2 0.2 farthest.1
  61.5 5.4 %collective-permute-start.12 = (f32[80,384]{1,0:T(8,128)S(1)}, f32[80,384]{1,0:T(8,128)S(1)}, u32[]{:S(2)}, u32[]{:S(2)}) collective-permute-start(f32[80,384]{1,0:T(8,128)S(1)} %get-tuple-element.36.refs_3_), channel_id=1, source_target_pairs={{0,7},{1,0},{2,1},{3,2},{4,3},{5,4},{6,5},{7,6},{8,15},{9,8},{10,9... | collective-permute-start | bytes 368648 | tf_op jit(solution)/shard_map/ppermute | solution.py:284
  66.9 1.9 %collective-permute-start.16 = (f32[80,384]{1,0:T(8,128)S(1)}, f32[80,384]{1,0:T(8,128)S(1)}, u32[]{:S(2)}, u32[]{:S(2)}) collective-permute-start(f32[80,384]{1,0:T(8,128)S(1)} %get-tuple-element.41), channel_id=1, source_target_pairs={{0,1},{1,2},{2,3},{3,4},{4,5},{5,6},{6,7},{7,0},{8,9},{9,10},{10,1... | collective-permute-start | bytes 368648 | tf_op jit(solution)/shard_map/ppermute | solution.py:284
  68.8 0.8 nearer.1
  69.6 0.0 collective-permute-done.12
  69.6 5.3 %collective-permute-start.13 = (f32[160,384]{1,0:T(8,128)S(1)}, f32[160,384]{1,0:T(8,128)S(1)}, u32[]{:S(2)}, u32[]{:S(2)}) collective-permute-start(f32[160,384]{1,0:T(8,128)S(1)} %pad_add_fusion.1), channel_id=1, source_target_pairs={{0,7},{1,0},{2,1},{3,2},{4,3},{5,4},{6,5},{7,6},{8,15},{9,8},{10,9... | collective-permute-start | bytes 737288 | tf_op jit(solution)/shard_map/ppermute | solution.py:284
  74.9 0.0 collective-permute-done.16
  74.9 1.9 %collective-permute-start.17 = (f32[160,384]{1,0:T(8,128)S(1)}, f32[160,384]{1,0:T(8,128)S(1)}, u32[]{:S(2)}, u32[]{:S(2)}) collective-permute-start(f32[160,384]{1,0:T(8,128)S(1)} %pad_add_fusion), channel_id=1, source_target_pairs={{0,1},{1,2},{2,3},{3,4},{4,5},{5,6},{6,7},{7,0},{8,9},{9,10},{10,1... | collective-permute-start | bytes 737288 | tf_op jit(solution)/shard_map/ppermute | solution.py:284
  76.8 2.0 %collective-permute-done.13 = f32[160,384]{1,0:T(8,128)S(1)} collective-permute-done((f32[160,384]{1,0:T(8,128)S(1)}, f32[160,384]{1,0:T(8,128)S(1)}, u32[]{:S(2)}, u32[]{:S(2)}) %collective-permute-start.13) | collective-permute-done | bytes 245792 | tf_op jit(solution)/shard_map/ppermute | solution.py:284
  78.8 5.6 %collective-permute-start.14 = (f32[160,384]{1,0:T(8,128)S(1)}, f32[160,384]{1,0:T(8,128)S(1)}, u32[]{:S(2)}, u32[]{:S(2)}) collective-permute-start(f32[160,384]{1,0:T(8,128)S(1)} %add.29), channel_id=1, source_target_pairs={{0,7},{1,0},{2,1},{3,2},{4,3},{5,4},{6,5},{7,6},{8,15},{9,8},{10,9... | collective-permute-start | bytes 737288 | tf_op jit(solution)/shard_map/ppermute | solution.py:284
  84.5 0.0 collective-permute-done.17
  84.5 1.9 %collective-permute-start.18 = (f32[160,384]{1,0:T(8,128)S(1)}, f32[160,384]{1,0:T(8,128)S(1)}, u32[]{:S(2)}, u32[]{:S(2)}) collective-permute-start(f32[160,384]{1,0:T(8,128)S(1)} %add.32), channel_id=1, source_target_pairs={{0,1},{1,2},{2,3},{3,4},{4,5},{5,6},{6,7},{7,0},{8,9},{9,10},{10,1... | collective-permute-start | bytes 737288 | tf_op jit(solution)/shard_map/ppermute | solution.py:284
  86.4 1.7 %collective-permute-done.14 = f32[160,384]{1,0:T(8,128)S(1)} collective-permute-done((f32[160,384]{1,0:T(8,128)S(1)}, f32[160,384]{1,0:T(8,128)S(1)}, u32[]{:S(2)}, u32[]{:S(2)}) %collective-permute-start.14) | collective-permute-done | bytes 245792 | tf_op jit(solution)/shard_map/ppermute | solution.py:284
  88.2 5.6 %collective-permute-start.15 = (f32[160,384]{1,0:T(8,128)S(1)}, f32[160,384]{1,0:T(8,128)S(1)}, u32[]{:S(2)}, u32[]{:S(2)}) collective-permute-start(f32[160,384]{1,0:T(8,128)S(1)} %add.30), channel_id=1, source_target_pairs={{0,7},{1,0},{2,1},{3,2},{4,3},{5,4},{6,5},{7,6},{8,15},{9,8},{10,9... | collective-permute-start | bytes 737288 | tf_op jit(solution)/shard_map/ppermute | solution.py:284
  93.8 0.0 collective-permute-done.18
  93.8 1.9 %collective-permute-start.19 = (f32[160,384]{1,0:T(8,128)S(1)}, f32[160,384]{1,0:T(8,128)S(1)}, u32[]{:S(2)}, u32[]{:S(2)}) collective-permute-start(f32[160,384]{1,0:T(8,128)S(1)} %add.33), channel_id=1, source_target_pairs={{0,1},{1,2},{2,3},{3,4},{4,5},{5,6},{6,7},{7,0},{8,9},{9,10},{10,1... | collective-permute-start | bytes 737288 | tf_op jit(solution)/shard_map/ppermute | solution.py:284
  95.8 1.7 %collective-permute-done.15 = f32[160,384]{1,0:T(8,128)S(1)} collective-permute-done((f32[160,384]{1,0:T(8,128)S(1)}, f32[160,384]{1,0:T(8,128)S(1)}, u32[]{:S(2)}, u32[]{:S(2)}) %collective-permute-start.15) | collective-permute-done | bytes 245792 | tf_op jit(solution)/shard_map/ppermute | solution.py:284
  97.5 5.7 %collective-permute-done.19 = f32[160,384]{1,0:T(8,128)S(1)} collective-permute-done((f32[160,384]{1,0:T(8,128)S(1)}, f32[160,384]{1,0:T(8,128)S(1)}, u32[]{:S(2)}, u32[]{:S(2)}) %collective-permute-start.19) | collective-permute-done | bytes 245792 | tf_op jit(solution)/shard_map/ppermute | solution.py:284
  103.1 0.7 add_convert_fusion
  (16 shorter events, 0.2 us)
Async XLA Ops:
  0.0 5.1 %copy-start.5 = (bf16[160,256]{1,0:T(8,128)(2,1)S(1)}, bf16[160,256]{1,0:T(8,128)(2,1)}, u32[]{:S(2)}) copy-start(bf16[160,256]{1,0:T(8,128)(2,1)} %refs_1_.3) | copy-start | bytes 245764
  0.0 5.1 %copy-start.6 = (bf16[160,256]{1,0:T(8,128)(2,1)S(1)}, bf16[160,256]{1,0:T(8,128)(2,1)}, u32[]{:S(2)}) copy-start(bf16[160,256]{1,0:T(8,128)(2,1)} %refs_0_.2) | copy-start | bytes 245764
  0.0 5.1 %copy-start.7 = (f32[2,160]{1,0:T(2,128)S(1)}, f32[2,160]{1,0:T(2,128)}, u32[]{:S(2)}) copy-start(f32[2,160]{1,0:T(2,128)} %refs_2_.3) | copy-start | bytes 3844
  0.0 11.4 %copy-start = (bf16[256,6144]{1,0:T(8,128)(2,1)S(1)}, bf16[256,6144]{1,0:T(8,128)(2,1)}, u32[]{:S(2)}) copy-start(bf16[256,6144]{1,0:T(8,128)(2,1)} %w_hbm.1) | copy-start | bytes 9437188
  3.1 3.2 %collective-permute-start = (f32[128,256]{1,0:T(8,128)S(1)}, f32[128,256]{1,0:T(8,128)S(1)}, u32[]{:S(2)}, u32[]{:S(2)}) collective-permute-start(f32[128,256]{1,0:T(8,128)S(1)} %get-tuple-element.26), channel_id=1, source_target_pairs={{0,16},{16,0},{1,17},{17,1},{2,18},{18,2},{3,19},{19,3},{4,20},{20... | collective-permute-start | bytes 393224 | tf_op jit(solution)/shard_map/ppermute | solution.py:279
  5.5 0.7 copy-start.1
  7.1 11.1 %collective-permute-start.1 = (f32[128,256]{1,0:T(8,128)S(1)}, f32[128,256]{1,0:T(8,128)S(1)}, u32[]{:S(2)}, u32[]{:S(2)}) collective-permute-start(f32[128,256]{1,0:T(8,128)S(1)} %get-tuple-element.29.later_ref.refs_1_), channel_id=1, source_target_pairs={{0,32},{32,0},{64,96},{96,64},{128,160},{160,128},{192,224},{224,1... | collective-permute-start | bytes 393224 | tf_op jit(solution)/shard_map/ppermute | solution.py:305
  12.7 24.0 %collective-permute-start.7 = (f32[64,3072]{1,0:T(8,128)}, f32[64,3072]{1,0:T(8,128)S(1)}, u32[]{:S(2)}, u32[]{:S(2)}) collective-permute-start(f32[64,3072]{1,0:T(8,128)} %get-tuple-element.30.refs_3_), channel_id=1, source_target_pairs={{0,8},{8,0},{1,9},{9,1},{2,10},{10,2},{3,11},{11,3},{4,12},{12,4},... | collective-permute-start | bytes 2359304 | tf_op jit(solution)/shard_map/ppermute | solution.py:279
  18.4 11.2 %collective-permute-start.2 = (f32[128,256]{1,0:T(8,128)S(1)}, f32[128,256]{1,0:T(8,128)S(1)}, u32[]{:S(2)}, u32[]{:S(2)}) collective-permute-start(f32[128,256]{1,0:T(8,128)S(1)} %join_chips.1.refs_3_.refs_1_), channel_id=1, source_target_pairs={{0,64},{32,96},{64,0},{96,32},{128,192},{160,224},{192,128},{224,1... | collective-permute-start | bytes 393224 | tf_op jit(solution)/shard_map/ppermute | solution.py:305
  21.7 27.7 %collective-permute-start.10 = (f32[64,3072]{1,0:T(8,128)}, f32[64,3072]{1,0:T(8,128)S(1)}, u32[]{:S(2)}, u32[]{:S(2)}) collective-permute-start(f32[64,3072]{1,0:T(8,128)} %get-tuple-element.35), channel_id=1, source_target_pairs={{0,264},{8,256},{256,8},{264,0},{1,265},{9,257},{257,9},{265,1},{2... | collective-permute-start | bytes 2359304 | tf_op jit(solution)/shard_map/ppermute | solution.py:279
  25.5 13.1 %copy-start.3 = (f32[2,128,128]{2,1,0:T(8,128)S(1)}, f32[2,128,128]{2,1,0:T(8,128)}, u32[]{:S(2)}) copy-start(f32[2,128,128]{2,1,0:T(8,128)} %refs_0_.3) | copy-start | bytes 393220
  29.7 10.9 %collective-permute-start.3 = (f32[128,256]{1,0:T(8,128)S(1)}, f32[128,256]{1,0:T(8,128)S(1)}, u32[]{:S(2)}, u32[]{:S(2)}) collective-permute-start(f32[128,256]{1,0:T(8,128)S(1)} %join_pairs.1.refs_4_.refs_1_.refs_2_), channel_id=1, source_target_pairs={{0,224},{32,192},{64,160},{96,128},{128,96},{160,64},{192,32},{224... | collective-permute-start | bytes 393224 | tf_op jit(solution)/shard_map/ppermute | solution.py:305
  36.7 15.9 %collective-permute-start.8 = (f32[64,3072]{1,0:T(8,128)S(1)}, f32[64,3072]{1,0:T(8,128)S(1)}, u32[]{:S(2)}, u32[]{:S(2)}) collective-permute-start(f32[64,3072]{1,0:T(8,128)S(1)} %collective-permute-done.7.n0), channel_id=1, source_target_pairs={{0,16},{16,0},{1,17},{17,1},{2,18},{18,2},{3,19},{19,3},{4,20},{20... | collective-permute-start | bytes 2359304 | tf_op jit(solution)/shard_map/ppermute | solution.py:279
  38.9 8.0 %copy-start.4 = (f32[128,256]{1,0:T(8,128)S(1)}, f32[128,256]{1,0:T(8,128)}, u32[]{:S(2)}) copy-start(f32[128,256]{1,0:T(8,128)} %get-tuple-element.31.refs_5_) | copy-start | bytes 393220
  38.9 10.5 %copy-start.2 = (f32[160,512]{1,0:T(8,128)S(1)}, f32[160,512]{1,0:T(8,128)}, u32[]{:S(2)}) copy-start(f32[160,512]{1,0:T(8,128)} %copy-done.1) | copy-start | bytes 983044
  41.0 10.8 %collective-permute-start.6 = (f32[128,128]{1,0:T(8,128)S(1)}, f32[128,128]{1,0:T(8,128)S(1)}, u32[]{:S(2)}, u32[]{:S(2)}) collective-permute-start(f32[128,128]{1,0:T(8,128)S(1)} %join_ring.1.refs_6_.refs_1_), channel_id=1, source_target_pairs={{0,272},{16,256},{1,273},{17,257},{2,274},{18,258},{3,275},{19,259... | collective-permute-start | bytes 196616 | tf_op jit(solution)/shard_map/ppermute | solution.py:332
  44.3 7.5 %collective-permute-start.5 = (f32[128,128]{1,0:T(8,128)S(1)}, f32[128,128]{1,0:T(8,128)}, u32[]{:S(2)}, u32[]{:S(2)}) collective-permute-start(f32[128,128]{1,0:T(8,128)S(1)} %join_ring.1.refs_6_.refs_1_), channel_id=1, source_target_pairs={{0,256},{16,272},{1,257},{17,273},{2,258},{18,274},{3,259},{19,275... | collective-permute-start | bytes 196616 | tf_op jit(solution)/shard_map/ppermute | solution.py:331
  47.4 5.3 %collective-permute-start.4 = (f32[128,256]{1,0:T(8,128)S(1)}, f32[128,256]{1,0:T(8,128)S(1)}, u32[]{:S(2)}, u32[]{:S(2)}) collective-permute-start(f32[128,256]{1,0:T(8,128)S(1)} %get-tuple-element.33), channel_id=1, source_target_pairs={{0,16},{16,0},{1,17},{17,1},{2,18},{18,2},{3,19},{19,3},{4,20},{20... | collective-permute-start | bytes 393224 | tf_op jit(solution)/shard_map/ppermute | solution.py:279
  49.5 7.0 %collective-permute-start.11 = (f32[64,3072]{1,0:T(8,128)S(1)}, f32[64,3072]{1,0:T(8,128)S(1)}, u32[]{:S(2)}, u32[]{:S(2)}) collective-permute-start(f32[64,3072]{1,0:T(8,128)S(1)} %collective-permute-done.10.f0), channel_id=1, source_target_pairs={{0,16},{16,0},{1,17},{17,1},{2,18},{18,2},{3,19},{19,3},{4,20},{20... | collective-permute-start | bytes 2359304 | tf_op jit(solution)/shard_map/ppermute | solution.py:279
  53.1 8.1 %collective-permute-start.9 = (f32[160,256]{1,0:T(8,128)S(1)}, f32[160,256]{1,0:T(8,128)S(1)}, u32[]{:S(2)}, u32[]{:S(2)}) collective-permute-start(f32[160,256]{1,0:T(8,128)S(1)} %outputs.1.later_ref.refs_0_), channel_id=1, source_target_pairs={{0,8},{8,0},{1,9},{9,1},{2,10},{10,2},{3,11},{11,3},{4,12},{12,4},... | collective-permute-start | bytes 491528 | tf_op jit(solution)/shard_map/ppermute | solution.py:279
  61.5 8.1 %collective-permute-start.12 = (f32[80,384]{1,0:T(8,128)S(1)}, f32[80,384]{1,0:T(8,128)S(1)}, u32[]{:S(2)}, u32[]{:S(2)}) collective-permute-start(f32[80,384]{1,0:T(8,128)S(1)} %get-tuple-element.36.refs_3_), channel_id=1, source_target_pairs={{0,7},{1,0},{2,1},{3,2},{4,3},{5,4},{6,5},{7,6},{8,15},{9,8},{10,9... | collective-permute-start | bytes 368648 | tf_op jit(solution)/shard_map/ppermute | solution.py:284
  66.9 8.0 %collective-permute-start.16 = (f32[80,384]{1,0:T(8,128)S(1)}, f32[80,384]{1,0:T(8,128)S(1)}, u32[]{:S(2)}, u32[]{:S(2)}) collective-permute-start(f32[80,384]{1,0:T(8,128)S(1)} %get-tuple-element.41), channel_id=1, source_target_pairs={{0,1},{1,2},{2,3},{3,4},{4,5},{5,6},{6,7},{7,0},{8,9},{9,10},{10,1... | collective-permute-start | bytes 368648 | tf_op jit(solution)/shard_map/ppermute | solution.py:284
  69.6 9.2 %collective-permute-start.13 = (f32[160,384]{1,0:T(8,128)S(1)}, f32[160,384]{1,0:T(8,128)S(1)}, u32[]{:S(2)}, u32[]{:S(2)}) collective-permute-start(f32[160,384]{1,0:T(8,128)S(1)} %pad_add_fusion.1), channel_id=1, source_target_pairs={{0,7},{1,0},{2,1},{3,2},{4,3},{5,4},{6,5},{7,6},{8,15},{9,8},{10,9... | collective-permute-start | bytes 737288 | tf_op jit(solution)/shard_map/ppermute | solution.py:284
  74.9 9.5 %collective-permute-start.17 = (f32[160,384]{1,0:T(8,128)S(1)}, f32[160,384]{1,0:T(8,128)S(1)}, u32[]{:S(2)}, u32[]{:S(2)}) collective-permute-start(f32[160,384]{1,0:T(8,128)S(1)} %pad_add_fusion), channel_id=1, source_target_pairs={{0,1},{1,2},{2,3},{3,4},{4,5},{5,6},{6,7},{7,0},{8,9},{9,10},{10,1... | collective-permute-start | bytes 737288 | tf_op jit(solution)/shard_map/ppermute | solution.py:284
  78.8 9.3 %collective-permute-start.14 = (f32[160,384]{1,0:T(8,128)S(1)}, f32[160,384]{1,0:T(8,128)S(1)}, u32[]{:S(2)}, u32[]{:S(2)}) collective-permute-start(f32[160,384]{1,0:T(8,128)S(1)} %add.29), channel_id=1, source_target_pairs={{0,7},{1,0},{2,1},{3,2},{4,3},{5,4},{6,5},{7,6},{8,15},{9,8},{10,9... | collective-permute-start | bytes 737288 | tf_op jit(solution)/shard_map/ppermute | solution.py:284
  84.5 9.3 %collective-permute-start.18 = (f32[160,384]{1,0:T(8,128)S(1)}, f32[160,384]{1,0:T(8,128)S(1)}, u32[]{:S(2)}, u32[]{:S(2)}) collective-permute-start(f32[160,384]{1,0:T(8,128)S(1)} %add.32), channel_id=1, source_target_pairs={{0,1},{1,2},{2,3},{3,4},{4,5},{5,6},{6,7},{7,0},{8,9},{9,10},{10,1... | collective-permute-start | bytes 737288 | tf_op jit(solution)/shard_map/ppermute | solution.py:284
  88.2 9.3 %collective-permute-start.15 = (f32[160,384]{1,0:T(8,128)S(1)}, f32[160,384]{1,0:T(8,128)S(1)}, u32[]{:S(2)}, u32[]{:S(2)}) collective-permute-start(f32[160,384]{1,0:T(8,128)S(1)} %add.30), channel_id=1, source_target_pairs={{0,7},{1,0},{2,1},{3,2},{4,3},{5,4},{6,5},{7,6},{8,15},{9,8},{10,9... | collective-permute-start | bytes 737288 | tf_op jit(solution)/shard_map/ppermute | solution.py:284
  93.8 9.3 %collective-permute-start.19 = (f32[160,384]{1,0:T(8,128)S(1)}, f32[160,384]{1,0:T(8,128)S(1)}, u32[]{:S(2)}, u32[]{:S(2)}) collective-permute-start(f32[160,384]{1,0:T(8,128)S(1)} %add.33), channel_id=1, source_target_pairs={{0,1},{1,2},{2,3},{3,4},{4,5},{5,6},{6,7},{7,0},{8,9},{9,10},{10,1... | collective-permute-start | bytes 737288 | tf_op jit(solution)/shard_map/ppermute | solution.py:284

commit v12 on v11

--- a/solution.py
+++ b/solution.py
@@ -331,7 +331,7 @@
     here = lax.ppermute(end, (XH, CORE), [(0, 2), (1, 3)])
     there = lax.ppermute(end, (XH, CORE), [(0, 3), (1, 2)])
     mine, other = call(shard_prefixes, [wide, wide], [z, core], four, got_four, pre, early, later=[end], us=0.1)
-    (begin,) = call(ring_states, [((2, HW, HW), f32)], [x_hi, core], here, there, first, us=5)
+    (begin,) = call(ring_states, [((2, HW, HW), f32)], [x_hi, core], here, there, first, us=8)
     (late_rows,) = call(fetched, [((rows, 4 * HW), f32)], [], own_rows, later=[end], us=0.1)
     (z_rows,) = call(
         outputs, [((rows, 2 * HW), f32)], [core], mine, swapped(other, (CORE,)), begin, late_rows, later=[near_other], us=4

time: 105 us -> 107 us (1.019)
  waiting for transfers between devices: 20 us -> 22.6 us
    ppermute x3, waiting for transfers between devices: 5.6 us -> 7.46 us  [across_z(): return lax.ppermute(x, Z, [(i, to(i)) for i in range(SIZES[1])])]
  transfers between devices with their start and end apart: 20 -> 20, of which waited for: 8 -> 8; matrix products, arithmetic and copies ran while one was open for 0% -> 0% of each run, Pallas kernels for 7% -> 6%
where the time goes in v12:
time: 107 us; the launch traced here: 106 us
  starting transfers between devices  71 us (66%)
  waiting for transfers between devices  22.6 us (21%)
  Pallas kernels  10.6 us (10%)
    ppermute x8, starting transfers between devices, passed(): return lax.ppermute(x, axis, [(i, (i + by) % n) for i in range(n)])  29.5 us
    ppermute x7, starting transfers between devices, swapped(): return lax.ppermute(x, axes, [(i, n - 1 - i) for i in range(n)])  20.5 us
    ppermute x3, starting transfers between devices, across_z(): return lax.ppermute(x, Z, [(i, to(i)) for i in range(SIZES[1])])  15 us
    ppermute x8, waiting for transfers between devices, passed(): return lax.ppermute(x, axis, [(i, (i + by) % n) for i in range(n)])  11.4 us
    ppermute x3, waiting for transfers between devices, across_z(): return lax.ppermute(x, Z, [(i, to(i)) for i in range(SIZES[1])])  7.46 us
    pallas_call x14, Pallas kernels, call(): pl.pallas_call(body, name=kernel.__name__, out_shape=outs, in_specs=[SM]...  7.28 us
    ppermute x7, waiting for transfers between devices, swapped(): return lax.ppermute(x, axes, [(i, n - 1 - i) for i in range(n)])  3.74 us
    ppermute x1, starting transfers between devices, local(): there = lax.ppermute(end, (XH, CORE), [(0, 3), (1, 2)])  3.35 us
  transfers between devices with their start and end apart: 20, of which 8 were waited for; matrix products, arithmetic and copies ran while one was open for 0% of the time, Pallas kernels for 6%

profile of v12, /device:TPU:2, one launch (start us, length us, event | category | flops | bytes accessed | tf_op | source)
XLA Modules:
  0.0 106.4 jit_solution(6360380591734480991)
XLA Ops:
  0.0 0.0 copy-start
  0.0 3.1 %shard_maps.1 = (f32[128,256]{1,0:T(8,128)S(1)}, f32[128,256]{1,0:T(8,128)S(1)}, f32[2,160,256]{2,1,0:T(8,128)S(1)}) custom-call(s32[1]{0:T(128)} %bitcast.refs_0_.core_ref.row_ref.refs_1_, bf16[160,256]{1,0:T(8,128)(2,1)} %refs_1_.3, bf16[160,256]{1,0:T(8,128)(2,1)} %refs_2_.2, f32[2,160]{1,0:T(2,128)} %refs_2_.3), custom_call_target="tpu_custom_call" | custom-call | flops 3000000000 | bytes 131072 | tf_op jit(solution)/shard_map/shard_maps/pallas_call | solution.py:36
  3.1 1.9 %collective-permute-start = (f32[128,256]{1,0:T(8,128)S(1)}, f32[128,256]{1,0:T(8,128)S(1)}, u32[]{:S(2)}, u32[]{:S(2)}) collective-permute-start(f32[128,256]{1,0:T(8,128)S(1)} %get-tuple-element.26), channel_id=1, source_target_pairs={{0,16},{16,0},{1,17},{17,1},{2,18},{18,2},{3,19},{19,3},{4,20},{20... | collective-permute-start | bytes 393224 | tf_op jit(solution)/shard_map/ppermute | solution.py:279
  5.1 0.0 copy-done.5
  5.1 0.0 copy-done.6
  5.1 0.0 copy-done.7
  5.1 0.4 shard_rows.1
  5.5 0.0 copy-start.1
  5.5 0.7 copy-done.1
  6.3 0.1 collective-permute-done.got_ref
  6.4 0.7 chip_map.1
  7.1 4.3 %collective-permute-start.1 = (f32[128,256]{1,0:T(8,128)S(1)}, f32[128,256]{1,0:T(8,128)S(1)}, u32[]{:S(2)}, u32[]{:S(2)}) collective-permute-start(f32[128,256]{1,0:T(8,128)S(1)} %get-tuple-element.29.later_ref.refs_1_), channel_id=1, source_target_pairs={{0,32},{32,0},{64,96},{96,64},{128,160},{160,128},{192,224},{224,1... | collective-permute-start | bytes 393224 | tf_op jit(solution)/shard_map/ppermute | solution.py:305
  11.4 0.0 copy-done
  11.4 1.1 %share_weights.1 = (f32[64,3072]{1,0:T(8,128)S(1)}, f32[64,3072]{1,0:T(8,128)}) custom-call(s32[1]{0:T(128)S(6)} %sub.3.column_ref, s32[1]{0:T(128)} %bitcast.refs_0_.core_ref.row_ref.refs_1_, bf16[256,6144]{1,0:T(8,128)(2,1)S(1)} %copy-done, bf16[256,6144]{1,0:T(8,128)(2,1)S(1)} %copy-done, f32[128,256]{1,0:T(8,128)S(1)} %get-tuple-element.29.later_ref.refs_1_), custom_call_target="tpu_custom_call" | custom-call | tf_op jit(solution)/shard_map/share_weights/pallas_call | solution.py:214
  12.5 5.4 %collective-permute-start.7 = (f32[64,3072]{1,0:T(8,128)S(1)}, f32[64,3072]{1,0:T(8,128)S(1)}, u32[]{:S(2)}, u32[]{:S(2)}) collective-permute-start(f32[64,3072]{1,0:T(8,128)S(1)} %get-tuple-element.30.refs_3_), channel_id=1, source_target_pairs={{0,8},{8,0},{1,9},{9,1},{2,10},{10,2},{3,11},{11,3},{4,12},{12,4},... | collective-permute-start | bytes 2359304 | tf_op jit(solution)/shard_map/ppermute | solution.py:279
  18.0 0.0 collective-permute-done.1.refs_2_
  18.0 0.2 join_chips.1.refs_3_.refs_1_
  18.2 3.5 %collective-permute-start.2 = (f32[128,256]{1,0:T(8,128)S(1)}, f32[128,256]{1,0:T(8,128)S(1)}, u32[]{:S(2)}, u32[]{:S(2)}) collective-permute-start(f32[128,256]{1,0:T(8,128)S(1)} %join_chips.1.refs_3_.refs_1_), channel_id=1, source_target_pairs={{0,64},{32,96},{64,0},{96,32},{128,192},{160,224},{192,128},{224,1... | collective-permute-start | bytes 393224 | tf_op jit(solution)/shard_map/ppermute | solution.py:305
  21.7 3.7 %collective-permute-start.10 = (f32[64,3072]{1,0:T(8,128)}, f32[64,3072]{1,0:T(8,128)S(1)}, u32[]{:S(2)}, u32[]{:S(2)}) collective-permute-start(f32[64,3072]{1,0:T(8,128)} %get-tuple-element.35), channel_id=1, source_target_pairs={{0,264},{8,256},{256,8},{264,0},{1,265},{9,257},{257,9},{265,1},{2... | collective-permute-start | bytes 2359304 | tf_op jit(solution)/shard_map/ppermute | solution.py:279
  25.4 0.0 copy-start.3
  25.4 3.9 %collective-permute-done.2.refs_2_ = f32[128,256]{1,0:T(8,128)S(1)} collective-permute-done((f32[128,256]{1,0:T(8,128)S(1)}, f32[128,256]{1,0:T(8,128)S(1)}, u32[]{:S(2)}, u32[]{:S(2)}) %collective-permute-start.2) | collective-permute-done | bytes 131104 | tf_op jit(solution)/shard_map/ppermute | solution.py:305
  29.3 0.2 join_pairs.1.refs_4_.refs_1_.refs_2_
  29.5 7.2 %collective-permute-start.3 = (f32[128,256]{1,0:T(8,128)S(1)}, f32[128,256]{1,0:T(8,128)S(1)}, u32[]{:S(2)}, u32[]{:S(2)}) collective-permute-start(f32[128,256]{1,0:T(8,128)S(1)} %join_pairs.1.refs_4_.refs_1_.refs_2_), channel_id=1, source_target_pairs={{0,224},{32,192},{64,160},{96,128},{128,96},{160,64},{192,32},{224... | collective-permute-start | bytes 393224 | tf_op jit(solution)/shard_map/ppermute | solution.py:305
  36.7 0.0 copy-done.3
  36.7 0.2 before_pairs.1.refs_5_.refs_4_
  37.0 3.6 %collective-permute-done.3.refs_3_ = f32[128,256]{1,0:T(8,128)S(1)} collective-permute-done((f32[128,256]{1,0:T(8,128)S(1)}, f32[128,256]{1,0:T(8,128)S(1)}, u32[]{:S(2)}, u32[]{:S(2)}) %collective-permute-start.3) | collective-permute-done | bytes 131104 | tf_op jit(solution)/shard_map/ppermute | solution.py:305
  40.6 0.3 join_ring.1.refs_6_.refs_1_
  40.9 3.3 %collective-permute-start.6 = (f32[128,128]{1,0:T(8,128)S(1)}, f32[128,128]{1,0:T(8,128)S(1)}, u32[]{:S(2)}, u32[]{:S(2)}) collective-permute-start(f32[128,128]{1,0:T(8,128)S(1)} %join_ring.1.refs_6_.refs_1_), channel_id=1, source_target_pairs={{0,272},{16,256},{1,273},{17,257},{2,274},{18,258},{3,275},{19,259... | collective-permute-start | bytes 196616 | tf_op jit(solution)/shard_map/ppermute | solution.py:332
  44.3 2.6 %collective-permute-start.5 = (f32[128,128]{1,0:T(8,128)S(1)}, f32[128,128]{1,0:T(8,128)}, u32[]{:S(2)}, u32[]{:S(2)}) collective-permute-start(f32[128,128]{1,0:T(8,128)S(1)} %join_ring.1.refs_6_.refs_1_), channel_id=1, source_target_pairs={{0,256},{16,272},{1,257},{17,273},{2,258},{18,274},{3,259},{19,275... | collective-permute-start | bytes 196616 | tf_op jit(solution)/shard_map/ppermute | solution.py:331
  46.9 0.0 collective-permute-done.7.n0
  46.9 2.0 %collective-permute-start.8 = (f32[64,3072]{1,0:T(8,128)S(1)}, f32[64,3072]{1,0:T(8,128)S(1)}, u32[]{:S(2)}, u32[]{:S(2)}) collective-permute-start(f32[64,3072]{1,0:T(8,128)S(1)} %collective-permute-done.7.n0), channel_id=1, source_target_pairs={{0,16},{16,0},{1,17},{17,1},{2,18},{18,2},{3,19},{19,3},{4,20},{20... | collective-permute-start | bytes 2359304 | tf_op jit(solution)/shard_map/ppermute | solution.py:279
  48.9 0.4 shard_prefixes.1
  49.4 2.3 %collective-permute-start.4 = (f32[128,256]{1,0:T(8,128)S(1)}, f32[128,256]{1,0:T(8,128)S(1)}, u32[]{:S(2)}, u32[]{:S(2)}) collective-permute-start(f32[128,256]{1,0:T(8,128)S(1)} %get-tuple-element.33), channel_id=1, source_target_pairs={{0,16},{16,0},{1,17},{17,1},{2,18},{18,2},{3,19},{19,3},{4,20},{20... | collective-permute-start | bytes 393224 | tf_op jit(solution)/shard_map/ppermute | solution.py:279
  51.7 0.0 collective-permute-done.10.f0
  51.7 2.0 %collective-permute-start.11 = (f32[64,3072]{1,0:T(8,128)S(1)}, f32[64,3072]{1,0:T(8,128)S(1)}, u32[]{:S(2)}, u32[]{:S(2)}) collective-permute-start(f32[64,3072]{1,0:T(8,128)S(1)} %collective-permute-done.10.f0), channel_id=1, source_target_pairs={{0,16},{16,0},{1,17},{17,1},{2,18},{18,2},{3,19},{19,3},{4,20},{20... | collective-permute-start | bytes 2359304 | tf_op jit(solution)/shard_map/ppermute | solution.py:279
  53.8 0.0 collective-permute-done.6.refs_3_
  53.8 0.0 collective-permute-done.5.refs_2_
  53.8 0.9 ring_states.1.refs_3_
  54.7 0.0 collective-permute-done.4.refs_2_
  54.7 0.0 collective-permute-done.8.refs_5_.n1
  54.7 0.4 outputs.1.later_ref.refs_0_
  55.1 3.2 %collective-permute-start.9 = (f32[160,256]{1,0:T(8,128)S(1)}, f32[160,256]{1,0:T(8,128)S(1)}, u32[]{:S(2)}, u32[]{:S(2)}) collective-permute-start(f32[160,256]{1,0:T(8,128)S(1)} %outputs.1.later_ref.refs_0_), channel_id=1, source_target_pairs={{0,8},{8,0},{1,9},{9,1},{2,10},{10,2},{3,11},{11,3},{4,12},{12,4},... | collective-permute-start | bytes 491528 | tf_op jit(solution)/shard_map/ppermute | solution.py:279
  58.3 0.0 collective-permute-done.11.f1
  58.3 1.6 %piece_weights.1.refs_2_ = bf16[8,512,384]{2,1,0:T(8,128)(2,1)S(1)} custom-call(s32[1]{0:T(128)} %bitcast.2.x_lo_ref, s32[1]{0:T(128)} %bitcast.4.y_ref, s32[1]{0:T(128)} %bitcast.refs_0_.core_ref.row_ref.refs_1_, bf16[256,6144]{1,0:T(8,128)(2,1)} %w_hbm.1, f32[64,3072]{1,0:T(8,128)S(1)} %collective-permute-done.7.n0, ...), custom_call_target="tpu_custom_call" | custom-call | flops 3000000000 | bytes 131072 | tf_op jit(solution)/shard_map/piece_weights/pallas_call | solution.py:340
  59.9 3.6 %collective-permute-done.9.refs_1_ = f32[160,256]{1,0:T(8,128)S(1)} collective-permute-done((f32[160,256]{1,0:T(8,128)S(1)}, f32[160,256]{1,0:T(8,128)S(1)}, u32[]{:S(2)}, u32[]{:S(2)}) %collective-permute-start.9) | collective-permute-done | bytes 163872 | tf_op jit(solution)/shard_map/ppermute | solution.py:279
  63.5 0.2 farthest.1
  63.7 5.4 %collective-permute-start.12 = (f32[80,384]{1,0:T(8,128)S(1)}, f32[80,384]{1,0:T(8,128)S(1)}, u32[]{:S(2)}, u32[]{:S(2)}) collective-permute-start(f32[80,384]{1,0:T(8,128)S(1)} %get-tuple-element.36.refs_3_), channel_id=1, source_target_pairs={{0,7},{1,0},{2,1},{3,2},{4,3},{5,4},{6,5},{7,6},{8,15},{9,8},{10,9... | collective-permute-start | bytes 368648 | tf_op jit(solution)/shard_map/ppermute | solution.py:284
  69.1 1.9 %collective-permute-start.16 = (f32[80,384]{1,0:T(8,128)S(1)}, f32[80,384]{1,0:T(8,128)S(1)}, u32[]{:S(2)}, u32[]{:S(2)}) collective-permute-start(f32[80,384]{1,0:T(8,128)S(1)} %get-tuple-element.41), channel_id=1, source_target_pairs={{0,1},{1,2},{2,3},{3,4},{4,5},{5,6},{6,7},{7,0},{8,9},{9,10},{10,1... | collective-permute-start | bytes 368648 | tf_op jit(solution)/shard_map/ppermute | solution.py:284
  71.0 0.8 nearer.1
  71.8 0.0 collective-permute-done.12
  71.9 5.3 %collective-permute-start.13 = (f32[160,384]{1,0:T(8,128)S(1)}, f32[160,384]{1,0:T(8,128)S(1)}, u32[]{:S(2)}, u32[]{:S(2)}) collective-permute-start(f32[160,384]{1,0:T(8,128)S(1)} %pad_add_fusion.1), channel_id=1, source_target_pairs={{0,7},{1,0},{2,1},{3,2},{4,3},{5,4},{6,5},{7,6},{8,15},{9,8},{10,9... | collective-permute-start | bytes 737288 | tf_op jit(solution)/shard_map/ppermute | solution.py:284
  77.1 0.0 collective-permute-done.16
  77.2 1.9 %collective-permute-start.17 = (f32[160,384]{1,0:T(8,128)S(1)}, f32[160,384]{1,0:T(8,128)S(1)}, u32[]{:S(2)}, u32[]{:S(2)}) collective-permute-start(f32[160,384]{1,0:T(8,128)S(1)} %pad_add_fusion), channel_id=1, source_target_pairs={{0,1},{1,2},{2,3},{3,4},{4,5},{5,6},{6,7},{7,0},{8,9},{9,10},{10,1... | collective-permute-start | bytes 737288 | tf_op jit(solution)/shard_map/ppermute | solution.py:284
  79.1 2.3 %collective-permute-done.13 = f32[160,384]{1,0:T(8,128)S(1)} collective-permute-done((f32[160,384]{1,0:T(8,128)S(1)}, f32[160,384]{1,0:T(8,128)S(1)}, u32[]{:S(2)}, u32[]{:S(2)}) %collective-permute-start.13) | collective-permute-done | bytes 245792 | tf_op jit(solution)/shard_map/ppermute | solution.py:284
  81.4 5.6 %collective-permute-start.14 = (f32[160,384]{1,0:T(8,128)S(1)}, f32[160,384]{1,0:T(8,128)S(1)}, u32[]{:S(2)}, u32[]{:S(2)}) collective-permute-start(f32[160,384]{1,0:T(8,128)S(1)} %add.29), channel_id=1, source_target_pairs={{0,7},{1,0},{2,1},{3,2},{4,3},{5,4},{6,5},{7,6},{8,15},{9,8},{10,9... | collective-permute-start | bytes 737288 | tf_op jit(solution)/shard_map/ppermute | solution.py:284
  87.0 0.0 collective-permute-done.17
  87.0 1.9 %collective-permute-start.18 = (f32[160,384]{1,0:T(8,128)S(1)}, f32[160,384]{1,0:T(8,128)S(1)}, u32[]{:S(2)}, u32[]{:S(2)}) collective-permute-start(f32[160,384]{1,0:T(8,128)S(1)} %add.32), channel_id=1, source_target_pairs={{0,1},{1,2},{2,3},{3,4},{4,5},{5,6},{6,7},{7,0},{8,9},{9,10},{10,1... | collective-permute-start | bytes 737288 | tf_op jit(solution)/shard_map/ppermute | solution.py:284
  89.0 1.7 %collective-permute-done.14 = f32[160,384]{1,0:T(8,128)S(1)} collective-permute-done((f32[160,384]{1,0:T(8,128)S(1)}, f32[160,384]{1,0:T(8,128)S(1)}, u32[]{:S(2)}, u32[]{:S(2)}) %collective-permute-start.14) | collective-permute-done | bytes 245792 | tf_op jit(solution)/shard_map/ppermute | solution.py:284
  90.7 5.6 %collective-permute-start.15 = (f32[160,384]{1,0:T(8,128)S(1)}, f32[160,384]{1,0:T(8,128)S(1)}, u32[]{:S(2)}, u32[]{:S(2)}) collective-permute-start(f32[160,384]{1,0:T(8,128)S(1)} %add.30), channel_id=1, source_target_pairs={{0,7},{1,0},{2,1},{3,2},{4,3},{5,4},{6,5},{7,6},{8,15},{9,8},{10,9... | collective-permute-start | bytes 737288 | tf_op jit(solution)/shard_map/ppermute | solution.py:284
  96.3 0.0 collective-permute-done.18
  96.4 1.9 %collective-permute-start.19 = (f32[160,384]{1,0:T(8,128)S(1)}, f32[160,384]{1,0:T(8,128)S(1)}, u32[]{:S(2)}, u32[]{:S(2)}) collective-permute-start(f32[160,384]{1,0:T(8,128)S(1)} %add.33), channel_id=1, source_target_pairs={{0,1},{1,2},{2,3},{3,4},{4,5},{5,6},{6,7},{7,0},{8,9},{9,10},{10,1... | collective-permute-start | bytes 737288 | tf_op jit(solution)/shard_map/ppermute | solution.py:284
  98.3 1.7 %collective-permute-done.15 = f32[160,384]{1,0:T(8,128)S(1)} collective-permute-done((f32[160,384]{1,0:T(8,128)S(1)}, f32[160,384]{1,0:T(8,128)S(1)}, u32[]{:S(2)}, u32[]{:S(2)}) %collective-permute-start.15) | collective-permute-done | bytes 245792 | tf_op jit(solution)/shard_map/ppermute | solution.py:284
  100.0 5.7 %collective-permute-done.19 = f32[160,384]{1,0:T(8,128)S(1)} collective-permute-done((f32[160,384]{1,0:T(8,128)S(1)}, f32[160,384]{1,0:T(8,128)S(1)}, u32[]{:S(2)}, u32[]{:S(2)}) %collective-permute-start.19) | collective-permute-done | bytes 245792 | tf_op jit(solution)/shard_map/ppermute | solution.py:284
  105.7 0.7 add_convert_fusion
  (16 shorter events, 0.2 us)
Async XLA Ops:
  0.0 5.1 %copy-start.5 = (bf16[160,256]{1,0:T(8,128)(2,1)S(1)}, bf16[160,256]{1,0:T(8,128)(2,1)}, u32[]{:S(2)}) copy-start(bf16[160,256]{1,0:T(8,128)(2,1)} %refs_1_.3) | copy-start | bytes 245764
  0.0 5.1 %copy-start.6 = (bf16[160,256]{1,0:T(8,128)(2,1)S(1)}, bf16[160,256]{1,0:T(8,128)(2,1)}, u32[]{:S(2)}) copy-start(bf16[160,256]{1,0:T(8,128)(2,1)} %refs_0_.2) | copy-start | bytes 245764
  0.0 5.1 %copy-start.7 = (f32[2,160]{1,0:T(2,128)S(1)}, f32[2,160]{1,0:T(2,128)}, u32[]{:S(2)}) copy-start(f32[2,160]{1,0:T(2,128)} %refs_2_.3) | copy-start | bytes 3844
  0.0 11.4 %copy-start = (bf16[256,6144]{1,0:T(8,128)(2,1)S(1)}, bf16[256,6144]{1,0:T(8,128)(2,1)}, u32[]{:S(2)}) copy-start(bf16[256,6144]{1,0:T(8,128)(2,1)} %w_hbm.1) | copy-start | bytes 9437188
  3.1 3.2 %collective-permute-start = (f32[128,256]{1,0:T(8,128)S(1)}, f32[128,256]{1,0:T(8,128)S(1)}, u32[]{:S(2)}, u32[]{:S(2)}) collective-permute-start(f32[128,256]{1,0:T(8,128)S(1)} %get-tuple-element.26), channel_id=1, source_target_pairs={{0,16},{16,0},{1,17},{17,1},{2,18},{18,2},{3,19},{19,3},{4,20},{20... | collective-permute-start | bytes 393224 | tf_op jit(solution)/shard_map/ppermute | solution.py:279
  5.5 0.7 copy-start.1
  7.1 10.9 %collective-permute-start.1 = (f32[128,256]{1,0:T(8,128)S(1)}, f32[128,256]{1,0:T(8,128)S(1)}, u32[]{:S(2)}, u32[]{:S(2)}) collective-permute-start(f32[128,256]{1,0:T(8,128)S(1)} %get-tuple-element.29.later_ref.refs_1_), channel_id=1, source_target_pairs={{0,32},{32,0},{64,96},{96,64},{128,160},{160,128},{192,224},{224,1... | collective-permute-start | bytes 393224 | tf_op jit(solution)/shard_map/ppermute | solution.py:305
  12.5 34.4 %collective-permute-start.7 = (f32[64,3072]{1,0:T(8,128)S(1)}, f32[64,3072]{1,0:T(8,128)S(1)}, u32[]{:S(2)}, u32[]{:S(2)}) collective-permute-start(f32[64,3072]{1,0:T(8,128)S(1)} %get-tuple-element.30.refs_3_), channel_id=1, source_target_pairs={{0,8},{8,0},{1,9},{9,1},{2,10},{10,2},{3,11},{11,3},{4,12},{12,4},... | collective-permute-start | bytes 2359304 | tf_op jit(solution)/shard_map/ppermute | solution.py:279
  18.2 11.1 %collective-permute-start.2 = (f32[128,256]{1,0:T(8,128)S(1)}, f32[128,256]{1,0:T(8,128)S(1)}, u32[]{:S(2)}, u32[]{:S(2)}) collective-permute-start(f32[128,256]{1,0:T(8,128)S(1)} %join_chips.1.refs_3_.refs_1_), channel_id=1, source_target_pairs={{0,64},{32,96},{64,0},{96,32},{128,192},{160,224},{192,128},{224,1... | collective-permute-start | bytes 393224 | tf_op jit(solution)/shard_map/ppermute | solution.py:305
  21.7 30.0 %collective-permute-start.10 = (f32[64,3072]{1,0:T(8,128)}, f32[64,3072]{1,0:T(8,128)S(1)}, u32[]{:S(2)}, u32[]{:S(2)}) collective-permute-start(f32[64,3072]{1,0:T(8,128)} %get-tuple-element.35), channel_id=1, source_target_pairs={{0,264},{8,256},{256,8},{264,0},{1,265},{9,257},{257,9},{265,1},{2... | collective-permute-start | bytes 2359304 | tf_op jit(solution)/shard_map/ppermute | solution.py:279
  25.4 11.3 %copy-start.3 = (f32[2,128,128]{2,1,0:T(8,128)S(1)}, f32[2,128,128]{2,1,0:T(8,128)}, u32[]{:S(2)}) copy-start(f32[2,128,128]{2,1,0:T(8,128)} %refs_0_.3) | copy-start | bytes 393220
  29.5 11.1 %collective-permute-start.3 = (f32[128,256]{1,0:T(8,128)S(1)}, f32[128,256]{1,0:T(8,128)S(1)}, u32[]{:S(2)}, u32[]{:S(2)}) collective-permute-start(f32[128,256]{1,0:T(8,128)S(1)} %join_pairs.1.refs_4_.refs_1_.refs_2_), channel_id=1, source_target_pairs={{0,224},{32,192},{64,160},{96,128},{128,96},{160,64},{192,32},{224... | collective-permute-start | bytes 393224 | tf_op jit(solution)/shard_map/ppermute | solution.py:305
  37.0 12.0 %copy-start.4 = (f32[128,256]{1,0:T(8,128)S(1)}, f32[128,256]{1,0:T(8,128)}, u32[]{:S(2)}) copy-start(f32[128,256]{1,0:T(8,128)} %get-tuple-element.31.refs_5_) | copy-start | bytes 393220
  37.0 14.7 %copy-start.2 = (f32[160,512]{1,0:T(8,128)S(1)}, f32[160,512]{1,0:T(8,128)}, u32[]{:S(2)}) copy-start(f32[160,512]{1,0:T(8,128)} %copy-done.1) | copy-start | bytes 983044
  40.9 12.9 %collective-permute-start.6 = (f32[128,128]{1,0:T(8,128)S(1)}, f32[128,128]{1,0:T(8,128)S(1)}, u32[]{:S(2)}, u32[]{:S(2)}) collective-permute-start(f32[128,128]{1,0:T(8,128)S(1)} %join_ring.1.refs_6_.refs_1_), channel_id=1, source_target_pairs={{0,272},{16,256},{1,273},{17,257},{2,274},{18,258},{3,275},{19,259... | collective-permute-start | bytes 196616 | tf_op jit(solution)/shard_map/ppermute | solution.py:332
  44.3 9.5 %collective-permute-start.5 = (f32[128,128]{1,0:T(8,128)S(1)}, f32[128,128]{1,0:T(8,128)}, u32[]{:S(2)}, u32[]{:S(2)}) collective-permute-start(f32[128,128]{1,0:T(8,128)S(1)} %join_ring.1.refs_6_.refs_1_), channel_id=1, source_target_pairs={{0,256},{16,272},{1,257},{17,273},{2,258},{18,274},{3,259},{19,275... | collective-permute-start | bytes 196616 | tf_op jit(solution)/shard_map/ppermute | solution.py:331
  46.9 7.8 %collective-permute-start.8 = (f32[64,3072]{1,0:T(8,128)S(1)}, f32[64,3072]{1,0:T(8,128)S(1)}, u32[]{:S(2)}, u32[]{:S(2)}) collective-permute-start(f32[64,3072]{1,0:T(8,128)S(1)} %collective-permute-done.7.n0), channel_id=1, source_target_pairs={{0,16},{16,0},{1,17},{17,1},{2,18},{18,2},{3,19},{19,3},{4,20},{20... | collective-permute-start | bytes 2359304 | tf_op jit(solution)/shard_map/ppermute | solution.py:279
  49.4 5.3 %collective-permute-start.4 = (f32[128,256]{1,0:T(8,128)S(1)}, f32[128,256]{1,0:T(8,128)S(1)}, u32[]{:S(2)}, u32[]{:S(2)}) collective-permute-start(f32[128,256]{1,0:T(8,128)S(1)} %get-tuple-element.33), channel_id=1, source_target_pairs={{0,16},{16,0},{1,17},{17,1},{2,18},{18,2},{3,19},{19,3},{4,20},{20... | collective-permute-start | bytes 393224 | tf_op jit(solution)/shard_map/ppermute | solution.py:279
  51.7 6.6 %collective-permute-start.11 = (f32[64,3072]{1,0:T(8,128)S(1)}, f32[64,3072]{1,0:T(8,128)S(1)}, u32[]{:S(2)}, u32[]{:S(2)}) collective-permute-start(f32[64,3072]{1,0:T(8,128)S(1)} %collective-permute-done.10.f0), channel_id=1, source_target_pairs={{0,16},{16,0},{1,17},{17,1},{2,18},{18,2},{3,19},{19,3},{4,20},{20... | collective-permute-start | bytes 2359304 | tf_op jit(solution)/shard_map/ppermute | solution.py:279
  55.1 8.4 %collective-permute-start.9 = (f32[160,256]{1,0:T(8,128)S(1)}, f32[160,256]{1,0:T(8,128)S(1)}, u32[]{:S(2)}, u32[]{:S(2)}) collective-permute-start(f32[160,256]{1,0:T(8,128)S(1)} %outputs.1.later_ref.refs_0_), channel_id=1, source_target_pairs={{0,8},{8,0},{1,9},{9,1},{2,10},{10,2},{3,11},{11,3},{4,12},{12,4},... | collective-permute-start | bytes 491528 | tf_op jit(solution)/shard_map/ppermute | solution.py:279
  63.7 8.1 %collective-permute-start.12 = (f32[80,384]{1,0:T(8,128)S(1)}, f32[80,384]{1,0:T(8,128)S(1)}, u32[]{:S(2)}, u32[]{:S(2)}) collective-permute-start(f32[80,384]{1,0:T(8,128)S(1)} %get-tuple-element.36.refs_3_), channel_id=1, source_target_pairs={{0,7},{1,0},{2,1},{3,2},{4,3},{5,4},{6,5},{7,6},{8,15},{9,8},{10,9... | collective-permute-start | bytes 368648 | tf_op jit(solution)/shard_map/ppermute | solution.py:284
  69.1 8.0 %collective-permute-start.16 = (f32[80,384]{1,0:T(8,128)S(1)}, f32[80,384]{1,0:T(8,128)S(1)}, u32[]{:S(2)}, u32[]{:S(2)}) collective-permute-start(f32[80,384]{1,0:T(8,128)S(1)} %get-tuple-element.41), channel_id=1, source_target_pairs={{0,1},{1,2},{2,3},{3,4},{4,5},{5,6},{6,7},{7,0},{8,9},{9,10},{10,1... | collective-permute-start | bytes 368648 | tf_op jit(solution)/shard_map/ppermute | solution.py:284
  71.9 9.5 %collective-permute-start.13 = (f32[160,384]{1,0:T(8,128)S(1)}, f32[160,384]{1,0:T(8,128)S(1)}, u32[]{:S(2)}, u32[]{:S(2)}) collective-permute-start(f32[160,384]{1,0:T(8,128)S(1)} %pad_add_fusion.1), channel_id=1, source_target_pairs={{0,7},{1,0},{2,1},{3,2},{4,3},{5,4},{6,5},{7,6},{8,15},{9,8},{10,9... | collective-permute-start | bytes 737288 | tf_op jit(solution)/shard_map/ppermute | solution.py:284
  77.2 9.8 %collective-permute-start.17 = (f32[160,384]{1,0:T(8,128)S(1)}, f32[160,384]{1,0:T(8,128)S(1)}, u32[]{:S(2)}, u32[]{:S(2)}) collective-permute-start(f32[160,384]{1,0:T(8,128)S(1)} %pad_add_fusion), channel_id=1, source_target_pairs={{0,1},{1,2},{2,3},{3,4},{4,5},{5,6},{6,7},{7,0},{8,9},{9,10},{10,1... | collective-permute-start | bytes 737288 | tf_op jit(solution)/shard_map/ppermute | solution.py:284
  81.4 9.3 %collective-permute-start.14 = (f32[160,384]{1,0:T(8,128)S(1)}, f32[160,384]{1,0:T(8,128)S(1)}, u32[]{:S(2)}, u32[]{:S(2)}) collective-permute-start(f32[160,384]{1,0:T(8,128)S(1)} %add.29), channel_id=1, source_target_pairs={{0,7},{1,0},{2,1},{3,2},{4,3},{5,4},{6,5},{7,6},{8,15},{9,8},{10,9... | collective-permute-start | bytes 737288 | tf_op jit(solution)/shard_map/ppermute | solution.py:284
  87.0 9.3 %collective-permute-start.18 = (f32[160,384]{1,0:T(8,128)S(1)}, f32[160,384]{1,0:T(8,128)S(1)}, u32[]{:S(2)}, u32[]{:S(2)}) collective-permute-start(f32[160,384]{1,0:T(8,128)S(1)} %add.32), channel_id=1, source_target_pairs={{0,1},{1,2},{2,3},{3,4},{4,5},{5,6},{6,7},{7,0},{8,9},{9,10},{10,1... | collective-permute-start | bytes 737288 | tf_op jit(solution)/shard_map/ppermute | solution.py:284
  90.7 9.3 %collective-permute-start.15 = (f32[160,384]{1,0:T(8,128)S(1)}, f32[160,384]{1,0:T(8,128)S(1)}, u32[]{:S(2)}, u32[]{:S(2)}) collective-permute-start(f32[160,384]{1,0:T(8,128)S(1)} %add.30), channel_id=1, source_target_pairs={{0,7},{1,0},{2,1},{3,2},{4,3},{5,4},{6,5},{7,6},{8,15},{9,8},{10,9... | collective-permute-start | bytes 737288 | tf_op jit(solution)/shard_map/ppermute | solution.py:284
  96.4 9.3 %collective-permute-start.19 = (f32[160,384]{1,0:T(8,128)S(1)}, f32[160,384]{1,0:T(8,128)S(1)}, u32[]{:S(2)}, u32[]{:S(2)}) collective-permute-start(f32[160,384]{1,0:T(8,128)S(1)} %add.33), channel_id=1, source_target_pairs={{0,1},{1,2},{2,3},{3,4},{4,5},{5,6},{6,7},{7,0},{8,9},{9,10},{10,1... | collective-permute-start | bytes 737288 | tf_op jit(solution)/shard_map/ppermute | solution.py:284
